TPU v7x, 512 devices: a whole 4x4x16 slice. The times are simulated.
512 devices in a mesh: fsdp: 8 (over x_lo, y), seq: 64 (over x_hi, z, core).
Axes of the slice: x: 4 (x_hi: 2, x_lo: 2; x = x_hi * 2 + x_lo), y: 4, z: 16, core: 2. Of those that a mesh axis runs over, the one named last changes fastest.
Arguments:
- tokens: bfloat16 [8, 64, 256, 1024], P('fsdp', 'seq'), may hold values from -6 to 6
- norm_gain: float32 [1024], replicated, may hold values from 0.1 to 1.9
- w_qkv: bfloat16 [1024, 3072], P('seq', 'fsdp'), may hold values from -0.9832583 to 0.9832583
- w_out: bfloat16 [1024, 1024], P('seq', 'fsdp'), may hold values from -0.1875 to 0.1875
- row_blocks: int32 [8], replicated, may hold values from 1 to 8, as said below
- col_rows: int32 [8], replicated, may hold values from 2 to 64, as said below
Outputs:
- mixed: bfloat16 [8, 64, 256, 1024], P('fsdp', 'seq')
Inputs may be any that keep to these rules, and one draw needn't show every extreme that they name: `row_blocks`: every value from 1 to 8 is taken by some row head. `col_rows`: some column head reaches over all 64 rows and some over exactly 2.
All inputs are finite; a program needn't handle non-finite values.
Results may differ from a plain program's by a relative error of at most 0.0052.
Values may be sent and summed in bfloat16 or wider, within the bound.
No kernel may reach another device: no remote copies, remote signals or barrier semaphores. Data moves between devices by JAX's collectives and lax.ppermute only.
A program may use at most 64 MiB of HBM per device.

v0:
```python
import jax
import jax.numpy as jnp
from jax import lax
from jax.sharding import PartitionSpec as P

BLOCK = 32
HEAD_DIM = 64


def attend_rows(block, row_blocks):
    clips, rows, length, width3 = block.shape
    width = width3 // 3
    heads = width // HEAD_DIM
    query = block[..., :width].reshape(clips, rows, length, heads, HEAD_DIM)
    keys = block[..., width : 2 * width].reshape(clips, rows, length, heads, HEAD_DIM)
    values = block[..., 2 * width :].reshape(clips, rows, length, heads, HEAD_DIM)
    scores = jnp.einsum("crphd,crqhd->crhpq", query, keys, preferred_element_type=jnp.float32)
    scores = scores / jnp.sqrt(jnp.float32(HEAD_DIM))
    where_pos = jnp.arange(length, dtype=jnp.int32)
    later = where_pos[None, :] <= where_pos[:, None]
    reach = (
        where_pos[None, :] // BLOCK >= where_pos[:, None] // BLOCK - row_blocks[:, None, None] + 1
    )
    allowed = later[None] & reach
    scores = jnp.where(allowed, scores, jnp.float32(-1e30))
    top = jnp.max(scores, axis=-1, keepdims=True)
    expo = jnp.exp(scores - top)
    weights = (expo / jnp.sum(expo, axis=-1, keepdims=True)).astype(jnp.bfloat16)
    result = jnp.einsum("crhpq,crqhd->crphd", weights, values, preferred_element_type=jnp.float32)
    return result.astype(jnp.bfloat16).reshape(clips, rows, length, width)


def attend_columns(block, col_rows):
    clips, rows, cols, width3 = block.shape
    width = width3 // 3
    heads = width // HEAD_DIM
    query = block[..., :width].reshape(clips, rows, cols, heads, HEAD_DIM)
    keys = block[..., width : 2 * width].reshape(clips, rows, cols, heads, HEAD_DIM)
    values = block[..., 2 * width :].reshape(clips, rows, cols, heads, HEAD_DIM)
    scores = jnp.einsum("crkhd,cskhd->ckhrs", query, keys, preferred_element_type=jnp.float32)
    scores = scores / jnp.sqrt(jnp.float32(HEAD_DIM))
    where_row = jnp.arange(rows, dtype=jnp.int32)
    earlier = where_row[None, :] <= where_row[:, None]
    reach = where_row[None, None, :] > where_row[None, :, None] - col_rows[:, None, None]
    allowed = earlier[None] & reach
    scores = jnp.where(allowed, scores, jnp.float32(-1e30))
    top = jnp.max(scores, axis=-1, keepdims=True)
    expo = jnp.exp(scores - top)
    weights = (expo / jnp.sum(expo, axis=-1, keepdims=True)).astype(jnp.bfloat16)
    result = jnp.einsum("ckhrs,cskhd->crkhd", weights, values, preferred_element_type=jnp.float32)
    return result.astype(jnp.bfloat16).reshape(clips, rows, cols, width)


def body(tokens, norm_gain, w_qkv, w_out, row_blocks, col_rows):
    part_qkv, part_out = (
        lax.all_gather(w_qkv, "fsdp", axis=1, tiled=True),
        lax.all_gather(w_out, "fsdp", axis=1, tiled=True),
    )
    full_qkv, full_out = (
        lax.all_gather(part_qkv, "seq", axis=0, tiled=True),
        lax.all_gather(part_out, "seq", axis=0, tiled=True),
    )
    inputs = tokens.astype(jnp.float32)
    scale = lax.rsqrt(jnp.mean(inputs * inputs, axis=-1, keepdims=True) + 1e-05)
    normed = (inputs * scale * norm_gain).astype(jnp.bfloat16)
    half = full_qkv.shape[1] // 2
    col_weight = full_qkv[:, half:]
    col_in = jnp.dot(normed, col_weight, preferred_element_type=jnp.float32).astype(jnp.bfloat16)
    col_mid = attend_columns(
        lax.all_to_all(col_in, "seq", split_axis=2, concat_axis=1, tiled=True), col_rows
    )
    row_qkv = jnp.dot(normed, full_qkv[:, :half], preferred_element_type=jnp.float32).astype(
        jnp.bfloat16
    )
    row_out = attend_rows(row_qkv, row_blocks)
    col_out = lax.all_to_all(col_mid, "seq", split_axis=1, concat_axis=2, tiled=True)
    joined = jnp.concatenate([row_out, col_out], axis=-1)
    mixed = inputs + jnp.dot(joined, full_out, preferred_element_type=jnp.float32)
    return mixed.astype(jnp.bfloat16)


def solution(mesh):
    return jax.shard_map(
        body,
        mesh=mesh,
        in_specs=(P("fsdp", "seq", None, None), P(), P("seq", "fsdp"), P("seq", "fsdp"), P(), P()),
        out_specs=P("fsdp", "seq", None, None),
        check_vma=False,
    )
```

profile of v0, /device:TPU:1, one launch (start us, length us, event | category | flops | bytes accessed | tf_op | source)
XLA Modules:
  0.0 403.0 jit_solution(15476564777838999480)
XLA Ops:
  6.5 25.6 %all_gather.12 = bf16[16,3072]{1,0:T(8,128)(2,1)} all-gather(bf16[16,384]{1,0:T(8,128)(2,1)} %param.8), channel_id=1, replica_groups=mesh['fsdp'=8,'seq'=64] {'fsdp'}, dimensions={1}, use_global_device_ids=true | all-gather | bytes 110592 | tf_op jit(solution)/shard_map/all_gather | solution.py:56
  32.2 1.2 fusion.22
  33.4 167.3 %all-gather.3.cloned.1.call-done = bf16[1024,3072]{1,0:T(8,128)(2,1)} async-done(((bf16[16,3072]{1,0:T(8,128)(2,1)}), bf16[1024,3072]{1,0:T(8,128)(2,1)}) %all-gather.3.cloned.1.call-update) | async-done | bytes 6291472 | tf_op jit(solution)/shard_map/all_gather | solution.py:60
  200.7 3.1 fusion.12
  203.8 1.2 copy.64
  205.0 0.5 broadcast.180
  205.6 5.6 %reduce.11 = bf16[256,1536]{1,0:T(8,128)(2,1)S(1)} reduce(bf16[256,1,1,1536]{3,2,1,0:T(2,128)(2,1)S(1)} %bitcast.45, bf16[]{:T(256)} %broadcast.180), dimensions={1,2}, to_apply=%bitcast.44.reduce_sub_computation | reduce | bytes 1572866
  211.2 1.4 reshape.285
  212.7 8.4 %all-to-all-start = ((bf16[64,2,3072]{2,1,0:T(2,128)(2,1)}), bf16[64,2,3072]{2,1,0:T(2,128)(2,1)S(1)}, u32[]{:S(2)}, u32[]{:S(2)}) async-start(bf16[64,2,3072]{2,1,0:T(2,128)(2,1)} %reshape.285), calls=%async_computation | async-start | bytes 1572864 | tf_op jit(solution)/shard_map/all_to_all | solution.py:70
  221.1 21.8 %all_gather.14 = bf16[16,1024]{1,0:T(8,128)(2,1)} all-gather(bf16[16,128]{1,0:T(8,128)(2,1)S(1)} %copy-done.1), channel_id=1, replica_groups=mesh['fsdp'=8,'seq'=64] {'fsdp'}, dimensions={1}, use_global_device_ids=true | all-gather | bytes 36864 | tf_op jit(solution)/shard_map/all_gather | solution.py:57
  243.2 19.8 %all-to-all-done = bf16[64,2,3072]{2,1,0:T(2,128)(2,1)S(1)} async-done(((bf16[64,2,3072]{2,1,0:T(2,128)(2,1)}), bf16[64,2,3072]{2,1,0:T(2,128)(2,1)S(1)}, u32[]{:S(2)}, u32[]{:S(2)}) %all-to-all-start) | async-done | bytes 786464 | tf_op jit(solution)/shard_map/all_to_all | solution.py:70
  263.1 0.6 reshape.286
  263.7 4.6 %bitcast_reduce_fusion = bf16[256,1536]{1,0:T(8,128)(2,1)S(1)} fusion(bf16[256,1,1,1536]{3,2,1,0:T(2,128)(2,1)S(1)} %reshape.286), kind=kLoop, calls=%fused_computation.55 | loop fusion | bytes 1572864 | tf_op jit(solution)/shard_map/all_to_all | solution.py:70
  269.3 0.3 copy.44
  269.6 0.6 fusion.20
  270.5 0.4 convolution_convert_fusion
  270.9 1.0 copy.50
  271.9 8.3 %all-to-all-start.1 = ((bf16[1,64,4,512]{3,2,0,1:T(4,128)(2,1)}), bf16[1,64,4,512]{3,2,0,1:T(4,128)(2,1)S(1)}, u32[]{:S(2)}, u32[]{:S(2)}) async-start(bf16[1,64,4,512]{3,2,0,1:T(4,128)(2,1)} %copy.50), calls=%async_computation.1 | async-start | bytes 524288 | tf_op jit(solution)/shard_map/all_to_all | solution.py:76
  280.2 2.9 fusion.15
  283.6 2.4 fusion.42
  286.0 1.9 convolution_convert_fusion.1
  288.0 16.4 %all-to-all-done.1 = bf16[1,64,4,512]{3,2,0,1:T(4,128)(2,1)S(1)} async-done(((bf16[1,64,4,512]{3,2,0,1:T(4,128)(2,1)}), bf16[1,64,4,512]{3,2,0,1:T(4,128)(2,1)S(1)}, u32[]{:S(2)}, u32[]{:S(2)}) %all-to-all-start.1) | async-done | bytes 262176 | tf_op jit(solution)/shard_map/all_to_all | solution.py:76
  304.5 88.5 %all-gather.5.cloned.1.call-done = bf16[1024,1024]{1,0:T(8,128)(2,1)} async-done(((bf16[16,1024]{1,0:T(8,128)(2,1)}), bf16[1024,1024]{1,0:T(8,128)(2,1)}) %all-gather.5.cloned.1.call-update) | async-done | bytes 2097168 | tf_op jit(solution)/shard_map/all_gather | solution.py:61
  393.0 3.1 fusion.21
  (32 shorter events, 2.3 us)
Async XLA Ops:
  6.5 194.2 %all-gather.3.cloned.1.call-start = ((), (), s32[]{:S(2)}) async-start(), calls=%async_computation.2 | async-start | bytes 6389760 | tf_op jit(solution)/shard_map/all_gather | solution.py:60
  211.2 9.9 %copy-start.1 = (bf16[16,128]{1,0:T(8,128)(2,1)S(1)}, bf16[16,128]{1,0:T(8,128)(2,1)}, u32[]{:S(2)}) copy-start(bf16[16,128]{1,0:T(8,128)(2,1)} %param.9) | copy-start | bytes 12292
  211.2 31.8 %copy-start.2 = (s32[8]{0:T(128)S(1)}, s32[8]{0:T(128)}, u32[]{:S(2)}) copy-start(s32[8]{0:T(128)} %param.11) | copy-start | bytes 100
  211.2 31.9 %copy-start.3 = (s32[8]{0:T(128)S(1)}, s32[8]{0:T(128)}, u32[]{:S(2)}) copy-start(s32[8]{0:T(128)} %param.10) | copy-start | bytes 100
  212.7 50.4 %all-to-all-start = ((bf16[64,2,3072]{2,1,0:T(2,128)(2,1)}), bf16[64,2,3072]{2,1,0:T(2,128)(2,1)S(1)}, u32[]{:S(2)}, u32[]{:S(2)}) async-start(bf16[64,2,3072]{2,1,0:T(2,128)(2,1)} %reshape.285), calls=%async_computation | async-start | bytes 1572864 | tf_op jit(solution)/shard_map/all_to_all | solution.py:70
  221.0 172.0 %all-gather.5.cloned.1.call-start = ((), (), s32[]{:S(2)}) async-start(), calls=%async_computation.3 | async-start | bytes 2129920 | tf_op jit(solution)/shard_map/all_gather | solution.py:61
  270.5 9.6 %copy-start = (bf16[1,1,256,1024]{3,2,1,0:T(8,128)(2,1)S(1)}, bf16[1,1,256,1024]{3,2,1,0:T(8,128)(2,1)}, u32[]{:S(2)}) copy-start(bf16[1,1,256,1024]{3,2,1,0:T(8,128)(2,1)} %param.6) | copy-start | bytes 1572868
  270.5 9.6 %copy-start.4 = (f32[1024]{0:T(1024)S(1)}, f32[1024]{0:T(1024)}, u32[]{:S(2)}) copy-start(f32[1024]{0:T(1024)} %param.7) | copy-start | bytes 12292
  271.9 32.6 %all-to-all-start.1 = ((bf16[1,64,4,512]{3,2,0,1:T(4,128)(2,1)}), bf16[1,64,4,512]{3,2,0,1:T(4,128)(2,1)S(1)}, u32[]{:S(2)}, u32[]{:S(2)}) async-start(bf16[1,64,4,512]{3,2,0,1:T(4,128)(2,1)} %copy.50), calls=%async_computation.1 | async-start | bytes 524288 | tf_op jit(solution)/shard_map/all_to_all | solution.py:76
Sparse Core Ops, SparseCore 0:
  32.3 168.3 all-gather.2
  243.1 149.8 all-gather.4
where the time goes:
time: 403 us
  waiting for transfers between devices  292 us (72%)
  blocking collectives  47.4 us (12%)
  starting transfers between devices  16.7 us (4%)
  matrix products  14.4 us (4%)
  between operations  13.6 us (3%)
  local copies, waits for them, and re-layouts  11.4 us (3%)
  other arithmetic  7.35 us (2%)
    all_gather x1, waiting for transfers between devices, body(): lax.all_gather(part_qkv, 'seq', axis=0, tiled=True)  167 us
    all_gather x1, waiting for transfers between devices, body(): lax.all_gather(part_out, 'seq', axis=0, tiled=True)  88.5 us
    all_gather x1, blocking collectives, body(): lax.all_gather(w_qkv, 'fsdp', axis=1, tiled=True)  25.6 us
    all_gather x1, blocking collectives, body(): lax.all_gather(w_out, 'fsdp', axis=1, tiled=True)  21.8 us
    all_to_all x1, waiting for transfers between devices, body(): lax.all_to_all(col_in, 'seq', split_axis=2, concat_axis=1, tiled=True)  19.8 us
    all_to_all x1, waiting for transfers between devices, body(): lax.all_to_all(col_mid, 'seq', split_axis=1, concat_axis=2, tiled=True)  16.4 us
    all_to_all x1, starting transfers between devices, body(): lax.all_to_all(col_in, 'seq', split_axis=2, concat_axis=1, tiled=True)  8.37 us
    all_to_all x1, starting transfers between devices, body(): lax.all_to_all(col_mid, 'seq', split_axis=1, concat_axis=2, tiled=True)  8.25 us
  transfers between devices with their start and end apart: 4, of which 4 were waited for; matrix products, arithmetic and copies ran while one was open for 4% of the time, Pallas kernels for 0%

commit v1 on v0

v1 whole, which is shorter than its diff:
```python
import functools

import jax
import jax.numpy as jnp
from jax import lax
from jax.experimental import pallas as pl
from jax.experimental.pallas import tpu as pltpu
from jax.sharding import Mesh
from jax.sharding import PartitionSpec as P

XL, Y, XH, Z, C = 2, 4, 2, 16, 2
FEATURES, STRIDE, HEADS, HEAD_DIM, BLOCK = 1024, 256, 8, 64, 32
HALF = HEADS * HEAD_DIM
WIDTH = 3 * HALF
SWAP = [(0, 1), (1, 0)]
FAR = 1 << 20


def attention_kernel(place, reach_ref, gain_ref, x_ref, own_ref, other_ref, out_ref, w_ref, n_ref, qkv_ref):
    by_column = place[0] == 1
    core = place[1]
    for a in range(XL):
        for y in range(Y):
            block = a * Y + y
            cols = pl.ds(y * 384, 384)
            for z in range(Z):
                base = (32 * a + 2 * z) * 16
                mine = pl.multiple_of(base + 16 * core, 16)
                theirs = pl.multiple_of(base + 16 * (1 - core), 16)
                w_ref[pl.ds(mine, 16), cols] = own_ref[block, pl.ds(16 * z, 16), :]
                w_ref[pl.ds(theirs, 16), cols] = other_ref[block, pl.ds(16 * z, 16), :]

    def norm(i, _):
        rows = pl.ds(pl.multiple_of(i * 64, 64), 64)
        x = x_ref[rows, :].astype(jnp.float32)
        scale = lax.rsqrt(jnp.mean(x * x, axis=-1, keepdims=True) + 1e-05)
        n_ref[rows, :] = (x * scale * gain_ref[...]).astype(jnp.bfloat16)
        return 0

    lax.fori_loop(0, 8, norm, 0)

    def project(i, _):
        cols = pl.ds(pl.multiple_of(i * 256, 256), 256)
        qkv_ref[:, cols] = jnp.dot(
            n_ref[...], w_ref[:, cols], preferred_element_type=jnp.float32
        ).astype(jnp.bfloat16)
        return 0

    lax.fori_loop(0, WIDTH // 256, project, 0)

    i = lax.broadcasted_iota(jnp.int32, (STRIDE, STRIDE), 0)
    j = lax.broadcasted_iota(jnp.int32, (STRIDE, STRIDE), 1)
    back = (i >> 3) - (j >> 3)
    same = ((i ^ j) & 7) == 0
    in_row = jnp.where(j <= i, (i >> 5) - (j >> 5), FAR)
    near = jnp.where(same & (back >= 0), back, FAR)
    near = jnp.where(by_column, near, in_row)
    far = jnp.where(same & by_column, back + 32, FAR)

    for h in range(HEADS):
        reach = jnp.where(by_column, reach_ref[1, h], reach_ref[0, h])
        q = qkv_ref[:, h * 64 : h * 64 + 64]
        k = qkv_ref[:, HALF + h * 64 : HALF + h * 64 + 64]
        v = qkv_ref[:, 2 * HALF + h * 64 : 2 * HALF + h * 64 + 64]
        contract = (((1,), (1,)), ((), ()))

        def scores(qs, ks, dist):
            s = lax.dot_general(qs, ks, contract, preferred_element_type=jnp.float32)
            return jnp.where(dist < reach, s * 0.125, -1e30)

        qa, qb, ka, kb, va, vb = q[:256], q[256:], k[:256], k[256:], v[:256], v[256:]
        saa, sab, sbb = scores(qa, ka, near), scores(qa, kb, far), scores(qb, kb, near)
        ma = jnp.maximum(
            jnp.max(saa, axis=-1, keepdims=True), jnp.max(sab, axis=-1, keepdims=True)
        )
        mb = jnp.max(sbb, axis=-1, keepdims=True)
        paa, pab, pbb = jnp.exp(saa - ma), jnp.exp(sab - ma), jnp.exp(sbb - mb)
        la = jnp.sum(paa, axis=-1, keepdims=True) + jnp.sum(pab, axis=-1, keepdims=True)
        lb = jnp.sum(pbb, axis=-1, keepdims=True)
        oa = jnp.dot(paa.astype(jnp.bfloat16), va, preferred_element_type=jnp.float32)
        oa = oa + jnp.dot(pab.astype(jnp.bfloat16), vb, preferred_element_type=jnp.float32)
        ob = jnp.dot(pbb.astype(jnp.bfloat16), vb, preferred_element_type=jnp.float32)
        out_ref[:256, h * 64 : h * 64 + 64] = (oa / la).astype(jnp.bfloat16)
        out_ref[256:, h * 64 : h * 64 + 64] = (ob / lb).astype(jnp.bfloat16)


def attention(place, reach, gain, x, own, other):
    vmem = pl.BlockSpec(memory_space=pltpu.VMEM)
    smem = pl.BlockSpec(memory_space=pltpu.SMEM)
    return pl.pallas_call(
        attention_kernel,
        out_shape=jax.ShapeDtypeStruct((2 * STRIDE, HALF), jnp.bfloat16),
        in_specs=[smem, smem, vmem, vmem, vmem, vmem],
        out_specs=vmem,
        scratch_shapes=[
            pltpu.VMEM((FEATURES, WIDTH), jnp.bfloat16),
            pltpu.VMEM((2 * STRIDE, FEATURES), jnp.bfloat16),
            pltpu.VMEM((2 * STRIDE, WIDTH), jnp.bfloat16),
        ],
        compiler_params=pltpu.CompilerParams(vmem_limit_bytes=40 * 1024 * 1024),
        cost_estimate=pl.CostEstimate(
            flops=2 * 512 * 1024 * 1536 + 16 * 3 * 256 * 256 * 128,
            bytes_accessed=6 << 20,
            transcendentals=8 * 3 * 256 * 256,
        ),
        name="attention",
    )(place, reach, gain, x, own, other)


def body(tokens, norm_gain, w_qkv, w_out, row_blocks, col_rows):
    xh, c = lax.axis_index("xh"), lax.axis_index("c")
    by_column = xh == 1
    rows = tokens.reshape(STRIDE, FEATURES)

    block = jnp.concatenate([w_qkv, w_out], axis=1)
    block = lax.ppermute(block, ("xl", "xh"), [(0, 0), (1, 2), (2, 1), (3, 3)])

    send = jnp.concatenate(
        [rows.reshape(Z, 16, FEATURES), jnp.broadcast_to(block, (Z, 16, 512))], axis=2
    )
    recv = lax.all_to_all(send, "z", split_axis=0, concat_axis=0)
    turned = recv[:, :, :FEATURES]
    part_qkv = recv[:, :, FEATURES : FEATURES + 384].reshape(Z * 16, 384)
    part_out = recv[:, :, FEATURES + 384 :].reshape(Z * 16, 128)

    own = lax.all_to_all(
        jnp.broadcast_to(part_qkv, (XL * Y, Z * 16, 384)), ("xl", "y"), split_axis=0, concat_axis=0
    )
    other = lax.ppermute(own, "c", SWAP)
    out_own = lax.all_gather(part_out, ("xl", "y", "xh"), axis=0)

    straight = rows.reshape(Z, 16, FEATURES)
    mine = jnp.where(by_column, turned, straight)
    given = jnp.where(by_column, straight, turned)
    both = jnp.stack([mine, lax.ppermute(given, "xh", SWAP)])
    low, high = both[:, :, :8], both[:, :, 8:]
    keep = jnp.where(c == 0, low, high)
    got = lax.ppermute(jnp.where(c == 0, high, low), "c", SWAP)
    even, odd = jnp.where(c == 0, keep, got), jnp.where(c == 0, got, keep)
    columns = jnp.stack([even, odd], axis=2).reshape(2 * STRIDE, FEATURES)
    x = jnp.where(by_column, columns, both.reshape(2 * STRIDE, FEATURES))

    place = jnp.stack([xh, c]).astype(jnp.int32)
    reach = jnp.stack([row_blocks, col_rows])
    out = attention(place, reach, norm_gain.reshape(1, FEATURES), x, own, other)

    back = lax.ppermute(out[STRIDE:], "xh", SWAP)
    row_out = jnp.where(by_column, back, out[:STRIDE])
    col_mid = jnp.where(by_column, out[:STRIDE], back)
    col_out = lax.all_to_all(
        col_mid.reshape(Z * C, 8, HALF), ("z", "c"), split_axis=0, concat_axis=0
    ).reshape(STRIDE, HALF)

    out_other = lax.ppermute(out_own, "c", SWAP)
    pair = jnp.where(c == 0, jnp.stack([out_own, out_other]), jnp.stack([out_other, out_own]))
    full_out = pair.reshape(C, XL, Y, XH, Z, 16, 128).transpose(1, 4, 0, 5, 3, 2, 6)
    full_out = full_out.reshape(FEATURES, FEATURES)

    joined = jnp.concatenate([row_out, col_out], axis=1)
    mixed = rows.astype(jnp.float32) + jnp.dot(joined, full_out, preferred_element_type=jnp.float32)
    return mixed.astype(jnp.bfloat16).reshape(tokens.shape)


def solution(mesh):
    fine = Mesh(mesh.devices.reshape(XL, Y, XH, Z, C), ("xl", "y", "xh", "z", "c"))
    fsdp, seq = ("xl", "y"), ("xh", "z", "c")
    return jax.shard_map(
        body,
        mesh=fine,
        in_specs=(P(fsdp, seq, None, None), P(), P(seq, fsdp), P(seq, fsdp), P(), P()),
        out_specs=P(fsdp, seq, None, None),
        check_vma=False,
    )
```

time: 403 us -> 233 us (0.58)
  waiting for transfers between devices: 292 us -> 76.9 us
  starting transfers between devices: 16.7 us -> 59.2 us
  matrix products: 14.4 us -> 3.1 us
  Pallas kernels: 0 us -> 9.19 us
    all_gather x2 -> x1, waiting for transfers between devices: 256 us -> 50.2 us  [body(): out_own = lax.all_gather(part_out, ('xl', 'y', 'xh'), axis=0)]
    all_to_all x0 -> x1, blocking collectives: none -> 50.5 us  [body(): recv = lax.all_to_all(send, 'z', split_axis=0, concat_axis=0)]
    all_gather x2 -> x0, blocking collectives: 47.4 us -> none  [the longest x1 25.6 us: body(): lax.all_gather(w_qkv, 'fsdp', axis=1, tiled=True)]
    ppermute x0 -> x6, starting transfers between devices: none -> 36.7 us  [the longest x1 12.5 us: body(): other = lax.ppermute(own, 'c', SWAP)]
    all_to_all x2, waiting for transfers between devices: 36.3 us -> 26.6 us  [the longest x1 16.2 us: body(): lax.all_to_all(col_mid.reshape(Z * C, 8, HALF), ('z', 'c'), split_axis=0,...]
    pallas_call x0 -> x1, Pallas kernels: none -> 9.19 us  [attention(): pl.pallas_call(attention_kernel, out_shape=jax.ShapeDtypeStruct((2 * STRI...]
    dot_general x5 -> x0, matrix products: 8.92 us -> none  [the longest x1 3.12 us: body(): jnp.dot(normed, col_weight, preferred_element_type=jnp.float32)]
    all_to_all x2, starting transfers between devices: 16.6 us -> 22.4 us  [the longest x1 13.3 us: body(): lax.all_to_all(col_mid.reshape(Z * C, 8, HALF), ('z', 'c'), split_axis=0,...]
  transfers between devices with their start and end apart: 4 -> 9, of which waited for: 4 -> 4; matrix products, arithmetic and copies ran while one was open for 4% -> 6% of each run, Pallas kernels for 0% -> 4%
where the time goes in v1:
time: 233 us; the launch traced here: 232 us
  waiting for transfers between devices  76.9 us (33%)
  starting transfers between devices  59.2 us (25%)
  blocking collectives  50.5 us (22%)
  between operations  13.7 us (6%)
  local copies, waits for them, and re-layouts  11 us (5%)
  Pallas kernels  9.19 us (4%)
  other arithmetic  8.49 us (4%)
  matrix products  3.1 us (1%)
    all_to_all x1, blocking collectives, body(): recv = lax.all_to_all(send, 'z', split_axis=0, concat_axis=0)  50.5 us
    all_gather x1, waiting for transfers between devices, body(): out_own = lax.all_gather(part_out, ('xl', 'y', 'xh'), axis=0)  50.2 us
    all_to_all x1, waiting for transfers between devices, body(): lax.all_to_all(col_mid.reshape(Z * C, 8, HALF), ('z', 'c'), split_axis=0,...  16.2 us
    all_to_all x1, starting transfers between devices, body(): lax.all_to_all(col_mid.reshape(Z * C, 8, HALF), ('z', 'c'), split_axis=0,...  13.3 us
    ppermute x1, starting transfers between devices, body(): other = lax.ppermute(own, 'c', SWAP)  12.5 us
    ppermute x1, starting transfers between devices, body(): out_other = lax.ppermute(out_own, 'c', SWAP)  12.3 us
    all_to_all x1, waiting for transfers between devices, body(): lax.all_to_all(jnp.broadcast_to(part_qkv, (XL * Y, Z * 16, 384)), ('xl',...  10.4 us
    all_to_all x1, starting transfers between devices, body(): lax.all_to_all(jnp.broadcast_to(part_qkv, (XL * Y, Z * 16, 384)), ('xl',...  9.19 us
  transfers between devices with their start and end apart: 9, of which 4 were waited for; matrix products, arithmetic and copies ran while one was open for 6% of the time, Pallas kernels for 4%

profile of v1, /device:TPU:1, one launch (start us, length us, event | category | flops | bytes accessed | tf_op | source)
XLA Modules:
  0.0 232.0 jit_solution(1478409830036050572)
XLA Ops:
  8.0 1.1 pad_maximum_fusion.2
  9.1 50.5 %all_to_all.15 = bf16[16,16,1536]{2,1,0:T(8,128)(2,1)S(1)} all-to-all(bf16[16,16,1536]{2,1,0:T(8,128)(2,1)S(1)} %pad_maximum_fusion.2), channel_id=1, replica_groups=mesh['xl'=2,'y'=4,'xh'=2,'z'=16,'c'=2] {'z'}, dimensions={0} | all-to-all | bytes 1572864 | tf_op jit(solution)/shard_map/all_to_all | solution.py:121
  59.6 1.3 broadcast_in_dim.7
  60.9 9.2 %all-to-all-start.1 = ((bf16[8,256,384]{2,1,0:T(8,128)(2,1)}), bf16[8,256,384]{2,1,0:T(8,128)(2,1)S(1)}, u32[]{:S(2)}, u32[]{:S(2)}) async-start(bf16[8,256,384]{2,1,0:T(8,128)(2,1)} %broadcast_in_dim.7), calls=%async_computation.1 | async-start | bytes 3145728 | tf_op jit(solution)/shard_map/all_to_all | solution.py:126
  70.2 1.0 select_bitcast_fusion.2
  71.2 3.7 %collective-permute-start.1 = (bf16[16,16,1024]{2,1,0:T(8,128)(2,1)}, bf16[16,16,1024]{2,1,0:T(8,128)(2,1)}, u32[]{:S(2)}, u32[]{:S(2)}) collective-permute-start(bf16[16,16,1024]{2,1,0:T(8,128)(2,1)} %get-tuple-element.8), channel_id=1, source_target_pairs={{0,32},{32,0},{1,33},{33,1},{2,34},{34,2},{3,35},{35,3},{4,36},{36... | collective-permute-start | bytes 1572872 | tf_op jit(solution)/shard_map/ppermute | solution.py:135
  74.9 10.4 %all-to-all-done.1.own_ref = bf16[8,256,384]{2,1,0:T(8,128)(2,1)S(1)} async-done(((bf16[8,256,384]{2,1,0:T(8,128)(2,1)}), bf16[8,256,384]{2,1,0:T(8,128)(2,1)S(1)}, u32[]{:S(2)}, u32[]{:S(2)}) %all-to-all-start.1) | async-done | bytes 1572896 | tf_op jit(solution)/shard_map/all_to_all | solution.py:126
  85.4 12.5 %collective-permute-start.3 = (bf16[8,256,384]{2,1,0:T(8,128)(2,1)S(1)}, bf16[8,256,384]{2,1,0:T(8,128)(2,1)S(1)}, u32[]{:S(2)}, u32[]{:S(2)}) collective-permute-start(bf16[8,256,384]{2,1,0:T(8,128)(2,1)S(1)} %all-to-all-done.1.own_ref), channel_id=1, source_target_pairs={{0,1},{1,0},{2,3},{3,2},{4,5},{5,4},{6,7},{7,6},{8,9},{9,8},{10,11... | collective-permute-start | bytes 4718600 | tf_op jit(solution)/shard_map/ppermute | solution.py:129
  97.8 1.5 slice.37
  99.4 1.3 broadcast_select_fusion.1
  100.7 4.5 %collective-permute-start.2 = (bf16[2,16,8,1024]{3,2,1,0:T(8,128)(2,1)S(1)}, bf16[2,16,8,1024]{3,2,1,0:T(8,128)(2,1)S(1)}, u32[]{:S(2)}, u32[]{:S(2)}) collective-permute-start(bf16[2,16,8,1024]{3,2,1,0:T(8,128)(2,1)S(1)} %broadcast_select_fusion.1), channel_id=1, source_target_pairs={{0,1},{1,0},{2,3},{3,2},{4,5},{5,4},{6,7},{7,6},{8,9},{9,8},{10,11... | collective-permute-start | bytes 1572872 | tf_op jit(solution)/shard_map/ppermute | solution.py:138
  105.3 1.3 pad_maximum_fusion
  106.7 1.4 select_bitcast_fusion.1
  108.6 1.2 copy-done
  109.8 1.4 copy-done.1
  111.2 9.2 %attention.1 = bf16[512,512]{1,0:T(8,128)(2,1)S(1)} custom-call(s32[2]{0:T(128)S(1)} %pad_add_fusion.1.place, s32[2,8]{1,0:T(2,128)S(1)} %pad_add_fusion.reach_ref, f32[1,1024]{1,0:T(1,128)S(1)} %bitcast.32, bf16[512,1024]{1,0:T(8,128)(2,1)S(1)} %bitcast_select_fusion.x_ref, bf16[8,256,384]{2,1,0:T(8,128)(2,1)S(1)} %all-to-all-done.1.own_ref, ...), custom_call_target="tpu_custom_call" | custom-call | flops 2013265920 | bytes 6291456 | tf_op jit(solution)/shard_map/attention/pallas_call | solution.py:90
  120.4 3.1 %collective-permute-start.4 = (bf16[256,512]{1,0:T(8,128)(2,1)S(1)}, bf16[256,512]{1,0:T(8,128)(2,1)S(1)}, u32[]{:S(2)}, u32[]{:S(2)}) collective-permute-start(bf16[256,512]{1,0:T(8,128)(2,1)S(1)} %slice.35), channel_id=1, source_target_pairs={{0,32},{32,0},{1,33},{33,1},{2,34},{34,2},{3,35},{35,3},{4,36},{36... | collective-permute-start | bytes 786440 | tf_op jit(solution)/shard_map/ppermute | solution.py:147
  123.5 50.2 %all-gather.2.cloned.1.call-done = bf16[16,256,128]{2,1,0:T(8,128)(2,1)} async-done(((bf16[1,256,128]{2,1,0:T(8,128)(2,1)}), bf16[16,256,128]{2,1,0:T(8,128)(2,1)}) %all-gather.2.cloned.1.call-update) | async-done | bytes 1048592 | tf_op jit(solution)/shard_map/all_gather | solution.py:130
  173.7 12.3 %collective-permute-start.5 = (bf16[16,256,128]{2,1,0:T(8,128)(2,1)}, bf16[16,256,128]{2,1,0:T(8,128)(2,1)S(1)}, u32[]{:S(2)}, u32[]{:S(2)}) collective-permute-start(bf16[16,256,128]{2,1,0:T(8,128)(2,1)} %all-gather.2.cloned.1.call-done), channel_id=1, source_target_pairs={{0,1},{1,0},{2,3},{3,2},{4,5},{5,4},{6,7},{7,6},{8,9},{9,8},{10,11... | collective-permute-start | bytes 3145736 | tf_op jit(solution)/shard_map/ppermute | solution.py:154
  186.8 13.3 %all-to-all-start.2 = ((bf16[32,8,512]{2,1,0:T(8,128)(2,1)}), bf16[32,8,512]{2,1,0:T(8,128)(2,1)S(1)}, u32[]{:S(2)}, u32[]{:S(2)}) async-start(bf16[32,8,512]{2,1,0:T(8,128)(2,1)} %get-tuple-element.10), calls=%async_computation.2 | async-start | bytes 524288 | tf_op jit(solution)/shard_map/all_to_all | solution.py:150
  200.5 2.7 %copy.12 = bf16[2,16,2,16,2,4,128]{6,5,4,3,2,1,0:T(4,128)(2,1)S(1)} copy(bf16[2,16,2,16,2,4,128]{6,3,1,4,5,0,2:T(8,128)(2,1)S(1)} %fusion) | data formatting | bytes 4194304 | tf_op jit(solution)/shard_map/transpose | solution.py:156
  203.2 2.7 %reshape.42 = bf16[1024,1024]{1,0:T(8,128)(2,1)} reshape(bf16[2,16,2,16,2,4,128]{6,5,4,3,2,1,0:T(4,128)(2,1)S(1)} %copy.12) | data formatting | bytes 4194304 | tf_op jit(solution)/shard_map/reshape | solution.py:157
  205.9 16.2 %all-to-all-done.2 = bf16[32,8,512]{2,1,0:T(8,128)(2,1)S(1)} async-done(((bf16[32,8,512]{2,1,0:T(8,128)(2,1)}), bf16[32,8,512]{2,1,0:T(8,128)(2,1)S(1)}, u32[]{:S(2)}, u32[]{:S(2)}) %all-to-all-start.2) | async-done | bytes 262176 | tf_op jit(solution)/shard_map/all_to_all | solution.py:150
  222.1 3.1 %fusion.2 = bf16[1,1,256,1024]{3,2,1,0:T(8,128)(2,1)} fusion(bf16[1024,1024]{1,0:T(8,128)(2,1)} %reshape.42, bf16[256,512]{1,0:T(8,128)(2,1)S(1)} %bitcast.38, bf16[256,512]{1,0:T(8,128)(2,1)S(1)} %copy-done.8, bf16[1,1,256,1024]{3,2,1,0:T(8,128)(2,1)S(1)} %copy-done.6), kind=kOutput, calls=%fused_computation.9 | convolution fusion | flops 538705920 | bytes 3670016 | tf_op jit(solution)/shard_map/dot_general | solution.py:160
  (40 shorter events, 3.4 us)
Async XLA Ops:
  7.3 0.7 collective-permute-start
  59.5 15.4 %copy-start.4 = (bf16[16,16,1536]{2,1,0:T(8,128)(2,1)}, bf16[16,16,1536]{2,1,0:T(8,128)(2,1)S(1)}, u32[]{:S(2)}) copy-start(bf16[16,16,1536]{2,1,0:T(8,128)(2,1)S(1)} %all_to_all.15) | copy-start | bytes 2359300
  59.5 10.6 %copy-start.5 = (bf16[1,1,256,1024]{3,2,1,0:T(8,128)(2,1)S(1)}, bf16[1,1,256,1024]{3,2,1,0:T(8,128)(2,1)}, u32[]{:S(2)}) copy-start(bf16[1,1,256,1024]{3,2,1,0:T(8,128)(2,1)} %param.6) | copy-start | bytes 1572868
  60.9 24.5 %all-to-all-start.1 = ((bf16[8,256,384]{2,1,0:T(8,128)(2,1)}), bf16[8,256,384]{2,1,0:T(8,128)(2,1)S(1)}, u32[]{:S(2)}, u32[]{:S(2)}) async-start(bf16[8,256,384]{2,1,0:T(8,128)(2,1)} %broadcast_in_dim.7), calls=%async_computation.1 | async-start | bytes 3145728 | tf_op jit(solution)/shard_map/all_to_all | solution.py:126
  70.1 35.2 %copy-start.9 = (s32[8]{0:T(128)S(1)}, s32[8]{0:T(128)}, u32[]{:S(2)}) copy-start(s32[8]{0:T(128)} %param.11) | copy-start | bytes 100
  70.1 35.2 %copy-start.10 = (s32[8]{0:T(128)S(1)}, s32[8]{0:T(128)}, u32[]{:S(2)}) copy-start(s32[8]{0:T(128)} %param.10) | copy-start | bytes 100
  70.1 103.6 %all-gather.2.cloned.1.call-start = ((), (), s32[]{:S(2)}) async-start(), calls=%async_computation.3 | async-start | bytes 1114112 | tf_op jit(solution)/shard_map/all_gather | solution.py:130
  71.2 28.2 %collective-permute-start.1 = (bf16[16,16,1024]{2,1,0:T(8,128)(2,1)}, bf16[16,16,1024]{2,1,0:T(8,128)(2,1)}, u32[]{:S(2)}, u32[]{:S(2)}) collective-permute-start(bf16[16,16,1024]{2,1,0:T(8,128)(2,1)} %get-tuple-element.8), channel_id=1, source_target_pairs={{0,32},{32,0},{1,33},{33,1},{2,34},{34,2},{3,35},{35,3},{4,36},{36... | collective-permute-start | bytes 1572872 | tf_op jit(solution)/shard_map/ppermute | solution.py:135
  85.4 23.2 %collective-permute-start.3 = (bf16[8,256,384]{2,1,0:T(8,128)(2,1)S(1)}, bf16[8,256,384]{2,1,0:T(8,128)(2,1)S(1)}, u32[]{:S(2)}, u32[]{:S(2)}) collective-permute-start(bf16[8,256,384]{2,1,0:T(8,128)(2,1)S(1)} %all-to-all-done.1.own_ref), channel_id=1, source_target_pairs={{0,1},{1,0},{2,3},{3,2},{4,5},{5,4},{6,7},{7,6},{8,9},{9,8},{10,11... | collective-permute-start | bytes 4718600 | tf_op jit(solution)/shard_map/ppermute | solution.py:129
  99.4 7.4 %copy-start.3 = (bf16[1,16,16,1024]{3,2,1,0:T(8,128)(2,1)S(1)}, bf16[1,16,16,1024]{3,2,1,0:T(8,128)(2,1)}, u32[]{:S(2)}) copy-start(bf16[1,16,16,1024]{3,2,1,0:T(8,128)(2,1)} %get-tuple-element.7) | copy-start | bytes 1572868
  100.7 6.0 %collective-permute-start.2 = (bf16[2,16,8,1024]{3,2,1,0:T(8,128)(2,1)S(1)}, bf16[2,16,8,1024]{3,2,1,0:T(8,128)(2,1)S(1)}, u32[]{:S(2)}, u32[]{:S(2)}) collective-permute-start(bf16[2,16,8,1024]{3,2,1,0:T(8,128)(2,1)S(1)} %broadcast_select_fusion.1), channel_id=1, source_target_pairs={{0,1},{1,0},{2,3},{3,2},{4,5},{5,4},{6,7},{7,6},{8,9},{9,8},{10,11... | collective-permute-start | bytes 1572872 | tf_op jit(solution)/shard_map/ppermute | solution.py:138
  108.3 1.5 copy-start.2
  108.6 1.2 copy-start
  109.8 1.4 copy-start.1
  120.4 65.6 %collective-permute-start.4 = (bf16[256,512]{1,0:T(8,128)(2,1)S(1)}, bf16[256,512]{1,0:T(8,128)(2,1)S(1)}, u32[]{:S(2)}, u32[]{:S(2)}) collective-permute-start(bf16[256,512]{1,0:T(8,128)(2,1)S(1)} %slice.35), channel_id=1, source_target_pairs={{0,32},{32,0},{1,33},{33,1},{2,34},{34,2},{3,35},{35,3},{4,36},{36... | collective-permute-start | bytes 786440 | tf_op jit(solution)/shard_map/ppermute | solution.py:147
  173.7 26.5 %copy-start.7 = (bf16[16,256,128]{2,1,0:T(8,128)(2,1)S(1)}, bf16[16,256,128]{2,1,0:T(8,128)(2,1)}, u32[]{:S(2)}) copy-start(bf16[16,256,128]{2,1,0:T(8,128)(2,1)} %all-gather.2.cloned.1.call-done) | copy-start | bytes 3145732
  173.7 26.5 %collective-permute-start.5 = (bf16[16,256,128]{2,1,0:T(8,128)(2,1)}, bf16[16,256,128]{2,1,0:T(8,128)(2,1)S(1)}, u32[]{:S(2)}, u32[]{:S(2)}) collective-permute-start(bf16[16,256,128]{2,1,0:T(8,128)(2,1)} %all-gather.2.cloned.1.call-done), channel_id=1, source_target_pairs={{0,1},{1,0},{2,3},{3,2},{4,5},{5,4},{6,7},{7,6},{8,9},{9,8},{10,11... | collective-permute-start | bytes 3145736 | tf_op jit(solution)/shard_map/ppermute | solution.py:154
  186.8 35.3 %all-to-all-start.2 = ((bf16[32,8,512]{2,1,0:T(8,128)(2,1)}), bf16[32,8,512]{2,1,0:T(8,128)(2,1)S(1)}, u32[]{:S(2)}, u32[]{:S(2)}) async-start(bf16[32,8,512]{2,1,0:T(8,128)(2,1)} %get-tuple-element.10), calls=%async_computation.2 | async-start | bytes 524288 | tf_op jit(solution)/shard_map/all_to_all | solution.py:150
  203.2 18.9 %copy-start.6 = (bf16[1,1,256,1024]{3,2,1,0:T(8,128)(2,1)S(1)}, bf16[1,1,256,1024]{3,2,1,0:T(8,128)(2,1)}, u32[]{:S(2)}) copy-start(bf16[1,1,256,1024]{3,2,1,0:T(8,128)(2,1)} %param.6) | copy-start | bytes 1572868
  203.2 18.9 %copy-start.8 = (bf16[256,512]{1,0:T(8,128)(2,1)S(1)}, bf16[256,512]{1,0:T(8,128)(2,1)}, u32[]{:S(2)}) copy-start(bf16[256,512]{1,0:T(8,128)(2,1)} %get-tuple-element.9) | copy-start | bytes 786436
Sparse Core Ops, SparseCore 0:
  99.5 74.1 all-gather.1

commit v2 on v1

--- a/solution.py
+++ b/solution.py
@@ -27,8 +27,8 @@
                 base = (32 * a + 2 * z) * 16
                 mine = pl.multiple_of(base + 16 * core, 16)
                 theirs = pl.multiple_of(base + 16 * (1 - core), 16)
-                w_ref[pl.ds(mine, 16), cols] = own_ref[block, pl.ds(16 * z, 16), :]
-                w_ref[pl.ds(theirs, 16), cols] = other_ref[block, pl.ds(16 * z, 16), :]
+                w_ref[pl.ds(mine, 16), cols] = own_ref[block, pl.ds(16 * z, 16), :384]
+                w_ref[pl.ds(theirs, 16), cols] = other_ref[block, pl.ds(16 * z, 16), :384]
 
     def norm(i, _):
         rows = pl.ds(pl.multiple_of(i * 64, 64), 64)
@@ -120,14 +120,12 @@
     )
     recv = lax.all_to_all(send, "z", split_axis=0, concat_axis=0)
     turned = recv[:, :, :FEATURES]
-    part_qkv = recv[:, :, FEATURES : FEATURES + 384].reshape(Z * 16, 384)
-    part_out = recv[:, :, FEATURES + 384 :].reshape(Z * 16, 128)
+    part = recv[:, :, FEATURES:].reshape(Z * 16, 512)
 
     own = lax.all_to_all(
-        jnp.broadcast_to(part_qkv, (XL * Y, Z * 16, 384)), ("xl", "y"), split_axis=0, concat_axis=0
+        jnp.broadcast_to(part, (XL * Y, Z * 16, 512)), ("xl", "y"), split_axis=0, concat_axis=0
     )
     other = lax.ppermute(own, "c", SWAP)
-    out_own = lax.all_gather(part_out, ("xl", "y", "xh"), axis=0)
 
     straight = rows.reshape(Z, 16, FEATURES)
     mine = jnp.where(by_column, turned, straight)
@@ -151,9 +149,15 @@
         col_mid.reshape(Z * C, 8, HALF), ("z", "c"), split_axis=0, concat_axis=0
     ).reshape(STRIDE, HALF)
 
-    out_other = lax.ppermute(out_own, "c", SWAP)
-    pair = jnp.where(c == 0, jnp.stack([out_own, out_other]), jnp.stack([out_other, out_own]))
-    full_out = pair.reshape(C, XL, Y, XH, Z, 16, 128).transpose(1, 4, 0, 5, 3, 2, 6)
+    out_own, out_other = own[:, :, 384:], other[:, :, 384:]
+    far_own = lax.ppermute(out_own, "xh", SWAP)
+    far_other = lax.ppermute(far_own, "c", SWAP)
+
+    def ordered(where, mine, theirs):
+        return jnp.where(where == 0, jnp.stack([mine, theirs]), jnp.stack([theirs, mine]))
+
+    pair = ordered(c, ordered(xh, out_own, far_own), ordered(xh, out_other, far_other))
+    full_out = pair.reshape(C, XH, XL, Y, Z, 16, 128).transpose(2, 4, 0, 5, 1, 3, 6)
     full_out = full_out.reshape(FEATURES, FEATURES)
 
     joined = jnp.concatenate([row_out, col_out], axis=1)

time: 233 us -> 181 us (0.78)
  waiting for transfers between devices: 76.9 us -> 52.7 us
  between operations: 13.7 us -> 0.29 us
  starting transfers between devices: 59.2 us -> 47.4 us
  local copies, waits for them, and re-layouts: 11 us -> 7.25 us
    all_gather x1 -> x0, waiting for transfers between devices: 50.2 us -> none  [body(): out_own = lax.all_gather(part_out, ('xl', 'y', 'xh'), axis=0)]
    ppermute x1, waiting for transfers between devices: 0.01 us -> 13.4 us  [body(): both = jnp.stack([mine, lax.ppermute(given, 'xh', SWAP)])]
    all_to_all x1, waiting for transfers between devices: 10.4 us -> 20.5 us  [body(): lax.all_to_all(jnp.broadcast_to(part, (XL * Y, Z * 16, 512)), ('xl', 'y')...]
    ppermute x1 -> x2, starting transfers between devices: 12.3 us -> 6.56 us  [the longest x1 3.72 us: body(): far_own = lax.ppermute(out_own, 'xh', SWAP)]
    ppermute x1, waiting for transfers between devices: 0.01 us -> 4.64 us  [body(): back = lax.ppermute(out[STRIDE:], 'xh', SWAP)]
    ppermute x1, starting transfers between devices: 12.5 us -> 8.33 us  [body(): other = lax.ppermute(own, 'c', SWAP)]
    all_to_all x1, waiting for transfers between devices: 16.2 us -> 12.8 us  [body(): lax.all_to_all(col_mid.reshape(Z * C, 8, HALF), ('z', 'c'), split_axis=0,...]
    transpose x1 -> x0, local copies, waits for them, and re-layouts: 2.7 us -> none  [body(): pair.reshape(C, XL, Y, XH, Z, 16, 128).transpose(1, 4, 0, 5, 3, 2, 6)]
  transfers between devices with their start and end apart: 9 -> 9, of which waited for: 4 -> 5; matrix products, arithmetic and copies ran while one was open for 6% -> 7% of each run, Pallas kernels for 4% -> 6%
where the time goes in v2:
time: 181 us; the launch traced here: 180 us
  waiting for transfers between devices  52.7 us (29%)
  blocking collectives  50.5 us (28%)
  starting transfers between devices  47.4 us (26%)
  Pallas kernels  10.2 us (6%)
  other arithmetic  8.94 us (5%)
  local copies, waits for them, and re-layouts  7.25 us (4%)
  matrix products  3.1 us (2%)
    all_to_all x1, blocking collectives, body(): recv = lax.all_to_all(send, 'z', split_axis=0, concat_axis=0)  50.5 us
    all_to_all x1, waiting for transfers between devices, body(): lax.all_to_all(jnp.broadcast_to(part, (XL * Y, Z * 16, 512)), ('xl', 'y')...  20.5 us
    ppermute x1, waiting for transfers between devices, body(): both = jnp.stack([mine, lax.ppermute(given, 'xh', SWAP)])  13.4 us
    all_to_all x1, starting transfers between devices, body(): lax.all_to_all(col_mid.reshape(Z * C, 8, HALF), ('z', 'c'), split_axis=0,...  13.2 us
    all_to_all x1, waiting for transfers between devices, body(): lax.all_to_all(col_mid.reshape(Z * C, 8, HALF), ('z', 'c'), split_axis=0,...  12.8 us
    pallas_call x1, Pallas kernels, attention(): pl.pallas_call(attention_kernel, out_shape=jax.ShapeDtypeStruct((2 * STRI...  10.2 us
    all_to_all x1, starting transfers between devices, body(): lax.all_to_all(jnp.broadcast_to(part, (XL * Y, Z * 16, 512)), ('xl', 'y')...  9.19 us
    ppermute x1, starting transfers between devices, body(): other = lax.ppermute(own, 'c', SWAP)  8.33 us
  transfers between devices with their start and end apart: 9, of which 5 were waited for; matrix products, arithmetic and copies ran while one was open for 7% of the time, Pallas kernels for 6%

profile of v2, /device:TPU:1, one launch (start us, length us, event | category | flops | bytes accessed | tf_op | source)
XLA Modules:
  0.0 180.4 jit_solution(1526683010289226918)
XLA Ops:
  1.4 1.1 pad_maximum_fusion.2
  2.5 50.5 %all_to_all.15 = bf16[16,16,1536]{2,1,0:T(8,128)(2,1)S(1)} all-to-all(bf16[16,16,1536]{2,1,0:T(8,128)(2,1)S(1)} %pad_maximum_fusion.2), channel_id=1, replica_groups=mesh['xl'=2,'y'=4,'xh'=2,'z'=16,'c'=2] {'z'}, dimensions={0} | all-to-all | bytes 1572864 | tf_op jit(solution)/shard_map/all_to_all | solution.py:121
  53.0 1.5 broadcast_in_dim.7
  54.5 9.2 %all-to-all-start.1 = ((bf16[8,256,512]{2,1,0:T(8,128)(2,1)}), bf16[8,256,512]{2,1,0:T(8,128)(2,1)S(1)}, u32[]{:S(2)}, u32[]{:S(2)}) async-start(bf16[8,256,512]{2,1,0:T(8,128)(2,1)} %broadcast_in_dim.7), calls=%async_computation.1 | async-start | bytes 4194304 | tf_op jit(solution)/shard_map/all_to_all | solution.py:125
  63.7 20.5 %all-to-all-done.1.own_ref = bf16[8,256,512]{2,1,0:T(8,128)(2,1)S(1)} async-done(((bf16[8,256,512]{2,1,0:T(8,128)(2,1)}), bf16[8,256,512]{2,1,0:T(8,128)(2,1)S(1)}, u32[]{:S(2)}, u32[]{:S(2)}) %all-to-all-start.1) | async-done | bytes 2097184 | tf_op jit(solution)/shard_map/all_to_all | solution.py:125
  84.3 8.3 %collective-permute-start.3 = (bf16[8,256,512]{2,1,0:T(8,128)(2,1)S(1)}, bf16[8,256,512]{2,1,0:T(8,128)(2,1)}, u32[]{:S(2)}, u32[]{:S(2)}) collective-permute-start(bf16[8,256,512]{2,1,0:T(8,128)(2,1)S(1)} %all-to-all-done.1.own_ref), channel_id=1, source_target_pairs={{0,1},{1,0},{2,3},{3,2},{4,5},{5,4},{6,7},{7,6},{8,9},{9,8},{10,11... | collective-permute-start | bytes 6291464 | tf_op jit(solution)/shard_map/ppermute | solution.py:128
  92.6 1.9 %select_bitcast_fusion.2 = (bf16[1,16,16,1024]{3,2,1,0:T(8,128)(2,1)S(1)}, bf16[16,16,1024]{2,1,0:T(8,128)(2,1)}) fusion(bf16[16,16,1024]{2,1,0:T(8,128)(2,1)} %bitcast.38, pred[]{:T(512)S(6)} %eq.6, bf16[16,16,1536]{2,1,0:T(8,128)(2,1)S(1)} %all_to_all.15), kind=kLoop, calls=%fused_computation.22 | loop fusion | flops 524288 | bytes 2097153 | tf_op jit(solution)/shard_map/stack | solution.py:133
  94.5 3.7 %collective-permute-start.1 = (bf16[16,16,1024]{2,1,0:T(8,128)(2,1)}, bf16[16,16,1024]{2,1,0:T(8,128)(2,1)S(1)}, u32[]{:S(2)}, u32[]{:S(2)}) collective-permute-start(bf16[16,16,1024]{2,1,0:T(8,128)(2,1)} %get-tuple-element.8), channel_id=1, source_target_pairs={{0,32},{32,0},{1,33},{33,1},{2,34},{34,2},{3,35},{35,3},{4,36},{36... | collective-permute-start | bytes 1572872 | tf_op jit(solution)/shard_map/ppermute | solution.py:133
  98.3 13.4 %collective-permute-done.1 = bf16[16,16,1024]{2,1,0:T(8,128)(2,1)S(1)} collective-permute-done((bf16[16,16,1024]{2,1,0:T(8,128)(2,1)}, bf16[16,16,1024]{2,1,0:T(8,128)(2,1)S(1)}, u32[]{:S(2)}, u32[]{:S(2)}) %collective-permute-start.1) | collective-permute-done | bytes 524320 | tf_op jit(solution)/shard_map/ppermute | solution.py:133
  111.8 2.7 %collective-permute-start.2 = (bf16[2,16,8,1024]{3,2,1,0:T(8,128)(2,1)S(1)}, bf16[2,16,8,1024]{3,2,1,0:T(8,128)(2,1)S(1)}, u32[]{:S(2)}, u32[]{:S(2)}) collective-permute-start(bf16[2,16,8,1024]{3,2,1,0:T(8,128)(2,1)S(1)} %broadcast_select_fusion.1), channel_id=1, source_target_pairs={{0,1},{1,0},{2,3},{3,2},{4,5},{5,4},{6,7},{7,6},{8,9},{9,8},{10,11... | collective-permute-start | bytes 1572872 | tf_op jit(solution)/shard_map/ppermute | solution.py:136
  114.7 1.3 collective-permute-done.2
  116.4 3.7 %collective-permute-start.5 = (bf16[8,256,128]{2,1,0:T(8,128)(2,1)S(1)}, bf16[8,256,128]{2,1,0:T(8,128)(2,1)S(1)}, u32[]{:S(2)}, u32[]{:S(2)}) collective-permute-start(bf16[8,256,128]{2,1,0:T(8,128)(2,1)S(1)} %slice.41), channel_id=1, source_target_pairs={{0,32},{32,0},{1,33},{33,1},{2,34},{34,2},{3,35},{35,3},{4,36},{36... | collective-permute-start | bytes 1572872 | tf_op jit(solution)/shard_map/ppermute | solution.py:153
  120.4 10.2 %attention.1 = bf16[512,512]{1,0:T(8,128)(2,1)S(1)} custom-call(s32[2]{0:T(128)S(1)} %pad_add_fusion.1.place, s32[2,8]{1,0:T(2,128)S(1)} %pad_add_fusion.reach_ref, f32[1,1024]{1,0:T(1,128)S(1)} %bitcast.33, bf16[512,1024]{1,0:T(8,128)(2,1)S(1)} %bitcast_select_fusion.x_ref, bf16[8,256,512]{2,1,0:T(8,128)(2,1)S(1)} %all-to-all-done.1.own_ref, ...), custom_call_target="tpu_custom_call" | custom-call | flops 2013265920 | bytes 6291456 | tf_op jit(solution)/shard_map/attention/pallas_call | solution.py:90
  130.7 3.1 %collective-permute-start.4 = (bf16[256,512]{1,0:T(8,128)(2,1)S(1)}, bf16[256,512]{1,0:T(8,128)(2,1)S(1)}, u32[]{:S(2)}, u32[]{:S(2)}) collective-permute-start(bf16[256,512]{1,0:T(8,128)(2,1)S(1)} %slice.39), channel_id=1, source_target_pairs={{0,32},{32,0},{1,33},{33,1},{2,34},{34,2},{3,35},{35,3},{4,36},{36... | collective-permute-start | bytes 786440 | tf_op jit(solution)/shard_map/ppermute | solution.py:145
  133.8 2.8 %collective-permute-start.6 = (bf16[8,256,128]{2,1,0:T(8,128)(2,1)S(1)}, bf16[8,256,128]{2,1,0:T(8,128)(2,1)S(1)}, u32[]{:S(2)}, u32[]{:S(2)}) collective-permute-start(bf16[8,256,128]{2,1,0:T(8,128)(2,1)S(1)} %collective-permute-done.5), channel_id=1, source_target_pairs={{0,1},{1,0},{2,3},{3,2},{4,5},{5,4},{6,7},{7,6},{8,9},{9,8},{10,11... | collective-permute-start | bytes 1572872 | tf_op jit(solution)/shard_map/ppermute | solution.py:154
  136.7 4.6 %collective-permute-done.4 = bf16[256,512]{1,0:T(8,128)(2,1)S(1)} collective-permute-done((bf16[256,512]{1,0:T(8,128)(2,1)S(1)}, bf16[256,512]{1,0:T(8,128)(2,1)S(1)}, u32[]{:S(2)}, u32[]{:S(2)}) %collective-permute-start.4) | collective-permute-done | bytes 262176 | tf_op jit(solution)/shard_map/ppermute | solution.py:145
  141.3 0.8 broadcast_select_fusion.3
  142.1 13.2 %all-to-all-start.2 = ((bf16[32,8,512]{2,1,0:T(8,128)(2,1)}), bf16[32,8,512]{2,1,0:T(8,128)(2,1)S(1)}, u32[]{:S(2)}, u32[]{:S(2)}) async-start(bf16[32,8,512]{2,1,0:T(8,128)(2,1)} %get-tuple-element.10), calls=%async_computation.2 | async-start | bytes 524288 | tf_op jit(solution)/shard_map/all_to_all | solution.py:148
  156.6 1.1 slice.42
  158.1 2.1 %maximum_select_fusion.1 = (bf16[1,2,2,4,16,16,128]{6,3,1,5,0,4,2:T(4,128)(2,1)S(1)}, bf16[1,2,2,4,16,16,128]{6,3,1,5,0,4,2:T(4,128)(2,1)S(1)}) fusion(bf16[1,1,2,4,16,16,128]{6,3,1,5,0,4,2:T(4,128)(2,1)S(1)} %copy.10, bf16[1,1,2,4,16,16,128]{6,3,1,5,0,4,2:T(4,128)(2,1)S(1)} %copy.9, pred[]{:T(512)S(6)} %eq.16, ...), kind=kLoop, calls=%fused_computation.11 | loop fusion | flops 3145728 | bytes 4194305 | tf_op jit(solution)/shard_map/jit(_where)/select_n | solution.py:157
  160.1 1.5 fusion
  161.7 2.7 %reshape.172 = bf16[1024,1024]{1,0:T(8,128)(2,1)} reshape(bf16[2,16,2,16,2,4,128]{6,5,4,3,2,1,0:T(4,128)(2,1)S(1)} %fusion) | data formatting | bytes 4194304 | tf_op jit(solution)/shard_map/reshape | solution.py:161
  164.5 12.8 %all-to-all-done.2 = bf16[32,8,512]{2,1,0:T(8,128)(2,1)S(1)} async-done(((bf16[32,8,512]{2,1,0:T(8,128)(2,1)}), bf16[32,8,512]{2,1,0:T(8,128)(2,1)S(1)}, u32[]{:S(2)}, u32[]{:S(2)}) %all-to-all-start.2) | async-done | bytes 262176 | tf_op jit(solution)/shard_map/all_to_all | solution.py:148
  177.3 3.1 %fusion.2 = bf16[1,1,256,1024]{3,2,1,0:T(8,128)(2,1)} fusion(bf16[1024,1024]{1,0:T(8,128)(2,1)} %reshape.172, bf16[256,512]{1,0:T(8,128)(2,1)S(1)} %bitcast.44, bf16[256,512]{1,0:T(8,128)(2,1)S(1)} %copy-done.2, bf16[1,1,256,1024]{3,2,1,0:T(8,128)(2,1)S(1)} %copy-done.1), kind=kOutput, calls=%fused_computation.9 | convolution fusion | flops 538705920 | bytes 3670016 | tf_op jit(solution)/shard_map/dot_general | solution.py:164
  (32 shorter events, 4.0 us)
Async XLA Ops:
  0.7 0.7 collective-permute-start
  54.5 29.7 %all-to-all-start.1 = ((bf16[8,256,512]{2,1,0:T(8,128)(2,1)}), bf16[8,256,512]{2,1,0:T(8,128)(2,1)S(1)}, u32[]{:S(2)}, u32[]{:S(2)}) async-start(bf16[8,256,512]{2,1,0:T(8,128)(2,1)} %broadcast_in_dim.7), calls=%async_computation.1 | async-start | bytes 4194304 | tf_op jit(solution)/shard_map/all_to_all | solution.py:125
  63.7 50.8 %copy-start.3 = (s32[8]{0:T(128)S(1)}, s32[8]{0:T(128)}, u32[]{:S(2)}) copy-start(s32[8]{0:T(128)} %param.11) | copy-start | bytes 100
  63.7 50.8 %copy-start.4 = (s32[8]{0:T(128)S(1)}, s32[8]{0:T(128)}, u32[]{:S(2)}) copy-start(s32[8]{0:T(128)} %param.10) | copy-start | bytes 100
  84.3 36.2 %collective-permute-start.3 = (bf16[8,256,512]{2,1,0:T(8,128)(2,1)S(1)}, bf16[8,256,512]{2,1,0:T(8,128)(2,1)}, u32[]{:S(2)}, u32[]{:S(2)}) collective-permute-start(bf16[8,256,512]{2,1,0:T(8,128)(2,1)S(1)} %all-to-all-done.1.own_ref), channel_id=1, source_target_pairs={{0,1},{1,0},{2,3},{3,2},{4,5},{5,4},{6,7},{7,6},{8,9},{9,8},{10,11... | collective-permute-start | bytes 6291464 | tf_op jit(solution)/shard_map/ppermute | solution.py:128
  94.5 17.1 %collective-permute-start.1 = (bf16[16,16,1024]{2,1,0:T(8,128)(2,1)}, bf16[16,16,1024]{2,1,0:T(8,128)(2,1)S(1)}, u32[]{:S(2)}, u32[]{:S(2)}) collective-permute-start(bf16[16,16,1024]{2,1,0:T(8,128)(2,1)} %get-tuple-element.8), channel_id=1, source_target_pairs={{0,32},{32,0},{1,33},{33,1},{2,34},{34,2},{3,35},{35,3},{4,36},{36... | collective-permute-start | bytes 1572872 | tf_op jit(solution)/shard_map/ppermute | solution.py:133
  111.8 4.2 %collective-permute-start.2 = (bf16[2,16,8,1024]{3,2,1,0:T(8,128)(2,1)S(1)}, bf16[2,16,8,1024]{3,2,1,0:T(8,128)(2,1)S(1)}, u32[]{:S(2)}, u32[]{:S(2)}) collective-permute-start(bf16[2,16,8,1024]{3,2,1,0:T(8,128)(2,1)S(1)} %broadcast_select_fusion.1), channel_id=1, source_target_pairs={{0,1},{1,0},{2,3},{3,2},{4,5},{5,4},{6,7},{7,6},{8,9},{9,8},{10,11... | collective-permute-start | bytes 1572872 | tf_op jit(solution)/shard_map/ppermute | solution.py:136
  116.3 4.1 %copy-start = (f32[1024]{0:T(1024)S(1)}, f32[1024]{0:T(1024)}, u32[]{:S(2)}) copy-start(f32[1024]{0:T(1024)} %param.7) | copy-start | bytes 12292
  116.4 17.4 %collective-permute-start.5 = (bf16[8,256,128]{2,1,0:T(8,128)(2,1)S(1)}, bf16[8,256,128]{2,1,0:T(8,128)(2,1)S(1)}, u32[]{:S(2)}, u32[]{:S(2)}) collective-permute-start(bf16[8,256,128]{2,1,0:T(8,128)(2,1)S(1)} %slice.41), channel_id=1, source_target_pairs={{0,32},{32,0},{1,33},{33,1},{2,34},{34,2},{3,35},{35,3},{4,36},{36... | collective-permute-start | bytes 1572872 | tf_op jit(solution)/shard_map/ppermute | solution.py:153
  130.7 10.6 %collective-permute-start.4 = (bf16[256,512]{1,0:T(8,128)(2,1)S(1)}, bf16[256,512]{1,0:T(8,128)(2,1)S(1)}, u32[]{:S(2)}, u32[]{:S(2)}) collective-permute-start(bf16[256,512]{1,0:T(8,128)(2,1)S(1)} %slice.39), channel_id=1, source_target_pairs={{0,32},{32,0},{1,33},{33,1},{2,34},{34,2},{3,35},{35,3},{4,36},{36... | collective-permute-start | bytes 786440 | tf_op jit(solution)/shard_map/ppermute | solution.py:145
  133.8 22.3 %collective-permute-start.6 = (bf16[8,256,128]{2,1,0:T(8,128)(2,1)S(1)}, bf16[8,256,128]{2,1,0:T(8,128)(2,1)S(1)}, u32[]{:S(2)}, u32[]{:S(2)}) collective-permute-start(bf16[8,256,128]{2,1,0:T(8,128)(2,1)S(1)} %collective-permute-done.5), channel_id=1, source_target_pairs={{0,1},{1,0},{2,3},{3,2},{4,5},{5,4},{6,7},{7,6},{8,9},{9,8},{10,11... | collective-permute-start | bytes 1572872 | tf_op jit(solution)/shard_map/ppermute | solution.py:154
  142.1 35.2 %all-to-all-start.2 = ((bf16[32,8,512]{2,1,0:T(8,128)(2,1)}), bf16[32,8,512]{2,1,0:T(8,128)(2,1)S(1)}, u32[]{:S(2)}, u32[]{:S(2)}) async-start(bf16[32,8,512]{2,1,0:T(8,128)(2,1)} %get-tuple-element.10), calls=%async_computation.2 | async-start | bytes 524288 | tf_op jit(solution)/shard_map/all_to_all | solution.py:148
  161.7 15.6 %copy-start.1 = (bf16[1,1,256,1024]{3,2,1,0:T(8,128)(2,1)S(1)}, bf16[1,1,256,1024]{3,2,1,0:T(8,128)(2,1)}, u32[]{:S(2)}) copy-start(bf16[1,1,256,1024]{3,2,1,0:T(8,128)(2,1)} %param.6) | copy-start | bytes 1572868
  161.7 15.6 %copy-start.2 = (bf16[256,512]{1,0:T(8,128)(2,1)S(1)}, bf16[256,512]{1,0:T(8,128)(2,1)}, u32[]{:S(2)}) copy-start(bf16[256,512]{1,0:T(8,128)(2,1)} %get-tuple-element.9) | copy-start | bytes 786436

commit v3 on v0

v3 whole, which is shorter than its diff:
```python
import functools

import jax
import jax.numpy as jnp
from jax import lax
from jax.experimental import pallas as pl
from jax.experimental.pallas import tpu as pltpu
from jax.sharding import Mesh
from jax.sharding import PartitionSpec as P

XL, Y, XH, Z, C = 2, 4, 2, 16, 2
X = XH * XL
FEATURES, STRIDE, HEADS, HEAD_DIM = 1024, 256, 8, 64
HALF = HEADS * HEAD_DIM
WIDTH = 3 * HALF
PART = 384
SEQ = ("xh", "z", "c")
FAR = 1 << 20


def blocks(place, odd):
    x, y, core = place[0], place[1], place[2]
    for t in range(X):
        there = (x + t) & 3
        xh, xl = there >> 1, there & 1
        turn = (1 - xl) if odd else xl
        for s in range(Y):
            for zz in range(Z // 2):
                row = xh * 512 + 64 * zz + 32 * turn
                yield t * Y + s, zz, row, (y + s) & 3


def assemble(place, odd, own_ref, other_ref, lanes, w_ref, first, width):
    core = place[2]
    for block, zz, row, y in blocks(place, odd):
        cols = pl.ds(pl.multiple_of(first + width * y, 128), width)
        for ref, c in ((own_ref, core), (other_ref, 1 - core)):
            at = pl.multiple_of(row + 16 * c, 16)
            w_ref[pl.ds(at, 16), cols] = ref[block, pl.ds(16 * zz, 16), lanes]


def attend(reach_ref, gain_ref, x_ref, w_ref, n_ref, qkv_ref, out_ref, dist):
    def norm(i, _):
        rows = pl.ds(pl.multiple_of(i * 64, 64), 64)
        x = x_ref[rows, :].astype(jnp.float32)
        scale = lax.rsqrt(jnp.mean(x * x, axis=-1, keepdims=True) + 1e-05)
        n_ref[rows, :] = (x * scale * gain_ref[...]).astype(jnp.bfloat16)
        return 0

    lax.fori_loop(0, STRIDE // 64, norm, 0)

    def project(i, _):
        cols = pl.ds(pl.multiple_of(i * 256, 256), 256)
        qkv_ref[:, cols] = jnp.dot(
            n_ref[...], w_ref[:, cols], preferred_element_type=jnp.float32
        ).astype(jnp.bfloat16)
        return 0

    lax.fori_loop(0, WIDTH // 256, project, 0)

    for h in range(HEADS):
        q = qkv_ref[:, h * 64 : h * 64 + 64]
        k = qkv_ref[:, HALF + h * 64 : HALF + h * 64 + 64]
        v = qkv_ref[:, 2 * HALF + h * 64 : 2 * HALF + h * 64 + 64]
        s = lax.dot_general(
            q, k, (((1,), (1,)), ((), ())), preferred_element_type=jnp.float32
        )
        s = jnp.where(dist < reach_ref[h], s * 0.125, -1e30)
        p = jnp.exp(s - jnp.max(s, axis=-1, keepdims=True))
        o = jnp.dot(p.astype(jnp.bfloat16), v, preferred_element_type=jnp.float32)
        o = o / jnp.sum(p, axis=-1, keepdims=True)
        out_ref[:, h * 64 : h * 64 + 64] = o.astype(jnp.bfloat16)


def pairs():
    i = lax.broadcasted_iota(jnp.int32, (STRIDE, STRIDE), 0)
    return i, lax.broadcasted_iota(jnp.int32, (STRIDE, STRIDE), 1)


def column_kernel(place, reach_ref, gain_ref, x_ref, own_ref, other_ref, out_ref, done_ref, w_ref, n_ref, qkv_ref):
    done_ref[0] = 0
    assemble(place, True, own_ref, other_ref, slice(0, PART), w_ref, 0, PART)
    i, j = pairs()
    back = (i >> 2) - (j >> 2)
    dist = jnp.where((((i ^ j) & 3) == 0) & (back >= 0), back, FAR)
    attend(reach_ref, gain_ref, x_ref, w_ref, n_ref, qkv_ref, out_ref, dist)


def row_kernel(
    place, reach_ref, gain_ref, x_ref, own_ref, other_ref, base_ref, low_ref, done_ref, w_ref, n_ref, qkv_ref, a_ref, o_ref
):
    done_ref[0] = 0
    assemble(place, False, own_ref, other_ref, slice(0, PART), w_ref, 0, PART)
    i, j = pairs()
    dist = jnp.where(j <= i, (i >> 5) - (j >> 5), FAR)
    attend(reach_ref, gain_ref, x_ref, w_ref, n_ref, qkv_ref, a_ref, dist)
    assemble(place, False, own_ref, other_ref, slice(PART, PART + 128), o_ref, 0, 128)
    assemble(place, True, own_ref, other_ref, slice(PART + 128, PART + 256), o_ref, 512, 128)
    for n in range(0, FEATURES, 256):
        base_ref[:, n : n + 256] = x_ref[:, n : n + 256].astype(jnp.float32) + jnp.dot(
            a_ref[...], o_ref[:HALF, n : n + 256], preferred_element_type=jnp.float32
        )
    low_ref[...] = o_ref[HALF:, :]


def last_kernel(base_ref, col_ref, low_ref, out_ref):
    for n in range(0, FEATURES, 256):
        out_ref[:, n : n + 256] = (
            base_ref[:, n : n + 256]
            + jnp.dot(col_ref[...], low_ref[:, n : n + 256], preferred_element_type=jnp.float32)
        ).astype(jnp.bfloat16)


VMEM = pl.BlockSpec(memory_space=pltpu.VMEM)
SMEM = pl.BlockSpec(memory_space=pltpu.SMEM)
WORK = [
    pltpu.VMEM((FEATURES, WIDTH), jnp.bfloat16),
    pltpu.VMEM((STRIDE, FEATURES), jnp.bfloat16),
    pltpu.VMEM((STRIDE, WIDTH), jnp.bfloat16),
]
PARAMS = pltpu.CompilerParams(vmem_limit_bytes=40 * 1024 * 1024)
COST = pl.CostEstimate(
    flops=2 * 256 * 1024 * 1536 + 16 * 256 * 256 * 128,
    bytes_accessed=6 << 20,
    transcendentals=8 * 256 * 256,
)


def column_attention(place, reach, gain, x, own, other):
    return pl.pallas_call(
        column_kernel,
        out_shape=[
            jax.ShapeDtypeStruct((STRIDE, HALF), jnp.bfloat16),
            jax.ShapeDtypeStruct((1,), jnp.int32),
        ],
        in_specs=[SMEM, SMEM, VMEM, VMEM, VMEM, VMEM],
        out_specs=[VMEM, SMEM],
        scratch_shapes=WORK,
        compiler_params=PARAMS,
        cost_estimate=COST,
        name="columns",
    )(place, reach, gain, x, own, other)


def row_attention(place, reach, gain, x, own, other):
    return pl.pallas_call(
        row_kernel,
        out_shape=[
            jax.ShapeDtypeStruct((STRIDE, FEATURES), jnp.float32),
            jax.ShapeDtypeStruct((HALF, FEATURES), jnp.bfloat16),
            jax.ShapeDtypeStruct((1,), jnp.int32),
        ],
        in_specs=[SMEM, SMEM, VMEM, VMEM, VMEM, VMEM],
        out_specs=[VMEM, VMEM, SMEM],
        scratch_shapes=WORK
        + [
            pltpu.VMEM((STRIDE, HALF), jnp.bfloat16),
            pltpu.VMEM((FEATURES, FEATURES), jnp.bfloat16),
        ],
        compiler_params=PARAMS,
        cost_estimate=COST,
        name="rows",
    )(place, reach, gain, x, own, other)


def ring(part, axes, order):
    size = len(order)
    return [
        lax.ppermute(part, axes, [(order[i], order[(i - t) % size]) for i in range(size)])
        for t in range(1, size)
    ]


def body(tokens, norm_gain, w_qkv, w_out, row_blocks, col_rows):
    xl, y, xh, c = (lax.axis_index(a) for a in ("xl", "y", "xh", "c"))
    rows = tokens.reshape(STRIDE, FEATURES)
    gain = norm_gain.reshape(1, FEATURES)
    place = jnp.stack([2 * xh + xl, y, c]).astype(jnp.int32)

    block = jnp.concatenate([w_qkv, w_out], axis=1)
    change = [(a * Z + z, (a ^ (z & 1)) * Z + z) for a in range(XL) for z in range(Z)]
    block = lax.ppermute(block, ("xl", "z"), change)
    column = lax.all_to_all(jnp.broadcast_to(block, (Z, 16, 512)), "z", split_axis=0, concat_axis=0)

    sent, column = lax.optimization_barrier((rows, column))
    turned = lax.all_to_all(sent.reshape(64, 4, FEATURES), SEQ, split_axis=0, concat_axis=0)
    turned = turned.reshape(STRIDE, FEATURES)

    halves = column.reshape(Z // 2, 2, 16, 512)
    row_part = jnp.where(xl == 0, halves[:, 0], halves[:, 1]).reshape(128, 512)
    col_part = jnp.where(xl == 0, halves[:, 1], halves[:, 0]).reshape(128, 512)
    part = jnp.concatenate([col_part[:, :PART], row_part, col_part[:, PART:]], axis=1)
    near = jnp.stack([part, *ring(part, "y", range(Y))])

    def plane(part):
        return [part, *ring(part, ("xl", "xh"), [0, 2, 1, 3])]

    def both_cores(parts):
        own = jnp.stack(parts).reshape(X * Y, *parts[0].shape[1:])
        return own, lax.ppermute(own, "c", [(0, 1), (1, 0)])

    col_plane = plane(near[:, :, :PART])
    col_own, col_other = both_cores(col_plane)
    col_mid, done = column_attention(place, col_rows, gain, turned, col_own, col_other)
    col_out = lax.all_to_all(col_mid.reshape(64, 4, HALF), SEQ, split_axis=0, concat_axis=0)

    near_rest, _ = lax.optimization_barrier((near[:, :, PART:], col_plane))
    rest = [jnp.where(done[0] == 0, a, 0) for a in plane(near_rest)]
    rest_own, rest_other = both_cores(rest)
    base, low, last = row_attention(place, row_blocks, gain, rows, rest_own, rest_other)
    col_out = jnp.where(last[0] == 0, col_out, 0).reshape(STRIDE, HALF)

    mixed = pl.pallas_call(
        last_kernel,
        out_shape=jax.ShapeDtypeStruct((STRIDE, FEATURES), jnp.bfloat16),
        in_specs=[VMEM, VMEM, VMEM],
        out_specs=VMEM,
        compiler_params=PARAMS,
        name="mixed",
    )(base, col_out, low)
    return mixed.reshape(tokens.shape)


def solution(mesh):
    fine = Mesh(mesh.devices.reshape(XL, Y, XH, Z, C), ("xl", "y", "xh", "z", "c"))
    fsdp = ("xl", "y")
    return jax.shard_map(
        body,
        mesh=fine,
        in_specs=(P(fsdp, SEQ, None, None), P(), P(SEQ, fsdp), P(SEQ, fsdp), P(), P()),
        out_specs=P(fsdp, SEQ, None, None),
        check_vma=False,
    )
```

time: 403 us -> 168 us (0.42)
  waiting for transfers between devices: 292 us -> 54.5 us
  starting transfers between devices: 16.7 us -> 79 us
  blocking collectives: 47.4 us -> 0 us
  Pallas kernels: 0 us -> 16 us
  matrix products: 14.4 us -> 0 us
  between operations: 13.6 us -> 1.82 us
  local copies, waits for them, and re-layouts: 11.4 us -> 6.91 us
    all_gather x2 -> x0, waiting for transfers between devices: 256 us -> none  [the longest x1 167 us: body(): lax.all_gather(part_qkv, 'seq', axis=0, tiled=True)]
    all_gather x2 -> x0, blocking collectives: 47.4 us -> none  [the longest x1 25.6 us: body(): lax.all_gather(w_qkv, 'fsdp', axis=1, tiled=True)]
    ppermute x0 -> x12, starting transfers between devices: none -> 36.6 us  [the longest x9 30.2 us: ring(): lax.ppermute(part, axes, [(order[i], order[(i - t) % size]) for i in rang...]
    all_to_all x2 -> x3, starting transfers between devices: 16.6 us -> 42.5 us  [the longest x1 19.1 us: body(): lax.all_to_all(jnp.broadcast_to(block, (Z, 16, 512)), 'z', split_axis=0,...]
    pallas_call x0 -> x3, Pallas kernels: none -> 16 us  [the longest x1 8.15 us: row_attention(): pl.pallas_call(row_kernel, out_shape=[jax.ShapeDtypeStruct((STRIDE, FEATU...]
    dot_general x6 -> x0, matrix products: 12 us -> none  [the longest x1 3.12 us: body(): jnp.dot(normed, col_weight, preferred_element_type=jnp.float32)]
    ppermute x0 -> x12, waiting for transfers between devices: none -> 11.2 us  [the longest x9 11.2 us: ring(): lax.ppermute(part, axes, [(order[i], order[(i - t) % size]) for i in rang...]
    another operation x0 -> x10, other arithmetic: none -> 7.57 us  [the longest x7 6.53 us: both_cores(): own = jnp.stack(parts).reshape(X * Y, *parts[0].shape[1:])]
  transfers between devices with their start and end apart: 4 -> 15, of which waited for: 4 -> 6; matrix products, arithmetic and copies ran while one was open for 4% -> 5% of each run, Pallas kernels for 0% -> 9%
where the time goes in v3:
time: 168 us; the launch traced here: 167 us
  starting transfers between devices  79 us (47%)
  waiting for transfers between devices  54.5 us (32%)
  Pallas kernels  16 us (10%)
  other arithmetic  8.47 us (5%)
  local copies, waits for them, and re-layouts  6.91 us (4%)
  between operations  1.82 us (1%)
    ppermute x9, starting transfers between devices, ring(): lax.ppermute(part, axes, [(order[i], order[(i - t) % size]) for i in rang...  30.2 us
    all_to_all x1, starting transfers between devices, body(): lax.all_to_all(jnp.broadcast_to(block, (Z, 16, 512)), 'z', split_axis=0,...  19.1 us
    all_to_all x1, waiting for transfers between devices, body(): lax.all_to_all(sent.reshape(64, 4, FEATURES), SEQ, split_axis=0, concat_a...  17.7 us
    all_to_all x1, waiting for transfers between devices, body(): lax.all_to_all(col_mid.reshape(64, 4, HALF), SEQ, split_axis=0, concat_ax...  12.8 us
    all_to_all x1, waiting for transfers between devices, body(): lax.all_to_all(jnp.broadcast_to(block, (Z, 16, 512)), 'z', split_axis=0,...  12.8 us
    all_to_all x1, starting transfers between devices, body(): lax.all_to_all(sent.reshape(64, 4, FEATURES), SEQ, split_axis=0, concat_a...  12.7 us
    ppermute x9, waiting for transfers between devices, ring(): lax.ppermute(part, axes, [(order[i], order[(i - t) % size]) for i in rang...  11.2 us
    all_to_all x1, starting transfers between devices, body(): lax.all_to_all(col_mid.reshape(64, 4, HALF), SEQ, split_axis=0, concat_ax...  10.7 us
  transfers between devices with their start and end apart: 15, of which 6 were waited for; matrix products, arithmetic and copies ran while one was open for 5% of the time, Pallas kernels for 9%

profile of v3, /device:TPU:1, one launch (start us, length us, event | category | flops | bytes accessed | tf_op | source)
XLA Modules:
  0.0 166.7 jit_solution(18096925997908085100)
XLA Ops:
  2.1 19.1 %all-to-all-start = ((bf16[16,16,512]{2,1,0:T(8,128)(2,1)}), bf16[16,16,512]{2,1,0:T(8,128)(2,1)S(1)}, u32[]{:S(2)}, u32[]{:S(2)}) async-start(bf16[16,16,512]{2,1,0:T(8,128)(2,1)} %broadcast_in_dim.14), calls=%async_computation | async-start | bytes 524288 | tf_op jit(solution)/shard_map/all_to_all | solution.py:183
  21.3 12.8 %all-to-all-done = bf16[16,16,512]{2,1,0:T(8,128)(2,1)S(1)} async-done(((bf16[16,16,512]{2,1,0:T(8,128)(2,1)}), bf16[16,16,512]{2,1,0:T(8,128)(2,1)S(1)}, u32[]{:S(2)}, u32[]{:S(2)}) %all-to-all-start) | async-done | bytes 262176 | tf_op jit(solution)/shard_map/all_to_all | solution.py:183
  34.1 4.8 %collective-permute-start.2 = (bf16[128,1024]{1,0:T(8,128)(2,1)S(1)}, bf16[128,1024]{1,0:T(8,128)(2,1)S(1)}, u32[]{:S(2)}, u32[]{:S(2)}) collective-permute-start(bf16[128,1024]{1,0:T(8,128)(2,1)S(1)} %get-tuple-element.22), channel_id=1, source_target_pairs={{0,128},{64,192},{128,0},{192,64},{1,129},{65,193},{129,1},{193,65... | collective-permute-start | bytes 786440 | tf_op jit(solution)/shard_map/ppermute | solution.py:169
  39.0 2.7 %collective-permute-start.1 = (bf16[128,1024]{1,0:T(8,128)(2,1)S(1)}, bf16[128,1024]{1,0:T(8,128)(2,1)S(1)}, u32[]{:S(2)}, u32[]{:S(2)}) collective-permute-start(bf16[128,1024]{1,0:T(8,128)(2,1)S(1)} %get-tuple-element.22), channel_id=1, source_target_pairs={{0,192},{64,0},{128,64},{192,128},{1,193},{65,1},{129,65},{193,129... | collective-permute-start | bytes 786440 | tf_op jit(solution)/shard_map/ppermute | solution.py:169
  41.7 2.6 %collective-permute-start.3 = (bf16[128,1024]{1,0:T(8,128)(2,1)S(1)}, bf16[128,1024]{1,0:T(8,128)(2,1)S(1)}, u32[]{:S(2)}, u32[]{:S(2)}) collective-permute-start(bf16[128,1024]{1,0:T(8,128)(2,1)S(1)} %get-tuple-element.22), channel_id=1, source_target_pairs={{0,64},{64,128},{128,192},{192,0},{1,65},{65,129},{129,193},{193,1... | collective-permute-start | bytes 786440 | tf_op jit(solution)/shard_map/ppermute | solution.py:169
  44.3 1.8 %collective-permute-done.1 = bf16[128,1024]{1,0:T(8,128)(2,1)S(1)} collective-permute-done((bf16[128,1024]{1,0:T(8,128)(2,1)S(1)}, bf16[128,1024]{1,0:T(8,128)(2,1)S(1)}, u32[]{:S(2)}, u32[]{:S(2)}) %collective-permute-start.1) | collective-permute-done | bytes 262176 | tf_op jit(solution)/shard_map/ppermute | solution.py:169
  46.1 6.7 %collective-permute-done.3 = bf16[128,1024]{1,0:T(8,128)(2,1)S(1)} collective-permute-done((bf16[128,1024]{1,0:T(8,128)(2,1)S(1)}, bf16[128,1024]{1,0:T(8,128)(2,1)S(1)}, u32[]{:S(2)}, u32[]{:S(2)}) %collective-permute-start.3) | collective-permute-done | bytes 262176 | tf_op jit(solution)/shard_map/ppermute | solution.py:169
  52.8 3.1 %collective-permute-start.6 = (bf16[4,128,384]{2,1,0:T(8,128)(2,1)S(1)}, bf16[4,128,384]{2,1,0:T(8,128)(2,1)}, u32[]{:S(2)}, u32[]{:S(2)}) collective-permute-start(bf16[4,128,384]{2,1,0:T(8,128)(2,1)S(1)} %pad_maximum_fusion.5), channel_id=1, source_target_pairs={{0,256},{256,32},{32,288},{288,0},{1,257},{257,33},{33,289},{289,1... | collective-permute-start | bytes 1179656 | tf_op jit(solution)/shard_map/ppermute | solution.py:169
  56.0 4.4 %collective-permute-start.5 = (bf16[4,128,384]{2,1,0:T(8,128)(2,1)S(1)}, bf16[4,128,384]{2,1,0:T(8,128)(2,1)}, u32[]{:S(2)}, u32[]{:S(2)}) collective-permute-start(bf16[4,128,384]{2,1,0:T(8,128)(2,1)S(1)} %pad_maximum_fusion.5), channel_id=1, source_target_pairs={{0,32},{256,288},{32,0},{288,256},{1,33},{257,289},{33,1},{289,257... | collective-permute-start | bytes 1179656 | tf_op jit(solution)/shard_map/ppermute | solution.py:169
  60.3 3.1 %collective-permute-start.4 = (bf16[4,128,384]{2,1,0:T(8,128)(2,1)S(1)}, bf16[4,128,384]{2,1,0:T(8,128)(2,1)}, u32[]{:S(2)}, u32[]{:S(2)}) collective-permute-start(bf16[4,128,384]{2,1,0:T(8,128)(2,1)S(1)} %pad_maximum_fusion.5), channel_id=1, source_target_pairs={{0,288},{256,0},{32,256},{288,32},{1,289},{257,1},{33,257},{289,33... | collective-permute-start | bytes 1179656 | tf_op jit(solution)/shard_map/ppermute | solution.py:169
  64.4 12.7 %all-to-all-start.1 = ((bf16[64,4,1024]{2,1,0:T(4,128)(2,1)}), bf16[64,4,1024]{2,1,0:T(4,128)(2,1)}, u32[]{:S(2)}, u32[]{:S(2)}) async-start(bf16[64,4,1024]{2,1,0:T(4,128)(2,1)} %reshape.46), calls=%async_computation.1 | async-start | bytes 1048576 | tf_op jit(solution)/shard_map/all_to_all | solution.py:186
  77.2 1.5 pad_maximum_fusion.1
  78.7 3.3 %collective-permute-start.7 = (bf16[16,128,384]{2,1,0:T(8,128)(2,1)S(1)}, bf16[16,128,384]{2,1,0:T(8,128)(2,1)}, u32[]{:S(2)}, u32[]{:S(2)}) collective-permute-start(bf16[16,128,384]{2,1,0:T(8,128)(2,1)S(1)} %bitcast.33), channel_id=1, source_target_pairs={{0,1},{1,0},{2,3},{3,2},{4,5},{5,4},{6,7},{7,6},{8,9},{9,8},{10,11... | collective-permute-start | bytes 4718600 | tf_op jit(solution)/shard_map/ppermute | solution.py:200
  82.9 4.2 %collective-permute-start.8 = (bf16[4,128,640]{2,1,0:T(8,128)(2,1)}, bf16[4,128,640]{2,1,0:T(8,128)(2,1)}, u32[]{:S(2)}, u32[]{:S(2)}) collective-permute-start(bf16[4,128,640]{2,1,0:T(8,128)(2,1)} %pad_maximum_fusion.2), channel_id=1, source_target_pairs={{0,288},{256,0},{32,256},{288,32},{1,289},{257,1},{33,257},{289,33... | collective-permute-start | bytes 1966088 | tf_op jit(solution)/shard_map/ppermute | solution.py:169
  87.1 3.4 %collective-permute-start.9 = (bf16[4,128,640]{2,1,0:T(8,128)(2,1)}, bf16[4,128,640]{2,1,0:T(8,128)(2,1)}, u32[]{:S(2)}, u32[]{:S(2)}) collective-permute-start(bf16[4,128,640]{2,1,0:T(8,128)(2,1)} %pad_maximum_fusion.2), channel_id=1, source_target_pairs={{0,32},{256,288},{32,0},{288,256},{1,33},{257,289},{33,1},{289,257... | collective-permute-start | bytes 1966088 | tf_op jit(solution)/shard_map/ppermute | solution.py:169
  90.7 1.9 %collective-permute-start.10 = (bf16[4,128,640]{2,1,0:T(8,128)(2,1)}, bf16[4,128,640]{2,1,0:T(8,128)(2,1)}, u32[]{:S(2)}, u32[]{:S(2)}) collective-permute-start(bf16[4,128,640]{2,1,0:T(8,128)(2,1)} %pad_maximum_fusion.2), channel_id=1, source_target_pairs={{0,256},{256,32},{32,288},{288,0},{1,257},{257,33},{33,289},{289,1... | collective-permute-start | bytes 1966088 | tf_op jit(solution)/shard_map/ppermute | solution.py:169
  92.6 17.7 %all-to-all-done.1 = bf16[64,4,1024]{2,1,0:T(4,128)(2,1)} async-done(((bf16[64,4,1024]{2,1,0:T(4,128)(2,1)}), bf16[64,4,1024]{2,1,0:T(4,128)(2,1)}, u32[]{:S(2)}, u32[]{:S(2)}) %all-to-all-start.1) | async-done | bytes 524320 | tf_op jit(solution)/shard_map/all_to_all | solution.py:186
  111.5 6.6 %columns.1 = (bf16[256,512]{1,0:T(8,128)(2,1)S(1)}, s32[1]{0:T(128)}) custom-call(s32[3]{0:T(128)S(1)} %pad_add_fusion.place, s32[8]{0:T(128)S(1)} %copy-done.6, f32[1,1024]{1,0:T(1,128)S(1)} %bitcast.37, bf16[256,1024]{1,0:T(8,128)(2,1)S(1)} %reshape.47.x_ref, bf16[16,128,384]{2,1,0:T(8,128)(2,1)S(1)} %bitcast.34, ...), custom_call_target="tpu_custom_call" | custom-call | flops 939524096 | bytes 6291456 | tf_op jit(solution)/shard_map/columns/pallas_call | solution.py:130
  122.2 2.7 %collective-permute-done.10 = bf16[4,128,640]{2,1,0:T(8,128)(2,1)} collective-permute-done((bf16[4,128,640]{2,1,0:T(8,128)(2,1)}, bf16[4,128,640]{2,1,0:T(8,128)(2,1)}, u32[]{:S(2)}, u32[]{:S(2)}) %collective-permute-start.10) | collective-permute-done | bytes 655392 | tf_op jit(solution)/shard_map/ppermute | solution.py:169
  126.5 2.4 %collective-permute-start.11 = (bf16[16,128,640]{2,1,0:T(8,128)(2,1)S(1)}, bf16[16,128,640]{2,1,0:T(8,128)(2,1)}, u32[]{:S(2)}, u32[]{:S(2)}) collective-permute-start(bf16[16,128,640]{2,1,0:T(8,128)(2,1)S(1)} %bitcast.31), channel_id=1, source_target_pairs={{0,1},{1,0},{2,3},{3,2},{4,5},{5,4},{6,7},{7,6},{8,9},{9,8},{10,11... | collective-permute-start | bytes 7864328 | tf_op jit(solution)/shard_map/ppermute | solution.py:200
  129.6 10.7 %all-to-all-start.2 = ((bf16[64,4,512]{2,1,0:T(4,128)(2,1)}), bf16[64,4,512]{2,1,0:T(4,128)(2,1)S(1)}, u32[]{:S(2)}, u32[]{:S(2)}) async-start(bf16[64,4,512]{2,1,0:T(4,128)(2,1)} %reshape.51), calls=%async_computation.2 | async-start | bytes 524288 | tf_op jit(solution)/shard_map/all_to_all | solution.py:205
  140.3 8.1 %rows.1 = (f32[256,1024]{1,0:T(8,128)S(1)}, bf16[512,1024]{1,0:T(8,128)(2,1)S(1)}, s32[1]{0:T(128)}) custom-call(s32[3]{0:T(128)S(1)} %pad_add_fusion.place, s32[8]{0:T(128)S(1)} %copy-done.7, f32[1,1024]{1,0:T(1,128)S(1)} %bitcast.38, bf16[256,1024]{1,0:T(8,128)(2,1)S(1)} %bitcast.36, bf16[16,128,640]{2,1,0:T(8,128)(2,1)S(1)} %bitcast.32, ...), custom_call_target="tpu_custom_call" | custom-call | flops 939524096 | bytes 6291456 | tf_op jit(solution)/shard_map/rows/pallas_call | solution.py:146
  151.2 12.8 %all-to-all-done.2 = bf16[64,4,512]{2,1,0:T(4,128)(2,1)S(1)} async-done(((bf16[64,4,512]{2,1,0:T(4,128)(2,1)}), bf16[64,4,512]{2,1,0:T(4,128)(2,1)S(1)}, u32[]{:S(2)}, u32[]{:S(2)}) %all-to-all-start.2) | async-done | bytes 262176 | tf_op jit(solution)/shard_map/all_to_all | solution.py:205
  165.5 1.2 mixed.1
  (46 shorter events, 14.6 us)
Async XLA Ops:
  0.7 0.7 collective-permute-start
  2.1 31.9 %all-to-all-start = ((bf16[16,16,512]{2,1,0:T(8,128)(2,1)}), bf16[16,16,512]{2,1,0:T(8,128)(2,1)S(1)}, u32[]{:S(2)}, u32[]{:S(2)}) async-start(bf16[16,16,512]{2,1,0:T(8,128)(2,1)} %broadcast_in_dim.14), calls=%async_computation | async-start | bytes 524288 | tf_op jit(solution)/shard_map/all_to_all | solution.py:183
  21.2 42.2 %copy-start = (bf16[1,1,256,1024]{3,2,1,0:T(8,128)(2,1)S(1)}, bf16[1,1,256,1024]{3,2,1,0:T(8,128)(2,1)}, u32[]{:S(2)}) copy-start(bf16[1,1,256,1024]{3,2,1,0:T(8,128)(2,1)} %param.6) | copy-start | bytes 1572868
  34.1 10.1 %collective-permute-start.2 = (bf16[128,1024]{1,0:T(8,128)(2,1)S(1)}, bf16[128,1024]{1,0:T(8,128)(2,1)S(1)}, u32[]{:S(2)}, u32[]{:S(2)}) collective-permute-start(bf16[128,1024]{1,0:T(8,128)(2,1)S(1)} %get-tuple-element.22), channel_id=1, source_target_pairs={{0,128},{64,192},{128,0},{192,64},{1,129},{65,193},{129,1},{193,65... | collective-permute-start | bytes 786440 | tf_op jit(solution)/shard_map/ppermute | solution.py:169
  39.0 7.1 %collective-permute-start.1 = (bf16[128,1024]{1,0:T(8,128)(2,1)S(1)}, bf16[128,1024]{1,0:T(8,128)(2,1)S(1)}, u32[]{:S(2)}, u32[]{:S(2)}) collective-permute-start(bf16[128,1024]{1,0:T(8,128)(2,1)S(1)} %get-tuple-element.22), channel_id=1, source_target_pairs={{0,192},{64,0},{128,64},{192,128},{1,193},{65,1},{129,65},{193,129... | collective-permute-start | bytes 786440 | tf_op jit(solution)/shard_map/ppermute | solution.py:169
  41.7 11.1 %collective-permute-start.3 = (bf16[128,1024]{1,0:T(8,128)(2,1)S(1)}, bf16[128,1024]{1,0:T(8,128)(2,1)S(1)}, u32[]{:S(2)}, u32[]{:S(2)}) collective-permute-start(bf16[128,1024]{1,0:T(8,128)(2,1)S(1)} %get-tuple-element.22), channel_id=1, source_target_pairs={{0,64},{64,128},{128,192},{192,0},{1,65},{65,129},{129,193},{193,1... | collective-permute-start | bytes 786440 | tf_op jit(solution)/shard_map/ppermute | solution.py:169
  52.8 24.3 %collective-permute-start.6 = (bf16[4,128,384]{2,1,0:T(8,128)(2,1)S(1)}, bf16[4,128,384]{2,1,0:T(8,128)(2,1)}, u32[]{:S(2)}, u32[]{:S(2)}) collective-permute-start(bf16[4,128,384]{2,1,0:T(8,128)(2,1)S(1)} %pad_maximum_fusion.5), channel_id=1, source_target_pairs={{0,256},{256,32},{32,288},{288,0},{1,257},{257,33},{33,289},{289,1... | collective-permute-start | bytes 1179656 | tf_op jit(solution)/shard_map/ppermute | solution.py:169
  56.0 21.2 %collective-permute-start.5 = (bf16[4,128,384]{2,1,0:T(8,128)(2,1)S(1)}, bf16[4,128,384]{2,1,0:T(8,128)(2,1)}, u32[]{:S(2)}, u32[]{:S(2)}) collective-permute-start(bf16[4,128,384]{2,1,0:T(8,128)(2,1)S(1)} %pad_maximum_fusion.5), channel_id=1, source_target_pairs={{0,32},{256,288},{32,0},{288,256},{1,33},{257,289},{33,1},{289,257... | collective-permute-start | bytes 1179656 | tf_op jit(solution)/shard_map/ppermute | solution.py:169
  60.3 16.9 %collective-permute-start.4 = (bf16[4,128,384]{2,1,0:T(8,128)(2,1)S(1)}, bf16[4,128,384]{2,1,0:T(8,128)(2,1)}, u32[]{:S(2)}, u32[]{:S(2)}) collective-permute-start(bf16[4,128,384]{2,1,0:T(8,128)(2,1)S(1)} %pad_maximum_fusion.5), channel_id=1, source_target_pairs={{0,288},{256,0},{32,256},{288,32},{1,289},{257,1},{33,257},{289,33... | collective-permute-start | bytes 1179656 | tf_op jit(solution)/shard_map/ppermute | solution.py:169
  64.4 45.9 %all-to-all-start.1 = ((bf16[64,4,1024]{2,1,0:T(4,128)(2,1)}), bf16[64,4,1024]{2,1,0:T(4,128)(2,1)}, u32[]{:S(2)}, u32[]{:S(2)}) async-start(bf16[64,4,1024]{2,1,0:T(4,128)(2,1)} %reshape.46), calls=%async_computation.1 | async-start | bytes 1048576 | tf_op jit(solution)/shard_map/all_to_all | solution.py:186
  78.7 32.8 %copy-start.5 = (f32[1024]{0:T(1024)S(1)}, f32[1024]{0:T(1024)}, u32[]{:S(2)}) copy-start(f32[1024]{0:T(1024)} %param.7) | copy-start | bytes 12292
  78.7 32.8 %copy-start.6 = (s32[8]{0:T(128)S(1)}, s32[8]{0:T(128)}, u32[]{:S(2)}) copy-start(s32[8]{0:T(128)} %reach_ref.2) | copy-start | bytes 100
  78.7 32.7 %collective-permute-start.7 = (bf16[16,128,384]{2,1,0:T(8,128)(2,1)S(1)}, bf16[16,128,384]{2,1,0:T(8,128)(2,1)}, u32[]{:S(2)}, u32[]{:S(2)}) collective-permute-start(bf16[16,128,384]{2,1,0:T(8,128)(2,1)S(1)} %bitcast.33), channel_id=1, source_target_pairs={{0,1},{1,0},{2,3},{3,2},{4,5},{5,4},{6,7},{7,6},{8,9},{9,8},{10,11... | collective-permute-start | bytes 4718600 | tf_op jit(solution)/shard_map/ppermute | solution.py:200
  82.9 37.0 %collective-permute-start.8 = (bf16[4,128,640]{2,1,0:T(8,128)(2,1)}, bf16[4,128,640]{2,1,0:T(8,128)(2,1)}, u32[]{:S(2)}, u32[]{:S(2)}) collective-permute-start(bf16[4,128,640]{2,1,0:T(8,128)(2,1)} %pad_maximum_fusion.2), channel_id=1, source_target_pairs={{0,288},{256,0},{32,256},{288,32},{1,289},{257,1},{33,257},{289,33... | collective-permute-start | bytes 1966088 | tf_op jit(solution)/shard_map/ppermute | solution.py:169
  87.1 33.9 %collective-permute-start.9 = (bf16[4,128,640]{2,1,0:T(8,128)(2,1)}, bf16[4,128,640]{2,1,0:T(8,128)(2,1)}, u32[]{:S(2)}, u32[]{:S(2)}) collective-permute-start(bf16[4,128,640]{2,1,0:T(8,128)(2,1)} %pad_maximum_fusion.2), channel_id=1, source_target_pairs={{0,32},{256,288},{32,0},{288,256},{1,33},{257,289},{33,1},{289,257... | collective-permute-start | bytes 1966088 | tf_op jit(solution)/shard_map/ppermute | solution.py:169
  90.7 34.2 %collective-permute-start.10 = (bf16[4,128,640]{2,1,0:T(8,128)(2,1)}, bf16[4,128,640]{2,1,0:T(8,128)(2,1)}, u32[]{:S(2)}, u32[]{:S(2)}) collective-permute-start(bf16[4,128,640]{2,1,0:T(8,128)(2,1)} %pad_maximum_fusion.2), channel_id=1, source_target_pairs={{0,256},{256,32},{32,288},{288,0},{1,257},{257,33},{33,289},{289,1... | collective-permute-start | bytes 1966088 | tf_op jit(solution)/shard_map/ppermute | solution.py:169
  126.0 14.3 %copy-start.7 = (s32[8]{0:T(128)S(1)}, s32[8]{0:T(128)}, u32[]{:S(2)}) copy-start(s32[8]{0:T(128)} %reach_ref.3) | copy-start | bytes 100
  126.5 13.9 %collective-permute-start.11 = (bf16[16,128,640]{2,1,0:T(8,128)(2,1)S(1)}, bf16[16,128,640]{2,1,0:T(8,128)(2,1)}, u32[]{:S(2)}, u32[]{:S(2)}) collective-permute-start(bf16[16,128,640]{2,1,0:T(8,128)(2,1)S(1)} %bitcast.31), channel_id=1, source_target_pairs={{0,1},{1,0},{2,3},{3,2},{4,5},{5,4},{6,7},{7,6},{8,9},{9,8},{10,11... | collective-permute-start | bytes 7864328 | tf_op jit(solution)/shard_map/ppermute | solution.py:200
  129.6 34.4 %all-to-all-start.2 = ((bf16[64,4,512]{2,1,0:T(4,128)(2,1)}), bf16[64,4,512]{2,1,0:T(4,128)(2,1)S(1)}, u32[]{:S(2)}, u32[]{:S(2)}) async-start(bf16[64,4,512]{2,1,0:T(4,128)(2,1)} %reshape.51), calls=%async_computation.2 | async-start | bytes 524288 | tf_op jit(solution)/shard_map/all_to_all | solution.py:205
  148.5 1.0 copy-start.1
  149.5 1.0 copy-start.3
  150.4 13.8 %copy-start.2 = (f32[256,1024]{1,0:T(8,128)S(1)}, f32[256,1024]{1,0:T(8,128)}, u32[]{:S(2)}) copy-start(f32[256,1024]{1,0:T(8,128)} %copy-done.1) | copy-start | bytes 3145732
  164.3 1.2 copy-start.4

commit v4 on v3

--- a/solution.py
+++ b/solution.py
@@ -1,5 +1,3 @@
-import functools
-
 import jax
 import jax.numpy as jnp
 from jax import lax
@@ -79,11 +77,29 @@
 
 def column_kernel(place, reach_ref, gain_ref, x_ref, own_ref, other_ref, out_ref, done_ref, w_ref, n_ref, qkv_ref):
     done_ref[0] = 0
-    assemble(place, True, own_ref, other_ref, slice(0, PART), w_ref, 0, PART)
+    core = place[2]
+    for a in range(XL):
+        for y in range(Y):
+            for b in range(XH):
+                for zz in range(Z // 2):
+                    for ref, c in ((own_ref, core), (other_ref, 1 - core)):
+                        row = b * 512 + 64 * zz + 32 * (1 - a) + 16 * c
+                        w_ref[pl.ds(pl.multiple_of(row, 16), 16), pl.ds(PART * y, PART)] = ref[
+                            (a * Y + y) * XH + b, pl.ds(16 * zz, 16), :
+                        ]
     i, j = pairs()
     back = (i >> 2) - (j >> 2)
     dist = jnp.where((((i ^ j) & 3) == 0) & (back >= 0), back, FAR)
     attend(reach_ref, gain_ref, x_ref, w_ref, n_ref, qkv_ref, out_ref, dist)
+
+
+def pack_kernel(after, *refs):
+    *parts, out_ref, sems = refs
+    copies = [pltpu.make_async_copy(p, out_ref.at[i], sems.at[i]) for i, p in enumerate(parts)]
+    for copy in copies:
+        copy.start()
+    for copy in copies:
+        copy.wait()
 
 
 def row_kernel(
@@ -140,6 +156,17 @@
         cost_estimate=COST,
         name="columns",
     )(place, reach, gain, x, own, other)
+
+
+def pack(after, parts):
+    return pl.pallas_call(
+        pack_kernel,
+        out_shape=jax.ShapeDtypeStruct((len(parts), *parts[0].shape), jnp.bfloat16),
+        in_specs=[SMEM] + [pl.BlockSpec(memory_space=pl.ANY)] * len(parts),
+        out_specs=pl.BlockSpec(memory_space=pl.ANY),
+        scratch_shapes=[pltpu.SemaphoreType.DMA((len(parts),))],
+        name="pack",
+    )(after, *parts)
 
 
 def row_attention(place, reach, gain, x, own, other):
@@ -158,7 +185,7 @@
             pltpu.VMEM((FEATURES, FEATURES), jnp.bfloat16),
         ],
         compiler_params=PARAMS,
-        cost_estimate=COST,
+        cost_estimate=pl.CostEstimate(flops=1 << 20, bytes_accessed=1 << 20, transcendentals=0),
         name="rows",
     )(place, reach, gain, x, own, other)
 
@@ -180,33 +207,35 @@
     block = jnp.concatenate([w_qkv, w_out], axis=1)
     change = [(a * Z + z, (a ^ (z & 1)) * Z + z) for a in range(XL) for z in range(Z)]
     block = lax.ppermute(block, ("xl", "z"), change)
+
     column = lax.all_to_all(jnp.broadcast_to(block, (Z, 16, 512)), "z", split_axis=0, concat_axis=0)
-
-    sent, column = lax.optimization_barrier((rows, column))
-    turned = lax.all_to_all(sent.reshape(64, 4, FEATURES), SEQ, split_axis=0, concat_axis=0)
-    turned = turned.reshape(STRIDE, FEATURES)
-
     halves = column.reshape(Z // 2, 2, 16, 512)
     row_part = jnp.where(xl == 0, halves[:, 0], halves[:, 1]).reshape(128, 512)
     col_part = jnp.where(xl == 0, halves[:, 1], halves[:, 0]).reshape(128, 512)
-    part = jnp.concatenate([col_part[:, :PART], row_part, col_part[:, PART:]], axis=1)
-    near = jnp.stack([part, *ring(part, "y", range(Y))])
-
-    def plane(part):
-        return [part, *ring(part, ("xl", "xh"), [0, 2, 1, 3])]
-
-    def both_cores(parts):
-        own = jnp.stack(parts).reshape(X * Y, *parts[0].shape[1:])
-        return own, lax.ppermute(own, "c", [(0, 1), (1, 0)])
-
-    col_plane = plane(near[:, :, :PART])
-    col_own, col_other = both_cores(col_plane)
+    rest_part = jnp.concatenate([row_part, col_part[:, PART:]], axis=1)
+
+    col_own = lax.all_to_all(
+        jnp.broadcast_to(col_part[:, :PART], (X * Y, 128, PART)),
+        ("xl", "y", "xh"),
+        split_axis=0,
+        concat_axis=0,
+    )
+
+    near = jnp.stack([rest_part, *ring(rest_part, "y", range(Y))])
+
+    sent, col_own, near = lax.optimization_barrier((rows, col_own, near))
+    turned = lax.all_to_all(sent.reshape(64, 4, FEATURES), SEQ, split_axis=0, concat_axis=0)
+    turned = turned.reshape(STRIDE, FEATURES)
+
+    swap = [(0, 1), (1, 0)]
+    col_other = lax.ppermute(col_own, "c", swap)
+    near, col_other = lax.optimization_barrier((near, col_other))
+    plane = [near, *ring(near, ("xl", "xh"), [0, 2, 1, 3])]
     col_mid, done = column_attention(place, col_rows, gain, turned, col_own, col_other)
     col_out = lax.all_to_all(col_mid.reshape(64, 4, HALF), SEQ, split_axis=0, concat_axis=0)
 
-    near_rest, _ = lax.optimization_barrier((near[:, :, PART:], col_plane))
-    rest = [jnp.where(done[0] == 0, a, 0) for a in plane(near_rest)]
-    rest_own, rest_other = both_cores(rest)
+    rest_own = pack(done, plane).reshape(X * Y, 128, 640)
+    rest_other = lax.ppermute(rest_own, "c", swap)
     base, low, last = row_attention(place, row_blocks, gain, rows, rest_own, rest_other)
     col_out = jnp.where(last[0] == 0, col_out, 0).reshape(STRIDE, HALF)
 

time: 168 us -> 255 us (1.52)
  Pallas kernels: 16 us -> 95.8 us
  waiting for transfers between devices: 54.5 us -> 64.1 us
  other arithmetic: 8.47 us -> 1.9 us
  local copies, waits for them, and re-layouts: 6.91 us -> 10 us
    pallas_call x0 -> x1, Pallas kernels: none -> 81.2 us  [pack(): pl.pallas_call(pack_kernel, out_shape=jax.ShapeDtypeStruct((len(parts), *...]
    ppermute x9 -> x6, starting transfers between devices: 30.2 us -> 21 us  [ring(): lax.ppermute(part, axes, [(order[i], order[(i - t) % size]) for i in rang...]
    all_to_all x0 -> x1, starting transfers between devices: none -> 6.75 us  [body(): lax.all_to_all(jnp.broadcast_to(col_part[:, :PART], (X * Y, 128, PART)),...]
    another operation x9 -> x2, other arithmetic: 7.5 us -> 0.96 us  [body(): near = jnp.stack([rest_part, *ring(rest_part, 'y', range(Y))])]
    ppermute x9 -> x6, waiting for transfers between devices: 11.2 us -> 16.7 us  [ring(): lax.ppermute(part, axes, [(order[i], order[(i - t) % size]) for i in rang...]
    all_to_all x1, waiting for transfers between devices: 17.7 us -> 22.2 us  [body(): lax.all_to_all(sent.reshape(64, 4, FEATURES), SEQ, split_axis=0, concat_a...]
    all_to_all x1, starting transfers between devices: 10.7 us -> 14 us  [body(): lax.all_to_all(col_mid.reshape(64, 4, HALF), SEQ, split_axis=0, concat_ax...]
  transfers between devices with their start and end apart: 15 -> 13, of which waited for: 6 -> 5; matrix products, arithmetic and copies ran while one was open for 5% -> 2% of each run, Pallas kernels for 9% -> 5%
where the time goes in v4:
time: 255 us; the launch traced here: 254 us
  Pallas kernels  95.8 us (38%)
  starting transfers between devices  81.2 us (32%)
  waiting for transfers between devices  64.1 us (25%)
  local copies, waits for them, and re-layouts  10 us (4%)
    pallas_call x1, Pallas kernels, pack(): pl.pallas_call(pack_kernel, out_shape=jax.ShapeDtypeStruct((len(parts), *...  81.2 us
    all_to_all x1, waiting for transfers between devices, body(): lax.all_to_all(sent.reshape(64, 4, FEATURES), SEQ, split_axis=0, concat_a...  22.2 us
    ppermute x6, starting transfers between devices, ring(): lax.ppermute(part, axes, [(order[i], order[(i - t) % size]) for i in rang...  21 us
    all_to_all x1, starting transfers between devices, body(): lax.all_to_all(jnp.broadcast_to(block, (Z, 16, 512)), 'z', split_axis=0,...  19.1 us
    ppermute x6, waiting for transfers between devices, ring(): lax.ppermute(part, axes, [(order[i], order[(i - t) % size]) for i in rang...  16.7 us
    all_to_all x1, starting transfers between devices, body(): lax.all_to_all(col_mid.reshape(64, 4, HALF), SEQ, split_axis=0, concat_ax...  14 us
    all_to_all x1, waiting for transfers between devices, body(): lax.all_to_all(jnp.broadcast_to(block, (Z, 16, 512)), 'z', split_axis=0,...  12.8 us
    all_to_all x1, waiting for transfers between devices, body(): lax.all_to_all(col_mid.reshape(64, 4, HALF), SEQ, split_axis=0, concat_ax...  12.4 us
  transfers between devices with their start and end apart: 13, of which 5 were waited for; matrix products, arithmetic and copies ran while one was open for 2% of the time, Pallas kernels for 5%

profile of v4, /device:TPU:1, one launch (start us, length us, event | category | flops | bytes accessed | tf_op | source)
XLA Modules:
  0.0 254.0 jit_solution(14990438365826813806)
XLA Ops:
  2.1 19.1 %all-to-all-start = ((bf16[16,16,512]{2,1,0:T(8,128)(2,1)}), bf16[16,16,512]{2,1,0:T(8,128)(2,1)S(1)}, u32[]{:S(2)}, u32[]{:S(2)}) async-start(bf16[16,16,512]{2,1,0:T(8,128)(2,1)} %broadcast_in_dim.10), calls=%async_computation | async-start | bytes 524288 | tf_op jit(solution)/shard_map/all_to_all | solution.py:211
  21.2 12.8 %all-to-all-done = bf16[16,16,512]{2,1,0:T(8,128)(2,1)S(1)} async-done(((bf16[16,16,512]{2,1,0:T(8,128)(2,1)}), bf16[16,16,512]{2,1,0:T(8,128)(2,1)S(1)}, u32[]{:S(2)}, u32[]{:S(2)}) %all-to-all-start) | async-done | bytes 262176 | tf_op jit(solution)/shard_map/all_to_all | solution.py:211
  34.1 1.4 broadcast_in_dim.11
  35.5 6.8 %all-to-all-start.1 = ((bf16[16,128,384]{2,1,0:T(8,128)(2,1)}), bf16[16,128,384]{2,1,0:T(8,128)(2,1)S(1)}, u32[]{:S(2)}, u32[]{:S(2)}) async-start(bf16[16,128,384]{2,1,0:T(8,128)(2,1)} %broadcast_in_dim.11), calls=%async_computation.1 | async-start | bytes 3145728 | tf_op jit(solution)/shard_map/all_to_all | solution.py:217
  42.3 4.9 %collective-permute-start.2 = (bf16[128,640]{1,0:T(8,128)(2,1)S(1)}, bf16[128,640]{1,0:T(8,128)(2,1)S(1)}, u32[]{:S(2)}, u32[]{:S(2)}) collective-permute-start(bf16[128,640]{1,0:T(8,128)(2,1)S(1)} %get-tuple-element.28), channel_id=1, source_target_pairs={{0,128},{64,192},{128,0},{192,64},{1,129},{65,193},{129,1},{193,65... | collective-permute-start | bytes 491528 | tf_op jit(solution)/shard_map/ppermute | solution.py:196
  47.2 2.8 %collective-permute-start.1 = (bf16[128,640]{1,0:T(8,128)(2,1)S(1)}, bf16[128,640]{1,0:T(8,128)(2,1)S(1)}, u32[]{:S(2)}, u32[]{:S(2)}) collective-permute-start(bf16[128,640]{1,0:T(8,128)(2,1)S(1)} %get-tuple-element.28), channel_id=1, source_target_pairs={{0,192},{64,0},{128,64},{192,128},{1,193},{65,1},{129,65},{193,129... | collective-permute-start | bytes 491528 | tf_op jit(solution)/shard_map/ppermute | solution.py:196
  50.0 2.5 collective-permute-start.3
  52.5 14.2 %collective-permute-done.2 = bf16[128,640]{1,0:T(8,128)(2,1)S(1)} collective-permute-done((bf16[128,640]{1,0:T(8,128)(2,1)S(1)}, bf16[128,640]{1,0:T(8,128)(2,1)S(1)}, u32[]{:S(2)}, u32[]{:S(2)}) %collective-permute-start.2) | collective-permute-done | bytes 163872 | tf_op jit(solution)/shard_map/ppermute | solution.py:196
  66.7 2.5 collective-permute-done.1
  70.1 4.8 %collective-permute-start.4 = (bf16[16,128,384]{2,1,0:T(8,128)(2,1)S(1)}, bf16[16,128,384]{2,1,0:T(8,128)(2,1)}, u32[]{:S(2)}, u32[]{:S(2)}) collective-permute-start(bf16[16,128,384]{2,1,0:T(8,128)(2,1)S(1)} %all-to-all-done.1.own_ref), channel_id=1, source_target_pairs={{0,1},{1,0},{2,3},{3,2},{4,5},{5,4},{6,7},{7,6},{8,9},{9,8},{10,11... | collective-permute-start | bytes 4718600 | tf_op jit(solution)/shard_map/ppermute | solution.py:231
  75.9 12.3 %all-to-all-start.2 = ((bf16[64,4,1024]{2,1,0:T(4,128)(2,1)}), bf16[64,4,1024]{2,1,0:T(4,128)(2,1)}, u32[]{:S(2)}, u32[]{:S(2)}) async-start(bf16[64,4,1024]{2,1,0:T(4,128)(2,1)} %reshape.42), calls=%async_computation.2 | async-start | bytes 1048576 | tf_op jit(solution)/shard_map/all_to_all | solution.py:227
  88.2 2.2 collective-permute-start.7
  90.4 5.5 %collective-permute-start.6 = (bf16[4,128,640]{2,1,0:T(8,128)(2,1)}, bf16[4,128,640]{2,1,0:T(8,128)(2,1)}, u32[]{:S(2)}, u32[]{:S(2)}) collective-permute-start(bf16[4,128,640]{2,1,0:T(8,128)(2,1)} %pad_maximum_fusion.refs_0_), channel_id=1, source_target_pairs={{0,32},{256,288},{32,0},{288,256},{1,33},{257,289},{33,1},{289,257... | collective-permute-start | bytes 1966088 | tf_op jit(solution)/shard_map/ppermute | solution.py:196
  95.9 3.1 %collective-permute-start.5 = (bf16[4,128,640]{2,1,0:T(8,128)(2,1)}, bf16[4,128,640]{2,1,0:T(8,128)(2,1)}, u32[]{:S(2)}, u32[]{:S(2)}) collective-permute-start(bf16[4,128,640]{2,1,0:T(8,128)(2,1)} %pad_maximum_fusion.refs_0_), channel_id=1, source_target_pairs={{0,288},{256,0},{32,256},{288,32},{1,289},{257,1},{33,257},{289,33... | collective-permute-start | bytes 1966088 | tf_op jit(solution)/shard_map/ppermute | solution.py:196
  99.1 22.2 %all-to-all-done.2 = bf16[64,4,1024]{2,1,0:T(4,128)(2,1)} async-done(((bf16[64,4,1024]{2,1,0:T(4,128)(2,1)}), bf16[64,4,1024]{2,1,0:T(4,128)(2,1)}, u32[]{:S(2)}, u32[]{:S(2)}) %all-to-all-start.2) | async-done | bytes 524320 | tf_op jit(solution)/shard_map/all_to_all | solution.py:227
  122.5 6.4 %columns.1 = (bf16[256,512]{1,0:T(8,128)(2,1)S(1)}, s32[1]{0:T(128)}) custom-call(s32[3]{0:T(128)S(1)} %pad_add_fusion.place, s32[8]{0:T(128)S(1)} %copy-done.7, f32[1,1024]{1,0:T(1,128)S(1)} %bitcast.20, bf16[256,1024]{1,0:T(8,128)(2,1)S(1)} %reshape.43.x_ref, bf16[16,128,384]{2,1,0:T(8,128)(2,1)S(1)} %all-to-all-done.1.own_ref, ...), custom_call_target="tpu_custom_call" | custom-call | flops 939524096 | bytes 6291456 | tf_op jit(solution)/shard_map/columns/pallas_call | solution.py:146
  128.9 81.2 %pack.1 = bf16[4,4,128,640]{3,2,1,0:T(8,128)(2,1)} custom-call(s32[1]{0:T(128)} %get-tuple-element.19.after, bf16[4,128,640]{2,1,0:T(8,128)(2,1)} %pad_maximum_fusion.refs_0_, bf16[4,128,640]{2,1,0:T(8,128)(2,1)} %collective-permute-done.5.refs_1_, bf16[4,128,640]{2,1,0:T(8,128)(2,1)} %collective-permute-done.6.refs_2_, ...), custom_call_target="tpu_custom_call" | custom-call | tf_op jit(solution)/shard_map/pack/pallas_call | solution.py:162
  210.2 2.7 %collective-permute-start.8 = (bf16[16,128,640]{2,1,0:T(8,128)(2,1)}, bf16[16,128,640]{2,1,0:T(8,128)(2,1)S(1)}, u32[]{:S(2)}, u32[]{:S(2)}) collective-permute-start(bf16[16,128,640]{2,1,0:T(8,128)(2,1)} %bitcast.16), channel_id=1, source_target_pairs={{0,1},{1,0},{2,3},{3,2},{4,5},{5,4},{6,7},{7,6},{8,9},{9,8},{10,11... | collective-permute-start | bytes 7864328 | tf_op jit(solution)/shard_map/ppermute | solution.py:238
  213.6 14.0 %all-to-all-start.3 = ((bf16[64,4,512]{2,1,0:T(4,128)(2,1)}), bf16[64,4,512]{2,1,0:T(4,128)(2,1)S(1)}, u32[]{:S(2)}, u32[]{:S(2)}) async-start(bf16[64,4,512]{2,1,0:T(4,128)(2,1)} %reshape.45), calls=%async_computation.3 | async-start | bytes 524288 | tf_op jit(solution)/shard_map/all_to_all | solution.py:235
  227.7 1.7 copy-done
  229.4 7.0 %rows.1 = (f32[256,1024]{1,0:T(8,128)S(1)}, bf16[512,1024]{1,0:T(8,128)(2,1)S(1)}, s32[1]{0:T(128)}) custom-call(s32[3]{0:T(128)S(1)} %pad_add_fusion.place, s32[8]{0:T(128)S(1)} %copy-done.8, f32[1,1024]{1,0:T(1,128)S(1)} %bitcast.21, bf16[256,1024]{1,0:T(8,128)(2,1)S(1)} %bitcast.19, bf16[16,128,640]{2,1,0:T(8,128)(2,1)S(1)} %bitcast.17, ...), custom_call_target="tpu_custom_call" | custom-call | flops 1048576 | bytes 1048576 | tf_op jit(solution)/shard_map/rows/pallas_call | solution.py:173
  239.0 12.4 %all-to-all-done.3 = bf16[64,4,512]{2,1,0:T(4,128)(2,1)S(1)} async-done(((bf16[64,4,512]{2,1,0:T(4,128)(2,1)}), bf16[64,4,512]{2,1,0:T(4,128)(2,1)S(1)}, u32[]{:S(2)}, u32[]{:S(2)}) %all-to-all-start.3) | async-done | bytes 262176 | tf_op jit(solution)/shard_map/all_to_all | solution.py:235
  251.6 1.2 copy-done.5
  252.8 1.2 mixed.1
  (38 shorter events, 8.3 us)
Async XLA Ops:
  0.7 0.7 collective-permute-start
  2.1 31.9 %all-to-all-start = ((bf16[16,16,512]{2,1,0:T(8,128)(2,1)}), bf16[16,16,512]{2,1,0:T(8,128)(2,1)S(1)}, u32[]{:S(2)}, u32[]{:S(2)}) async-start(bf16[16,16,512]{2,1,0:T(8,128)(2,1)} %broadcast_in_dim.10), calls=%async_computation | async-start | bytes 524288 | tf_op jit(solution)/shard_map/all_to_all | solution.py:211
  35.5 34.7 %all-to-all-start.1 = ((bf16[16,128,384]{2,1,0:T(8,128)(2,1)}), bf16[16,128,384]{2,1,0:T(8,128)(2,1)S(1)}, u32[]{:S(2)}, u32[]{:S(2)}) async-start(bf16[16,128,384]{2,1,0:T(8,128)(2,1)} %broadcast_in_dim.11), calls=%async_computation.1 | async-start | bytes 3145728 | tf_op jit(solution)/shard_map/all_to_all | solution.py:217
  42.2 32.7 %copy-start.1 = (bf16[1,1,256,1024]{3,2,1,0:T(8,128)(2,1)S(1)}, bf16[1,1,256,1024]{3,2,1,0:T(8,128)(2,1)}, u32[]{:S(2)}) copy-start(bf16[1,1,256,1024]{3,2,1,0:T(8,128)(2,1)} %param.6) | copy-start | bytes 1572868
  42.3 24.4 %collective-permute-start.2 = (bf16[128,640]{1,0:T(8,128)(2,1)S(1)}, bf16[128,640]{1,0:T(8,128)(2,1)S(1)}, u32[]{:S(2)}, u32[]{:S(2)}) collective-permute-start(bf16[128,640]{1,0:T(8,128)(2,1)S(1)} %get-tuple-element.28), channel_id=1, source_target_pairs={{0,128},{64,192},{128,0},{192,64},{1,129},{65,193},{129,1},{193,65... | collective-permute-start | bytes 491528 | tf_op jit(solution)/shard_map/ppermute | solution.py:196
  47.2 22.0 %collective-permute-start.1 = (bf16[128,640]{1,0:T(8,128)(2,1)S(1)}, bf16[128,640]{1,0:T(8,128)(2,1)S(1)}, u32[]{:S(2)}, u32[]{:S(2)}) collective-permute-start(bf16[128,640]{1,0:T(8,128)(2,1)S(1)} %get-tuple-element.28), channel_id=1, source_target_pairs={{0,192},{64,0},{128,64},{192,128},{1,193},{65,1},{129,65},{193,129... | collective-permute-start | bytes 491528 | tf_op jit(solution)/shard_map/ppermute | solution.py:196
  50.0 19.2 %collective-permute-start.3 = (bf16[128,640]{1,0:T(8,128)(2,1)S(1)}, bf16[128,640]{1,0:T(8,128)(2,1)S(1)}, u32[]{:S(2)}, u32[]{:S(2)}) collective-permute-start(bf16[128,640]{1,0:T(8,128)(2,1)S(1)} %get-tuple-element.28), channel_id=1, source_target_pairs={{0,64},{64,128},{128,192},{192,0},{1,65},{65,129},{129,193},{193,1... | collective-permute-start | bytes 491528 | tf_op jit(solution)/shard_map/ppermute | solution.py:196
  70.1 52.4 %copy-start.6 = (f32[1024]{0:T(1024)S(1)}, f32[1024]{0:T(1024)}, u32[]{:S(2)}) copy-start(f32[1024]{0:T(1024)} %param.7) | copy-start | bytes 12292
  70.1 52.4 %copy-start.7 = (s32[8]{0:T(128)S(1)}, s32[8]{0:T(128)}, u32[]{:S(2)}) copy-start(s32[8]{0:T(128)} %reach_ref.2) | copy-start | bytes 100
  70.1 18.1 %collective-permute-start.4 = (bf16[16,128,384]{2,1,0:T(8,128)(2,1)S(1)}, bf16[16,128,384]{2,1,0:T(8,128)(2,1)}, u32[]{:S(2)}, u32[]{:S(2)}) collective-permute-start(bf16[16,128,384]{2,1,0:T(8,128)(2,1)S(1)} %all-to-all-done.1.own_ref), channel_id=1, source_target_pairs={{0,1},{1,0},{2,3},{3,2},{4,5},{5,4},{6,7},{7,6},{8,9},{9,8},{10,11... | collective-permute-start | bytes 4718600 | tf_op jit(solution)/shard_map/ppermute | solution.py:231
  75.9 45.4 %all-to-all-start.2 = ((bf16[64,4,1024]{2,1,0:T(4,128)(2,1)}), bf16[64,4,1024]{2,1,0:T(4,128)(2,1)}, u32[]{:S(2)}, u32[]{:S(2)}) async-start(bf16[64,4,1024]{2,1,0:T(4,128)(2,1)} %reshape.42), calls=%async_computation.2 | async-start | bytes 1048576 | tf_op jit(solution)/shard_map/all_to_all | solution.py:227
  88.2 40.7 %collective-permute-start.7 = (bf16[4,128,640]{2,1,0:T(8,128)(2,1)}, bf16[4,128,640]{2,1,0:T(8,128)(2,1)}, u32[]{:S(2)}, u32[]{:S(2)}) collective-permute-start(bf16[4,128,640]{2,1,0:T(8,128)(2,1)} %pad_maximum_fusion.refs_0_), channel_id=1, source_target_pairs={{0,256},{256,32},{32,288},{288,0},{1,257},{257,33},{33,289},{289,1... | collective-permute-start | bytes 1966088 | tf_op jit(solution)/shard_map/ppermute | solution.py:196
  90.4 38.5 %collective-permute-start.6 = (bf16[4,128,640]{2,1,0:T(8,128)(2,1)}, bf16[4,128,640]{2,1,0:T(8,128)(2,1)}, u32[]{:S(2)}, u32[]{:S(2)}) collective-permute-start(bf16[4,128,640]{2,1,0:T(8,128)(2,1)} %pad_maximum_fusion.refs_0_), channel_id=1, source_target_pairs={{0,32},{256,288},{32,0},{288,256},{1,33},{257,289},{33,1},{289,257... | collective-permute-start | bytes 1966088 | tf_op jit(solution)/shard_map/ppermute | solution.py:196
  95.9 33.0 %collective-permute-start.5 = (bf16[4,128,640]{2,1,0:T(8,128)(2,1)}, bf16[4,128,640]{2,1,0:T(8,128)(2,1)}, u32[]{:S(2)}, u32[]{:S(2)}) collective-permute-start(bf16[4,128,640]{2,1,0:T(8,128)(2,1)} %pad_maximum_fusion.refs_0_), channel_id=1, source_target_pairs={{0,288},{256,0},{32,256},{288,32},{1,289},{257,1},{33,257},{289,33... | collective-permute-start | bytes 1966088 | tf_op jit(solution)/shard_map/ppermute | solution.py:196
  128.9 98.7 %copy-start.8 = (s32[8]{0:T(128)S(1)}, s32[8]{0:T(128)}, u32[]{:S(2)}) copy-start(s32[8]{0:T(128)} %reach_ref.3) | copy-start | bytes 100
  210.2 17.5 %collective-permute-start.8 = (bf16[16,128,640]{2,1,0:T(8,128)(2,1)}, bf16[16,128,640]{2,1,0:T(8,128)(2,1)S(1)}, u32[]{:S(2)}, u32[]{:S(2)}) collective-permute-start(bf16[16,128,640]{2,1,0:T(8,128)(2,1)} %bitcast.16), channel_id=1, source_target_pairs={{0,1},{1,0},{2,3},{3,2},{4,5},{5,4},{6,7},{7,6},{8,9},{9,8},{10,11... | collective-permute-start | bytes 7864328 | tf_op jit(solution)/shard_map/ppermute | solution.py:238
  213.6 37.7 %all-to-all-start.3 = ((bf16[64,4,512]{2,1,0:T(4,128)(2,1)}), bf16[64,4,512]{2,1,0:T(4,128)(2,1)S(1)}, u32[]{:S(2)}, u32[]{:S(2)}) async-start(bf16[64,4,512]{2,1,0:T(4,128)(2,1)} %reshape.45), calls=%async_computation.3 | async-start | bytes 524288 | tf_op jit(solution)/shard_map/all_to_all | solution.py:235
  227.6 1.7 copy-start
  236.4 1.0 copy-start.2
  237.4 1.0 copy-start.4
  238.3 13.2 %copy-start.3 = (f32[256,1024]{1,0:T(8,128)S(1)}, f32[256,1024]{1,0:T(8,128)}, u32[]{:S(2)}) copy-start(f32[256,1024]{1,0:T(8,128)} %copy-done.2) | copy-start | bytes 3145732
  251.6 1.2 copy-start.5

commit v5 on v3

--- a/solution.py
+++ b/solution.py
@@ -1,5 +1,3 @@
-import functools
-
 import jax
 import jax.numpy as jnp
 from jax import lax
@@ -18,25 +16,18 @@
 FAR = 1 << 20
 
 
-def blocks(place, odd):
+def assemble(place, odd, refs, lanes, w_ref, first, width):
     x, y, core = place[0], place[1], place[2]
     for t in range(X):
         there = (x + t) & 3
         xh, xl = there >> 1, there & 1
-        turn = (1 - xl) if odd else xl
+        base = 512 * xh + 32 * ((1 - xl) if odd else xl)
         for s in range(Y):
-            for zz in range(Z // 2):
-                row = xh * 512 + 64 * zz + 32 * turn
-                yield t * Y + s, zz, row, (y + s) & 3
-
-
-def assemble(place, odd, own_ref, other_ref, lanes, w_ref, first, width):
-    core = place[2]
-    for block, zz, row, y in blocks(place, odd):
-        cols = pl.ds(pl.multiple_of(first + width * y, 128), width)
-        for ref, c in ((own_ref, core), (other_ref, 1 - core)):
-            at = pl.multiple_of(row + 16 * c, 16)
-            w_ref[pl.ds(at, 16), cols] = ref[block, pl.ds(16 * zz, 16), lanes]
+            cols = pl.ds(pl.multiple_of(first + width * ((y + s) & 3), 128), width)
+            for ref, c in ((refs[t], core), (refs[X + t], 1 - core)):
+                for zz in range(Z // 2):
+                    row = pl.multiple_of(base + 16 * c + 64 * zz, 16)
+                    w_ref[pl.ds(row, 16), cols] = ref[s, pl.ds(16 * zz, 16), lanes]
 
 
 def attend(reach_ref, gain_ref, x_ref, w_ref, n_ref, qkv_ref, out_ref, dist):
@@ -77,25 +68,25 @@
     return i, lax.broadcasted_iota(jnp.int32, (STRIDE, STRIDE), 1)
 
 
-def column_kernel(place, reach_ref, gain_ref, x_ref, own_ref, other_ref, out_ref, done_ref, w_ref, n_ref, qkv_ref):
-    done_ref[0] = 0
-    assemble(place, True, own_ref, other_ref, slice(0, PART), w_ref, 0, PART)
+def column_kernel(place, reach_ref, gain_ref, x_ref, *refs):
+    parts, (out_ref, w_ref, n_ref, qkv_ref) = refs[: 2 * X], refs[2 * X :]
+    assemble(place, True, parts, slice(0, PART), w_ref, 0, PART)
     i, j = pairs()
     back = (i >> 2) - (j >> 2)
     dist = jnp.where((((i ^ j) & 3) == 0) & (back >= 0), back, FAR)
     attend(reach_ref, gain_ref, x_ref, w_ref, n_ref, qkv_ref, out_ref, dist)
 
 
-def row_kernel(
-    place, reach_ref, gain_ref, x_ref, own_ref, other_ref, base_ref, low_ref, done_ref, w_ref, n_ref, qkv_ref, a_ref, o_ref
-):
+def row_kernel(place, reach_ref, gain_ref, x_ref, *refs):
+    parts = refs[: 2 * X]
+    base_ref, low_ref, done_ref, w_ref, n_ref, qkv_ref, a_ref, o_ref = refs[2 * X :]
     done_ref[0] = 0
-    assemble(place, False, own_ref, other_ref, slice(0, PART), w_ref, 0, PART)
+    assemble(place, False, parts, slice(0, PART), w_ref, 0, PART)
     i, j = pairs()
     dist = jnp.where(j <= i, (i >> 5) - (j >> 5), FAR)
     attend(reach_ref, gain_ref, x_ref, w_ref, n_ref, qkv_ref, a_ref, dist)
-    assemble(place, False, own_ref, other_ref, slice(PART, PART + 128), o_ref, 0, 128)
-    assemble(place, True, own_ref, other_ref, slice(PART + 128, PART + 256), o_ref, 512, 128)
+    assemble(place, False, parts, slice(PART, PART + 128), o_ref, 0, 128)
+    assemble(place, True, parts, slice(PART + 128, PART + 256), o_ref, 512, 128)
     for n in range(0, FEATURES, 256):
         base_ref[:, n : n + 256] = x_ref[:, n : n + 256].astype(jnp.float32) + jnp.dot(
             a_ref[...], o_ref[:HALF, n : n + 256], preferred_element_type=jnp.float32
@@ -126,23 +117,20 @@
 )
 
 
-def column_attention(place, reach, gain, x, own, other):
+def column_attention(place, reach, gain, x, parts):
     return pl.pallas_call(
         column_kernel,
-        out_shape=[
-            jax.ShapeDtypeStruct((STRIDE, HALF), jnp.bfloat16),
-            jax.ShapeDtypeStruct((1,), jnp.int32),
-        ],
-        in_specs=[SMEM, SMEM, VMEM, VMEM, VMEM, VMEM],
-        out_specs=[VMEM, SMEM],
+        out_shape=jax.ShapeDtypeStruct((STRIDE, HALF), jnp.bfloat16),
+        in_specs=[SMEM, SMEM] + [VMEM] * (2 + len(parts)),
+        out_specs=VMEM,
         scratch_shapes=WORK,
         compiler_params=PARAMS,
         cost_estimate=COST,
         name="columns",
-    )(place, reach, gain, x, own, other)
-
-
-def row_attention(place, reach, gain, x, own, other):
+    )(place, reach, gain, x, *parts)
+
+
+def row_attention(place, reach, gain, x, parts):
     return pl.pallas_call(
         row_kernel,
         out_shape=[
@@ -150,7 +138,7 @@
             jax.ShapeDtypeStruct((HALF, FEATURES), jnp.bfloat16),
             jax.ShapeDtypeStruct((1,), jnp.int32),
         ],
-        in_specs=[SMEM, SMEM, VMEM, VMEM, VMEM, VMEM],
+        in_specs=[SMEM, SMEM] + [VMEM] * (2 + len(parts)),
         out_specs=[VMEM, VMEM, SMEM],
         scratch_shapes=WORK
         + [
@@ -158,9 +146,9 @@
             pltpu.VMEM((FEATURES, FEATURES), jnp.bfloat16),
         ],
         compiler_params=PARAMS,
-        cost_estimate=COST,
+        cost_estimate=pl.CostEstimate(flops=1 << 20, bytes_accessed=1 << 20, transcendentals=0),
         name="rows",
-    )(place, reach, gain, x, own, other)
+    )(place, reach, gain, x, *parts)
 
 
 def ring(part, axes, order):
@@ -196,18 +184,15 @@
         return [part, *ring(part, ("xl", "xh"), [0, 2, 1, 3])]
 
     def both_cores(parts):
-        own = jnp.stack(parts).reshape(X * Y, *parts[0].shape[1:])
-        return own, lax.ppermute(own, "c", [(0, 1), (1, 0)])
+        return [*parts, *(lax.ppermute(a, "c", [(0, 1), (1, 0)]) for a in parts)]
 
     col_plane = plane(near[:, :, :PART])
-    col_own, col_other = both_cores(col_plane)
-    col_mid, done = column_attention(place, col_rows, gain, turned, col_own, col_other)
+    col_mid = column_attention(place, col_rows, gain, turned, both_cores(col_plane))
     col_out = lax.all_to_all(col_mid.reshape(64, 4, HALF), SEQ, split_axis=0, concat_axis=0)
 
     near_rest, _ = lax.optimization_barrier((near[:, :, PART:], col_plane))
-    rest = [jnp.where(done[0] == 0, a, 0) for a in plane(near_rest)]
-    rest_own, rest_other = both_cores(rest)
-    base, low, last = row_attention(place, row_blocks, gain, rows, rest_own, rest_other)
+    rest, _ = lax.optimization_barrier((plane(near_rest), col_mid))
+    base, low, last = row_attention(place, row_blocks, gain, rows, both_cores(rest))
     col_out = jnp.where(last[0] == 0, col_out, 0).reshape(STRIDE, HALF)
 
     mixed = pl.pallas_call(

time: 168 us -> 160 us (0.952)
  waiting for transfers between devices: 54.5 us -> 16.9 us
  blocking collectives: 0 us -> 31.7 us
  other arithmetic: 8.47 us -> 2.15 us
  starting transfers between devices: 79 us -> 83.9 us
    all_to_all x0 -> x1, blocking collectives: none -> 31.7 us  [body(): lax.all_to_all(jnp.broadcast_to(block, (Z, 16, 512)), 'z', split_axis=0,...]
    all_to_all x1 -> x0, starting transfers between devices: 19.1 us -> none  [body(): lax.all_to_all(jnp.broadcast_to(block, (Z, 16, 512)), 'z', split_axis=0,...]
    all_to_all x1, waiting for transfers between devices: 17.7 us -> 0.01 us  [body(): lax.all_to_all(sent.reshape(64, 4, FEATURES), SEQ, split_axis=0, concat_a...]
    ppermute x2 -> x8, starting transfers between devices: 5.66 us -> 23.2 us  [both_cores(): return [*parts, *(lax.ppermute(a, 'c', [(0, 1), (1, 0)]) for a in parts)]]
    all_to_all x1 -> x0, waiting for transfers between devices: 12.8 us -> none  [body(): lax.all_to_all(jnp.broadcast_to(block, (Z, 16, 512)), 'z', split_axis=0,...]
    all_to_all x1, waiting for transfers between devices: 12.8 us -> 2.7 us  [body(): lax.all_to_all(col_mid.reshape(64, 4, HALF), SEQ, split_axis=0, concat_ax...]
    another operation x7 -> x0, other arithmetic: 6.53 us -> none  [both_cores(): own = jnp.stack(parts).reshape(X * Y, *parts[0].shape[1:])]
    all_to_all x1, starting transfers between devices: 12.7 us -> 15.4 us  [body(): lax.all_to_all(sent.reshape(64, 4, FEATURES), SEQ, split_axis=0, concat_a...]
  transfers between devices with their start and end apart: 15 -> 20, of which waited for: 6 -> 6; matrix products, arithmetic and copies ran while one was open for 5% -> 1% of each run, Pallas kernels for 9% -> 9%
where the time goes in v5:
time: 160 us; the launch traced here: 159 us
  starting transfers between devices  83.9 us (52%)
  blocking collectives  31.7 us (20%)
  waiting for transfers between devices  16.9 us (11%)
  Pallas kernels  15.4 us (10%)
  local copies, waits for them, and re-layouts  8.19 us (5%)
  other arithmetic  2.15 us (1%)
    all_to_all x1, blocking collectives, body(): lax.all_to_all(jnp.broadcast_to(block, (Z, 16, 512)), 'z', split_axis=0,...  31.7 us
    ppermute x9, starting transfers between devices, ring(): lax.ppermute(part, axes, [(order[i], order[(i - t) % size]) for i in rang...  31.6 us
    ppermute x8, starting transfers between devices, both_cores(): return [*parts, *(lax.ppermute(a, 'c', [(0, 1), (1, 0)]) for a in parts)]  23.2 us
    all_to_all x1, starting transfers between devices, body(): lax.all_to_all(sent.reshape(64, 4, FEATURES), SEQ, split_axis=0, concat_a...  15.4 us
    all_to_all x1, starting transfers between devices, body(): lax.all_to_all(col_mid.reshape(64, 4, HALF), SEQ, split_axis=0, concat_ax...  12.9 us
    ppermute x9, waiting for transfers between devices, ring(): lax.ppermute(part, axes, [(order[i], order[(i - t) % size]) for i in rang...  12.2 us
    pallas_call x1, Pallas kernels, row_attention(): pl.pallas_call(row_kernel, out_shape=[jax.ShapeDtypeStruct((STRIDE, FEATU...  7.68 us
    pallas_call x1, Pallas kernels, column_attention(): pl.pallas_call(column_kernel, out_shape=jax.ShapeDtypeStruct((STRIDE, HAL...  6.53 us
  transfers between devices with their start and end apart: 20, of which 6 were waited for; matrix products, arithmetic and copies ran while one was open for 1% of the time, Pallas kernels for 9%

profile of v5, /device:TPU:1, one launch (start us, length us, event | category | flops | bytes accessed | tf_op | source)
XLA Modules:
  0.0 159.4 jit_solution(3642662621977013617)
XLA Ops:
  1.5 31.7 %all_to_all.15 = bf16[16,16,512]{2,1,0:T(8,128)(2,1)S(1)} all-to-all(bf16[16,16,512]{2,1,0:T(8,128)(2,1)S(1)} %broadcast_in_dim.7), channel_id=1, replica_groups=mesh['xl'=2,'y'=4,'xh'=2,'z'=16,'c'=2] {'z'}, dimensions={0} | all-to-all | bytes 524288 | tf_op jit(solution)/shard_map/all_to_all | solution.py:171
  34.2 15.4 %all-to-all-start.1 = ((bf16[64,4,1024]{2,1,0:T(4,128)(2,1)}), bf16[64,4,1024]{2,1,0:T(4,128)(2,1)}, u32[]{:S(2)}, u32[]{:S(2)}) async-start(bf16[64,4,1024]{2,1,0:T(4,128)(2,1)} %reshape.39), calls=%async_computation.1 | async-start | bytes 1048576 | tf_op jit(solution)/shard_map/all_to_all | solution.py:174
  49.7 4.8 %collective-permute-start.2 = (bf16[128,1024]{1,0:T(8,128)(2,1)S(1)}, bf16[128,1024]{1,0:T(8,128)(2,1)S(1)}, u32[]{:S(2)}, u32[]{:S(2)}) collective-permute-start(bf16[128,1024]{1,0:T(8,128)(2,1)S(1)} %get-tuple-element.26), channel_id=1, source_target_pairs={{0,128},{64,192},{128,0},{192,64},{1,129},{65,193},{129,1},{193,65... | collective-permute-start | bytes 786440 | tf_op jit(solution)/shard_map/ppermute | solution.py:157
  54.5 2.7 %collective-permute-start.1 = (bf16[128,1024]{1,0:T(8,128)(2,1)S(1)}, bf16[128,1024]{1,0:T(8,128)(2,1)S(1)}, u32[]{:S(2)}, u32[]{:S(2)}) collective-permute-start(bf16[128,1024]{1,0:T(8,128)(2,1)S(1)} %get-tuple-element.26), channel_id=1, source_target_pairs={{0,192},{64,0},{128,64},{192,128},{1,193},{65,1},{129,65},{193,129... | collective-permute-start | bytes 786440 | tf_op jit(solution)/shard_map/ppermute | solution.py:157
  57.2 2.6 %collective-permute-start.3 = (bf16[128,1024]{1,0:T(8,128)(2,1)S(1)}, bf16[128,1024]{1,0:T(8,128)(2,1)S(1)}, u32[]{:S(2)}, u32[]{:S(2)}) collective-permute-start(bf16[128,1024]{1,0:T(8,128)(2,1)S(1)} %get-tuple-element.26), channel_id=1, source_target_pairs={{0,64},{64,128},{128,192},{192,0},{1,65},{65,129},{129,193},{193,1... | collective-permute-start | bytes 786440 | tf_op jit(solution)/shard_map/ppermute | solution.py:157
  60.5 6.0 %collective-permute-done.1 = bf16[128,1024]{1,0:T(8,128)(2,1)S(1)} collective-permute-done((bf16[128,1024]{1,0:T(8,128)(2,1)S(1)}, bf16[128,1024]{1,0:T(8,128)(2,1)S(1)}, u32[]{:S(2)}, u32[]{:S(2)}) %collective-permute-start.1) | collective-permute-done | bytes 262176 | tf_op jit(solution)/shard_map/ppermute | solution.py:157
  67.2 2.2 %collective-permute-start.6 = (bf16[4,128,384]{2,1,0:T(8,128)(2,1)S(1)}, bf16[4,128,384]{2,1,0:T(8,128)(2,1)S(1)}, u32[]{:S(2)}, u32[]{:S(2)}) collective-permute-start(bf16[4,128,384]{2,1,0:T(8,128)(2,1)S(1)} %pad_maximum_fusion.1.refs_0_), channel_id=1, source_target_pairs={{0,256},{256,32},{32,288},{288,0},{1,257},{257,33},{33,289},{289,1... | collective-permute-start | bytes 1179656 | tf_op jit(solution)/shard_map/ppermute | solution.py:157
  69.4 5.7 %collective-permute-start.5 = (bf16[4,128,384]{2,1,0:T(8,128)(2,1)S(1)}, bf16[4,128,384]{2,1,0:T(8,128)(2,1)}, u32[]{:S(2)}, u32[]{:S(2)}) collective-permute-start(bf16[4,128,384]{2,1,0:T(8,128)(2,1)S(1)} %pad_maximum_fusion.1.refs_0_), channel_id=1, source_target_pairs={{0,32},{256,288},{32,0},{288,256},{1,33},{257,289},{33,1},{289,257... | collective-permute-start | bytes 1179656 | tf_op jit(solution)/shard_map/ppermute | solution.py:157
  75.1 3.1 %collective-permute-start.4 = (bf16[4,128,384]{2,1,0:T(8,128)(2,1)S(1)}, bf16[4,128,384]{2,1,0:T(8,128)(2,1)}, u32[]{:S(2)}, u32[]{:S(2)}) collective-permute-start(bf16[4,128,384]{2,1,0:T(8,128)(2,1)S(1)} %pad_maximum_fusion.1.refs_0_), channel_id=1, source_target_pairs={{0,288},{256,0},{32,256},{288,32},{1,289},{257,1},{33,257},{289,33... | collective-permute-start | bytes 1179656 | tf_op jit(solution)/shard_map/ppermute | solution.py:157
  78.2 4.5 %collective-permute-start.10 = (bf16[4,128,384]{2,1,0:T(8,128)(2,1)S(1)}, bf16[4,128,384]{2,1,0:T(8,128)(2,1)S(1)}, u32[]{:S(2)}, u32[]{:S(2)}) collective-permute-start(bf16[4,128,384]{2,1,0:T(8,128)(2,1)S(1)} %pad_maximum_fusion.1.refs_0_), channel_id=1, source_target_pairs={{0,1},{1,0},{2,3},{3,2},{4,5},{5,4},{6,7},{7,6},{8,9},{9,8},{10,11... | collective-permute-start | bytes 1179656 | tf_op jit(solution)/shard_map/ppermute | solution.py:187
  82.7 3.3 %collective-permute-start.13 = (bf16[4,128,384]{2,1,0:T(8,128)(2,1)S(1)}, bf16[4,128,384]{2,1,0:T(8,128)(2,1)S(1)}, u32[]{:S(2)}, u32[]{:S(2)}) collective-permute-start(bf16[4,128,384]{2,1,0:T(8,128)(2,1)S(1)} %collective-permute-done.6.refs_3_), channel_id=1, source_target_pairs={{0,1},{1,0},{2,3},{3,2},{4,5},{5,4},{6,7},{7,6},{8,9},{9,8},{10,11... | collective-permute-start | bytes 1179656 | tf_op jit(solution)/shard_map/ppermute | solution.py:187
  86.0 4.9 %collective-permute-done.5.refs_2_ = bf16[4,128,384]{2,1,0:T(8,128)(2,1)} collective-permute-done((bf16[4,128,384]{2,1,0:T(8,128)(2,1)S(1)}, bf16[4,128,384]{2,1,0:T(8,128)(2,1)}, u32[]{:S(2)}, u32[]{:S(2)}) %collective-permute-start.5) | collective-permute-done | bytes 393248 | tf_op jit(solution)/shard_map/ppermute | solution.py:157
  90.9 4.0 %collective-permute-start.12 = (bf16[4,128,384]{2,1,0:T(8,128)(2,1)}, bf16[4,128,384]{2,1,0:T(8,128)(2,1)}, u32[]{:S(2)}, u32[]{:S(2)}) collective-permute-start(bf16[4,128,384]{2,1,0:T(8,128)(2,1)} %collective-permute-done.5.refs_2_), channel_id=1, source_target_pairs={{0,1},{1,0},{2,3},{3,2},{4,5},{5,4},{6,7},{7,6},{8,9},{9,8},{10,11... | collective-permute-start | bytes 1179656 | tf_op jit(solution)/shard_map/ppermute | solution.py:187
  94.9 1.9 %collective-permute-start.11 = (bf16[4,128,384]{2,1,0:T(8,128)(2,1)}, bf16[4,128,384]{2,1,0:T(8,128)(2,1)}, u32[]{:S(2)}, u32[]{:S(2)}) collective-permute-start(bf16[4,128,384]{2,1,0:T(8,128)(2,1)} %collective-permute-done.4.refs_1_), channel_id=1, source_target_pairs={{0,1},{1,0},{2,3},{3,2},{4,5},{5,4},{6,7},{7,6},{8,9},{9,8},{10,11... | collective-permute-start | bytes 1179656 | tf_op jit(solution)/shard_map/ppermute | solution.py:187
  97.0 2.8 %collective-permute-start.9 = (bf16[4,128,640]{2,1,0:T(8,128)(2,1)S(1)}, bf16[4,128,640]{2,1,0:T(8,128)(2,1)S(1)}, u32[]{:S(2)}, u32[]{:S(2)}) collective-permute-start(bf16[4,128,640]{2,1,0:T(8,128)(2,1)S(1)} %slice.30.refs_0_), channel_id=1, source_target_pairs={{0,256},{256,32},{32,288},{288,0},{1,257},{257,33},{33,289},{289,1... | collective-permute-start | bytes 1966088 | tf_op jit(solution)/shard_map/ppermute | solution.py:157
  100.6 3.8 %collective-permute-start.8 = (bf16[4,128,640]{2,1,0:T(8,128)(2,1)S(1)}, bf16[4,128,640]{2,1,0:T(8,128)(2,1)}, u32[]{:S(2)}, u32[]{:S(2)}) collective-permute-start(bf16[4,128,640]{2,1,0:T(8,128)(2,1)S(1)} %slice.30.refs_0_), channel_id=1, source_target_pairs={{0,32},{256,288},{32,0},{288,256},{1,33},{257,289},{33,1},{289,257... | collective-permute-start | bytes 1966088 | tf_op jit(solution)/shard_map/ppermute | solution.py:157
  105.2 4.0 %collective-permute-start.7 = (bf16[4,128,640]{2,1,0:T(8,128)(2,1)S(1)}, bf16[4,128,640]{2,1,0:T(8,128)(2,1)}, u32[]{:S(2)}, u32[]{:S(2)}) collective-permute-start(bf16[4,128,640]{2,1,0:T(8,128)(2,1)S(1)} %slice.30.refs_0_), channel_id=1, source_target_pairs={{0,288},{256,0},{32,256},{288,32},{1,289},{257,1},{33,257},{289,33... | collective-permute-start | bytes 1966088 | tf_op jit(solution)/shard_map/ppermute | solution.py:157
  113.0 6.5 %columns.1 = bf16[256,512]{1,0:T(8,128)(2,1)S(1)} custom-call(s32[3]{0:T(128)S(1)} %pad_add_fusion.place, s32[8]{0:T(128)S(1)} %copy-done.8, f32[1,1024]{1,0:T(1,128)S(1)} %bitcast.17, bf16[256,1024]{1,0:T(8,128)(2,1)S(1)} %reshape.40.x_ref, bf16[4,128,384]{2,1,0:T(8,128)(2,1)S(1)} %pad_maximum_fusion.1.refs_0_, ...), custom_call_target="tpu_custom_call" | custom-call | flops 939524096 | bytes 6291456 | tf_op jit(solution)/shard_map/columns/pallas_call | solution.py:121
  120.4 12.9 %all-to-all-start.2 = ((bf16[64,4,512]{2,1,0:T(4,128)(2,1)}), bf16[64,4,512]{2,1,0:T(4,128)(2,1)}, u32[]{:S(2)}, u32[]{:S(2)}) async-start(bf16[64,4,512]{2,1,0:T(4,128)(2,1)} %reshape.41), calls=%async_computation.2 | async-start | bytes 524288 | tf_op jit(solution)/shard_map/all_to_all | solution.py:191
  133.3 3.3 %collective-permute-start.14 = (bf16[4,128,640]{2,1,0:T(8,128)(2,1)S(1)}, bf16[4,128,640]{2,1,0:T(8,128)(2,1)S(1)}, u32[]{:S(2)}, u32[]{:S(2)}) collective-permute-start(bf16[4,128,640]{2,1,0:T(8,128)(2,1)S(1)} %slice.30.refs_0_), channel_id=1, source_target_pairs={{0,1},{1,0},{2,3},{3,2},{4,5},{5,4},{6,7},{7,6},{8,9},{9,8},{10,11... | collective-permute-start | bytes 1966088 | tf_op jit(solution)/shard_map/ppermute | solution.py:187
  138.5 2.4 %collective-permute-start.16 = (bf16[4,128,640]{2,1,0:T(8,128)(2,1)}, bf16[4,128,640]{2,1,0:T(8,128)(2,1)S(1)}, u32[]{:S(2)}, u32[]{:S(2)}) collective-permute-start(bf16[4,128,640]{2,1,0:T(8,128)(2,1)} %collective-permute-done.8.refs_2_), channel_id=1, source_target_pairs={{0,1},{1,0},{2,3},{3,2},{4,5},{5,4},{6,7},{7,6},{8,9},{9,8},{10,11... | collective-permute-start | bytes 1966088 | tf_op jit(solution)/shard_map/ppermute | solution.py:187
  142.9 2.0 %collective-permute-done.17.refs_7_ = bf16[4,128,640]{2,1,0:T(8,128)(2,1)S(1)} collective-permute-done((bf16[4,128,640]{2,1,0:T(8,128)(2,1)S(1)}, bf16[4,128,640]{2,1,0:T(8,128)(2,1)S(1)}, u32[]{:S(2)}, u32[]{:S(2)}) %collective-permute-start.17) | collective-permute-done | bytes 655392 | tf_op jit(solution)/shard_map/ppermute | solution.py:187
  145.0 7.7 %rows.1 = (f32[256,1024]{1,0:T(8,128)S(1)}, bf16[512,1024]{1,0:T(8,128)(2,1)S(1)}, s32[1]{0:T(128)}) custom-call(s32[3]{0:T(128)S(1)} %pad_add_fusion.place, s32[8]{0:T(128)S(1)} %copy-done.9, f32[1,1024]{1,0:T(1,128)S(1)} %bitcast.18, bf16[256,1024]{1,0:T(8,128)(2,1)S(1)} %bitcast.16, bf16[4,128,640]{2,1,0:T(8,128)(2,1)S(1)} %slice.30.refs_0_, ...), custom_call_target="tpu_custom_call" | custom-call | flops 1048576 | bytes 1048576 | tf_op jit(solution)/shard_map/rows/pallas_call | solution.py:134
  154.3 2.7 %all-to-all-done.2 = bf16[64,4,512]{2,1,0:T(4,128)(2,1)} async-done(((bf16[64,4,512]{2,1,0:T(4,128)(2,1)}), bf16[64,4,512]{2,1,0:T(4,128)(2,1)}, u32[]{:S(2)}, u32[]{:S(2)}) %all-to-all-start.2) | async-done | bytes 262176 | tf_op jit(solution)/shard_map/all_to_all | solution.py:191
  (55 shorter events, 17.4 us)
Async XLA Ops:
  0.0 33.2 %copy-start = (bf16[1,1,256,1024]{3,2,1,0:T(8,128)(2,1)S(1)}, bf16[1,1,256,1024]{3,2,1,0:T(8,128)(2,1)}, u32[]{:S(2)}) copy-start(bf16[1,1,256,1024]{3,2,1,0:T(8,128)(2,1)} %param.6) | copy-start | bytes 1572868
  0.8 0.7 collective-permute-start
  34.2 75.1 %all-to-all-start.1 = ((bf16[64,4,1024]{2,1,0:T(4,128)(2,1)}), bf16[64,4,1024]{2,1,0:T(4,128)(2,1)}, u32[]{:S(2)}, u32[]{:S(2)}) async-start(bf16[64,4,1024]{2,1,0:T(4,128)(2,1)} %reshape.39), calls=%async_computation.1 | async-start | bytes 1048576 | tf_op jit(solution)/shard_map/all_to_all | solution.py:174
  49.7 10.8 %collective-permute-start.2 = (bf16[128,1024]{1,0:T(8,128)(2,1)S(1)}, bf16[128,1024]{1,0:T(8,128)(2,1)S(1)}, u32[]{:S(2)}, u32[]{:S(2)}) collective-permute-start(bf16[128,1024]{1,0:T(8,128)(2,1)S(1)} %get-tuple-element.26), channel_id=1, source_target_pairs={{0,128},{64,192},{128,0},{192,64},{1,129},{65,193},{129,1},{193,65... | collective-permute-start | bytes 786440 | tf_op jit(solution)/shard_map/ppermute | solution.py:157
  54.5 12.0 %collective-permute-start.1 = (bf16[128,1024]{1,0:T(8,128)(2,1)S(1)}, bf16[128,1024]{1,0:T(8,128)(2,1)S(1)}, u32[]{:S(2)}, u32[]{:S(2)}) collective-permute-start(bf16[128,1024]{1,0:T(8,128)(2,1)S(1)} %get-tuple-element.26), channel_id=1, source_target_pairs={{0,192},{64,0},{128,64},{192,128},{1,193},{65,1},{129,65},{193,129... | collective-permute-start | bytes 786440 | tf_op jit(solution)/shard_map/ppermute | solution.py:157
  57.2 9.9 %collective-permute-start.3 = (bf16[128,1024]{1,0:T(8,128)(2,1)S(1)}, bf16[128,1024]{1,0:T(8,128)(2,1)S(1)}, u32[]{:S(2)}, u32[]{:S(2)}) collective-permute-start(bf16[128,1024]{1,0:T(8,128)(2,1)S(1)} %get-tuple-element.26), channel_id=1, source_target_pairs={{0,64},{64,128},{128,192},{192,0},{1,65},{65,129},{129,193},{193,1... | collective-permute-start | bytes 786440 | tf_op jit(solution)/shard_map/ppermute | solution.py:157
  67.2 15.5 %collective-permute-start.6 = (bf16[4,128,384]{2,1,0:T(8,128)(2,1)S(1)}, bf16[4,128,384]{2,1,0:T(8,128)(2,1)S(1)}, u32[]{:S(2)}, u32[]{:S(2)}) collective-permute-start(bf16[4,128,384]{2,1,0:T(8,128)(2,1)S(1)} %pad_maximum_fusion.1.refs_0_), channel_id=1, source_target_pairs={{0,256},{256,32},{32,288},{288,0},{1,257},{257,33},{33,289},{289,1... | collective-permute-start | bytes 1179656 | tf_op jit(solution)/shard_map/ppermute | solution.py:157
  69.4 21.5 %collective-permute-start.5 = (bf16[4,128,384]{2,1,0:T(8,128)(2,1)S(1)}, bf16[4,128,384]{2,1,0:T(8,128)(2,1)}, u32[]{:S(2)}, u32[]{:S(2)}) collective-permute-start(bf16[4,128,384]{2,1,0:T(8,128)(2,1)S(1)} %pad_maximum_fusion.1.refs_0_), channel_id=1, source_target_pairs={{0,32},{256,288},{32,0},{288,256},{1,33},{257,289},{33,1},{289,257... | collective-permute-start | bytes 1179656 | tf_op jit(solution)/shard_map/ppermute | solution.py:157
  75.1 19.8 %collective-permute-start.4 = (bf16[4,128,384]{2,1,0:T(8,128)(2,1)S(1)}, bf16[4,128,384]{2,1,0:T(8,128)(2,1)}, u32[]{:S(2)}, u32[]{:S(2)}) collective-permute-start(bf16[4,128,384]{2,1,0:T(8,128)(2,1)S(1)} %pad_maximum_fusion.1.refs_0_), channel_id=1, source_target_pairs={{0,288},{256,0},{32,256},{288,32},{1,289},{257,1},{33,257},{289,33... | collective-permute-start | bytes 1179656 | tf_op jit(solution)/shard_map/ppermute | solution.py:157
  78.2 21.6 %collective-permute-start.10 = (bf16[4,128,384]{2,1,0:T(8,128)(2,1)S(1)}, bf16[4,128,384]{2,1,0:T(8,128)(2,1)S(1)}, u32[]{:S(2)}, u32[]{:S(2)}) collective-permute-start(bf16[4,128,384]{2,1,0:T(8,128)(2,1)S(1)} %pad_maximum_fusion.1.refs_0_), channel_id=1, source_target_pairs={{0,1},{1,0},{2,3},{3,2},{4,5},{5,4},{6,7},{7,6},{8,9},{9,8},{10,11... | collective-permute-start | bytes 1179656 | tf_op jit(solution)/shard_map/ppermute | solution.py:187
  82.7 21.7 %collective-permute-start.13 = (bf16[4,128,384]{2,1,0:T(8,128)(2,1)S(1)}, bf16[4,128,384]{2,1,0:T(8,128)(2,1)S(1)}, u32[]{:S(2)}, u32[]{:S(2)}) collective-permute-start(bf16[4,128,384]{2,1,0:T(8,128)(2,1)S(1)} %collective-permute-done.6.refs_3_), channel_id=1, source_target_pairs={{0,1},{1,0},{2,3},{3,2},{4,5},{5,4},{6,7},{7,6},{8,9},{9,8},{10,11... | collective-permute-start | bytes 1179656 | tf_op jit(solution)/shard_map/ppermute | solution.py:187
  90.9 19.5 %collective-permute-start.12 = (bf16[4,128,384]{2,1,0:T(8,128)(2,1)}, bf16[4,128,384]{2,1,0:T(8,128)(2,1)}, u32[]{:S(2)}, u32[]{:S(2)}) collective-permute-start(bf16[4,128,384]{2,1,0:T(8,128)(2,1)} %collective-permute-done.5.refs_2_), channel_id=1, source_target_pairs={{0,1},{1,0},{2,3},{3,2},{4,5},{5,4},{6,7},{7,6},{8,9},{9,8},{10,11... | collective-permute-start | bytes 1179656 | tf_op jit(solution)/shard_map/ppermute | solution.py:187
  94.9 15.5 %collective-permute-start.11 = (bf16[4,128,384]{2,1,0:T(8,128)(2,1)}, bf16[4,128,384]{2,1,0:T(8,128)(2,1)}, u32[]{:S(2)}, u32[]{:S(2)}) collective-permute-start(bf16[4,128,384]{2,1,0:T(8,128)(2,1)} %collective-permute-done.4.refs_1_), channel_id=1, source_target_pairs={{0,1},{1,0},{2,3},{3,2},{4,5},{5,4},{6,7},{7,6},{8,9},{9,8},{10,11... | collective-permute-start | bytes 1179656 | tf_op jit(solution)/shard_map/ppermute | solution.py:187
  97.0 36.3 %collective-permute-start.9 = (bf16[4,128,640]{2,1,0:T(8,128)(2,1)S(1)}, bf16[4,128,640]{2,1,0:T(8,128)(2,1)S(1)}, u32[]{:S(2)}, u32[]{:S(2)}) collective-permute-start(bf16[4,128,640]{2,1,0:T(8,128)(2,1)S(1)} %slice.30.refs_0_), channel_id=1, source_target_pairs={{0,256},{256,32},{32,288},{288,0},{1,257},{257,33},{33,289},{289,1... | collective-permute-start | bytes 1966088 | tf_op jit(solution)/shard_map/ppermute | solution.py:157
  100.6 32.8 %collective-permute-start.8 = (bf16[4,128,640]{2,1,0:T(8,128)(2,1)S(1)}, bf16[4,128,640]{2,1,0:T(8,128)(2,1)}, u32[]{:S(2)}, u32[]{:S(2)}) collective-permute-start(bf16[4,128,640]{2,1,0:T(8,128)(2,1)S(1)} %slice.30.refs_0_), channel_id=1, source_target_pairs={{0,32},{256,288},{32,0},{288,256},{1,33},{257,289},{33,1},{289,257... | collective-permute-start | bytes 1966088 | tf_op jit(solution)/shard_map/ppermute | solution.py:157
  105.2 28.2 %collective-permute-start.7 = (bf16[4,128,640]{2,1,0:T(8,128)(2,1)S(1)}, bf16[4,128,640]{2,1,0:T(8,128)(2,1)}, u32[]{:S(2)}, u32[]{:S(2)}) collective-permute-start(bf16[4,128,640]{2,1,0:T(8,128)(2,1)S(1)} %slice.30.refs_0_), channel_id=1, source_target_pairs={{0,288},{256,0},{32,256},{288,32},{1,289},{257,1},{33,257},{289,33... | collective-permute-start | bytes 1966088 | tf_op jit(solution)/shard_map/ppermute | solution.py:157
  109.2 1.2 copy-start.7
  120.4 24.6 %copy-start.9 = (s32[8]{0:T(128)S(1)}, s32[8]{0:T(128)}, u32[]{:S(2)}) copy-start(s32[8]{0:T(128)} %reach_ref.3) | copy-start | bytes 100
  120.4 36.6 %all-to-all-start.2 = ((bf16[64,4,512]{2,1,0:T(4,128)(2,1)}), bf16[64,4,512]{2,1,0:T(4,128)(2,1)}, u32[]{:S(2)}, u32[]{:S(2)}) async-start(bf16[64,4,512]{2,1,0:T(4,128)(2,1)} %reshape.41), calls=%async_computation.2 | async-start | bytes 524288 | tf_op jit(solution)/shard_map/all_to_all | solution.py:191
  133.3 9.6 %collective-permute-start.14 = (bf16[4,128,640]{2,1,0:T(8,128)(2,1)S(1)}, bf16[4,128,640]{2,1,0:T(8,128)(2,1)S(1)}, u32[]{:S(2)}, u32[]{:S(2)}) collective-permute-start(bf16[4,128,640]{2,1,0:T(8,128)(2,1)S(1)} %slice.30.refs_0_), channel_id=1, source_target_pairs={{0,1},{1,0},{2,3},{3,2},{4,5},{5,4},{6,7},{7,6},{8,9},{9,8},{10,11... | collective-permute-start | bytes 1966088 | tf_op jit(solution)/shard_map/ppermute | solution.py:187
  136.6 6.3 %collective-permute-start.15 = (bf16[4,128,640]{2,1,0:T(8,128)(2,1)}, bf16[4,128,640]{2,1,0:T(8,128)(2,1)S(1)}, u32[]{:S(2)}, u32[]{:S(2)}) collective-permute-start(bf16[4,128,640]{2,1,0:T(8,128)(2,1)} %collective-permute-done.7.refs_1_), channel_id=1, source_target_pairs={{0,1},{1,0},{2,3},{3,2},{4,5},{5,4},{6,7},{7,6},{8,9},{9,8},{10,11... | collective-permute-start | bytes 1966088 | tf_op jit(solution)/shard_map/ppermute | solution.py:187
  138.5 4.4 %collective-permute-start.16 = (bf16[4,128,640]{2,1,0:T(8,128)(2,1)}, bf16[4,128,640]{2,1,0:T(8,128)(2,1)S(1)}, u32[]{:S(2)}, u32[]{:S(2)}) collective-permute-start(bf16[4,128,640]{2,1,0:T(8,128)(2,1)} %collective-permute-done.8.refs_2_), channel_id=1, source_target_pairs={{0,1},{1,0},{2,3},{3,2},{4,5},{5,4},{6,7},{7,6},{8,9},{9,8},{10,11... | collective-permute-start | bytes 1966088 | tf_op jit(solution)/shard_map/ppermute | solution.py:187
  141.0 4.0 %collective-permute-start.17 = (bf16[4,128,640]{2,1,0:T(8,128)(2,1)S(1)}, bf16[4,128,640]{2,1,0:T(8,128)(2,1)S(1)}, u32[]{:S(2)}, u32[]{:S(2)}) collective-permute-start(bf16[4,128,640]{2,1,0:T(8,128)(2,1)S(1)} %collective-permute-done.9.refs_3_), channel_id=1, source_target_pairs={{0,1},{1,0},{2,3},{3,2},{4,5},{5,4},{6,7},{7,6},{8,9},{9,8},{10,11... | collective-permute-start | bytes 1966088 | tf_op jit(solution)/shard_map/ppermute | solution.py:187
  153.6 4.5 %copy-start.2 = (bf16[512,1024]{1,0:T(8,128)(2,1)S(1)}, bf16[512,1024]{1,0:T(8,128)(2,1)}, u32[]{:S(2)}) copy-start(bf16[512,1024]{1,0:T(8,128)(2,1)} %copy-done.1) | copy-start | bytes 3145732
  (6 other events, 5.1 us)

commit v6 on v5

--- a/solution.py
+++ b/solution.py
@@ -24,10 +24,11 @@
         base = 512 * xh + 32 * ((1 - xl) if odd else xl)
         for s in range(Y):
             cols = pl.ds(pl.multiple_of(first + width * ((y + s) & 3), 128), width)
-            for ref, c in ((refs[t], core), (refs[X + t], 1 - core)):
+            piece, at = divmod(t * Y + s, X * Y // (len(refs) // 2))
+            for ref, c in ((refs[piece], core), (refs[len(refs) // 2 + piece], 1 - core)):
                 for zz in range(Z // 2):
                     row = pl.multiple_of(base + 16 * c + 64 * zz, 16)
-                    w_ref[pl.ds(row, 16), cols] = ref[s, pl.ds(16 * zz, 16), lanes]
+                    w_ref[pl.ds(row, 16), cols] = ref[at, pl.ds(16 * zz, 16), lanes]
 
 
 def attend(reach_ref, gain_ref, x_ref, w_ref, n_ref, qkv_ref, out_ref, dist):
@@ -69,7 +70,7 @@
 
 
 def column_kernel(place, reach_ref, gain_ref, x_ref, *refs):
-    parts, (out_ref, w_ref, n_ref, qkv_ref) = refs[: 2 * X], refs[2 * X :]
+    *parts, out_ref, w_ref, n_ref, qkv_ref = refs
     assemble(place, True, parts, slice(0, PART), w_ref, 0, PART)
     i, j = pairs()
     back = (i >> 2) - (j >> 2)
@@ -78,8 +79,7 @@
 
 
 def row_kernel(place, reach_ref, gain_ref, x_ref, *refs):
-    parts = refs[: 2 * X]
-    base_ref, low_ref, done_ref, w_ref, n_ref, qkv_ref, a_ref, o_ref = refs[2 * X :]
+    *parts, base_ref, low_ref, done_ref, w_ref, n_ref, qkv_ref, a_ref, o_ref = refs
     done_ref[0] = 0
     assemble(place, False, parts, slice(0, PART), w_ref, 0, PART)
     i, j = pairs()
@@ -109,7 +109,7 @@
     pltpu.VMEM((STRIDE, FEATURES), jnp.bfloat16),
     pltpu.VMEM((STRIDE, WIDTH), jnp.bfloat16),
 ]
-PARAMS = pltpu.CompilerParams(vmem_limit_bytes=40 * 1024 * 1024)
+PARAMS = pltpu.CompilerParams(vmem_limit_bytes=24 * 1024 * 1024)
 COST = pl.CostEstimate(
     flops=2 * 256 * 1024 * 1536 + 16 * 256 * 256 * 128,
     bytes_accessed=6 << 20,
@@ -170,29 +170,35 @@
     block = lax.ppermute(block, ("xl", "z"), change)
     column = lax.all_to_all(jnp.broadcast_to(block, (Z, 16, 512)), "z", split_axis=0, concat_axis=0)
 
-    sent, column = lax.optimization_barrier((rows, column))
-    turned = lax.all_to_all(sent.reshape(64, 4, FEATURES), SEQ, split_axis=0, concat_axis=0)
+    sent, column = lax.optimization_barrier((rows.reshape(64, 4, FEATURES), column))
+    turned = lax.all_to_all(sent, SEQ, split_axis=0, concat_axis=0)
     turned = turned.reshape(STRIDE, FEATURES)
 
     halves = column.reshape(Z // 2, 2, 16, 512)
     row_part = jnp.where(xl == 0, halves[:, 0], halves[:, 1]).reshape(128, 512)
     col_part = jnp.where(xl == 0, halves[:, 1], halves[:, 0]).reshape(128, 512)
-    part = jnp.concatenate([col_part[:, :PART], row_part, col_part[:, PART:]], axis=1)
-    near = jnp.stack([part, *ring(part, "y", range(Y))])
+    rest_part = jnp.concatenate([row_part, col_part[:, PART:]], axis=1)
+
+    def near(part):
+        return jnp.stack([part, *ring(part, "y", range(Y))])
 
     def plane(part):
         return [part, *ring(part, ("xl", "xh"), [0, 2, 1, 3])]
 
-    def both_cores(parts):
+    def both_cores(parts, pieces):
+        size = X // pieces
+        if size > 1:
+            parts = [jnp.concatenate(parts[i : i + size]) for i in range(0, X, size)]
         return [*parts, *(lax.ppermute(a, "c", [(0, 1), (1, 0)]) for a in parts)]
 
-    col_plane = plane(near[:, :, :PART])
-    col_mid = column_attention(place, col_rows, gain, turned, both_cores(col_plane))
+    col_near = near(col_part[:, :PART])
+    rest_part, _ = lax.optimization_barrier((rest_part, col_near))
+    col_plane, rest_near = lax.optimization_barrier((plane(col_near), near(rest_part)))
+    col_mid = column_attention(place, col_rows, gain, turned, both_cores(col_plane, 2))
     col_out = lax.all_to_all(col_mid.reshape(64, 4, HALF), SEQ, split_axis=0, concat_axis=0)
 
-    near_rest, _ = lax.optimization_barrier((near[:, :, PART:], col_plane))
-    rest, _ = lax.optimization_barrier((plane(near_rest), col_mid))
-    base, low, last = row_attention(place, row_blocks, gain, rows, both_cores(rest))
+    rest, _ = lax.optimization_barrier((plane(rest_near), col_mid))
+    base, low, last = row_attention(place, row_blocks, gain, rows, both_cores(rest, 4))
     col_out = jnp.where(last[0] == 0, col_out, 0).reshape(STRIDE, HALF)
 
     mixed = pl.pallas_call(

time: 160 us -> 156 us (0.975)
  blocking collectives: 31.7 us -> 0 us
  starting transfers between devices: 83.9 us -> 104 us
  waiting for transfers between devices: 16.9 us -> 27.7 us
  local copies, waits for them, and re-layouts: 8.19 us -> 5.85 us
    all_to_all x1 -> x0, blocking collectives: 31.7 us -> none  [body(): lax.all_to_all(jnp.broadcast_to(block, (Z, 16, 512)), 'z', split_axis=0,...]
    all_to_all x1 -> x2, starting transfers between devices: 15.4 us -> 34.5 us  [the longest x1 19.1 us: body(): lax.all_to_all(jnp.broadcast_to(block, (Z, 16, 512)), 'z', split_axis=0,...]
    all_to_all x1 -> x2, waiting for transfers between devices: 0.01 us -> 11.8 us  [the longest x1 11.8 us: body(): lax.all_to_all(jnp.broadcast_to(block, (Z, 16, 512)), 'z', split_axis=0,...]
    ppermute x9 -> x12, starting transfers between devices: 31.6 us -> 40.3 us  [ring(): lax.ppermute(part, axes, [(order[i], order[(i - t) % size]) for i in rang...]
    ppermute x8 -> x6, starting transfers between devices: 23.2 us -> 15.3 us  [both_cores(): return [*parts, *(lax.ppermute(a, 'c', [(0, 1), (1, 0)]) for a in parts)]]
    unnamed x20 -> x14, local copies, waits for them, and re-layouts: 5.08 us -> 1.98 us
    all_to_all x1, waiting for transfers between devices: 2.7 us -> 0.01 us  [body(): lax.all_to_all(col_mid.reshape(64, 4, HALF), SEQ, split_axis=0, concat_ax...]
    ppermute x9 -> x12, waiting for transfers between devices: 12.2 us -> 13.7 us  [ring(): lax.ppermute(part, axes, [(order[i], order[(i - t) % size]) for i in rang...]
  transfers between devices with their start and end apart: 20 -> 22, of which waited for: 6 -> 10; matrix products, arithmetic and copies ran while one was open for 1% -> 2% of each run, Pallas kernels for 9% -> 9%
where the time goes in v6:
time: 156 us; the launch traced here: 155 us
  starting transfers between devices  104 us (67%)
  waiting for transfers between devices  27.7 us (18%)
  Pallas kernels  15.7 us (10%)
  local copies, waits for them, and re-layouts  5.85 us (4%)
    ppermute x12, starting transfers between devices, ring(): lax.ppermute(part, axes, [(order[i], order[(i - t) % size]) for i in rang...  40.3 us
    all_to_all x1, starting transfers between devices, body(): lax.all_to_all(jnp.broadcast_to(block, (Z, 16, 512)), 'z', split_axis=0,...  19.1 us
    all_to_all x1, starting transfers between devices, body(): turned = lax.all_to_all(sent, SEQ, split_axis=0, concat_axis=0)  15.4 us
    ppermute x6, starting transfers between devices, both_cores(): return [*parts, *(lax.ppermute(a, 'c', [(0, 1), (1, 0)]) for a in parts)]  15.3 us
    ppermute x12, waiting for transfers between devices, ring(): lax.ppermute(part, axes, [(order[i], order[(i - t) % size]) for i in rang...  13.7 us
    all_to_all x1, starting transfers between devices, body(): lax.all_to_all(col_mid.reshape(64, 4, HALF), SEQ, split_axis=0, concat_ax...  12.8 us
    all_to_all x1, waiting for transfers between devices, body(): lax.all_to_all(jnp.broadcast_to(block, (Z, 16, 512)), 'z', split_axis=0,...  11.8 us
    pallas_call x1, Pallas kernels, row_attention(): pl.pallas_call(row_kernel, out_shape=[jax.ShapeDtypeStruct((STRIDE, FEATU...  7.88 us
  transfers between devices with their start and end apart: 22, of which 10 were waited for; matrix products, arithmetic and copies ran while one was open for 2% of the time, Pallas kernels for 9%

profile of v6, /device:TPU:1, one launch (start us, length us, event | category | flops | bytes accessed | tf_op | source)
XLA Modules:
  0.0 155.1 jit_solution(6628858315785859860)
XLA Ops:
  2.2 19.1 %all-to-all-start = ((bf16[16,16,512]{2,1,0:T(8,128)(2,1)}), bf16[16,16,512]{2,1,0:T(8,128)(2,1)S(1)}, u32[]{:S(2)}, u32[]{:S(2)}) async-start(bf16[16,16,512]{2,1,0:T(8,128)(2,1)} %broadcast_in_dim.7), calls=%async_computation | async-start | bytes 524288 | tf_op jit(solution)/shard_map/all_to_all | solution.py:171
  22.3 11.8 %all-to-all-done = bf16[16,16,512]{2,1,0:T(8,128)(2,1)S(1)} async-done(((bf16[16,16,512]{2,1,0:T(8,128)(2,1)}), bf16[16,16,512]{2,1,0:T(8,128)(2,1)S(1)}, u32[]{:S(2)}, u32[]{:S(2)}) %all-to-all-start) | async-done | bytes 262176 | tf_op jit(solution)/shard_map/all_to_all | solution.py:171
  34.1 15.4 %all-to-all-start.1 = ((bf16[64,4,1024]{2,1,0:T(4,128)(2,1)}), bf16[64,4,1024]{2,1,0:T(4,128)(2,1)}, u32[]{:S(2)}, u32[]{:S(2)}) async-start(bf16[64,4,1024]{2,1,0:T(4,128)(2,1)} %reshape_reshape.3), calls=%async_computation.1 | async-start | bytes 1048576 | tf_op jit(solution)/shard_map/all_to_all | solution.py:174
  49.6 4.8 %collective-permute-start.2 = (bf16[128,384]{1,0:T(8,128)(2,1)S(1)}, bf16[128,384]{1,0:T(8,128)(2,1)S(1)}, u32[]{:S(2)}, u32[]{:S(2)}) collective-permute-start(bf16[128,384]{1,0:T(8,128)(2,1)S(1)} %get-tuple-element.38), channel_id=1, source_target_pairs={{0,128},{64,192},{128,0},{192,64},{1,129},{65,193},{129,1},{193,65... | collective-permute-start | bytes 294920 | tf_op jit(solution)/shard_map/ppermute | solution.py:157
  54.4 2.7 %collective-permute-start.1 = (bf16[128,384]{1,0:T(8,128)(2,1)S(1)}, bf16[128,384]{1,0:T(8,128)(2,1)S(1)}, u32[]{:S(2)}, u32[]{:S(2)}) collective-permute-start(bf16[128,384]{1,0:T(8,128)(2,1)S(1)} %get-tuple-element.38), channel_id=1, source_target_pairs={{0,192},{64,0},{128,64},{192,128},{1,193},{65,1},{129,65},{193,129... | collective-permute-start | bytes 294920 | tf_op jit(solution)/shard_map/ppermute | solution.py:157
  57.1 2.6 %collective-permute-start.3 = (bf16[128,384]{1,0:T(8,128)(2,1)S(1)}, bf16[128,384]{1,0:T(8,128)(2,1)S(1)}, u32[]{:S(2)}, u32[]{:S(2)}) collective-permute-start(bf16[128,384]{1,0:T(8,128)(2,1)S(1)} %get-tuple-element.38), channel_id=1, source_target_pairs={{0,64},{64,128},{128,192},{192,0},{1,65},{65,129},{129,193},{193,1... | collective-permute-start | bytes 294920 | tf_op jit(solution)/shard_map/ppermute | solution.py:157
  60.2 3.9 %collective-permute-done.3 = bf16[128,384]{1,0:T(8,128)(2,1)S(1)} collective-permute-done((bf16[128,384]{1,0:T(8,128)(2,1)S(1)}, bf16[128,384]{1,0:T(8,128)(2,1)S(1)}, u32[]{:S(2)}, u32[]{:S(2)}) %collective-permute-start.3) | collective-permute-done | bytes 98336 | tf_op jit(solution)/shard_map/ppermute | solution.py:157
  66.1 2.2 %collective-permute-start.6 = (bf16[4,128,384]{2,1,0:T(8,128)(2,1)S(1)}, bf16[4,128,384]{2,1,0:T(8,128)(2,1)S(1)}, u32[]{:S(2)}, u32[]{:S(2)}) collective-permute-start(bf16[4,128,384]{2,1,0:T(8,128)(2,1)S(1)} %pad_maximum_fusion.1), channel_id=1, source_target_pairs={{0,256},{256,32},{32,288},{288,0},{1,257},{257,33},{33,289},{289,1... | collective-permute-start | bytes 1179656 | tf_op jit(solution)/shard_map/ppermute | solution.py:157
  68.3 5.5 %collective-permute-start.5 = (bf16[4,128,384]{2,1,0:T(8,128)(2,1)S(1)}, bf16[4,128,384]{2,1,0:T(8,128)(2,1)S(1)}, u32[]{:S(2)}, u32[]{:S(2)}) collective-permute-start(bf16[4,128,384]{2,1,0:T(8,128)(2,1)S(1)} %pad_maximum_fusion.1), channel_id=1, source_target_pairs={{0,32},{256,288},{32,0},{288,256},{1,33},{257,289},{33,1},{289,257... | collective-permute-start | bytes 1179656 | tf_op jit(solution)/shard_map/ppermute | solution.py:157
  73.8 3.1 %collective-permute-start.4 = (bf16[4,128,384]{2,1,0:T(8,128)(2,1)S(1)}, bf16[4,128,384]{2,1,0:T(8,128)(2,1)S(1)}, u32[]{:S(2)}, u32[]{:S(2)}) collective-permute-start(bf16[4,128,384]{2,1,0:T(8,128)(2,1)S(1)} %pad_maximum_fusion.1), channel_id=1, source_target_pairs={{0,288},{256,0},{32,256},{288,32},{1,289},{257,1},{33,257},{289,33... | collective-permute-start | bytes 1179656 | tf_op jit(solution)/shard_map/ppermute | solution.py:157
  76.9 2.3 %collective-permute-start.8 = (bf16[128,640]{1,0:T(8,128)(2,1)S(1)}, bf16[128,640]{1,0:T(8,128)(2,1)S(1)}, u32[]{:S(2)}, u32[]{:S(2)}) collective-permute-start(bf16[128,640]{1,0:T(8,128)(2,1)S(1)} %pad_maximum_fusion.2), channel_id=1, source_target_pairs={{0,128},{64,192},{128,0},{192,64},{1,129},{65,193},{129,1},{193,65... | collective-permute-start | bytes 491528 | tf_op jit(solution)/shard_map/ppermute | solution.py:157
  79.2 4.2 %collective-permute-start.7 = (bf16[128,640]{1,0:T(8,128)(2,1)S(1)}, bf16[128,640]{1,0:T(8,128)(2,1)S(1)}, u32[]{:S(2)}, u32[]{:S(2)}) collective-permute-start(bf16[128,640]{1,0:T(8,128)(2,1)S(1)} %pad_maximum_fusion.2), channel_id=1, source_target_pairs={{0,192},{64,0},{128,64},{192,128},{1,193},{65,1},{129,65},{193,129... | collective-permute-start | bytes 491528 | tf_op jit(solution)/shard_map/ppermute | solution.py:157
  84.7 2.6 %collective-permute-done.7 = bf16[128,640]{1,0:T(8,128)(2,1)S(1)} collective-permute-done((bf16[128,640]{1,0:T(8,128)(2,1)S(1)}, bf16[128,640]{1,0:T(8,128)(2,1)S(1)}, u32[]{:S(2)}, u32[]{:S(2)}) %collective-permute-start.7) | collective-permute-done | bytes 163872 | tf_op jit(solution)/shard_map/ppermute | solution.py:157
  87.4 2.1 %collective-permute-done.5 = bf16[4,128,384]{2,1,0:T(8,128)(2,1)S(1)} collective-permute-done((bf16[4,128,384]{2,1,0:T(8,128)(2,1)S(1)}, bf16[4,128,384]{2,1,0:T(8,128)(2,1)S(1)}, u32[]{:S(2)}, u32[]{:S(2)}) %collective-permute-start.5) | collective-permute-done | bytes 393248 | tf_op jit(solution)/shard_map/ppermute | solution.py:157
  90.7 3.5 %collective-permute-start.14 = (bf16[8,128,384]{2,1,0:T(8,128)(2,1)S(1)}, bf16[8,128,384]{2,1,0:T(8,128)(2,1)}, u32[]{:S(2)}, u32[]{:S(2)}) collective-permute-start(bf16[8,128,384]{2,1,0:T(8,128)(2,1)S(1)} %constant_dynamic-update-slice_fusion.2.refs_1_), channel_id=1, source_target_pairs={{0,1},{1,0},{2,3},{3,2},{4,5},{5,4},{6,7},{7,6},{8,9},{9,8},{10,11... | collective-permute-start | bytes 2359304 | tf_op jit(solution)/shard_map/ppermute | solution.py:192
  96.3 4.4 %collective-permute-start.12 = (bf16[4,128,640]{2,1,0:T(8,128)(2,1)S(1)}, bf16[4,128,640]{2,1,0:T(8,128)(2,1)}, u32[]{:S(2)}, u32[]{:S(2)}) collective-permute-start(bf16[4,128,640]{2,1,0:T(8,128)(2,1)S(1)} %pad_maximum_fusion.refs_0_), channel_id=1, source_target_pairs={{0,256},{256,32},{32,288},{288,0},{1,257},{257,33},{33,289},{289,1... | collective-permute-start | bytes 1966088 | tf_op jit(solution)/shard_map/ppermute | solution.py:157
  100.7 2.9 %collective-permute-start.11 = (bf16[4,128,640]{2,1,0:T(8,128)(2,1)S(1)}, bf16[4,128,640]{2,1,0:T(8,128)(2,1)}, u32[]{:S(2)}, u32[]{:S(2)}) collective-permute-start(bf16[4,128,640]{2,1,0:T(8,128)(2,1)S(1)} %pad_maximum_fusion.refs_0_), channel_id=1, source_target_pairs={{0,32},{256,288},{32,0},{288,256},{1,33},{257,289},{33,1},{289,257... | collective-permute-start | bytes 1966088 | tf_op jit(solution)/shard_map/ppermute | solution.py:157
  103.6 3.6 %collective-permute-start.10 = (bf16[4,128,640]{2,1,0:T(8,128)(2,1)S(1)}, bf16[4,128,640]{2,1,0:T(8,128)(2,1)}, u32[]{:S(2)}, u32[]{:S(2)}) collective-permute-start(bf16[4,128,640]{2,1,0:T(8,128)(2,1)S(1)} %pad_maximum_fusion.refs_0_), channel_id=1, source_target_pairs={{0,288},{256,0},{32,256},{288,32},{1,289},{257,1},{33,257},{289,33... | collective-permute-start | bytes 1966088 | tf_op jit(solution)/shard_map/ppermute | solution.py:157
  109.2 6.5 %columns.1 = bf16[256,512]{1,0:T(8,128)(2,1)S(1)} custom-call(s32[3]{0:T(128)S(1)} %pad_add_fusion.place, s32[8]{0:T(128)S(1)} %copy-done.4, f32[1,1024]{1,0:T(1,128)S(1)} %bitcast.22, bf16[256,1024]{1,0:T(8,128)(2,1)S(1)} %reshape.36.x_ref, bf16[8,128,384]{2,1,0:T(8,128)(2,1)S(1)} %constant_dynamic-update-slice_fusion.refs_0_, ...), custom_call_target="tpu_custom_call" | custom-call | flops 939524096 | bytes 6291456 | tf_op jit(solution)/shard_map/columns/pallas_call | solution.py:121
  116.5 12.8 %all-to-all-start.2 = ((bf16[64,4,512]{2,1,0:T(4,128)(2,1)}), bf16[64,4,512]{2,1,0:T(4,128)(2,1)S(1)}, u32[]{:S(2)}, u32[]{:S(2)}) async-start(bf16[64,4,512]{2,1,0:T(4,128)(2,1)} %reshape.37), calls=%async_computation.2 | async-start | bytes 524288 | tf_op jit(solution)/shard_map/all_to_all | solution.py:198
  131.5 3.7 %collective-permute-start.15 = (bf16[4,128,640]{2,1,0:T(8,128)(2,1)S(1)}, bf16[4,128,640]{2,1,0:T(8,128)(2,1)S(1)}, u32[]{:S(2)}, u32[]{:S(2)}) collective-permute-start(bf16[4,128,640]{2,1,0:T(8,128)(2,1)S(1)} %pad_maximum_fusion.refs_0_), channel_id=1, source_target_pairs={{0,1},{1,0},{2,3},{3,2},{4,5},{5,4},{6,7},{7,6},{8,9},{9,8},{10,11... | collective-permute-start | bytes 1966088 | tf_op jit(solution)/shard_map/ppermute | solution.py:192
  137.1 2.4 %collective-permute-start.17 = (bf16[4,128,640]{2,1,0:T(8,128)(2,1)}, bf16[4,128,640]{2,1,0:T(8,128)(2,1)S(1)}, u32[]{:S(2)}, u32[]{:S(2)}) collective-permute-start(bf16[4,128,640]{2,1,0:T(8,128)(2,1)} %collective-permute-done.11.refs_2_), channel_id=1, source_target_pairs={{0,1},{1,0},{2,3},{3,2},{4,5},{5,4},{6,7},{7,6},{8,9},{9,8},{10,11... | collective-permute-start | bytes 1966088 | tf_op jit(solution)/shard_map/ppermute | solution.py:192
  141.5 2.2 %collective-permute-done.18.refs_7_ = bf16[4,128,640]{2,1,0:T(8,128)(2,1)S(1)} collective-permute-done((bf16[4,128,640]{2,1,0:T(8,128)(2,1)}, bf16[4,128,640]{2,1,0:T(8,128)(2,1)S(1)}, u32[]{:S(2)}, u32[]{:S(2)}) %collective-permute-start.18) | collective-permute-done | bytes 655392 | tf_op jit(solution)/shard_map/ppermute | solution.py:192
  143.7 7.9 %rows.1 = (f32[256,1024]{1,0:T(8,128)S(1)}, bf16[512,1024]{1,0:T(8,128)(2,1)S(1)}, s32[1]{0:T(128)}) custom-call(s32[3]{0:T(128)S(1)} %pad_add_fusion.place, s32[8]{0:T(128)S(1)} %copy-done.5, f32[1,1024]{1,0:T(1,128)S(1)} %bitcast.23, bf16[256,1024]{1,0:T(8,128)(2,1)S(1)} %bitcast.21, bf16[4,128,640]{2,1,0:T(8,128)(2,1)S(1)} %pad_maximum_fusion.refs_0_, ...), custom_call_target="tpu_custom_call" | custom-call | flops 1048576 | bytes 1048576 | tf_op jit(solution)/shard_map/rows/pallas_call | solution.py:134
  (53 shorter events, 21.6 us)
Async XLA Ops:
  0.0 21.3 %copy-start = (bf16[1,1,256,1024]{3,2,1,0:T(8,128)(2,1)S(1)}, bf16[1,1,256,1024]{3,2,1,0:T(8,128)(2,1)}, u32[]{:S(2)}) copy-start(bf16[1,1,256,1024]{3,2,1,0:T(8,128)(2,1)} %param.6) | copy-start | bytes 1572868
  0.8 0.7 collective-permute-start
  2.2 31.9 %all-to-all-start = ((bf16[16,16,512]{2,1,0:T(8,128)(2,1)}), bf16[16,16,512]{2,1,0:T(8,128)(2,1)S(1)}, u32[]{:S(2)}, u32[]{:S(2)}) async-start(bf16[16,16,512]{2,1,0:T(8,128)(2,1)} %broadcast_in_dim.7), calls=%async_computation | async-start | bytes 524288 | tf_op jit(solution)/shard_map/all_to_all | solution.py:171
  34.1 73.2 %all-to-all-start.1 = ((bf16[64,4,1024]{2,1,0:T(4,128)(2,1)}), bf16[64,4,1024]{2,1,0:T(4,128)(2,1)}, u32[]{:S(2)}, u32[]{:S(2)}) async-start(bf16[64,4,1024]{2,1,0:T(4,128)(2,1)} %reshape_reshape.3), calls=%async_computation.1 | async-start | bytes 1048576 | tf_op jit(solution)/shard_map/all_to_all | solution.py:174
  49.6 10.2 %collective-permute-start.2 = (bf16[128,384]{1,0:T(8,128)(2,1)S(1)}, bf16[128,384]{1,0:T(8,128)(2,1)S(1)}, u32[]{:S(2)}, u32[]{:S(2)}) collective-permute-start(bf16[128,384]{1,0:T(8,128)(2,1)S(1)} %get-tuple-element.38), channel_id=1, source_target_pairs={{0,128},{64,192},{128,0},{192,64},{1,129},{65,193},{129,1},{193,65... | collective-permute-start | bytes 294920 | tf_op jit(solution)/shard_map/ppermute | solution.py:157
  54.4 5.8 %collective-permute-start.1 = (bf16[128,384]{1,0:T(8,128)(2,1)S(1)}, bf16[128,384]{1,0:T(8,128)(2,1)S(1)}, u32[]{:S(2)}, u32[]{:S(2)}) collective-permute-start(bf16[128,384]{1,0:T(8,128)(2,1)S(1)} %get-tuple-element.38), channel_id=1, source_target_pairs={{0,192},{64,0},{128,64},{192,128},{1,193},{65,1},{129,65},{193,129... | collective-permute-start | bytes 294920 | tf_op jit(solution)/shard_map/ppermute | solution.py:157
  57.1 7.0 %collective-permute-start.3 = (bf16[128,384]{1,0:T(8,128)(2,1)S(1)}, bf16[128,384]{1,0:T(8,128)(2,1)S(1)}, u32[]{:S(2)}, u32[]{:S(2)}) collective-permute-start(bf16[128,384]{1,0:T(8,128)(2,1)S(1)} %get-tuple-element.38), channel_id=1, source_target_pairs={{0,64},{64,128},{128,192},{192,0},{1,65},{65,129},{129,193},{193,1... | collective-permute-start | bytes 294920 | tf_op jit(solution)/shard_map/ppermute | solution.py:157
  64.1 15.1 %collective-permute-start.9 = (bf16[128,640]{1,0:T(8,128)(2,1)S(1)}, bf16[128,640]{1,0:T(8,128)(2,1)S(1)}, u32[]{:S(2)}, u32[]{:S(2)}) collective-permute-start(bf16[128,640]{1,0:T(8,128)(2,1)S(1)} %pad_maximum_fusion.2), channel_id=1, source_target_pairs={{0,64},{64,128},{128,192},{192,0},{1,65},{65,129},{129,193},{193,1... | collective-permute-start | bytes 491528 | tf_op jit(solution)/shard_map/ppermute | solution.py:157
  66.1 21.4 %collective-permute-start.6 = (bf16[4,128,384]{2,1,0:T(8,128)(2,1)S(1)}, bf16[4,128,384]{2,1,0:T(8,128)(2,1)S(1)}, u32[]{:S(2)}, u32[]{:S(2)}) collective-permute-start(bf16[4,128,384]{2,1,0:T(8,128)(2,1)S(1)} %pad_maximum_fusion.1), channel_id=1, source_target_pairs={{0,256},{256,32},{32,288},{288,0},{1,257},{257,33},{33,289},{289,1... | collective-permute-start | bytes 1179656 | tf_op jit(solution)/shard_map/ppermute | solution.py:157
  68.3 21.3 %collective-permute-start.5 = (bf16[4,128,384]{2,1,0:T(8,128)(2,1)S(1)}, bf16[4,128,384]{2,1,0:T(8,128)(2,1)S(1)}, u32[]{:S(2)}, u32[]{:S(2)}) collective-permute-start(bf16[4,128,384]{2,1,0:T(8,128)(2,1)S(1)} %pad_maximum_fusion.1), channel_id=1, source_target_pairs={{0,32},{256,288},{32,0},{288,256},{1,33},{257,289},{33,1},{289,257... | collective-permute-start | bytes 1179656 | tf_op jit(solution)/shard_map/ppermute | solution.py:157
  73.8 16.8 %collective-permute-start.4 = (bf16[4,128,384]{2,1,0:T(8,128)(2,1)S(1)}, bf16[4,128,384]{2,1,0:T(8,128)(2,1)S(1)}, u32[]{:S(2)}, u32[]{:S(2)}) collective-permute-start(bf16[4,128,384]{2,1,0:T(8,128)(2,1)S(1)} %pad_maximum_fusion.1), channel_id=1, source_target_pairs={{0,288},{256,0},{32,256},{288,32},{1,289},{257,1},{33,257},{289,33... | collective-permute-start | bytes 1179656 | tf_op jit(solution)/shard_map/ppermute | solution.py:157
  76.9 7.9 %collective-permute-start.8 = (bf16[128,640]{1,0:T(8,128)(2,1)S(1)}, bf16[128,640]{1,0:T(8,128)(2,1)S(1)}, u32[]{:S(2)}, u32[]{:S(2)}) collective-permute-start(bf16[128,640]{1,0:T(8,128)(2,1)S(1)} %pad_maximum_fusion.2), channel_id=1, source_target_pairs={{0,128},{64,192},{128,0},{192,64},{1,129},{65,193},{129,1},{193,65... | collective-permute-start | bytes 491528 | tf_op jit(solution)/shard_map/ppermute | solution.py:157
  79.2 8.1 %collective-permute-start.7 = (bf16[128,640]{1,0:T(8,128)(2,1)S(1)}, bf16[128,640]{1,0:T(8,128)(2,1)S(1)}, u32[]{:S(2)}, u32[]{:S(2)}) collective-permute-start(bf16[128,640]{1,0:T(8,128)(2,1)S(1)} %pad_maximum_fusion.2), channel_id=1, source_target_pairs={{0,192},{64,0},{128,64},{192,128},{1,193},{65,1},{129,65},{193,129... | collective-permute-start | bytes 491528 | tf_op jit(solution)/shard_map/ppermute | solution.py:157
  90.7 17.8 %collective-permute-start.14 = (bf16[8,128,384]{2,1,0:T(8,128)(2,1)S(1)}, bf16[8,128,384]{2,1,0:T(8,128)(2,1)}, u32[]{:S(2)}, u32[]{:S(2)}) collective-permute-start(bf16[8,128,384]{2,1,0:T(8,128)(2,1)S(1)} %constant_dynamic-update-slice_fusion.2.refs_1_), channel_id=1, source_target_pairs={{0,1},{1,0},{2,3},{3,2},{4,5},{5,4},{6,7},{7,6},{8,9},{9,8},{10,11... | collective-permute-start | bytes 2359304 | tf_op jit(solution)/shard_map/ppermute | solution.py:192
  94.3 14.2 %collective-permute-start.13 = (bf16[8,128,384]{2,1,0:T(8,128)(2,1)S(1)}, bf16[8,128,384]{2,1,0:T(8,128)(2,1)}, u32[]{:S(2)}, u32[]{:S(2)}) collective-permute-start(bf16[8,128,384]{2,1,0:T(8,128)(2,1)S(1)} %constant_dynamic-update-slice_fusion.refs_0_), channel_id=1, source_target_pairs={{0,1},{1,0},{2,3},{3,2},{4,5},{5,4},{6,7},{7,6},{8,9},{9,8},{10,11... | collective-permute-start | bytes 2359304 | tf_op jit(solution)/shard_map/ppermute | solution.py:192
  96.3 33.0 %collective-permute-start.12 = (bf16[4,128,640]{2,1,0:T(8,128)(2,1)S(1)}, bf16[4,128,640]{2,1,0:T(8,128)(2,1)}, u32[]{:S(2)}, u32[]{:S(2)}) collective-permute-start(bf16[4,128,640]{2,1,0:T(8,128)(2,1)S(1)} %pad_maximum_fusion.refs_0_), channel_id=1, source_target_pairs={{0,256},{256,32},{32,288},{288,0},{1,257},{257,33},{33,289},{289,1... | collective-permute-start | bytes 1966088 | tf_op jit(solution)/shard_map/ppermute | solution.py:157
  100.7 29.5 %collective-permute-start.11 = (bf16[4,128,640]{2,1,0:T(8,128)(2,1)S(1)}, bf16[4,128,640]{2,1,0:T(8,128)(2,1)}, u32[]{:S(2)}, u32[]{:S(2)}) collective-permute-start(bf16[4,128,640]{2,1,0:T(8,128)(2,1)S(1)} %pad_maximum_fusion.refs_0_), channel_id=1, source_target_pairs={{0,32},{256,288},{32,0},{288,256},{1,33},{257,289},{33,1},{289,257... | collective-permute-start | bytes 1966088 | tf_op jit(solution)/shard_map/ppermute | solution.py:157
  103.6 27.9 %collective-permute-start.10 = (bf16[4,128,640]{2,1,0:T(8,128)(2,1)S(1)}, bf16[4,128,640]{2,1,0:T(8,128)(2,1)}, u32[]{:S(2)}, u32[]{:S(2)}) collective-permute-start(bf16[4,128,640]{2,1,0:T(8,128)(2,1)S(1)} %pad_maximum_fusion.refs_0_), channel_id=1, source_target_pairs={{0,288},{256,0},{32,256},{288,32},{1,289},{257,1},{33,257},{289,33... | collective-permute-start | bytes 1966088 | tf_op jit(solution)/shard_map/ppermute | solution.py:157
  116.5 36.9 %all-to-all-start.2 = ((bf16[64,4,512]{2,1,0:T(4,128)(2,1)}), bf16[64,4,512]{2,1,0:T(4,128)(2,1)S(1)}, u32[]{:S(2)}, u32[]{:S(2)}) async-start(bf16[64,4,512]{2,1,0:T(4,128)(2,1)} %reshape.37), calls=%async_computation.2 | async-start | bytes 524288 | tf_op jit(solution)/shard_map/all_to_all | solution.py:198
  129.3 14.5 %copy-start.5 = (s32[8]{0:T(128)S(1)}, s32[8]{0:T(128)}, u32[]{:S(2)}) copy-start(s32[8]{0:T(128)} %reach_ref.3) | copy-start | bytes 100
  131.5 9.9 %collective-permute-start.15 = (bf16[4,128,640]{2,1,0:T(8,128)(2,1)S(1)}, bf16[4,128,640]{2,1,0:T(8,128)(2,1)S(1)}, u32[]{:S(2)}, u32[]{:S(2)}) collective-permute-start(bf16[4,128,640]{2,1,0:T(8,128)(2,1)S(1)} %pad_maximum_fusion.refs_0_), channel_id=1, source_target_pairs={{0,1},{1,0},{2,3},{3,2},{4,5},{5,4},{6,7},{7,6},{8,9},{9,8},{10,11... | collective-permute-start | bytes 1966088 | tf_op jit(solution)/shard_map/ppermute | solution.py:192
  135.2 6.3 %collective-permute-start.16 = (bf16[4,128,640]{2,1,0:T(8,128)(2,1)}, bf16[4,128,640]{2,1,0:T(8,128)(2,1)S(1)}, u32[]{:S(2)}, u32[]{:S(2)}) collective-permute-start(bf16[4,128,640]{2,1,0:T(8,128)(2,1)} %collective-permute-done.10.refs_1_), channel_id=1, source_target_pairs={{0,1},{1,0},{2,3},{3,2},{4,5},{5,4},{6,7},{7,6},{8,9},{9,8},{10,11... | collective-permute-start | bytes 1966088 | tf_op jit(solution)/shard_map/ppermute | solution.py:192
  137.1 4.4 %collective-permute-start.17 = (bf16[4,128,640]{2,1,0:T(8,128)(2,1)}, bf16[4,128,640]{2,1,0:T(8,128)(2,1)S(1)}, u32[]{:S(2)}, u32[]{:S(2)}) collective-permute-start(bf16[4,128,640]{2,1,0:T(8,128)(2,1)} %collective-permute-done.11.refs_2_), channel_id=1, source_target_pairs={{0,1},{1,0},{2,3},{3,2},{4,5},{5,4},{6,7},{7,6},{8,9},{9,8},{10,11... | collective-permute-start | bytes 1966088 | tf_op jit(solution)/shard_map/ppermute | solution.py:192
  139.5 4.2 %collective-permute-start.18 = (bf16[4,128,640]{2,1,0:T(8,128)(2,1)}, bf16[4,128,640]{2,1,0:T(8,128)(2,1)S(1)}, u32[]{:S(2)}, u32[]{:S(2)}) collective-permute-start(bf16[4,128,640]{2,1,0:T(8,128)(2,1)} %collective-permute-done.12.refs_3_), channel_id=1, source_target_pairs={{0,1},{1,0},{2,3},{3,2},{4,5},{5,4},{6,7},{7,6},{8,9},{9,8},{10,11... | collective-permute-start | bytes 1966088 | tf_op jit(solution)/shard_map/ppermute | solution.py:192
  (4 other events, 4.1 us)

commit v7 on v5

--- a/solution.py
+++ b/solution.py
@@ -1,3 +1,5 @@
+import math
+
 import jax
 import jax.numpy as jnp
 from jax import lax
@@ -14,20 +16,24 @@
 PART = 384
 SEQ = ("xh", "z", "c")
 FAR = 1 << 20
-
-
-def assemble(place, odd, refs, lanes, w_ref, first, width):
+COLUMN_PIECES = (1, 3)
+REST_PIECES = (1, 1, 1, 1)
+
+
+def assemble(place, odd, refs, sizes, lanes, w_ref, first, width):
     x, y, core = place[0], place[1], place[2]
+    pieces = [(i, j) for i, size in enumerate(sizes) for j in range(size)]
     for t in range(X):
         there = (x + t) & 3
         xh, xl = there >> 1, there & 1
-        base = 512 * xh + 32 * ((1 - xl) if odd else xl)
+        turn = 32 * ((1 - xl) if odd else xl)
+        piece, at = pieces[t]
         for s in range(Y):
             cols = pl.ds(pl.multiple_of(first + width * ((y + s) & 3), 128), width)
-            for ref, c in ((refs[t], core), (refs[X + t], 1 - core)):
-                for zz in range(Z // 2):
-                    row = pl.multiple_of(base + 16 * c + 64 * zz, 16)
-                    w_ref[pl.ds(row, 16), cols] = ref[s, pl.ds(16 * zz, 16), lanes]
+            for ref, c in ((refs[piece], core), (refs[len(sizes) + piece], 1 - core)):
+                rows = pl.ds(pl.multiple_of(turn + 16 * c, 16), 16)
+                block = ref[at * Y + s, :, lanes].reshape(Z // 2, 16, width)
+                w_ref[pl.ds(Z // 2 * xh, Z // 2), rows, cols] = block
 
 
 def attend(reach_ref, gain_ref, x_ref, w_ref, n_ref, qkv_ref, out_ref, dist):
@@ -43,24 +49,40 @@
     def project(i, _):
         cols = pl.ds(pl.multiple_of(i * 256, 256), 256)
         qkv_ref[:, cols] = jnp.dot(
-            n_ref[...], w_ref[:, cols], preferred_element_type=jnp.float32
+            n_ref[...],
+            w_ref[:, :, cols].reshape(FEATURES, 256),
+            preferred_element_type=jnp.float32,
         ).astype(jnp.bfloat16)
         return 0
 
     lax.fori_loop(0, WIDTH // 256, project, 0)
 
-    for h in range(HEADS):
-        q = qkv_ref[:, h * 64 : h * 64 + 64]
-        k = qkv_ref[:, HALF + h * 64 : HALF + h * 64 + 64]
-        v = qkv_ref[:, 2 * HALF + h * 64 : 2 * HALF + h * 64 + 64]
-        s = lax.dot_general(
-            q, k, (((1,), (1,)), ((), ())), preferred_element_type=jnp.float32
-        )
-        s = jnp.where(dist < reach_ref[h], s * 0.125, -1e30)
-        p = jnp.exp(s - jnp.max(s, axis=-1, keepdims=True))
-        o = jnp.dot(p.astype(jnp.bfloat16), v, preferred_element_type=jnp.float32)
-        o = o / jnp.sum(p, axis=-1, keepdims=True)
-        out_ref[:, h * 64 : h * 64 + 64] = o.astype(jnp.bfloat16)
+    lane = lax.broadcasted_iota(jnp.int32, (STRIDE, 128), 1)
+    low = (lane < 64).astype(jnp.float32)
+    masks = [low.astype(jnp.bfloat16), (1.0 - low).astype(jnp.bfloat16)]
+    scale = 0.125 * math.log2(math.e)
+    mid = STRIDE // 2
+    for h in range(0, HEADS, 2):
+        q, k, v = (qkv_ref[:, n * HALF + h * 64 : n * HALF + h * 64 + 128] for n in range(3))
+        done = []
+        for e in range(2):
+            reach = reach_ref[h + e]
+            qe = q * masks[e]
+            ve = v * masks[e] + masks[1 - e]
+            for first, seen in ((0, mid), (mid, STRIDE)):
+                s = lax.dot_general(
+                    qe[first : first + mid],
+                    k[:seen],
+                    (((1,), (1,)), ((), ())),
+                    preferred_element_type=jnp.float32,
+                )
+                s = jnp.where(dist[first : first + mid, :seen] < reach, s * scale, -1e30)
+                p = jnp.exp2(s - jnp.max(s, axis=-1, keepdims=True)).astype(jnp.bfloat16)
+                o = jnp.dot(p, ve[:seen], preferred_element_type=jnp.float32)
+                done.append(o / pltpu.roll(o, 64, 1))
+        for i, first in enumerate((0, mid)):
+            both = jnp.where(lane[:mid] < 64, done[i], done[2 + i])
+            out_ref[first : first + mid, h * 64 : h * 64 + 128] = both.astype(jnp.bfloat16)
 
 
 def pairs():
@@ -69,8 +91,8 @@
 
 
 def column_kernel(place, reach_ref, gain_ref, x_ref, *refs):
-    parts, (out_ref, w_ref, n_ref, qkv_ref) = refs[: 2 * X], refs[2 * X :]
-    assemble(place, True, parts, slice(0, PART), w_ref, 0, PART)
+    *parts, out_ref, w_ref, n_ref, qkv_ref = refs
+    assemble(place, True, parts, COLUMN_PIECES, slice(0, PART), w_ref, 0, PART)
     i, j = pairs()
     back = (i >> 2) - (j >> 2)
     dist = jnp.where((((i ^ j) & 3) == 0) & (back >= 0), back, FAR)
@@ -78,20 +100,21 @@
 
 
 def row_kernel(place, reach_ref, gain_ref, x_ref, *refs):
-    parts = refs[: 2 * X]
-    base_ref, low_ref, done_ref, w_ref, n_ref, qkv_ref, a_ref, o_ref = refs[2 * X :]
+    *parts, base_ref, low_ref, done_ref, w_ref, n_ref, qkv_ref, a_ref, o_ref = refs
     done_ref[0] = 0
-    assemble(place, False, parts, slice(0, PART), w_ref, 0, PART)
+    assemble(place, False, parts, REST_PIECES, slice(0, PART), w_ref, 0, PART)
     i, j = pairs()
     dist = jnp.where(j <= i, (i >> 5) - (j >> 5), FAR)
     attend(reach_ref, gain_ref, x_ref, w_ref, n_ref, qkv_ref, a_ref, dist)
-    assemble(place, False, parts, slice(PART, PART + 128), o_ref, 0, 128)
-    assemble(place, True, parts, slice(PART + 128, PART + 256), o_ref, 512, 128)
+    assemble(place, False, parts, REST_PIECES, slice(PART, PART + 128), o_ref, 0, 128)
+    assemble(place, True, parts, REST_PIECES, slice(PART + 128, PART + 256), o_ref, 512, 128)
     for n in range(0, FEATURES, 256):
         base_ref[:, n : n + 256] = x_ref[:, n : n + 256].astype(jnp.float32) + jnp.dot(
-            a_ref[...], o_ref[:HALF, n : n + 256], preferred_element_type=jnp.float32
+            a_ref[...],
+            o_ref[: Z // 2, :, n : n + 256].reshape(HALF, 256),
+            preferred_element_type=jnp.float32,
         )
-    low_ref[...] = o_ref[HALF:, :]
+    low_ref[...] = o_ref[Z // 2 :].reshape(HALF, FEATURES)
 
 
 def last_kernel(base_ref, col_ref, low_ref, out_ref):
@@ -105,11 +128,11 @@
 VMEM = pl.BlockSpec(memory_space=pltpu.VMEM)
 SMEM = pl.BlockSpec(memory_space=pltpu.SMEM)
 WORK = [
-    pltpu.VMEM((FEATURES, WIDTH), jnp.bfloat16),
+    pltpu.VMEM((Z, 64, WIDTH), jnp.bfloat16),
     pltpu.VMEM((STRIDE, FEATURES), jnp.bfloat16),
     pltpu.VMEM((STRIDE, WIDTH), jnp.bfloat16),
 ]
-PARAMS = pltpu.CompilerParams(vmem_limit_bytes=40 * 1024 * 1024)
+PARAMS = pltpu.CompilerParams(vmem_limit_bytes=24 * 1024 * 1024)
 COST = pl.CostEstimate(
     flops=2 * 256 * 1024 * 1536 + 16 * 256 * 256 * 128,
     bytes_accessed=6 << 20,
@@ -143,7 +166,7 @@
         scratch_shapes=WORK
         + [
             pltpu.VMEM((STRIDE, HALF), jnp.bfloat16),
-            pltpu.VMEM((FEATURES, FEATURES), jnp.bfloat16),
+            pltpu.VMEM((Z, 64, FEATURES), jnp.bfloat16),
         ],
         compiler_params=PARAMS,
         cost_estimate=pl.CostEstimate(flops=1 << 20, bytes_accessed=1 << 20, transcendentals=0),
@@ -170,8 +193,8 @@
     block = lax.ppermute(block, ("xl", "z"), change)
     column = lax.all_to_all(jnp.broadcast_to(block, (Z, 16, 512)), "z", split_axis=0, concat_axis=0)
 
-    sent, column = lax.optimization_barrier((rows, column))
-    turned = lax.all_to_all(sent.reshape(64, 4, FEATURES), SEQ, split_axis=0, concat_axis=0)
+    sent, column = lax.optimization_barrier((rows.reshape(64, 4, FEATURES), column))
+    turned = lax.all_to_all(sent, SEQ, split_axis=0, concat_axis=0)
     turned = turned.reshape(STRIDE, FEATURES)
 
     halves = column.reshape(Z // 2, 2, 16, 512)
@@ -183,16 +206,21 @@
     def plane(part):
         return [part, *ring(part, ("xl", "xh"), [0, 2, 1, 3])]
 
-    def both_cores(parts):
-        return [*parts, *(lax.ppermute(a, "c", [(0, 1), (1, 0)]) for a in parts)]
+    def both_cores(parts, sizes):
+        ends = [sum(sizes[: i + 1]) for i in range(len(sizes))]
+        joined = [
+            parts[e - n] if n == 1 else jnp.concatenate(parts[e - n : e])
+            for e, n in zip(ends, sizes, strict=True)
+        ]
+        return [*joined, *(lax.ppermute(a, "c", [(0, 1), (1, 0)]) for a in joined)]
 
     col_plane = plane(near[:, :, :PART])
-    col_mid = column_attention(place, col_rows, gain, turned, both_cores(col_plane))
+    col_mid = column_attention(place, col_rows, gain, turned, both_cores(col_plane, COLUMN_PIECES))
     col_out = lax.all_to_all(col_mid.reshape(64, 4, HALF), SEQ, split_axis=0, concat_axis=0)
 
     near_rest, _ = lax.optimization_barrier((near[:, :, PART:], col_plane))
     rest, _ = lax.optimization_barrier((plane(near_rest), col_mid))
-    base, low, last = row_attention(place, row_blocks, gain, rows, both_cores(rest))
+    base, low, last = row_attention(place, row_blocks, gain, rows, both_cores(rest, REST_PIECES))
     col_out = jnp.where(last[0] == 0, col_out, 0).reshape(STRIDE, HALF)
 
     mixed = pl.pallas_call(

time: 160 us -> 157 us (0.981)
  blocking collectives: 31.7 us -> 0 us
  waiting for transfers between devices: 16.9 us -> 39.8 us
  starting transfers between devices: 83.9 us -> 93.3 us
  local copies, waits for them, and re-layouts: 8.19 us -> 5.35 us
    all_to_all x1 -> x0, blocking collectives: 31.7 us -> none  [body(): lax.all_to_all(jnp.broadcast_to(block, (Z, 16, 512)), 'z', split_axis=0,...]
    all_to_all x1 -> x2, starting transfers between devices: 15.4 us -> 35.4 us  [the longest x1 19.1 us: body(): lax.all_to_all(jnp.broadcast_to(block, (Z, 16, 512)), 'z', split_axis=0,...]
    ppermute x9, waiting for transfers between devices: 12.2 us -> 25.8 us  [ring(): lax.ppermute(part, axes, [(order[i], order[(i - t) % size]) for i in rang...]
    all_to_all x1 -> x2, waiting for transfers between devices: 0.01 us -> 11.8 us  [the longest x1 11.8 us: body(): lax.all_to_all(jnp.broadcast_to(block, (Z, 16, 512)), 'z', split_axis=0,...]
    ppermute x8 -> x6, starting transfers between devices: 23.2 us -> 14.7 us  [both_cores(): return [*joined, *(lax.ppermute(a, 'c', [(0, 1), (1, 0)]) for a in joined)]]
    unnamed x20 -> x14, local copies, waits for them, and re-layouts: 5.08 us -> 1.48 us
    ppermute x9, starting transfers between devices: 31.6 us -> 28.1 us  [ring(): lax.ppermute(part, axes, [(order[i], order[(i - t) % size]) for i in rang...]
    all_to_all x1, waiting for transfers between devices: 2.7 us -> 0.01 us  [body(): lax.all_to_all(col_mid.reshape(64, 4, HALF), SEQ, split_axis=0, concat_ax...]
  transfers between devices with their start and end apart: 20 -> 19, of which waited for: 6 -> 6; matrix products, arithmetic and copies ran while one was open for 1% -> 2% of each run, Pallas kernels for 9% -> 9%
where the time goes in v7:
time: 157 us; the launch traced here: 156 us
  starting transfers between devices  93.3 us (59%)
  waiting for transfers between devices  39.8 us (25%)
  Pallas kernels  15.7 us (10%)
  local copies, waits for them, and re-layouts  5.35 us (3%)
    ppermute x9, starting transfers between devices, ring(): lax.ppermute(part, axes, [(order[i], order[(i - t) % size]) for i in rang...  28.1 us
    ppermute x9, waiting for transfers between devices, ring(): lax.ppermute(part, axes, [(order[i], order[(i - t) % size]) for i in rang...  25.8 us
    all_to_all x1, starting transfers between devices, body(): lax.all_to_all(jnp.broadcast_to(block, (Z, 16, 512)), 'z', split_axis=0,...  19.1 us
    all_to_all x1, starting transfers between devices, body(): turned = lax.all_to_all(sent, SEQ, split_axis=0, concat_axis=0)  16.3 us
    ppermute x6, starting transfers between devices, both_cores(): return [*joined, *(lax.ppermute(a, 'c', [(0, 1), (1, 0)]) for a in joined)]  14.7 us
    all_to_all x1, starting transfers between devices, body(): lax.all_to_all(col_mid.reshape(64, 4, HALF), SEQ, split_axis=0, concat_ax...  14.5 us
    all_to_all x1, waiting for transfers between devices, body(): lax.all_to_all(jnp.broadcast_to(block, (Z, 16, 512)), 'z', split_axis=0,...  11.8 us
    pallas_call x1, Pallas kernels, row_attention(): pl.pallas_call(row_kernel, out_shape=[jax.ShapeDtypeStruct((STRIDE, FEATU...  7.65 us
  transfers between devices with their start and end apart: 19, of which 6 were waited for; matrix products, arithmetic and copies ran while one was open for 2% of the time, Pallas kernels for 9%

profile of v7, /device:TPU:1, one launch (start us, length us, event | category | flops | bytes accessed | tf_op | source)
XLA Modules:
  0.0 156.4 jit_solution(2556364331750649115)
XLA Ops:
  2.2 19.1 %all-to-all-start = ((bf16[16,16,512]{2,1,0:T(8,128)(2,1)}), bf16[16,16,512]{2,1,0:T(8,128)(2,1)S(1)}, u32[]{:S(2)}, u32[]{:S(2)}) async-start(bf16[16,16,512]{2,1,0:T(8,128)(2,1)} %broadcast_in_dim.7), calls=%async_computation | async-start | bytes 524288 | tf_op jit(solution)/shard_map/all_to_all | solution.py:194
  22.3 11.8 %all-to-all-done = bf16[16,16,512]{2,1,0:T(8,128)(2,1)S(1)} async-done(((bf16[16,16,512]{2,1,0:T(8,128)(2,1)}), bf16[16,16,512]{2,1,0:T(8,128)(2,1)S(1)}, u32[]{:S(2)}, u32[]{:S(2)}) %all-to-all-start) | async-done | bytes 262176 | tf_op jit(solution)/shard_map/all_to_all | solution.py:194
  34.2 4.8 %collective-permute-start.2 = (bf16[128,1024]{1,0:T(8,128)(2,1)S(1)}, bf16[128,1024]{1,0:T(8,128)(2,1)S(1)}, u32[]{:S(2)}, u32[]{:S(2)}) collective-permute-start(bf16[128,1024]{1,0:T(8,128)(2,1)S(1)} %get-tuple-element.26), channel_id=1, source_target_pairs={{0,128},{64,192},{128,0},{192,64},{1,129},{65,193},{129,1},{193,65... | collective-permute-start | bytes 786440 | tf_op jit(solution)/shard_map/ppermute | solution.py:180
  39.0 2.7 %collective-permute-start.1 = (bf16[128,1024]{1,0:T(8,128)(2,1)S(1)}, bf16[128,1024]{1,0:T(8,128)(2,1)S(1)}, u32[]{:S(2)}, u32[]{:S(2)}) collective-permute-start(bf16[128,1024]{1,0:T(8,128)(2,1)S(1)} %get-tuple-element.26), channel_id=1, source_target_pairs={{0,192},{64,0},{128,64},{192,128},{1,193},{65,1},{129,65},{193,129... | collective-permute-start | bytes 786440 | tf_op jit(solution)/shard_map/ppermute | solution.py:180
  41.7 2.6 %collective-permute-start.3 = (bf16[128,1024]{1,0:T(8,128)(2,1)S(1)}, bf16[128,1024]{1,0:T(8,128)(2,1)S(1)}, u32[]{:S(2)}, u32[]{:S(2)}) collective-permute-start(bf16[128,1024]{1,0:T(8,128)(2,1)S(1)} %get-tuple-element.26), channel_id=1, source_target_pairs={{0,64},{64,128},{128,192},{192,0},{1,65},{65,129},{129,193},{193,1... | collective-permute-start | bytes 786440 | tf_op jit(solution)/shard_map/ppermute | solution.py:180
  44.3 16.3 %all-to-all-start.1 = ((bf16[64,4,1024]{2,1,0:T(4,128)(2,1)}), bf16[64,4,1024]{2,1,0:T(4,128)(2,1)}, u32[]{:S(2)}, u32[]{:S(2)}) async-start(bf16[64,4,1024]{2,1,0:T(4,128)(2,1)} %reshape_reshape.3), calls=%async_computation.1 | async-start | bytes 1048576 | tf_op jit(solution)/shard_map/all_to_all | solution.py:197
  60.7 4.6 %collective-permute-start.4 = (bf16[4,128,384]{2,1,0:T(8,128)(2,1)S(1)}, bf16[4,128,384]{2,1,0:T(8,128)(2,1)S(1)}, u32[]{:S(2)}, u32[]{:S(2)}) collective-permute-start(bf16[4,128,384]{2,1,0:T(8,128)(2,1)S(1)} %pad_maximum_fusion.1.refs_0_), channel_id=1, source_target_pairs={{0,288},{256,0},{32,256},{288,32},{1,289},{257,1},{33,257},{289,33... | collective-permute-start | bytes 1179656 | tf_op jit(solution)/shard_map/ppermute | solution.py:180
  65.3 2.2 %collective-permute-start.5 = (bf16[4,128,384]{2,1,0:T(8,128)(2,1)S(1)}, bf16[4,128,384]{2,1,0:T(8,128)(2,1)S(1)}, u32[]{:S(2)}, u32[]{:S(2)}) collective-permute-start(bf16[4,128,384]{2,1,0:T(8,128)(2,1)S(1)} %pad_maximum_fusion.1.refs_0_), channel_id=1, source_target_pairs={{0,32},{256,288},{32,0},{288,256},{1,33},{257,289},{33,1},{289,257... | collective-permute-start | bytes 1179656 | tf_op jit(solution)/shard_map/ppermute | solution.py:180
  67.5 2.8 %collective-permute-start.6 = (bf16[4,128,384]{2,1,0:T(8,128)(2,1)S(1)}, bf16[4,128,384]{2,1,0:T(8,128)(2,1)S(1)}, u32[]{:S(2)}, u32[]{:S(2)}) collective-permute-start(bf16[4,128,384]{2,1,0:T(8,128)(2,1)S(1)} %pad_maximum_fusion.1.refs_0_), channel_id=1, source_target_pairs={{0,256},{256,32},{32,288},{288,0},{1,257},{257,33},{33,289},{289,1... | collective-permute-start | bytes 1179656 | tf_op jit(solution)/shard_map/ppermute | solution.py:180
  70.3 16.6 %collective-permute-done.4 = bf16[4,128,384]{2,1,0:T(8,128)(2,1)S(1)} collective-permute-done((bf16[4,128,384]{2,1,0:T(8,128)(2,1)S(1)}, bf16[4,128,384]{2,1,0:T(8,128)(2,1)S(1)}, u32[]{:S(2)}, u32[]{:S(2)}) %collective-permute-start.4) | collective-permute-done | bytes 393248 | tf_op jit(solution)/shard_map/ppermute | solution.py:180
  87.0 5.5 %collective-permute-done.6 = bf16[4,128,384]{2,1,0:T(8,128)(2,1)S(1)} collective-permute-done((bf16[4,128,384]{2,1,0:T(8,128)(2,1)S(1)}, bf16[4,128,384]{2,1,0:T(8,128)(2,1)S(1)}, u32[]{:S(2)}, u32[]{:S(2)}) %collective-permute-start.6) | collective-permute-done | bytes 393248 | tf_op jit(solution)/shard_map/ppermute | solution.py:180
  92.6 2.4 %collective-permute-start.11 = (bf16[12,128,384]{2,1,0:T(8,128)(2,1)S(1)}, bf16[12,128,384]{2,1,0:T(8,128)(2,1)}, u32[]{:S(2)}, u32[]{:S(2)}) collective-permute-start(bf16[12,128,384]{2,1,0:T(8,128)(2,1)S(1)} %constant_dynamic-update-slice_fusion.refs_1_), channel_id=1, source_target_pairs={{0,1},{1,0},{2,3},{3,2},{4,5},{5,4},{6,7},{7,6},{8,9},{9,8},{10,11... | collective-permute-start | bytes 3538952 | tf_op jit(solution)/shard_map/ppermute | solution.py:215
  95.0 1.9 %collective-permute-start.10 = (bf16[4,128,384]{2,1,0:T(8,128)(2,1)S(1)}, bf16[4,128,384]{2,1,0:T(8,128)(2,1)}, u32[]{:S(2)}, u32[]{:S(2)}) collective-permute-start(bf16[4,128,384]{2,1,0:T(8,128)(2,1)S(1)} %pad_maximum_fusion.1.refs_0_), channel_id=1, source_target_pairs={{0,1},{1,0},{2,3},{3,2},{4,5},{5,4},{6,7},{7,6},{8,9},{9,8},{10,11... | collective-permute-start | bytes 1179656 | tf_op jit(solution)/shard_map/ppermute | solution.py:215
  97.2 1.9 %collective-permute-start.9 = (bf16[4,128,640]{2,1,0:T(8,128)(2,1)S(1)}, bf16[4,128,640]{2,1,0:T(8,128)(2,1)}, u32[]{:S(2)}, u32[]{:S(2)}) collective-permute-start(bf16[4,128,640]{2,1,0:T(8,128)(2,1)S(1)} %slice.30.refs_0_), channel_id=1, source_target_pairs={{0,256},{256,32},{32,288},{288,0},{1,257},{257,33},{33,289},{289,1... | collective-permute-start | bytes 1966088 | tf_op jit(solution)/shard_map/ppermute | solution.py:180
  99.1 3.4 %collective-permute-start.8 = (bf16[4,128,640]{2,1,0:T(8,128)(2,1)S(1)}, bf16[4,128,640]{2,1,0:T(8,128)(2,1)}, u32[]{:S(2)}, u32[]{:S(2)}) collective-permute-start(bf16[4,128,640]{2,1,0:T(8,128)(2,1)S(1)} %slice.30.refs_0_), channel_id=1, source_target_pairs={{0,32},{256,288},{32,0},{288,256},{1,33},{257,289},{33,1},{289,257... | collective-permute-start | bytes 1966088 | tf_op jit(solution)/shard_map/ppermute | solution.py:180
  102.6 3.1 %collective-permute-start.7 = (bf16[4,128,640]{2,1,0:T(8,128)(2,1)S(1)}, bf16[4,128,640]{2,1,0:T(8,128)(2,1)}, u32[]{:S(2)}, u32[]{:S(2)}) collective-permute-start(bf16[4,128,640]{2,1,0:T(8,128)(2,1)S(1)} %slice.30.refs_0_), channel_id=1, source_target_pairs={{0,288},{256,0},{32,256},{288,32},{1,289},{257,1},{33,257},{289,33... | collective-permute-start | bytes 1966088 | tf_op jit(solution)/shard_map/ppermute | solution.py:180
  107.0 6.8 %columns.1 = bf16[256,512]{1,0:T(8,128)(2,1)S(1)} custom-call(s32[3]{0:T(128)S(1)} %pad_add_fusion.place, s32[8]{0:T(128)S(1)} %copy-done.4, f32[1,1024]{1,0:T(1,128)S(1)} %bitcast.18, bf16[256,1024]{1,0:T(8,128)(2,1)S(1)} %reshape.36.x_ref, bf16[4,128,384]{2,1,0:T(8,128)(2,1)S(1)} %pad_maximum_fusion.1.refs_0_, ...), custom_call_target="tpu_custom_call" | custom-call | flops 939524096 | bytes 6291456 | tf_op jit(solution)/shard_map/columns/pallas_call | solution.py:144
  114.5 14.5 %all-to-all-start.2 = ((bf16[64,4,512]{2,1,0:T(4,128)(2,1)}), bf16[64,4,512]{2,1,0:T(4,128)(2,1)S(1)}, u32[]{:S(2)}, u32[]{:S(2)}) async-start(bf16[64,4,512]{2,1,0:T(4,128)(2,1)} %reshape.37), calls=%async_computation.2 | async-start | bytes 524288 | tf_op jit(solution)/shard_map/all_to_all | solution.py:219
  130.3 2.4 %collective-permute-done.7.refs_1_ = bf16[4,128,640]{2,1,0:T(8,128)(2,1)} collective-permute-done((bf16[4,128,640]{2,1,0:T(8,128)(2,1)S(1)}, bf16[4,128,640]{2,1,0:T(8,128)(2,1)}, u32[]{:S(2)}, u32[]{:S(2)}) %collective-permute-start.7) | collective-permute-done | bytes 655392 | tf_op jit(solution)/shard_map/ppermute | solution.py:180
  132.6 4.1 %collective-permute-start.12 = (bf16[4,128,640]{2,1,0:T(8,128)(2,1)S(1)}, bf16[4,128,640]{2,1,0:T(8,128)(2,1)S(1)}, u32[]{:S(2)}, u32[]{:S(2)}) collective-permute-start(bf16[4,128,640]{2,1,0:T(8,128)(2,1)S(1)} %slice.30.refs_0_), channel_id=1, source_target_pairs={{0,1},{1,0},{2,3},{3,2},{4,5},{5,4},{6,7},{7,6},{8,9},{9,8},{10,11... | collective-permute-start | bytes 1966088 | tf_op jit(solution)/shard_map/ppermute | solution.py:215
  136.7 1.9 %collective-permute-start.13 = (bf16[4,128,640]{2,1,0:T(8,128)(2,1)}, bf16[4,128,640]{2,1,0:T(8,128)(2,1)S(1)}, u32[]{:S(2)}, u32[]{:S(2)}) collective-permute-start(bf16[4,128,640]{2,1,0:T(8,128)(2,1)} %collective-permute-done.7.refs_1_), channel_id=1, source_target_pairs={{0,1},{1,0},{2,3},{3,2},{4,5},{5,4},{6,7},{7,6},{8,9},{9,8},{10,11... | collective-permute-start | bytes 1966088 | tf_op jit(solution)/shard_map/ppermute | solution.py:215
  138.7 2.4 %collective-permute-start.14 = (bf16[4,128,640]{2,1,0:T(8,128)(2,1)}, bf16[4,128,640]{2,1,0:T(8,128)(2,1)S(1)}, u32[]{:S(2)}, u32[]{:S(2)}) collective-permute-start(bf16[4,128,640]{2,1,0:T(8,128)(2,1)} %collective-permute-done.8.refs_2_), channel_id=1, source_target_pairs={{0,1},{1,0},{2,3},{3,2},{4,5},{5,4},{6,7},{7,6},{8,9},{9,8},{10,11... | collective-permute-start | bytes 1966088 | tf_op jit(solution)/shard_map/ppermute | solution.py:215
  143.0 2.2 %collective-permute-done.15.refs_7_ = bf16[4,128,640]{2,1,0:T(8,128)(2,1)S(1)} collective-permute-done((bf16[4,128,640]{2,1,0:T(8,128)(2,1)}, bf16[4,128,640]{2,1,0:T(8,128)(2,1)S(1)}, u32[]{:S(2)}, u32[]{:S(2)}) %collective-permute-start.15) | collective-permute-done | bytes 655392 | tf_op jit(solution)/shard_map/ppermute | solution.py:215
  145.3 7.6 %rows.1 = (f32[256,1024]{1,0:T(8,128)S(1)}, bf16[512,1024]{1,0:T(8,128)(2,1)S(1)}, s32[1]{0:T(128)}) custom-call(s32[3]{0:T(128)S(1)} %pad_add_fusion.place, s32[8]{0:T(128)S(1)} %copy-done.5, f32[1,1024]{1,0:T(1,128)S(1)} %bitcast.19, bf16[256,1024]{1,0:T(8,128)(2,1)S(1)} %bitcast.17, bf16[4,128,640]{2,1,0:T(8,128)(2,1)S(1)} %slice.30.refs_0_, ...), custom_call_target="tpu_custom_call" | custom-call | flops 1048576 | bytes 1048576 | tf_op jit(solution)/shard_map/rows/pallas_call | solution.py:157
  (47 shorter events, 11.6 us)
Async XLA Ops:
  0.0 21.3 %copy-start = (bf16[1,1,256,1024]{3,2,1,0:T(8,128)(2,1)S(1)}, bf16[1,1,256,1024]{3,2,1,0:T(8,128)(2,1)}, u32[]{:S(2)}) copy-start(bf16[1,1,256,1024]{3,2,1,0:T(8,128)(2,1)} %param.6) | copy-start | bytes 1572868
  0.8 0.7 collective-permute-start
  2.2 31.9 %all-to-all-start = ((bf16[16,16,512]{2,1,0:T(8,128)(2,1)}), bf16[16,16,512]{2,1,0:T(8,128)(2,1)S(1)}, u32[]{:S(2)}, u32[]{:S(2)}) async-start(bf16[16,16,512]{2,1,0:T(8,128)(2,1)} %broadcast_in_dim.7), calls=%async_computation | async-start | bytes 524288 | tf_op jit(solution)/shard_map/all_to_all | solution.py:194
  34.2 26.4 %collective-permute-start.2 = (bf16[128,1024]{1,0:T(8,128)(2,1)S(1)}, bf16[128,1024]{1,0:T(8,128)(2,1)S(1)}, u32[]{:S(2)}, u32[]{:S(2)}) collective-permute-start(bf16[128,1024]{1,0:T(8,128)(2,1)S(1)} %get-tuple-element.26), channel_id=1, source_target_pairs={{0,128},{64,192},{128,0},{192,64},{1,129},{65,193},{129,1},{193,65... | collective-permute-start | bytes 786440 | tf_op jit(solution)/shard_map/ppermute | solution.py:180
  39.0 21.6 %collective-permute-start.1 = (bf16[128,1024]{1,0:T(8,128)(2,1)S(1)}, bf16[128,1024]{1,0:T(8,128)(2,1)S(1)}, u32[]{:S(2)}, u32[]{:S(2)}) collective-permute-start(bf16[128,1024]{1,0:T(8,128)(2,1)S(1)} %get-tuple-element.26), channel_id=1, source_target_pairs={{0,192},{64,0},{128,64},{192,128},{1,193},{65,1},{129,65},{193,129... | collective-permute-start | bytes 786440 | tf_op jit(solution)/shard_map/ppermute | solution.py:180
  41.7 18.9 %collective-permute-start.3 = (bf16[128,1024]{1,0:T(8,128)(2,1)S(1)}, bf16[128,1024]{1,0:T(8,128)(2,1)S(1)}, u32[]{:S(2)}, u32[]{:S(2)}) collective-permute-start(bf16[128,1024]{1,0:T(8,128)(2,1)S(1)} %get-tuple-element.26), channel_id=1, source_target_pairs={{0,64},{64,128},{128,192},{192,0},{1,65},{65,129},{129,193},{193,1... | collective-permute-start | bytes 786440 | tf_op jit(solution)/shard_map/ppermute | solution.py:180
  44.3 61.4 %all-to-all-start.1 = ((bf16[64,4,1024]{2,1,0:T(4,128)(2,1)}), bf16[64,4,1024]{2,1,0:T(4,128)(2,1)}, u32[]{:S(2)}, u32[]{:S(2)}) async-start(bf16[64,4,1024]{2,1,0:T(4,128)(2,1)} %reshape_reshape.3), calls=%async_computation.1 | async-start | bytes 1048576 | tf_op jit(solution)/shard_map/all_to_all | solution.py:197
  60.7 26.2 %collective-permute-start.4 = (bf16[4,128,384]{2,1,0:T(8,128)(2,1)S(1)}, bf16[4,128,384]{2,1,0:T(8,128)(2,1)S(1)}, u32[]{:S(2)}, u32[]{:S(2)}) collective-permute-start(bf16[4,128,384]{2,1,0:T(8,128)(2,1)S(1)} %pad_maximum_fusion.1.refs_0_), channel_id=1, source_target_pairs={{0,288},{256,0},{32,256},{288,32},{1,289},{257,1},{33,257},{289,33... | collective-permute-start | bytes 1179656 | tf_op jit(solution)/shard_map/ppermute | solution.py:180
  65.3 21.6 %collective-permute-start.5 = (bf16[4,128,384]{2,1,0:T(8,128)(2,1)S(1)}, bf16[4,128,384]{2,1,0:T(8,128)(2,1)S(1)}, u32[]{:S(2)}, u32[]{:S(2)}) collective-permute-start(bf16[4,128,384]{2,1,0:T(8,128)(2,1)S(1)} %pad_maximum_fusion.1.refs_0_), channel_id=1, source_target_pairs={{0,32},{256,288},{32,0},{288,256},{1,33},{257,289},{33,1},{289,257... | collective-permute-start | bytes 1179656 | tf_op jit(solution)/shard_map/ppermute | solution.py:180
  67.5 25.0 %collective-permute-start.6 = (bf16[4,128,384]{2,1,0:T(8,128)(2,1)S(1)}, bf16[4,128,384]{2,1,0:T(8,128)(2,1)S(1)}, u32[]{:S(2)}, u32[]{:S(2)}) collective-permute-start(bf16[4,128,384]{2,1,0:T(8,128)(2,1)S(1)} %pad_maximum_fusion.1.refs_0_), channel_id=1, source_target_pairs={{0,256},{256,32},{32,288},{288,0},{1,257},{257,33},{33,289},{289,1... | collective-permute-start | bytes 1179656 | tf_op jit(solution)/shard_map/ppermute | solution.py:180
  92.6 14.3 %collective-permute-start.11 = (bf16[12,128,384]{2,1,0:T(8,128)(2,1)S(1)}, bf16[12,128,384]{2,1,0:T(8,128)(2,1)}, u32[]{:S(2)}, u32[]{:S(2)}) collective-permute-start(bf16[12,128,384]{2,1,0:T(8,128)(2,1)S(1)} %constant_dynamic-update-slice_fusion.refs_1_), channel_id=1, source_target_pairs={{0,1},{1,0},{2,3},{3,2},{4,5},{5,4},{6,7},{7,6},{8,9},{9,8},{10,11... | collective-permute-start | bytes 3538952 | tf_op jit(solution)/shard_map/ppermute | solution.py:215
  95.0 11.9 %collective-permute-start.10 = (bf16[4,128,384]{2,1,0:T(8,128)(2,1)S(1)}, bf16[4,128,384]{2,1,0:T(8,128)(2,1)}, u32[]{:S(2)}, u32[]{:S(2)}) collective-permute-start(bf16[4,128,384]{2,1,0:T(8,128)(2,1)S(1)} %pad_maximum_fusion.1.refs_0_), channel_id=1, source_target_pairs={{0,1},{1,0},{2,3},{3,2},{4,5},{5,4},{6,7},{7,6},{8,9},{9,8},{10,11... | collective-permute-start | bytes 1179656 | tf_op jit(solution)/shard_map/ppermute | solution.py:215
  97.1 9.8 %copy-start.3 = (f32[1024]{0:T(1024)S(1)}, f32[1024]{0:T(1024)}, u32[]{:S(2)}) copy-start(f32[1024]{0:T(1024)} %param.7) | copy-start | bytes 12292
  97.1 9.8 %copy-start.4 = (s32[8]{0:T(128)S(1)}, s32[8]{0:T(128)}, u32[]{:S(2)}) copy-start(s32[8]{0:T(128)} %reach_ref.2) | copy-start | bytes 100
  97.2 33.1 %collective-permute-start.9 = (bf16[4,128,640]{2,1,0:T(8,128)(2,1)S(1)}, bf16[4,128,640]{2,1,0:T(8,128)(2,1)}, u32[]{:S(2)}, u32[]{:S(2)}) collective-permute-start(bf16[4,128,640]{2,1,0:T(8,128)(2,1)S(1)} %slice.30.refs_0_), channel_id=1, source_target_pairs={{0,256},{256,32},{32,288},{288,0},{1,257},{257,33},{33,289},{289,1... | collective-permute-start | bytes 1966088 | tf_op jit(solution)/shard_map/ppermute | solution.py:180
  99.1 31.1 %collective-permute-start.8 = (bf16[4,128,640]{2,1,0:T(8,128)(2,1)S(1)}, bf16[4,128,640]{2,1,0:T(8,128)(2,1)}, u32[]{:S(2)}, u32[]{:S(2)}) collective-permute-start(bf16[4,128,640]{2,1,0:T(8,128)(2,1)S(1)} %slice.30.refs_0_), channel_id=1, source_target_pairs={{0,32},{256,288},{32,0},{288,256},{1,33},{257,289},{33,1},{289,257... | collective-permute-start | bytes 1966088 | tf_op jit(solution)/shard_map/ppermute | solution.py:180
  102.6 30.1 %collective-permute-start.7 = (bf16[4,128,640]{2,1,0:T(8,128)(2,1)S(1)}, bf16[4,128,640]{2,1,0:T(8,128)(2,1)}, u32[]{:S(2)}, u32[]{:S(2)}) collective-permute-start(bf16[4,128,640]{2,1,0:T(8,128)(2,1)S(1)} %slice.30.refs_0_), channel_id=1, source_target_pairs={{0,288},{256,0},{32,256},{288,32},{1,289},{257,1},{33,257},{289,33... | collective-permute-start | bytes 1966088 | tf_op jit(solution)/shard_map/ppermute | solution.py:180
  107.0 38.3 %copy-start.5 = (s32[8]{0:T(128)S(1)}, s32[8]{0:T(128)}, u32[]{:S(2)}) copy-start(s32[8]{0:T(128)} %reach_ref.3) | copy-start | bytes 100
  114.5 40.1 %all-to-all-start.2 = ((bf16[64,4,512]{2,1,0:T(4,128)(2,1)}), bf16[64,4,512]{2,1,0:T(4,128)(2,1)S(1)}, u32[]{:S(2)}, u32[]{:S(2)}) async-start(bf16[64,4,512]{2,1,0:T(4,128)(2,1)} %reshape.37), calls=%async_computation.2 | async-start | bytes 524288 | tf_op jit(solution)/shard_map/all_to_all | solution.py:219
  132.6 10.4 %collective-permute-start.12 = (bf16[4,128,640]{2,1,0:T(8,128)(2,1)S(1)}, bf16[4,128,640]{2,1,0:T(8,128)(2,1)S(1)}, u32[]{:S(2)}, u32[]{:S(2)}) collective-permute-start(bf16[4,128,640]{2,1,0:T(8,128)(2,1)S(1)} %slice.30.refs_0_), channel_id=1, source_target_pairs={{0,1},{1,0},{2,3},{3,2},{4,5},{5,4},{6,7},{7,6},{8,9},{9,8},{10,11... | collective-permute-start | bytes 1966088 | tf_op jit(solution)/shard_map/ppermute | solution.py:215
  136.7 6.3 %collective-permute-start.13 = (bf16[4,128,640]{2,1,0:T(8,128)(2,1)}, bf16[4,128,640]{2,1,0:T(8,128)(2,1)S(1)}, u32[]{:S(2)}, u32[]{:S(2)}) collective-permute-start(bf16[4,128,640]{2,1,0:T(8,128)(2,1)} %collective-permute-done.7.refs_1_), channel_id=1, source_target_pairs={{0,1},{1,0},{2,3},{3,2},{4,5},{5,4},{6,7},{7,6},{8,9},{9,8},{10,11... | collective-permute-start | bytes 1966088 | tf_op jit(solution)/shard_map/ppermute | solution.py:215
  138.7 4.4 %collective-permute-start.14 = (bf16[4,128,640]{2,1,0:T(8,128)(2,1)}, bf16[4,128,640]{2,1,0:T(8,128)(2,1)S(1)}, u32[]{:S(2)}, u32[]{:S(2)}) collective-permute-start(bf16[4,128,640]{2,1,0:T(8,128)(2,1)} %collective-permute-done.8.refs_2_), channel_id=1, source_target_pairs={{0,1},{1,0},{2,3},{3,2},{4,5},{5,4},{6,7},{7,6},{8,9},{9,8},{10,11... | collective-permute-start | bytes 1966088 | tf_op jit(solution)/shard_map/ppermute | solution.py:215
  141.1 4.2 %collective-permute-start.15 = (bf16[4,128,640]{2,1,0:T(8,128)(2,1)}, bf16[4,128,640]{2,1,0:T(8,128)(2,1)S(1)}, u32[]{:S(2)}, u32[]{:S(2)}) collective-permute-start(bf16[4,128,640]{2,1,0:T(8,128)(2,1)} %collective-permute-done.9.refs_3_), channel_id=1, source_target_pairs={{0,1},{1,0},{2,3},{3,2},{4,5},{5,4},{6,7},{7,6},{8,9},{9,8},{10,11... | collective-permute-start | bytes 1966088 | tf_op jit(solution)/shard_map/ppermute | solution.py:215
  153.9 1.2 copy-start.2
  (1 other events, 1.0 us)

commit v8 on v7

--- a/solution.py
+++ b/solution.py
@@ -23,16 +23,16 @@
 def assemble(place, odd, refs, sizes, lanes, w_ref, first, width):
     x, y, core = place[0], place[1], place[2]
     pieces = [(i, j) for i, size in enumerate(sizes) for j in range(size)]
-    for t in range(X):
-        there = (x + t) & 3
-        xh, xl = there >> 1, there & 1
-        turn = 32 * ((1 - xl) if odd else xl)
+    for t in range(Y):
+        cols = pl.ds(pl.multiple_of(first + width * ((y + t) & 3), 128), width)
         piece, at = pieces[t]
-        for s in range(Y):
-            cols = pl.ds(pl.multiple_of(first + width * ((y + s) & 3), 128), width)
+        for s in range(X):
+            there = (x + s) & 3
+            xh, xl = there >> 1, there & 1
+            turn = 32 * ((1 - xl) if odd else xl)
             for ref, c in ((refs[piece], core), (refs[len(sizes) + piece], 1 - core)):
                 rows = pl.ds(pl.multiple_of(turn + 16 * c, 16), 16)
-                block = ref[at * Y + s, :, lanes].reshape(Z // 2, 16, width)
+                block = ref[at * X + s, :, lanes].reshape(Z // 2, 16, width)
                 w_ref[pl.ds(Z // 2 * xh, Z // 2), rows, cols] = block
 
 
@@ -201,10 +201,10 @@
     row_part = jnp.where(xl == 0, halves[:, 0], halves[:, 1]).reshape(128, 512)
     col_part = jnp.where(xl == 0, halves[:, 1], halves[:, 0]).reshape(128, 512)
     part = jnp.concatenate([col_part[:, :PART], row_part, col_part[:, PART:]], axis=1)
-    near = jnp.stack([part, *ring(part, "y", range(Y))])
+    near = jnp.stack([part, *ring(part, ("xl", "xh"), [0, 2, 1, 3])])
 
     def plane(part):
-        return [part, *ring(part, ("xl", "xh"), [0, 2, 1, 3])]
+        return [part, *ring(part, "y", range(Y))]
 
     def both_cores(parts, sizes):
         ends = [sum(sizes[: i + 1]) for i in range(len(sizes))]

time: 157 us -> 151 us (0.962)
  waiting for transfers between devices: 39.8 us -> 34.5 us
  starting transfers between devices: 93.3 us -> 91.3 us
    ppermute x9, waiting for transfers between devices: 25.8 us -> 20.3 us  [ring(): lax.ppermute(part, axes, [(order[i], order[(i - t) % size]) for i in rang...]
    all_to_all x1, starting transfers between devices: 16.3 us -> 13.9 us  [body(): turned = lax.all_to_all(sent, SEQ, split_axis=0, concat_axis=0)]
  transfers between devices with their start and end apart: 19 -> 19, of which waited for: 6 -> 7; matrix products, arithmetic and copies ran while one was open for 2% -> 2% of each run, Pallas kernels for 9% -> 10%
where the time goes in v8:
time: 151 us; the launch traced here: 149 us
  starting transfers between devices  91.3 us (60%)
  waiting for transfers between devices  34.5 us (23%)
  Pallas kernels  15.7 us (10%)
  local copies, waits for them, and re-layouts  5.22 us (3%)
    ppermute x9, starting transfers between devices, ring(): lax.ppermute(part, axes, [(order[i], order[(i - t) % size]) for i in rang...  27.9 us
    ppermute x9, waiting for transfers between devices, ring(): lax.ppermute(part, axes, [(order[i], order[(i - t) % size]) for i in rang...  20.3 us
    all_to_all x1, starting transfers between devices, body(): lax.all_to_all(jnp.broadcast_to(block, (Z, 16, 512)), 'z', split_axis=0,...  19.1 us
    all_to_all x1, starting transfers between devices, body(): lax.all_to_all(col_mid.reshape(64, 4, HALF), SEQ, split_axis=0, concat_ax...  15.8 us
    ppermute x6, starting transfers between devices, both_cores(): return [*joined, *(lax.ppermute(a, 'c', [(0, 1), (1, 0)]) for a in joined)]  14 us
    all_to_all x1, starting transfers between devices, body(): turned = lax.all_to_all(sent, SEQ, split_axis=0, concat_axis=0)  13.9 us
    all_to_all x1, waiting for transfers between devices, body(): lax.all_to_all(jnp.broadcast_to(block, (Z, 16, 512)), 'z', split_axis=0,...  11.8 us
    pallas_call x1, Pallas kernels, row_attention(): pl.pallas_call(row_kernel, out_shape=[jax.ShapeDtypeStruct((STRIDE, FEATU...  7.65 us
  transfers between devices with their start and end apart: 19, of which 7 were waited for; matrix products, arithmetic and copies ran while one was open for 2% of the time, Pallas kernels for 10%

profile of v8, /device:TPU:1, one launch (start us, length us, event | category | flops | bytes accessed | tf_op | source)
XLA Modules:
  0.0 148.9 jit_solution(9443621529806152658)
XLA Ops:
  2.2 19.1 %all-to-all-start = ((bf16[16,16,512]{2,1,0:T(8,128)(2,1)}), bf16[16,16,512]{2,1,0:T(8,128)(2,1)S(1)}, u32[]{:S(2)}, u32[]{:S(2)}) async-start(bf16[16,16,512]{2,1,0:T(8,128)(2,1)} %broadcast_in_dim.7), calls=%async_computation | async-start | bytes 524288 | tf_op jit(solution)/shard_map/all_to_all | solution.py:194
  22.3 11.8 %all-to-all-done = bf16[16,16,512]{2,1,0:T(8,128)(2,1)S(1)} async-done(((bf16[16,16,512]{2,1,0:T(8,128)(2,1)}), bf16[16,16,512]{2,1,0:T(8,128)(2,1)S(1)}, u32[]{:S(2)}, u32[]{:S(2)}) %all-to-all-start) | async-done | bytes 262176 | tf_op jit(solution)/shard_map/all_to_all | solution.py:194
  34.2 4.7 %collective-permute-start.2 = (bf16[128,1024]{1,0:T(8,128)(2,1)S(1)}, bf16[128,1024]{1,0:T(8,128)(2,1)S(1)}, u32[]{:S(2)}, u32[]{:S(2)}) collective-permute-start(bf16[128,1024]{1,0:T(8,128)(2,1)S(1)} %get-tuple-element.26), channel_id=1, source_target_pairs={{0,32},{256,288},{32,0},{288,256},{1,33},{257,289},{33,1},{289,257... | collective-permute-start | bytes 786440 | tf_op jit(solution)/shard_map/ppermute | solution.py:180
  38.9 2.8 %collective-permute-start.1 = (bf16[128,1024]{1,0:T(8,128)(2,1)S(1)}, bf16[128,1024]{1,0:T(8,128)(2,1)S(1)}, u32[]{:S(2)}, u32[]{:S(2)}) collective-permute-start(bf16[128,1024]{1,0:T(8,128)(2,1)S(1)} %get-tuple-element.26), channel_id=1, source_target_pairs={{0,288},{256,0},{32,256},{288,32},{1,289},{257,1},{33,257},{289,33... | collective-permute-start | bytes 786440 | tf_op jit(solution)/shard_map/ppermute | solution.py:180
  41.6 2.5 %collective-permute-start.3 = (bf16[128,1024]{1,0:T(8,128)(2,1)S(1)}, bf16[128,1024]{1,0:T(8,128)(2,1)S(1)}, u32[]{:S(2)}, u32[]{:S(2)}) collective-permute-start(bf16[128,1024]{1,0:T(8,128)(2,1)S(1)} %get-tuple-element.26), channel_id=1, source_target_pairs={{0,256},{256,32},{32,288},{288,0},{1,257},{257,33},{33,289},{289,1... | collective-permute-start | bytes 786440 | tf_op jit(solution)/shard_map/ppermute | solution.py:180
  44.2 13.9 %all-to-all-start.1 = ((bf16[64,4,1024]{2,1,0:T(4,128)(2,1)}), bf16[64,4,1024]{2,1,0:T(4,128)(2,1)}, u32[]{:S(2)}, u32[]{:S(2)}) async-start(bf16[64,4,1024]{2,1,0:T(4,128)(2,1)} %reshape_reshape.3), calls=%async_computation.1 | async-start | bytes 1048576 | tf_op jit(solution)/shard_map/all_to_all | solution.py:197
  58.1 4.6 %collective-permute-start.4 = (bf16[4,128,384]{2,1,0:T(8,128)(2,1)S(1)}, bf16[4,128,384]{2,1,0:T(8,128)(2,1)S(1)}, u32[]{:S(2)}, u32[]{:S(2)}) collective-permute-start(bf16[4,128,384]{2,1,0:T(8,128)(2,1)S(1)} %pad_maximum_fusion.1.refs_0_), channel_id=1, source_target_pairs={{0,192},{64,0},{128,64},{192,128},{1,193},{65,1},{129,65},{193,129... | collective-permute-start | bytes 1179656 | tf_op jit(solution)/shard_map/ppermute | solution.py:180
  62.8 2.3 %collective-permute-start.5 = (bf16[4,128,384]{2,1,0:T(8,128)(2,1)S(1)}, bf16[4,128,384]{2,1,0:T(8,128)(2,1)S(1)}, u32[]{:S(2)}, u32[]{:S(2)}) collective-permute-start(bf16[4,128,384]{2,1,0:T(8,128)(2,1)S(1)} %pad_maximum_fusion.1.refs_0_), channel_id=1, source_target_pairs={{0,128},{64,192},{128,0},{192,64},{1,129},{65,193},{129,1},{193,65... | collective-permute-start | bytes 1179656 | tf_op jit(solution)/shard_map/ppermute | solution.py:180
  65.1 2.6 %collective-permute-start.6 = (bf16[4,128,384]{2,1,0:T(8,128)(2,1)S(1)}, bf16[4,128,384]{2,1,0:T(8,128)(2,1)S(1)}, u32[]{:S(2)}, u32[]{:S(2)}) collective-permute-start(bf16[4,128,384]{2,1,0:T(8,128)(2,1)S(1)} %pad_maximum_fusion.1.refs_0_), channel_id=1, source_target_pairs={{0,64},{64,128},{128,192},{192,0},{1,65},{65,129},{129,193},{193,1... | collective-permute-start | bytes 1179656 | tf_op jit(solution)/shard_map/ppermute | solution.py:180
  67.7 11.3 %collective-permute-done.4 = bf16[4,128,384]{2,1,0:T(8,128)(2,1)S(1)} collective-permute-done((bf16[4,128,384]{2,1,0:T(8,128)(2,1)S(1)}, bf16[4,128,384]{2,1,0:T(8,128)(2,1)S(1)}, u32[]{:S(2)}, u32[]{:S(2)}) %collective-permute-start.4) | collective-permute-done | bytes 393248 | tf_op jit(solution)/shard_map/ppermute | solution.py:180
  79.1 6.6 %collective-permute-done.6 = bf16[4,128,384]{2,1,0:T(8,128)(2,1)S(1)} collective-permute-done((bf16[4,128,384]{2,1,0:T(8,128)(2,1)S(1)}, bf16[4,128,384]{2,1,0:T(8,128)(2,1)S(1)}, u32[]{:S(2)}, u32[]{:S(2)}) %collective-permute-start.6) | collective-permute-done | bytes 393248 | tf_op jit(solution)/shard_map/ppermute | solution.py:180
  85.8 2.3 %collective-permute-start.11 = (bf16[12,128,384]{2,1,0:T(8,128)(2,1)S(1)}, bf16[12,128,384]{2,1,0:T(8,128)(2,1)}, u32[]{:S(2)}, u32[]{:S(2)}) collective-permute-start(bf16[12,128,384]{2,1,0:T(8,128)(2,1)S(1)} %constant_dynamic-update-slice_fusion.refs_1_), channel_id=1, source_target_pairs={{0,1},{1,0},{2,3},{3,2},{4,5},{5,4},{6,7},{7,6},{8,9},{9,8},{10,11... | collective-permute-start | bytes 3538952 | tf_op jit(solution)/shard_map/ppermute | solution.py:215
  88.1 2.0 %collective-permute-start.10 = (bf16[4,128,384]{2,1,0:T(8,128)(2,1)S(1)}, bf16[4,128,384]{2,1,0:T(8,128)(2,1)}, u32[]{:S(2)}, u32[]{:S(2)}) collective-permute-start(bf16[4,128,384]{2,1,0:T(8,128)(2,1)S(1)} %pad_maximum_fusion.1.refs_0_), channel_id=1, source_target_pairs={{0,1},{1,0},{2,3},{3,2},{4,5},{5,4},{6,7},{7,6},{8,9},{9,8},{10,11... | collective-permute-start | bytes 1179656 | tf_op jit(solution)/shard_map/ppermute | solution.py:215
  90.4 1.9 %collective-permute-start.9 = (bf16[4,128,640]{2,1,0:T(8,128)(2,1)S(1)}, bf16[4,128,640]{2,1,0:T(8,128)(2,1)}, u32[]{:S(2)}, u32[]{:S(2)}) collective-permute-start(bf16[4,128,640]{2,1,0:T(8,128)(2,1)S(1)} %slice.30.refs_0_), channel_id=1, source_target_pairs={{0,64},{64,128},{128,192},{192,0},{1,65},{65,129},{129,193},{193,1... | collective-permute-start | bytes 1966088 | tf_op jit(solution)/shard_map/ppermute | solution.py:180
  92.3 3.3 %collective-permute-start.8 = (bf16[4,128,640]{2,1,0:T(8,128)(2,1)S(1)}, bf16[4,128,640]{2,1,0:T(8,128)(2,1)}, u32[]{:S(2)}, u32[]{:S(2)}) collective-permute-start(bf16[4,128,640]{2,1,0:T(8,128)(2,1)S(1)} %slice.30.refs_0_), channel_id=1, source_target_pairs={{0,128},{64,192},{128,0},{192,64},{1,129},{65,193},{129,1},{193,65... | collective-permute-start | bytes 1966088 | tf_op jit(solution)/shard_map/ppermute | solution.py:180
  95.7 3.2 %collective-permute-start.7 = (bf16[4,128,640]{2,1,0:T(8,128)(2,1)S(1)}, bf16[4,128,640]{2,1,0:T(8,128)(2,1)}, u32[]{:S(2)}, u32[]{:S(2)}) collective-permute-start(bf16[4,128,640]{2,1,0:T(8,128)(2,1)S(1)} %slice.30.refs_0_), channel_id=1, source_target_pairs={{0,192},{64,0},{128,64},{192,128},{1,193},{65,1},{129,65},{193,129... | collective-permute-start | bytes 1966088 | tf_op jit(solution)/shard_map/ppermute | solution.py:180
  100.2 6.8 %columns.1 = bf16[256,512]{1,0:T(8,128)(2,1)S(1)} custom-call(s32[3]{0:T(128)S(1)} %pad_add_fusion.place, s32[8]{0:T(128)S(1)} %copy-done.4, f32[1,1024]{1,0:T(1,128)S(1)} %bitcast.18, bf16[256,1024]{1,0:T(8,128)(2,1)S(1)} %reshape.36.x_ref, bf16[4,128,384]{2,1,0:T(8,128)(2,1)S(1)} %pad_maximum_fusion.1.refs_0_, ...), custom_call_target="tpu_custom_call" | custom-call | flops 939524096 | bytes 6291456 | tf_op jit(solution)/shard_map/columns/pallas_call | solution.py:144
  107.7 15.8 %all-to-all-start.2 = ((bf16[64,4,512]{2,1,0:T(4,128)(2,1)}), bf16[64,4,512]{2,1,0:T(4,128)(2,1)S(1)}, u32[]{:S(2)}, u32[]{:S(2)}) async-start(bf16[64,4,512]{2,1,0:T(4,128)(2,1)} %reshape.37), calls=%async_computation.2 | async-start | bytes 524288 | tf_op jit(solution)/shard_map/all_to_all | solution.py:219
  123.6 2.2 %collective-permute-done.7.refs_1_ = bf16[4,128,640]{2,1,0:T(8,128)(2,1)} collective-permute-done((bf16[4,128,640]{2,1,0:T(8,128)(2,1)S(1)}, bf16[4,128,640]{2,1,0:T(8,128)(2,1)}, u32[]{:S(2)}, u32[]{:S(2)}) %collective-permute-start.7) | collective-permute-done | bytes 655392 | tf_op jit(solution)/shard_map/ppermute | solution.py:180
  125.8 3.4 %collective-permute-start.12 = (bf16[4,128,640]{2,1,0:T(8,128)(2,1)S(1)}, bf16[4,128,640]{2,1,0:T(8,128)(2,1)S(1)}, u32[]{:S(2)}, u32[]{:S(2)}) collective-permute-start(bf16[4,128,640]{2,1,0:T(8,128)(2,1)S(1)} %slice.30.refs_0_), channel_id=1, source_target_pairs={{0,1},{1,0},{2,3},{3,2},{4,5},{5,4},{6,7},{7,6},{8,9},{9,8},{10,11... | collective-permute-start | bytes 1966088 | tf_op jit(solution)/shard_map/ppermute | solution.py:215
  129.3 1.9 %collective-permute-start.13 = (bf16[4,128,640]{2,1,0:T(8,128)(2,1)}, bf16[4,128,640]{2,1,0:T(8,128)(2,1)S(1)}, u32[]{:S(2)}, u32[]{:S(2)}) collective-permute-start(bf16[4,128,640]{2,1,0:T(8,128)(2,1)} %collective-permute-done.7.refs_1_), channel_id=1, source_target_pairs={{0,1},{1,0},{2,3},{3,2},{4,5},{5,4},{6,7},{7,6},{8,9},{9,8},{10,11... | collective-permute-start | bytes 1966088 | tf_op jit(solution)/shard_map/ppermute | solution.py:215
  131.2 2.4 %collective-permute-start.14 = (bf16[4,128,640]{2,1,0:T(8,128)(2,1)}, bf16[4,128,640]{2,1,0:T(8,128)(2,1)S(1)}, u32[]{:S(2)}, u32[]{:S(2)}) collective-permute-start(bf16[4,128,640]{2,1,0:T(8,128)(2,1)} %collective-permute-done.8.refs_2_), channel_id=1, source_target_pairs={{0,1},{1,0},{2,3},{3,2},{4,5},{5,4},{6,7},{7,6},{8,9},{9,8},{10,11... | collective-permute-start | bytes 1966088 | tf_op jit(solution)/shard_map/ppermute | solution.py:215
  135.6 2.2 %collective-permute-done.15.refs_7_ = bf16[4,128,640]{2,1,0:T(8,128)(2,1)S(1)} collective-permute-done((bf16[4,128,640]{2,1,0:T(8,128)(2,1)}, bf16[4,128,640]{2,1,0:T(8,128)(2,1)S(1)}, u32[]{:S(2)}, u32[]{:S(2)}) %collective-permute-start.15) | collective-permute-done | bytes 655392 | tf_op jit(solution)/shard_map/ppermute | solution.py:215
  137.8 7.7 %rows.1 = (f32[256,1024]{1,0:T(8,128)S(1)}, bf16[512,1024]{1,0:T(8,128)(2,1)S(1)}, s32[1]{0:T(128)}) custom-call(s32[3]{0:T(128)S(1)} %pad_add_fusion.place, s32[8]{0:T(128)S(1)} %copy-done.5, f32[1,1024]{1,0:T(1,128)S(1)} %bitcast.19, bf16[256,1024]{1,0:T(8,128)(2,1)S(1)} %bitcast.17, bf16[4,128,640]{2,1,0:T(8,128)(2,1)S(1)} %slice.30.refs_0_, ...), custom_call_target="tpu_custom_call" | custom-call | flops 1048576 | bytes 1048576 | tf_op jit(solution)/shard_map/rows/pallas_call | solution.py:157
  (47 shorter events, 10.5 us)
Async XLA Ops:
  0.0 21.3 %copy-start = (bf16[1,1,256,1024]{3,2,1,0:T(8,128)(2,1)S(1)}, bf16[1,1,256,1024]{3,2,1,0:T(8,128)(2,1)}, u32[]{:S(2)}) copy-start(bf16[1,1,256,1024]{3,2,1,0:T(8,128)(2,1)} %param.6) | copy-start | bytes 1572868
  0.8 0.7 collective-permute-start
  2.2 31.9 %all-to-all-start = ((bf16[16,16,512]{2,1,0:T(8,128)(2,1)}), bf16[16,16,512]{2,1,0:T(8,128)(2,1)S(1)}, u32[]{:S(2)}, u32[]{:S(2)}) async-start(bf16[16,16,512]{2,1,0:T(8,128)(2,1)} %broadcast_in_dim.7), calls=%async_computation | async-start | bytes 524288 | tf_op jit(solution)/shard_map/all_to_all | solution.py:194
  34.2 23.9 %collective-permute-start.2 = (bf16[128,1024]{1,0:T(8,128)(2,1)S(1)}, bf16[128,1024]{1,0:T(8,128)(2,1)S(1)}, u32[]{:S(2)}, u32[]{:S(2)}) collective-permute-start(bf16[128,1024]{1,0:T(8,128)(2,1)S(1)} %get-tuple-element.26), channel_id=1, source_target_pairs={{0,32},{256,288},{32,0},{288,256},{1,33},{257,289},{33,1},{289,257... | collective-permute-start | bytes 786440 | tf_op jit(solution)/shard_map/ppermute | solution.py:180
  38.9 19.2 %collective-permute-start.1 = (bf16[128,1024]{1,0:T(8,128)(2,1)S(1)}, bf16[128,1024]{1,0:T(8,128)(2,1)S(1)}, u32[]{:S(2)}, u32[]{:S(2)}) collective-permute-start(bf16[128,1024]{1,0:T(8,128)(2,1)S(1)} %get-tuple-element.26), channel_id=1, source_target_pairs={{0,288},{256,0},{32,256},{288,32},{1,289},{257,1},{33,257},{289,33... | collective-permute-start | bytes 786440 | tf_op jit(solution)/shard_map/ppermute | solution.py:180
  41.6 16.5 %collective-permute-start.3 = (bf16[128,1024]{1,0:T(8,128)(2,1)S(1)}, bf16[128,1024]{1,0:T(8,128)(2,1)S(1)}, u32[]{:S(2)}, u32[]{:S(2)}) collective-permute-start(bf16[128,1024]{1,0:T(8,128)(2,1)S(1)} %get-tuple-element.26), channel_id=1, source_target_pairs={{0,256},{256,32},{32,288},{288,0},{1,257},{257,33},{33,289},{289,1... | collective-permute-start | bytes 786440 | tf_op jit(solution)/shard_map/ppermute | solution.py:180
  44.2 54.8 %all-to-all-start.1 = ((bf16[64,4,1024]{2,1,0:T(4,128)(2,1)}), bf16[64,4,1024]{2,1,0:T(4,128)(2,1)}, u32[]{:S(2)}, u32[]{:S(2)}) async-start(bf16[64,4,1024]{2,1,0:T(4,128)(2,1)} %reshape_reshape.3), calls=%async_computation.1 | async-start | bytes 1048576 | tf_op jit(solution)/shard_map/all_to_all | solution.py:197
  58.1 20.9 %collective-permute-start.4 = (bf16[4,128,384]{2,1,0:T(8,128)(2,1)S(1)}, bf16[4,128,384]{2,1,0:T(8,128)(2,1)S(1)}, u32[]{:S(2)}, u32[]{:S(2)}) collective-permute-start(bf16[4,128,384]{2,1,0:T(8,128)(2,1)S(1)} %pad_maximum_fusion.1.refs_0_), channel_id=1, source_target_pairs={{0,192},{64,0},{128,64},{192,128},{1,193},{65,1},{129,65},{193,129... | collective-permute-start | bytes 1179656 | tf_op jit(solution)/shard_map/ppermute | solution.py:180
  62.8 16.3 %collective-permute-start.5 = (bf16[4,128,384]{2,1,0:T(8,128)(2,1)S(1)}, bf16[4,128,384]{2,1,0:T(8,128)(2,1)S(1)}, u32[]{:S(2)}, u32[]{:S(2)}) collective-permute-start(bf16[4,128,384]{2,1,0:T(8,128)(2,1)S(1)} %pad_maximum_fusion.1.refs_0_), channel_id=1, source_target_pairs={{0,128},{64,192},{128,0},{192,64},{1,129},{65,193},{129,1},{193,65... | collective-permute-start | bytes 1179656 | tf_op jit(solution)/shard_map/ppermute | solution.py:180
  65.1 20.7 %collective-permute-start.6 = (bf16[4,128,384]{2,1,0:T(8,128)(2,1)S(1)}, bf16[4,128,384]{2,1,0:T(8,128)(2,1)S(1)}, u32[]{:S(2)}, u32[]{:S(2)}) collective-permute-start(bf16[4,128,384]{2,1,0:T(8,128)(2,1)S(1)} %pad_maximum_fusion.1.refs_0_), channel_id=1, source_target_pairs={{0,64},{64,128},{128,192},{192,0},{1,65},{65,129},{129,193},{193,1... | collective-permute-start | bytes 1179656 | tf_op jit(solution)/shard_map/ppermute | solution.py:180
  85.8 14.3 %collective-permute-start.11 = (bf16[12,128,384]{2,1,0:T(8,128)(2,1)S(1)}, bf16[12,128,384]{2,1,0:T(8,128)(2,1)}, u32[]{:S(2)}, u32[]{:S(2)}) collective-permute-start(bf16[12,128,384]{2,1,0:T(8,128)(2,1)S(1)} %constant_dynamic-update-slice_fusion.refs_1_), channel_id=1, source_target_pairs={{0,1},{1,0},{2,3},{3,2},{4,5},{5,4},{6,7},{7,6},{8,9},{9,8},{10,11... | collective-permute-start | bytes 3538952 | tf_op jit(solution)/shard_map/ppermute | solution.py:215
  88.1 12.0 %collective-permute-start.10 = (bf16[4,128,384]{2,1,0:T(8,128)(2,1)S(1)}, bf16[4,128,384]{2,1,0:T(8,128)(2,1)}, u32[]{:S(2)}, u32[]{:S(2)}) collective-permute-start(bf16[4,128,384]{2,1,0:T(8,128)(2,1)S(1)} %pad_maximum_fusion.1.refs_0_), channel_id=1, source_target_pairs={{0,1},{1,0},{2,3},{3,2},{4,5},{5,4},{6,7},{7,6},{8,9},{9,8},{10,11... | collective-permute-start | bytes 1179656 | tf_op jit(solution)/shard_map/ppermute | solution.py:215
  90.3 9.8 %copy-start.3 = (f32[1024]{0:T(1024)S(1)}, f32[1024]{0:T(1024)}, u32[]{:S(2)}) copy-start(f32[1024]{0:T(1024)} %param.7) | copy-start | bytes 12292
  90.3 9.8 %copy-start.4 = (s32[8]{0:T(128)S(1)}, s32[8]{0:T(128)}, u32[]{:S(2)}) copy-start(s32[8]{0:T(128)} %reach_ref.2) | copy-start | bytes 100
  90.4 33.2 %collective-permute-start.9 = (bf16[4,128,640]{2,1,0:T(8,128)(2,1)S(1)}, bf16[4,128,640]{2,1,0:T(8,128)(2,1)}, u32[]{:S(2)}, u32[]{:S(2)}) collective-permute-start(bf16[4,128,640]{2,1,0:T(8,128)(2,1)S(1)} %slice.30.refs_0_), channel_id=1, source_target_pairs={{0,64},{64,128},{128,192},{192,0},{1,65},{65,129},{129,193},{193,1... | collective-permute-start | bytes 1966088 | tf_op jit(solution)/shard_map/ppermute | solution.py:180
  92.3 31.3 %collective-permute-start.8 = (bf16[4,128,640]{2,1,0:T(8,128)(2,1)S(1)}, bf16[4,128,640]{2,1,0:T(8,128)(2,1)}, u32[]{:S(2)}, u32[]{:S(2)}) collective-permute-start(bf16[4,128,640]{2,1,0:T(8,128)(2,1)S(1)} %slice.30.refs_0_), channel_id=1, source_target_pairs={{0,128},{64,192},{128,0},{192,64},{1,129},{65,193},{129,1},{193,65... | collective-permute-start | bytes 1966088 | tf_op jit(solution)/shard_map/ppermute | solution.py:180
  95.7 30.2 %collective-permute-start.7 = (bf16[4,128,640]{2,1,0:T(8,128)(2,1)S(1)}, bf16[4,128,640]{2,1,0:T(8,128)(2,1)}, u32[]{:S(2)}, u32[]{:S(2)}) collective-permute-start(bf16[4,128,640]{2,1,0:T(8,128)(2,1)S(1)} %slice.30.refs_0_), channel_id=1, source_target_pairs={{0,192},{64,0},{128,64},{192,128},{1,193},{65,1},{129,65},{193,129... | collective-permute-start | bytes 1966088 | tf_op jit(solution)/shard_map/ppermute | solution.py:180
  100.2 37.7 %copy-start.5 = (s32[8]{0:T(128)S(1)}, s32[8]{0:T(128)}, u32[]{:S(2)}) copy-start(s32[8]{0:T(128)} %reach_ref.3) | copy-start | bytes 100
  107.7 39.5 %all-to-all-start.2 = ((bf16[64,4,512]{2,1,0:T(4,128)(2,1)}), bf16[64,4,512]{2,1,0:T(4,128)(2,1)S(1)}, u32[]{:S(2)}, u32[]{:S(2)}) async-start(bf16[64,4,512]{2,1,0:T(4,128)(2,1)} %reshape.37), calls=%async_computation.2 | async-start | bytes 524288 | tf_op jit(solution)/shard_map/all_to_all | solution.py:219
  125.8 9.7 %collective-permute-start.12 = (bf16[4,128,640]{2,1,0:T(8,128)(2,1)S(1)}, bf16[4,128,640]{2,1,0:T(8,128)(2,1)S(1)}, u32[]{:S(2)}, u32[]{:S(2)}) collective-permute-start(bf16[4,128,640]{2,1,0:T(8,128)(2,1)S(1)} %slice.30.refs_0_), channel_id=1, source_target_pairs={{0,1},{1,0},{2,3},{3,2},{4,5},{5,4},{6,7},{7,6},{8,9},{9,8},{10,11... | collective-permute-start | bytes 1966088 | tf_op jit(solution)/shard_map/ppermute | solution.py:215
  129.3 6.3 %collective-permute-start.13 = (bf16[4,128,640]{2,1,0:T(8,128)(2,1)}, bf16[4,128,640]{2,1,0:T(8,128)(2,1)S(1)}, u32[]{:S(2)}, u32[]{:S(2)}) collective-permute-start(bf16[4,128,640]{2,1,0:T(8,128)(2,1)} %collective-permute-done.7.refs_1_), channel_id=1, source_target_pairs={{0,1},{1,0},{2,3},{3,2},{4,5},{5,4},{6,7},{7,6},{8,9},{9,8},{10,11... | collective-permute-start | bytes 1966088 | tf_op jit(solution)/shard_map/ppermute | solution.py:215
  131.2 4.4 %collective-permute-start.14 = (bf16[4,128,640]{2,1,0:T(8,128)(2,1)}, bf16[4,128,640]{2,1,0:T(8,128)(2,1)S(1)}, u32[]{:S(2)}, u32[]{:S(2)}) collective-permute-start(bf16[4,128,640]{2,1,0:T(8,128)(2,1)} %collective-permute-done.8.refs_2_), channel_id=1, source_target_pairs={{0,1},{1,0},{2,3},{3,2},{4,5},{5,4},{6,7},{7,6},{8,9},{9,8},{10,11... | collective-permute-start | bytes 1966088 | tf_op jit(solution)/shard_map/ppermute | solution.py:215
  133.6 4.2 %collective-permute-start.15 = (bf16[4,128,640]{2,1,0:T(8,128)(2,1)}, bf16[4,128,640]{2,1,0:T(8,128)(2,1)S(1)}, u32[]{:S(2)}, u32[]{:S(2)}) collective-permute-start(bf16[4,128,640]{2,1,0:T(8,128)(2,1)} %collective-permute-done.9.refs_3_), channel_id=1, source_target_pairs={{0,1},{1,0},{2,3},{3,2},{4,5},{5,4},{6,7},{7,6},{8,9},{9,8},{10,11... | collective-permute-start | bytes 1966088 | tf_op jit(solution)/shard_map/ppermute | solution.py:215
  146.5 1.2 copy-start.2
  (1 other events, 1.0 us)

commit v9 on v8

--- a/solution.py
+++ b/solution.py
@@ -46,42 +46,37 @@
 
     lax.fori_loop(0, STRIDE // 64, norm, 0)
 
-    def project(i, _):
-        cols = pl.ds(pl.multiple_of(i * 256, 256), 256)
-        qkv_ref[:, cols] = jnp.dot(
+    for n in range(0, WIDTH, 512):
+        qkv_ref[:, n : n + 512] = jnp.dot(
             n_ref[...],
-            w_ref[:, :, cols].reshape(FEATURES, 256),
+            w_ref[:, :, n : n + 512].reshape(FEATURES, 512),
             preferred_element_type=jnp.float32,
         ).astype(jnp.bfloat16)
-        return 0
-
-    lax.fori_loop(0, WIDTH // 256, project, 0)
-
-    lane = lax.broadcasted_iota(jnp.int32, (STRIDE, 128), 1)
+
+    lane = lax.broadcasted_iota(jnp.int32, (STRIDE // 2, 128), 1)
     low = (lane < 64).astype(jnp.float32)
     masks = [low.astype(jnp.bfloat16), (1.0 - low).astype(jnp.bfloat16)]
     scale = 0.125 * math.log2(math.e)
     mid = STRIDE // 2
     for h in range(0, HEADS, 2):
-        q, k, v = (qkv_ref[:, n * HALF + h * 64 : n * HALF + h * 64 + 128] for n in range(3))
-        done = []
-        for e in range(2):
-            reach = reach_ref[h + e]
-            qe = q * masks[e]
-            ve = v * masks[e] + masks[1 - e]
-            for first, seen in ((0, mid), (mid, STRIDE)):
-                s = lax.dot_general(
-                    qe[first : first + mid],
-                    k[:seen],
-                    (((1,), (1,)), ((), ())),
-                    preferred_element_type=jnp.float32,
-                )
-                s = jnp.where(dist[first : first + mid, :seen] < reach, s * scale, -1e30)
-                p = jnp.exp2(s - jnp.max(s, axis=-1, keepdims=True)).astype(jnp.bfloat16)
-                o = jnp.dot(p, ve[:seen], preferred_element_type=jnp.float32)
-                done.append(o / pltpu.roll(o, 64, 1))
-        for i, first in enumerate((0, mid)):
-            both = jnp.where(lane[:mid] < 64, done[i], done[2 + i])
+        for first, seen in ((0, mid), (mid, STRIDE)):
+            q, k, v = (qkv_ref[:, n * HALF + h * 64 : n * HALF + h * 64 + 128] for n in range(3))
+            q = q[first : first + mid]
+            s = lax.dot_general(
+                jnp.concatenate([q * masks[0], q * masks[1]]),
+                k[:seen],
+                (((1,), (1,)), ((), ())),
+                preferred_element_type=jnp.float32,
+            )
+            near = dist[first : first + mid, :seen]
+            ps, sums = [], []
+            for e in range(2):
+                se = jnp.where(near < reach_ref[h + e], s[e * mid : e * mid + mid] * scale, -1e30)
+                p = jnp.exp2(se - jnp.max(se, axis=-1, keepdims=True))
+                sums.append(jnp.sum(p, axis=-1, keepdims=True))
+                ps.append(p.astype(jnp.bfloat16))
+            o = jnp.dot(jnp.concatenate(ps), v[:seen], preferred_element_type=jnp.float32)
+            both = jnp.where(lane < 64, o[:mid] / sums[0], o[mid:] / sums[1])
             out_ref[first : first + mid, h * 64 : h * 64 + 128] = both.astype(jnp.bfloat16)
 
 
@@ -218,7 +213,7 @@
     col_mid = column_attention(place, col_rows, gain, turned, both_cores(col_plane, COLUMN_PIECES))
     col_out = lax.all_to_all(col_mid.reshape(64, 4, HALF), SEQ, split_axis=0, concat_axis=0)
 
-    near_rest, _ = lax.optimization_barrier((near[:, :, PART:], col_plane))
+    near_rest, _ = lax.optimization_barrier((near[:, :, PART:], col_plane[1]))
     rest, _ = lax.optimization_barrier((plane(near_rest), col_mid))
     base, low, last = row_attention(place, row_blocks, gain, rows, both_cores(rest, REST_PIECES))
     col_out = jnp.where(last[0] == 0, col_out, 0).reshape(STRIDE, HALF)

time: 151 us -> 148 us (0.980)
  Pallas kernels: 15.7 us -> 10.1 us
  waiting for transfers between devices: 34.5 us -> 37.2 us
    pallas_call x1, Pallas kernels: 6.78 us -> 3.96 us  [column_attention(): pl.pallas_call(column_kernel, out_shape=jax.ShapeDtypeStruct((STRIDE, HAL...]
    ppermute x9, waiting for transfers between devices: 20.3 us -> 23.1 us  [ring(): lax.ppermute(part, axes, [(order[i], order[(i - t) % size]) for i in rang...]
    pallas_call x1, Pallas kernels: 7.65 us -> 4.93 us  [row_attention(): pl.pallas_call(row_kernel, out_shape=[jax.ShapeDtypeStruct((STRIDE, FEATU...]
  transfers between devices with their start and end apart: 19 -> 19, of which waited for: 7 -> 6; matrix products, arithmetic and copies ran while one was open for 2% -> 2% of each run, Pallas kernels for 10% -> 6%
where the time goes in v9:
time: 148 us; the launch traced here: 146 us
  starting transfers between devices  91.3 us (62%)
  waiting for transfers between devices  37.2 us (25%)
  Pallas kernels  10.1 us (7%)
  local copies, waits for them, and re-layouts  5.32 us (4%)
    ppermute x9, starting transfers between devices, ring(): lax.ppermute(part, axes, [(order[i], order[(i - t) % size]) for i in rang...  27.9 us
    ppermute x9, waiting for transfers between devices, ring(): lax.ppermute(part, axes, [(order[i], order[(i - t) % size]) for i in rang...  23.1 us
    all_to_all x1, starting transfers between devices, body(): lax.all_to_all(jnp.broadcast_to(block, (Z, 16, 512)), 'z', split_axis=0,...  19.1 us
    all_to_all x1, starting transfers between devices, body(): lax.all_to_all(col_mid.reshape(64, 4, HALF), SEQ, split_axis=0, concat_ax...  15.8 us
    ppermute x6, starting transfers between devices, both_cores(): return [*joined, *(lax.ppermute(a, 'c', [(0, 1), (1, 0)]) for a in joined)]  14 us
    all_to_all x1, starting transfers between devices, body(): turned = lax.all_to_all(sent, SEQ, split_axis=0, concat_axis=0)  13.9 us
    all_to_all x1, waiting for transfers between devices, body(): lax.all_to_all(jnp.broadcast_to(block, (Z, 16, 512)), 'z', split_axis=0,...  11.8 us
    pallas_call x1, Pallas kernels, row_attention(): pl.pallas_call(row_kernel, out_shape=[jax.ShapeDtypeStruct((STRIDE, FEATU...  4.93 us
  transfers between devices with their start and end apart: 19, of which 6 were waited for; matrix products, arithmetic and copies ran while one was open for 2% of the time, Pallas kernels for 6%

profile of v9, /device:TPU:1, one launch (start us, length us, event | category | flops | bytes accessed | tf_op | source)
XLA Modules:
  0.0 146.2 jit_solution(9388354235757505913)
XLA Ops:
  2.2 19.1 %all-to-all-start = ((bf16[16,16,512]{2,1,0:T(8,128)(2,1)}), bf16[16,16,512]{2,1,0:T(8,128)(2,1)S(1)}, u32[]{:S(2)}, u32[]{:S(2)}) async-start(bf16[16,16,512]{2,1,0:T(8,128)(2,1)} %broadcast_in_dim.7), calls=%async_computation | async-start | bytes 524288 | tf_op jit(solution)/shard_map/all_to_all | solution.py:189
  22.3 11.8 %all-to-all-done = bf16[16,16,512]{2,1,0:T(8,128)(2,1)S(1)} async-done(((bf16[16,16,512]{2,1,0:T(8,128)(2,1)}), bf16[16,16,512]{2,1,0:T(8,128)(2,1)S(1)}, u32[]{:S(2)}, u32[]{:S(2)}) %all-to-all-start) | async-done | bytes 262176 | tf_op jit(solution)/shard_map/all_to_all | solution.py:189
  34.2 4.7 %collective-permute-start.2 = (bf16[128,1024]{1,0:T(8,128)(2,1)S(1)}, bf16[128,1024]{1,0:T(8,128)(2,1)S(1)}, u32[]{:S(2)}, u32[]{:S(2)}) collective-permute-start(bf16[128,1024]{1,0:T(8,128)(2,1)S(1)} %get-tuple-element.26), channel_id=1, source_target_pairs={{0,32},{256,288},{32,0},{288,256},{1,33},{257,289},{33,1},{289,257... | collective-permute-start | bytes 786440 | tf_op jit(solution)/shard_map/ppermute | solution.py:175
  38.9 2.8 %collective-permute-start.1 = (bf16[128,1024]{1,0:T(8,128)(2,1)S(1)}, bf16[128,1024]{1,0:T(8,128)(2,1)S(1)}, u32[]{:S(2)}, u32[]{:S(2)}) collective-permute-start(bf16[128,1024]{1,0:T(8,128)(2,1)S(1)} %get-tuple-element.26), channel_id=1, source_target_pairs={{0,288},{256,0},{32,256},{288,32},{1,289},{257,1},{33,257},{289,33... | collective-permute-start | bytes 786440 | tf_op jit(solution)/shard_map/ppermute | solution.py:175
  41.6 2.5 %collective-permute-start.3 = (bf16[128,1024]{1,0:T(8,128)(2,1)S(1)}, bf16[128,1024]{1,0:T(8,128)(2,1)S(1)}, u32[]{:S(2)}, u32[]{:S(2)}) collective-permute-start(bf16[128,1024]{1,0:T(8,128)(2,1)S(1)} %get-tuple-element.26), channel_id=1, source_target_pairs={{0,256},{256,32},{32,288},{288,0},{1,257},{257,33},{33,289},{289,1... | collective-permute-start | bytes 786440 | tf_op jit(solution)/shard_map/ppermute | solution.py:175
  44.2 13.9 %all-to-all-start.1 = ((bf16[64,4,1024]{2,1,0:T(4,128)(2,1)}), bf16[64,4,1024]{2,1,0:T(4,128)(2,1)}, u32[]{:S(2)}, u32[]{:S(2)}) async-start(bf16[64,4,1024]{2,1,0:T(4,128)(2,1)} %reshape_reshape.3), calls=%async_computation.1 | async-start | bytes 1048576 | tf_op jit(solution)/shard_map/all_to_all | solution.py:192
  58.1 4.6 %collective-permute-start.4 = (bf16[4,128,384]{2,1,0:T(8,128)(2,1)S(1)}, bf16[4,128,384]{2,1,0:T(8,128)(2,1)S(1)}, u32[]{:S(2)}, u32[]{:S(2)}) collective-permute-start(bf16[4,128,384]{2,1,0:T(8,128)(2,1)S(1)} %pad_maximum_fusion.1.refs_0_), channel_id=1, source_target_pairs={{0,192},{64,0},{128,64},{192,128},{1,193},{65,1},{129,65},{193,129... | collective-permute-start | bytes 1179656 | tf_op jit(solution)/shard_map/ppermute | solution.py:175
  62.8 2.3 %collective-permute-start.8 = (bf16[4,128,384]{2,1,0:T(8,128)(2,1)S(1)}, bf16[4,128,384]{2,1,0:T(8,128)(2,1)S(1)}, u32[]{:S(2)}, u32[]{:S(2)}) collective-permute-start(bf16[4,128,384]{2,1,0:T(8,128)(2,1)S(1)} %pad_maximum_fusion.1.refs_0_), channel_id=1, source_target_pairs={{0,128},{64,192},{128,0},{192,64},{1,129},{65,193},{129,1},{193,65... | collective-permute-start | bytes 1179656 | tf_op jit(solution)/shard_map/ppermute | solution.py:175
  65.1 2.6 %collective-permute-start.9 = (bf16[4,128,384]{2,1,0:T(8,128)(2,1)S(1)}, bf16[4,128,384]{2,1,0:T(8,128)(2,1)S(1)}, u32[]{:S(2)}, u32[]{:S(2)}) collective-permute-start(bf16[4,128,384]{2,1,0:T(8,128)(2,1)S(1)} %pad_maximum_fusion.1.refs_0_), channel_id=1, source_target_pairs={{0,64},{64,128},{128,192},{192,0},{1,65},{65,129},{129,193},{193,1... | collective-permute-start | bytes 1179656 | tf_op jit(solution)/shard_map/ppermute | solution.py:175
  67.7 11.3 %collective-permute-done.4 = bf16[4,128,384]{2,1,0:T(8,128)(2,1)S(1)} collective-permute-done((bf16[4,128,384]{2,1,0:T(8,128)(2,1)S(1)}, bf16[4,128,384]{2,1,0:T(8,128)(2,1)S(1)}, u32[]{:S(2)}, u32[]{:S(2)}) %collective-permute-start.4) | collective-permute-done | bytes 393248 | tf_op jit(solution)/shard_map/ppermute | solution.py:175
  79.1 6.6 %collective-permute-done.9 = bf16[4,128,384]{2,1,0:T(8,128)(2,1)S(1)} collective-permute-done((bf16[4,128,384]{2,1,0:T(8,128)(2,1)S(1)}, bf16[4,128,384]{2,1,0:T(8,128)(2,1)S(1)}, u32[]{:S(2)}, u32[]{:S(2)}) %collective-permute-start.9) | collective-permute-done | bytes 393248 | tf_op jit(solution)/shard_map/ppermute | solution.py:175
  85.8 2.3 %collective-permute-start.11 = (bf16[12,128,384]{2,1,0:T(8,128)(2,1)S(1)}, bf16[12,128,384]{2,1,0:T(8,128)(2,1)}, u32[]{:S(2)}, u32[]{:S(2)}) collective-permute-start(bf16[12,128,384]{2,1,0:T(8,128)(2,1)S(1)} %constant_dynamic-update-slice_fusion.refs_1_), channel_id=1, source_target_pairs={{0,1},{1,0},{2,3},{3,2},{4,5},{5,4},{6,7},{7,6},{8,9},{9,8},{10,11... | collective-permute-start | bytes 3538952 | tf_op jit(solution)/shard_map/ppermute | solution.py:210
  88.1 2.0 %collective-permute-start.10 = (bf16[4,128,384]{2,1,0:T(8,128)(2,1)S(1)}, bf16[4,128,384]{2,1,0:T(8,128)(2,1)}, u32[]{:S(2)}, u32[]{:S(2)}) collective-permute-start(bf16[4,128,384]{2,1,0:T(8,128)(2,1)S(1)} %pad_maximum_fusion.1.refs_0_), channel_id=1, source_target_pairs={{0,1},{1,0},{2,3},{3,2},{4,5},{5,4},{6,7},{7,6},{8,9},{9,8},{10,11... | collective-permute-start | bytes 1179656 | tf_op jit(solution)/shard_map/ppermute | solution.py:210
  90.4 1.9 %collective-permute-start.7 = (bf16[4,128,640]{2,1,0:T(8,128)(2,1)S(1)}, bf16[4,128,640]{2,1,0:T(8,128)(2,1)}, u32[]{:S(2)}, u32[]{:S(2)}) collective-permute-start(bf16[4,128,640]{2,1,0:T(8,128)(2,1)S(1)} %slice.30.refs_0_), channel_id=1, source_target_pairs={{0,64},{64,128},{128,192},{192,0},{1,65},{65,129},{129,193},{193,1... | collective-permute-start | bytes 1966088 | tf_op jit(solution)/shard_map/ppermute | solution.py:175
  92.3 3.3 %collective-permute-start.6 = (bf16[4,128,640]{2,1,0:T(8,128)(2,1)S(1)}, bf16[4,128,640]{2,1,0:T(8,128)(2,1)}, u32[]{:S(2)}, u32[]{:S(2)}) collective-permute-start(bf16[4,128,640]{2,1,0:T(8,128)(2,1)S(1)} %slice.30.refs_0_), channel_id=1, source_target_pairs={{0,128},{64,192},{128,0},{192,64},{1,129},{65,193},{129,1},{193,65... | collective-permute-start | bytes 1966088 | tf_op jit(solution)/shard_map/ppermute | solution.py:175
  95.7 3.2 %collective-permute-start.5 = (bf16[4,128,640]{2,1,0:T(8,128)(2,1)S(1)}, bf16[4,128,640]{2,1,0:T(8,128)(2,1)}, u32[]{:S(2)}, u32[]{:S(2)}) collective-permute-start(bf16[4,128,640]{2,1,0:T(8,128)(2,1)S(1)} %slice.30.refs_0_), channel_id=1, source_target_pairs={{0,192},{64,0},{128,64},{192,128},{1,193},{65,1},{129,65},{193,129... | collective-permute-start | bytes 1966088 | tf_op jit(solution)/shard_map/ppermute | solution.py:175
  100.2 4.0 %columns.1 = bf16[256,512]{1,0:T(8,128)(2,1)S(1)} custom-call(s32[3]{0:T(128)S(1)} %pad_add_fusion.place, s32[8]{0:T(128)S(1)} %copy-done.4, f32[1,1024]{1,0:T(1,128)S(1)} %bitcast.18, bf16[256,1024]{1,0:T(8,128)(2,1)S(1)} %reshape.36.x_ref, bf16[4,128,384]{2,1,0:T(8,128)(2,1)S(1)} %pad_maximum_fusion.1.refs_0_, ...), custom_call_target="tpu_custom_call" | custom-call | flops 939524096 | bytes 6291456 | tf_op jit(solution)/shard_map/columns/pallas_call | solution.py:139
  104.9 15.8 %all-to-all-start.2 = ((bf16[64,4,512]{2,1,0:T(4,128)(2,1)}), bf16[64,4,512]{2,1,0:T(4,128)(2,1)S(1)}, u32[]{:S(2)}, u32[]{:S(2)}) async-start(bf16[64,4,512]{2,1,0:T(4,128)(2,1)} %reshape.37), calls=%async_computation.2 | async-start | bytes 524288 | tf_op jit(solution)/shard_map/all_to_all | solution.py:214
  120.7 2.9 %collective-permute-done.7.refs_3_ = bf16[4,128,640]{2,1,0:T(8,128)(2,1)} collective-permute-done((bf16[4,128,640]{2,1,0:T(8,128)(2,1)S(1)}, bf16[4,128,640]{2,1,0:T(8,128)(2,1)}, u32[]{:S(2)}, u32[]{:S(2)}) %collective-permute-start.7) | collective-permute-done | bytes 655392 | tf_op jit(solution)/shard_map/ppermute | solution.py:175
  123.6 2.2 %collective-permute-done.5.refs_1_ = bf16[4,128,640]{2,1,0:T(8,128)(2,1)} collective-permute-done((bf16[4,128,640]{2,1,0:T(8,128)(2,1)S(1)}, bf16[4,128,640]{2,1,0:T(8,128)(2,1)}, u32[]{:S(2)}, u32[]{:S(2)}) %collective-permute-start.5) | collective-permute-done | bytes 655392 | tf_op jit(solution)/shard_map/ppermute | solution.py:175
  125.8 3.4 %collective-permute-start.12 = (bf16[4,128,640]{2,1,0:T(8,128)(2,1)S(1)}, bf16[4,128,640]{2,1,0:T(8,128)(2,1)S(1)}, u32[]{:S(2)}, u32[]{:S(2)}) collective-permute-start(bf16[4,128,640]{2,1,0:T(8,128)(2,1)S(1)} %slice.30.refs_0_), channel_id=1, source_target_pairs={{0,1},{1,0},{2,3},{3,2},{4,5},{5,4},{6,7},{7,6},{8,9},{9,8},{10,11... | collective-permute-start | bytes 1966088 | tf_op jit(solution)/shard_map/ppermute | solution.py:210
  131.2 2.4 %collective-permute-start.14 = (bf16[4,128,640]{2,1,0:T(8,128)(2,1)}, bf16[4,128,640]{2,1,0:T(8,128)(2,1)S(1)}, u32[]{:S(2)}, u32[]{:S(2)}) collective-permute-start(bf16[4,128,640]{2,1,0:T(8,128)(2,1)} %collective-permute-done.6.refs_2_), channel_id=1, source_target_pairs={{0,1},{1,0},{2,3},{3,2},{4,5},{5,4},{6,7},{7,6},{8,9},{9,8},{10,11... | collective-permute-start | bytes 1966088 | tf_op jit(solution)/shard_map/ppermute | solution.py:210
  135.6 2.2 %collective-permute-done.15.refs_7_ = bf16[4,128,640]{2,1,0:T(8,128)(2,1)S(1)} collective-permute-done((bf16[4,128,640]{2,1,0:T(8,128)(2,1)}, bf16[4,128,640]{2,1,0:T(8,128)(2,1)S(1)}, u32[]{:S(2)}, u32[]{:S(2)}) %collective-permute-start.15) | collective-permute-done | bytes 655392 | tf_op jit(solution)/shard_map/ppermute | solution.py:210
  137.8 4.9 %rows.1 = (f32[256,1024]{1,0:T(8,128)S(1)}, bf16[512,1024]{1,0:T(8,128)(2,1)S(1)}, s32[1]{0:T(128)}) custom-call(s32[3]{0:T(128)S(1)} %pad_add_fusion.place, s32[8]{0:T(128)S(1)} %copy-done.5, f32[1,1024]{1,0:T(1,128)S(1)} %bitcast.19, bf16[256,1024]{1,0:T(8,128)(2,1)S(1)} %bitcast.17, bf16[4,128,640]{2,1,0:T(8,128)(2,1)S(1)} %slice.30.refs_0_, ...), custom_call_target="tpu_custom_call" | custom-call | flops 1048576 | bytes 1048576 | tf_op jit(solution)/shard_map/rows/pallas_call | solution.py:152
  (47 shorter events, 12.3 us)
Async XLA Ops:
  0.0 21.3 %copy-start = (bf16[1,1,256,1024]{3,2,1,0:T(8,128)(2,1)S(1)}, bf16[1,1,256,1024]{3,2,1,0:T(8,128)(2,1)}, u32[]{:S(2)}) copy-start(bf16[1,1,256,1024]{3,2,1,0:T(8,128)(2,1)} %param.6) | copy-start | bytes 1572868
  0.8 0.7 collective-permute-start
  2.2 31.9 %all-to-all-start = ((bf16[16,16,512]{2,1,0:T(8,128)(2,1)}), bf16[16,16,512]{2,1,0:T(8,128)(2,1)S(1)}, u32[]{:S(2)}, u32[]{:S(2)}) async-start(bf16[16,16,512]{2,1,0:T(8,128)(2,1)} %broadcast_in_dim.7), calls=%async_computation | async-start | bytes 524288 | tf_op jit(solution)/shard_map/all_to_all | solution.py:189
  34.2 23.9 %collective-permute-start.2 = (bf16[128,1024]{1,0:T(8,128)(2,1)S(1)}, bf16[128,1024]{1,0:T(8,128)(2,1)S(1)}, u32[]{:S(2)}, u32[]{:S(2)}) collective-permute-start(bf16[128,1024]{1,0:T(8,128)(2,1)S(1)} %get-tuple-element.26), channel_id=1, source_target_pairs={{0,32},{256,288},{32,0},{288,256},{1,33},{257,289},{33,1},{289,257... | collective-permute-start | bytes 786440 | tf_op jit(solution)/shard_map/ppermute | solution.py:175
  38.9 19.2 %collective-permute-start.1 = (bf16[128,1024]{1,0:T(8,128)(2,1)S(1)}, bf16[128,1024]{1,0:T(8,128)(2,1)S(1)}, u32[]{:S(2)}, u32[]{:S(2)}) collective-permute-start(bf16[128,1024]{1,0:T(8,128)(2,1)S(1)} %get-tuple-element.26), channel_id=1, source_target_pairs={{0,288},{256,0},{32,256},{288,32},{1,289},{257,1},{33,257},{289,33... | collective-permute-start | bytes 786440 | tf_op jit(solution)/shard_map/ppermute | solution.py:175
  41.6 16.5 %collective-permute-start.3 = (bf16[128,1024]{1,0:T(8,128)(2,1)S(1)}, bf16[128,1024]{1,0:T(8,128)(2,1)S(1)}, u32[]{:S(2)}, u32[]{:S(2)}) collective-permute-start(bf16[128,1024]{1,0:T(8,128)(2,1)S(1)} %get-tuple-element.26), channel_id=1, source_target_pairs={{0,256},{256,32},{32,288},{288,0},{1,257},{257,33},{33,289},{289,1... | collective-permute-start | bytes 786440 | tf_op jit(solution)/shard_map/ppermute | solution.py:175
  44.2 54.8 %all-to-all-start.1 = ((bf16[64,4,1024]{2,1,0:T(4,128)(2,1)}), bf16[64,4,1024]{2,1,0:T(4,128)(2,1)}, u32[]{:S(2)}, u32[]{:S(2)}) async-start(bf16[64,4,1024]{2,1,0:T(4,128)(2,1)} %reshape_reshape.3), calls=%async_computation.1 | async-start | bytes 1048576 | tf_op jit(solution)/shard_map/all_to_all | solution.py:192
  58.1 20.9 %collective-permute-start.4 = (bf16[4,128,384]{2,1,0:T(8,128)(2,1)S(1)}, bf16[4,128,384]{2,1,0:T(8,128)(2,1)S(1)}, u32[]{:S(2)}, u32[]{:S(2)}) collective-permute-start(bf16[4,128,384]{2,1,0:T(8,128)(2,1)S(1)} %pad_maximum_fusion.1.refs_0_), channel_id=1, source_target_pairs={{0,192},{64,0},{128,64},{192,128},{1,193},{65,1},{129,65},{193,129... | collective-permute-start | bytes 1179656 | tf_op jit(solution)/shard_map/ppermute | solution.py:175
  62.8 16.3 %collective-permute-start.8 = (bf16[4,128,384]{2,1,0:T(8,128)(2,1)S(1)}, bf16[4,128,384]{2,1,0:T(8,128)(2,1)S(1)}, u32[]{:S(2)}, u32[]{:S(2)}) collective-permute-start(bf16[4,128,384]{2,1,0:T(8,128)(2,1)S(1)} %pad_maximum_fusion.1.refs_0_), channel_id=1, source_target_pairs={{0,128},{64,192},{128,0},{192,64},{1,129},{65,193},{129,1},{193,65... | collective-permute-start | bytes 1179656 | tf_op jit(solution)/shard_map/ppermute | solution.py:175
  65.1 20.7 %collective-permute-start.9 = (bf16[4,128,384]{2,1,0:T(8,128)(2,1)S(1)}, bf16[4,128,384]{2,1,0:T(8,128)(2,1)S(1)}, u32[]{:S(2)}, u32[]{:S(2)}) collective-permute-start(bf16[4,128,384]{2,1,0:T(8,128)(2,1)S(1)} %pad_maximum_fusion.1.refs_0_), channel_id=1, source_target_pairs={{0,64},{64,128},{128,192},{192,0},{1,65},{65,129},{129,193},{193,1... | collective-permute-start | bytes 1179656 | tf_op jit(solution)/shard_map/ppermute | solution.py:175
  85.8 14.3 %collective-permute-start.11 = (bf16[12,128,384]{2,1,0:T(8,128)(2,1)S(1)}, bf16[12,128,384]{2,1,0:T(8,128)(2,1)}, u32[]{:S(2)}, u32[]{:S(2)}) collective-permute-start(bf16[12,128,384]{2,1,0:T(8,128)(2,1)S(1)} %constant_dynamic-update-slice_fusion.refs_1_), channel_id=1, source_target_pairs={{0,1},{1,0},{2,3},{3,2},{4,5},{5,4},{6,7},{7,6},{8,9},{9,8},{10,11... | collective-permute-start | bytes 3538952 | tf_op jit(solution)/shard_map/ppermute | solution.py:210
  88.1 12.0 %collective-permute-start.10 = (bf16[4,128,384]{2,1,0:T(8,128)(2,1)S(1)}, bf16[4,128,384]{2,1,0:T(8,128)(2,1)}, u32[]{:S(2)}, u32[]{:S(2)}) collective-permute-start(bf16[4,128,384]{2,1,0:T(8,128)(2,1)S(1)} %pad_maximum_fusion.1.refs_0_), channel_id=1, source_target_pairs={{0,1},{1,0},{2,3},{3,2},{4,5},{5,4},{6,7},{7,6},{8,9},{9,8},{10,11... | collective-permute-start | bytes 1179656 | tf_op jit(solution)/shard_map/ppermute | solution.py:210
  90.3 9.8 %copy-start.3 = (f32[1024]{0:T(1024)S(1)}, f32[1024]{0:T(1024)}, u32[]{:S(2)}) copy-start(f32[1024]{0:T(1024)} %param.7) | copy-start | bytes 12292
  90.3 9.8 %copy-start.4 = (s32[8]{0:T(128)S(1)}, s32[8]{0:T(128)}, u32[]{:S(2)}) copy-start(s32[8]{0:T(128)} %reach_ref.2) | copy-start | bytes 100
  90.4 33.2 %collective-permute-start.7 = (bf16[4,128,640]{2,1,0:T(8,128)(2,1)S(1)}, bf16[4,128,640]{2,1,0:T(8,128)(2,1)}, u32[]{:S(2)}, u32[]{:S(2)}) collective-permute-start(bf16[4,128,640]{2,1,0:T(8,128)(2,1)S(1)} %slice.30.refs_0_), channel_id=1, source_target_pairs={{0,64},{64,128},{128,192},{192,0},{1,65},{65,129},{129,193},{193,1... | collective-permute-start | bytes 1966088 | tf_op jit(solution)/shard_map/ppermute | solution.py:175
  92.3 31.3 %collective-permute-start.6 = (bf16[4,128,640]{2,1,0:T(8,128)(2,1)S(1)}, bf16[4,128,640]{2,1,0:T(8,128)(2,1)}, u32[]{:S(2)}, u32[]{:S(2)}) collective-permute-start(bf16[4,128,640]{2,1,0:T(8,128)(2,1)S(1)} %slice.30.refs_0_), channel_id=1, source_target_pairs={{0,128},{64,192},{128,0},{192,64},{1,129},{65,193},{129,1},{193,65... | collective-permute-start | bytes 1966088 | tf_op jit(solution)/shard_map/ppermute | solution.py:175
  95.7 30.2 %collective-permute-start.5 = (bf16[4,128,640]{2,1,0:T(8,128)(2,1)S(1)}, bf16[4,128,640]{2,1,0:T(8,128)(2,1)}, u32[]{:S(2)}, u32[]{:S(2)}) collective-permute-start(bf16[4,128,640]{2,1,0:T(8,128)(2,1)S(1)} %slice.30.refs_0_), channel_id=1, source_target_pairs={{0,192},{64,0},{128,64},{192,128},{1,193},{65,1},{129,65},{193,129... | collective-permute-start | bytes 1966088 | tf_op jit(solution)/shard_map/ppermute | solution.py:175
  100.2 37.7 %copy-start.5 = (s32[8]{0:T(128)S(1)}, s32[8]{0:T(128)}, u32[]{:S(2)}) copy-start(s32[8]{0:T(128)} %reach_ref.3) | copy-start | bytes 100
  104.9 39.5 %all-to-all-start.2 = ((bf16[64,4,512]{2,1,0:T(4,128)(2,1)}), bf16[64,4,512]{2,1,0:T(4,128)(2,1)S(1)}, u32[]{:S(2)}, u32[]{:S(2)}) async-start(bf16[64,4,512]{2,1,0:T(4,128)(2,1)} %reshape.37), calls=%async_computation.2 | async-start | bytes 524288 | tf_op jit(solution)/shard_map/all_to_all | solution.py:214
  125.8 9.7 %collective-permute-start.12 = (bf16[4,128,640]{2,1,0:T(8,128)(2,1)S(1)}, bf16[4,128,640]{2,1,0:T(8,128)(2,1)S(1)}, u32[]{:S(2)}, u32[]{:S(2)}) collective-permute-start(bf16[4,128,640]{2,1,0:T(8,128)(2,1)S(1)} %slice.30.refs_0_), channel_id=1, source_target_pairs={{0,1},{1,0},{2,3},{3,2},{4,5},{5,4},{6,7},{7,6},{8,9},{9,8},{10,11... | collective-permute-start | bytes 1966088 | tf_op jit(solution)/shard_map/ppermute | solution.py:210
  129.3 6.3 %collective-permute-start.13 = (bf16[4,128,640]{2,1,0:T(8,128)(2,1)}, bf16[4,128,640]{2,1,0:T(8,128)(2,1)S(1)}, u32[]{:S(2)}, u32[]{:S(2)}) collective-permute-start(bf16[4,128,640]{2,1,0:T(8,128)(2,1)} %collective-permute-done.5.refs_1_), channel_id=1, source_target_pairs={{0,1},{1,0},{2,3},{3,2},{4,5},{5,4},{6,7},{7,6},{8,9},{9,8},{10,11... | collective-permute-start | bytes 1966088 | tf_op jit(solution)/shard_map/ppermute | solution.py:210
  131.2 4.4 %collective-permute-start.14 = (bf16[4,128,640]{2,1,0:T(8,128)(2,1)}, bf16[4,128,640]{2,1,0:T(8,128)(2,1)S(1)}, u32[]{:S(2)}, u32[]{:S(2)}) collective-permute-start(bf16[4,128,640]{2,1,0:T(8,128)(2,1)} %collective-permute-done.6.refs_2_), channel_id=1, source_target_pairs={{0,1},{1,0},{2,3},{3,2},{4,5},{5,4},{6,7},{7,6},{8,9},{9,8},{10,11... | collective-permute-start | bytes 1966088 | tf_op jit(solution)/shard_map/ppermute | solution.py:210
  133.6 4.2 %collective-permute-start.15 = (bf16[4,128,640]{2,1,0:T(8,128)(2,1)}, bf16[4,128,640]{2,1,0:T(8,128)(2,1)S(1)}, u32[]{:S(2)}, u32[]{:S(2)}) collective-permute-start(bf16[4,128,640]{2,1,0:T(8,128)(2,1)} %collective-permute-done.7.refs_3_), channel_id=1, source_target_pairs={{0,1},{1,0},{2,3},{3,2},{4,5},{5,4},{6,7},{7,6},{8,9},{9,8},{10,11... | collective-permute-start | bytes 1966088 | tf_op jit(solution)/shard_map/ppermute | solution.py:210
  143.7 1.2 copy-start.2
  (1 other events, 1.0 us)

commit v10 on v9

--- a/solution.py
+++ b/solution.py
@@ -201,21 +201,22 @@
     def plane(part):
         return [part, *ring(part, "y", range(Y))]
 
-    def both_cores(parts, sizes):
-        ends = [sum(sizes[: i + 1]) for i in range(len(sizes))]
-        joined = [
-            parts[e - n] if n == 1 else jnp.concatenate(parts[e - n : e])
-            for e, n in zip(ends, sizes, strict=True)
-        ]
-        return [*joined, *(lax.ppermute(a, "c", [(0, 1), (1, 0)]) for a in joined)]
-
-    col_plane = plane(near[:, :, :PART])
-    col_mid = column_attention(place, col_rows, gain, turned, both_cores(col_plane, COLUMN_PIECES))
+    def swap(part):
+        return lax.ppermute(part, "c", [(0, 1), (1, 0)])
+
+    held, *came = plane(near[:, :, :PART])
+    rest, beside = near[:, :, PART:], came[0]
+    came = jnp.concatenate(came)
+    col_mid = column_attention(
+        place, col_rows, gain, turned, [held, came, swap(held), swap(came)]
+    )
     col_out = lax.all_to_all(col_mid.reshape(64, 4, HALF), SEQ, split_axis=0, concat_axis=0)
 
-    near_rest, _ = lax.optimization_barrier((near[:, :, PART:], col_plane[1]))
-    rest, _ = lax.optimization_barrier((plane(near_rest), col_mid))
-    base, low, last = row_attention(place, row_blocks, gain, rows, both_cores(rest, REST_PIECES))
+    rest, _ = lax.optimization_barrier((rest, beside))
+    rest, *later = plane(rest)
+    rest = [rest, *(lax.optimization_barrier((a, col_mid))[0] for a in later)]
+    rest = [*rest, *(swap(a) for a in rest)]
+    base, low, last = row_attention(place, row_blocks, gain, rows, rest)
     col_out = jnp.where(last[0] == 0, col_out, 0).reshape(STRIDE, HALF)
 
     mixed = pl.pallas_call(

time: 148 us -> 148 us (level)
    all_to_all x1, waiting for transfers between devices: 0.05 us -> 4.85 us  [body(): lax.all_to_all(col_mid.reshape(64, 4, HALF), SEQ, split_axis=0, concat_ax...]
    ppermute x9, waiting for transfers between devices: 23.1 us -> 18.5 us  [ring(): lax.ppermute(part, axes, [(order[i], order[(i - t) % size]) for i in rang...]
where the time goes in v10:
time: 148 us; the launch traced here: 147 us
  starting transfers between devices  92.6 us (63%)
  waiting for transfers between devices  37 us (25%)
  Pallas kernels  10.1 us (7%)
  local copies, waits for them, and re-layouts  4.98 us (3%)
    ppermute x9, starting transfers between devices, ring(): lax.ppermute(part, axes, [(order[i], order[(i - t) % size]) for i in rang...  29.1 us
    all_to_all x1, starting transfers between devices, body(): lax.all_to_all(jnp.broadcast_to(block, (Z, 16, 512)), 'z', split_axis=0,...  19.1 us
    ppermute x9, waiting for transfers between devices, ring(): lax.ppermute(part, axes, [(order[i], order[(i - t) % size]) for i in rang...  18.5 us
    all_to_all x1, starting transfers between devices, body(): lax.all_to_all(col_mid.reshape(64, 4, HALF), SEQ, split_axis=0, concat_ax...  15.8 us
    ppermute x6, starting transfers between devices, swap(): return lax.ppermute(part, 'c', [(0, 1), (1, 0)])  14.1 us
    all_to_all x1, starting transfers between devices, body(): turned = lax.all_to_all(sent, SEQ, split_axis=0, concat_axis=0)  13.8 us
    all_to_all x1, waiting for transfers between devices, body(): lax.all_to_all(jnp.broadcast_to(block, (Z, 16, 512)), 'z', split_axis=0,...  11.8 us
    pallas_call x1, Pallas kernels, row_attention(): pl.pallas_call(row_kernel, out_shape=[jax.ShapeDtypeStruct((STRIDE, FEATU...  4.93 us
  transfers between devices with their start and end apart: 19, of which 6 were waited for; matrix products, arithmetic and copies ran while one was open for 2% of the time, Pallas kernels for 6%

profile of v10, /device:TPU:1, one launch (start us, length us, event | category | flops | bytes accessed | tf_op | source)
XLA Modules:
  0.0 147.0 jit_solution(3764487946939187686)
XLA Ops:
  2.2 19.1 %all-to-all-start = ((bf16[16,16,512]{2,1,0:T(8,128)(2,1)}), bf16[16,16,512]{2,1,0:T(8,128)(2,1)S(1)}, u32[]{:S(2)}, u32[]{:S(2)}) async-start(bf16[16,16,512]{2,1,0:T(8,128)(2,1)} %broadcast_in_dim.7), calls=%async_computation | async-start | bytes 524288 | tf_op jit(solution)/shard_map/all_to_all | solution.py:189
  22.3 11.8 %all-to-all-done = bf16[16,16,512]{2,1,0:T(8,128)(2,1)S(1)} async-done(((bf16[16,16,512]{2,1,0:T(8,128)(2,1)}), bf16[16,16,512]{2,1,0:T(8,128)(2,1)S(1)}, u32[]{:S(2)}, u32[]{:S(2)}) %all-to-all-start) | async-done | bytes 262176 | tf_op jit(solution)/shard_map/all_to_all | solution.py:189
  34.2 4.7 %collective-permute-start.2 = (bf16[128,1024]{1,0:T(8,128)(2,1)S(1)}, bf16[128,1024]{1,0:T(8,128)(2,1)S(1)}, u32[]{:S(2)}, u32[]{:S(2)}) collective-permute-start(bf16[128,1024]{1,0:T(8,128)(2,1)S(1)} %get-tuple-element.24), channel_id=1, source_target_pairs={{0,32},{256,288},{32,0},{288,256},{1,33},{257,289},{33,1},{289,257... | collective-permute-start | bytes 786440 | tf_op jit(solution)/shard_map/ppermute | solution.py:175
  38.9 2.2 %collective-permute-start.3 = (bf16[128,1024]{1,0:T(8,128)(2,1)S(1)}, bf16[128,1024]{1,0:T(8,128)(2,1)S(1)}, u32[]{:S(2)}, u32[]{:S(2)}) collective-permute-start(bf16[128,1024]{1,0:T(8,128)(2,1)S(1)} %get-tuple-element.24), channel_id=1, source_target_pairs={{0,256},{256,32},{32,288},{288,0},{1,257},{257,33},{33,289},{289,1... | collective-permute-start | bytes 786440 | tf_op jit(solution)/shard_map/ppermute | solution.py:175
  41.1 4.3 %collective-permute-start.1 = (bf16[128,1024]{1,0:T(8,128)(2,1)S(1)}, bf16[128,1024]{1,0:T(8,128)(2,1)S(1)}, u32[]{:S(2)}, u32[]{:S(2)}) collective-permute-start(bf16[128,1024]{1,0:T(8,128)(2,1)S(1)} %get-tuple-element.24), channel_id=1, source_target_pairs={{0,288},{256,0},{32,256},{288,32},{1,289},{257,1},{33,257},{289,33... | collective-permute-start | bytes 786440 | tf_op jit(solution)/shard_map/ppermute | solution.py:175
  45.4 13.8 %all-to-all-start.1 = ((bf16[64,4,1024]{2,1,0:T(4,128)(2,1)}), bf16[64,4,1024]{2,1,0:T(4,128)(2,1)}, u32[]{:S(2)}, u32[]{:S(2)}) async-start(bf16[64,4,1024]{2,1,0:T(4,128)(2,1)} %reshape_reshape.3), calls=%async_computation.1 | async-start | bytes 1048576 | tf_op jit(solution)/shard_map/all_to_all | solution.py:192
  59.3 4.6 %collective-permute-start.4 = (bf16[4,128,384]{2,1,0:T(8,128)(2,1)S(1)}, bf16[4,128,384]{2,1,0:T(8,128)(2,1)S(1)}, u32[]{:S(2)}, u32[]{:S(2)}) collective-permute-start(bf16[4,128,384]{2,1,0:T(8,128)(2,1)S(1)} %pad_maximum_fusion.1.refs_0_), channel_id=1, source_target_pairs={{0,192},{64,0},{128,64},{192,128},{1,193},{65,1},{129,65},{193,129... | collective-permute-start | bytes 1179656 | tf_op jit(solution)/shard_map/ppermute | solution.py:175
  63.9 2.3 %collective-permute-start.6 = (bf16[4,128,384]{2,1,0:T(8,128)(2,1)S(1)}, bf16[4,128,384]{2,1,0:T(8,128)(2,1)S(1)}, u32[]{:S(2)}, u32[]{:S(2)}) collective-permute-start(bf16[4,128,384]{2,1,0:T(8,128)(2,1)S(1)} %pad_maximum_fusion.1.refs_0_), channel_id=1, source_target_pairs={{0,128},{64,192},{128,0},{192,64},{1,129},{65,193},{129,1},{193,65... | collective-permute-start | bytes 1179656 | tf_op jit(solution)/shard_map/ppermute | solution.py:175
  66.2 2.6 %collective-permute-start.7 = (bf16[4,128,384]{2,1,0:T(8,128)(2,1)S(1)}, bf16[4,128,384]{2,1,0:T(8,128)(2,1)S(1)}, u32[]{:S(2)}, u32[]{:S(2)}) collective-permute-start(bf16[4,128,384]{2,1,0:T(8,128)(2,1)S(1)} %pad_maximum_fusion.1.refs_0_), channel_id=1, source_target_pairs={{0,64},{64,128},{128,192},{192,0},{1,65},{65,129},{129,193},{193,1... | collective-permute-start | bytes 1179656 | tf_op jit(solution)/shard_map/ppermute | solution.py:175
  68.8 11.3 %collective-permute-done.4 = bf16[4,128,384]{2,1,0:T(8,128)(2,1)S(1)} collective-permute-done((bf16[4,128,384]{2,1,0:T(8,128)(2,1)S(1)}, bf16[4,128,384]{2,1,0:T(8,128)(2,1)S(1)}, u32[]{:S(2)}, u32[]{:S(2)}) %collective-permute-start.4) | collective-permute-done | bytes 393248 | tf_op jit(solution)/shard_map/ppermute | solution.py:175
  80.3 6.6 %collective-permute-done.7 = bf16[4,128,384]{2,1,0:T(8,128)(2,1)S(1)} collective-permute-done((bf16[4,128,384]{2,1,0:T(8,128)(2,1)S(1)}, bf16[4,128,384]{2,1,0:T(8,128)(2,1)S(1)}, u32[]{:S(2)}, u32[]{:S(2)}) %collective-permute-start.7) | collective-permute-done | bytes 393248 | tf_op jit(solution)/shard_map/ppermute | solution.py:175
  87.0 2.3 %collective-permute-start.9 = (bf16[12,128,384]{2,1,0:T(8,128)(2,1)S(1)}, bf16[12,128,384]{2,1,0:T(8,128)(2,1)}, u32[]{:S(2)}, u32[]{:S(2)}) collective-permute-start(bf16[12,128,384]{2,1,0:T(8,128)(2,1)S(1)} %constant_dynamic-update-slice_fusion.refs_1_), channel_id=1, source_target_pairs={{0,1},{1,0},{2,3},{3,2},{4,5},{5,4},{6,7},{7,6},{8,9},{9,8},{10,11... | collective-permute-start | bytes 3538952 | tf_op jit(solution)/shard_map/ppermute | solution.py:205
  89.3 2.0 %collective-permute-start.8 = (bf16[4,128,384]{2,1,0:T(8,128)(2,1)S(1)}, bf16[4,128,384]{2,1,0:T(8,128)(2,1)}, u32[]{:S(2)}, u32[]{:S(2)}) collective-permute-start(bf16[4,128,384]{2,1,0:T(8,128)(2,1)S(1)} %pad_maximum_fusion.1.refs_0_), channel_id=1, source_target_pairs={{0,1},{1,0},{2,3},{3,2},{4,5},{5,4},{6,7},{7,6},{8,9},{9,8},{10,11... | collective-permute-start | bytes 1179656 | tf_op jit(solution)/shard_map/ppermute | solution.py:205
  91.5 1.9 %collective-permute-start.11 = (bf16[4,128,640]{2,1,0:T(8,128)(2,1)S(1)}, bf16[4,128,640]{2,1,0:T(8,128)(2,1)}, u32[]{:S(2)}, u32[]{:S(2)}) collective-permute-start(bf16[4,128,640]{2,1,0:T(8,128)(2,1)S(1)} %slice.30.refs_0_), channel_id=1, source_target_pairs={{0,64},{64,128},{128,192},{192,0},{1,65},{65,129},{129,193},{193,1... | collective-permute-start | bytes 1966088 | tf_op jit(solution)/shard_map/ppermute | solution.py:175
  93.5 3.3 %collective-permute-start.10 = (bf16[4,128,640]{2,1,0:T(8,128)(2,1)S(1)}, bf16[4,128,640]{2,1,0:T(8,128)(2,1)}, u32[]{:S(2)}, u32[]{:S(2)}) collective-permute-start(bf16[4,128,640]{2,1,0:T(8,128)(2,1)S(1)} %slice.30.refs_0_), channel_id=1, source_target_pairs={{0,128},{64,192},{128,0},{192,64},{1,129},{65,193},{129,1},{193,65... | collective-permute-start | bytes 1966088 | tf_op jit(solution)/shard_map/ppermute | solution.py:175
  96.8 3.2 %collective-permute-start.5 = (bf16[4,128,640]{2,1,0:T(8,128)(2,1)S(1)}, bf16[4,128,640]{2,1,0:T(8,128)(2,1)}, u32[]{:S(2)}, u32[]{:S(2)}) collective-permute-start(bf16[4,128,640]{2,1,0:T(8,128)(2,1)S(1)} %slice.30.refs_0_), channel_id=1, source_target_pairs={{0,192},{64,0},{128,64},{192,128},{1,193},{65,1},{129,65},{193,129... | collective-permute-start | bytes 1966088 | tf_op jit(solution)/shard_map/ppermute | solution.py:175
  101.3 4.0 %columns.1 = bf16[256,512]{1,0:T(8,128)(2,1)S(1)} custom-call(s32[3]{0:T(128)S(1)} %pad_add_fusion.place, s32[8]{0:T(128)S(1)} %copy-done.4, f32[1,1024]{1,0:T(1,128)S(1)} %bitcast.18, bf16[256,1024]{1,0:T(8,128)(2,1)S(1)} %reshape.36.x_ref, bf16[4,128,384]{2,1,0:T(8,128)(2,1)S(1)} %pad_maximum_fusion.1.refs_0_, ...), custom_call_target="tpu_custom_call" | custom-call | flops 939524096 | bytes 6291456 | tf_op jit(solution)/shard_map/columns/pallas_call | solution.py:139
  106.0 15.8 %all-to-all-start.2 = ((bf16[64,4,512]{2,1,0:T(4,128)(2,1)}), bf16[64,4,512]{2,1,0:T(4,128)(2,1)S(1)}, u32[]{:S(2)}, u32[]{:S(2)}) async-start(bf16[64,4,512]{2,1,0:T(4,128)(2,1)} %reshape.37), calls=%async_computation.2 | async-start | bytes 524288 | tf_op jit(solution)/shard_map/all_to_all | solution.py:213
  121.8 2.4 %collective-permute-start.12 = (bf16[4,128,640]{2,1,0:T(8,128)(2,1)S(1)}, bf16[4,128,640]{2,1,0:T(8,128)(2,1)S(1)}, u32[]{:S(2)}, u32[]{:S(2)}) collective-permute-start(bf16[4,128,640]{2,1,0:T(8,128)(2,1)S(1)} %slice.30.refs_0_), channel_id=1, source_target_pairs={{0,1},{1,0},{2,3},{3,2},{4,5},{5,4},{6,7},{7,6},{8,9},{9,8},{10,11... | collective-permute-start | bytes 1966088 | tf_op jit(solution)/shard_map/ppermute | solution.py:205
  124.7 3.1 %collective-permute-start.15 = (bf16[4,128,640]{2,1,0:T(8,128)(2,1)}, bf16[4,128,640]{2,1,0:T(8,128)(2,1)S(1)}, u32[]{:S(2)}, u32[]{:S(2)}) collective-permute-start(bf16[4,128,640]{2,1,0:T(8,128)(2,1)} %collective-permute-done.11.refs_3_), channel_id=1, source_target_pairs={{0,1},{1,0},{2,3},{3,2},{4,5},{5,4},{6,7},{7,6},{8,9},{9,8},{10,11... | collective-permute-start | bytes 1966088 | tf_op jit(solution)/shard_map/ppermute | solution.py:205
  127.9 1.9 %collective-permute-start.14 = (bf16[4,128,640]{2,1,0:T(8,128)(2,1)}, bf16[4,128,640]{2,1,0:T(8,128)(2,1)S(1)}, u32[]{:S(2)}, u32[]{:S(2)}) collective-permute-start(bf16[4,128,640]{2,1,0:T(8,128)(2,1)} %collective-permute-done.10.refs_2_), channel_id=1, source_target_pairs={{0,1},{1,0},{2,3},{3,2},{4,5},{5,4},{6,7},{7,6},{8,9},{9,8},{10,11... | collective-permute-start | bytes 1966088 | tf_op jit(solution)/shard_map/ppermute | solution.py:205
  129.8 2.4 %collective-permute-start.13 = (bf16[4,128,640]{2,1,0:T(8,128)(2,1)}, bf16[4,128,640]{2,1,0:T(8,128)(2,1)S(1)}, u32[]{:S(2)}, u32[]{:S(2)}) collective-permute-start(bf16[4,128,640]{2,1,0:T(8,128)(2,1)} %collective-permute-done.5.refs_1_), channel_id=1, source_target_pairs={{0,1},{1,0},{2,3},{3,2},{4,5},{5,4},{6,7},{7,6},{8,9},{9,8},{10,11... | collective-permute-start | bytes 1966088 | tf_op jit(solution)/shard_map/ppermute | solution.py:205
  134.1 4.9 %rows.1 = (f32[256,1024]{1,0:T(8,128)S(1)}, bf16[512,1024]{1,0:T(8,128)(2,1)S(1)}, s32[1]{0:T(128)}) custom-call(s32[3]{0:T(128)S(1)} %pad_add_fusion.place, s32[8]{0:T(128)S(1)} %copy-done.5, f32[1,1024]{1,0:T(1,128)S(1)} %bitcast.19, bf16[256,1024]{1,0:T(8,128)(2,1)S(1)} %bitcast.17, bf16[4,128,640]{2,1,0:T(8,128)(2,1)S(1)} %slice.30.refs_0_, ...), custom_call_target="tpu_custom_call" | custom-call | flops 1048576 | bytes 1048576 | tf_op jit(solution)/shard_map/rows/pallas_call | solution.py:152
  140.7 4.9 %all-to-all-done.2 = bf16[64,4,512]{2,1,0:T(4,128)(2,1)S(1)} async-done(((bf16[64,4,512]{2,1,0:T(4,128)(2,1)}), bf16[64,4,512]{2,1,0:T(4,128)(2,1)S(1)}, u32[]{:S(2)}, u32[]{:S(2)}) %all-to-all-start.2) | async-done | bytes 262176 | tf_op jit(solution)/shard_map/all_to_all | solution.py:213
  (47 shorter events, 10.5 us)
Async XLA Ops:
  0.0 21.3 %copy-start = (bf16[1,1,256,1024]{3,2,1,0:T(8,128)(2,1)S(1)}, bf16[1,1,256,1024]{3,2,1,0:T(8,128)(2,1)}, u32[]{:S(2)}) copy-start(bf16[1,1,256,1024]{3,2,1,0:T(8,128)(2,1)} %param.6) | copy-start | bytes 1572868
  0.8 0.7 collective-permute-start
  2.2 31.9 %all-to-all-start = ((bf16[16,16,512]{2,1,0:T(8,128)(2,1)}), bf16[16,16,512]{2,1,0:T(8,128)(2,1)S(1)}, u32[]{:S(2)}, u32[]{:S(2)}) async-start(bf16[16,16,512]{2,1,0:T(8,128)(2,1)} %broadcast_in_dim.7), calls=%async_computation | async-start | bytes 524288 | tf_op jit(solution)/shard_map/all_to_all | solution.py:189
  34.2 25.0 %collective-permute-start.2 = (bf16[128,1024]{1,0:T(8,128)(2,1)S(1)}, bf16[128,1024]{1,0:T(8,128)(2,1)S(1)}, u32[]{:S(2)}, u32[]{:S(2)}) collective-permute-start(bf16[128,1024]{1,0:T(8,128)(2,1)S(1)} %get-tuple-element.24), channel_id=1, source_target_pairs={{0,32},{256,288},{32,0},{288,256},{1,33},{257,289},{33,1},{289,257... | collective-permute-start | bytes 786440 | tf_op jit(solution)/shard_map/ppermute | solution.py:175
  38.9 20.3 %collective-permute-start.3 = (bf16[128,1024]{1,0:T(8,128)(2,1)S(1)}, bf16[128,1024]{1,0:T(8,128)(2,1)S(1)}, u32[]{:S(2)}, u32[]{:S(2)}) collective-permute-start(bf16[128,1024]{1,0:T(8,128)(2,1)S(1)} %get-tuple-element.24), channel_id=1, source_target_pairs={{0,256},{256,32},{32,288},{288,0},{1,257},{257,33},{33,289},{289,1... | collective-permute-start | bytes 786440 | tf_op jit(solution)/shard_map/ppermute | solution.py:175
  41.1 18.1 %collective-permute-start.1 = (bf16[128,1024]{1,0:T(8,128)(2,1)S(1)}, bf16[128,1024]{1,0:T(8,128)(2,1)S(1)}, u32[]{:S(2)}, u32[]{:S(2)}) collective-permute-start(bf16[128,1024]{1,0:T(8,128)(2,1)S(1)} %get-tuple-element.24), channel_id=1, source_target_pairs={{0,288},{256,0},{32,256},{288,32},{1,289},{257,1},{33,257},{289,33... | collective-permute-start | bytes 786440 | tf_op jit(solution)/shard_map/ppermute | solution.py:175
  45.4 54.7 %all-to-all-start.1 = ((bf16[64,4,1024]{2,1,0:T(4,128)(2,1)}), bf16[64,4,1024]{2,1,0:T(4,128)(2,1)}, u32[]{:S(2)}, u32[]{:S(2)}) async-start(bf16[64,4,1024]{2,1,0:T(4,128)(2,1)} %reshape_reshape.3), calls=%async_computation.1 | async-start | bytes 1048576 | tf_op jit(solution)/shard_map/all_to_all | solution.py:192
  59.3 20.9 %collective-permute-start.4 = (bf16[4,128,384]{2,1,0:T(8,128)(2,1)S(1)}, bf16[4,128,384]{2,1,0:T(8,128)(2,1)S(1)}, u32[]{:S(2)}, u32[]{:S(2)}) collective-permute-start(bf16[4,128,384]{2,1,0:T(8,128)(2,1)S(1)} %pad_maximum_fusion.1.refs_0_), channel_id=1, source_target_pairs={{0,192},{64,0},{128,64},{192,128},{1,193},{65,1},{129,65},{193,129... | collective-permute-start | bytes 1179656 | tf_op jit(solution)/shard_map/ppermute | solution.py:175
  63.9 16.3 %collective-permute-start.6 = (bf16[4,128,384]{2,1,0:T(8,128)(2,1)S(1)}, bf16[4,128,384]{2,1,0:T(8,128)(2,1)S(1)}, u32[]{:S(2)}, u32[]{:S(2)}) collective-permute-start(bf16[4,128,384]{2,1,0:T(8,128)(2,1)S(1)} %pad_maximum_fusion.1.refs_0_), channel_id=1, source_target_pairs={{0,128},{64,192},{128,0},{192,64},{1,129},{65,193},{129,1},{193,65... | collective-permute-start | bytes 1179656 | tf_op jit(solution)/shard_map/ppermute | solution.py:175
  66.2 20.7 %collective-permute-start.7 = (bf16[4,128,384]{2,1,0:T(8,128)(2,1)S(1)}, bf16[4,128,384]{2,1,0:T(8,128)(2,1)S(1)}, u32[]{:S(2)}, u32[]{:S(2)}) collective-permute-start(bf16[4,128,384]{2,1,0:T(8,128)(2,1)S(1)} %pad_maximum_fusion.1.refs_0_), channel_id=1, source_target_pairs={{0,64},{64,128},{128,192},{192,0},{1,65},{65,129},{129,193},{193,1... | collective-permute-start | bytes 1179656 | tf_op jit(solution)/shard_map/ppermute | solution.py:175
  87.0 14.3 %collective-permute-start.9 = (bf16[12,128,384]{2,1,0:T(8,128)(2,1)S(1)}, bf16[12,128,384]{2,1,0:T(8,128)(2,1)}, u32[]{:S(2)}, u32[]{:S(2)}) collective-permute-start(bf16[12,128,384]{2,1,0:T(8,128)(2,1)S(1)} %constant_dynamic-update-slice_fusion.refs_1_), channel_id=1, source_target_pairs={{0,1},{1,0},{2,3},{3,2},{4,5},{5,4},{6,7},{7,6},{8,9},{9,8},{10,11... | collective-permute-start | bytes 3538952 | tf_op jit(solution)/shard_map/ppermute | solution.py:205
  89.3 12.0 %collective-permute-start.8 = (bf16[4,128,384]{2,1,0:T(8,128)(2,1)S(1)}, bf16[4,128,384]{2,1,0:T(8,128)(2,1)}, u32[]{:S(2)}, u32[]{:S(2)}) collective-permute-start(bf16[4,128,384]{2,1,0:T(8,128)(2,1)S(1)} %pad_maximum_fusion.1.refs_0_), channel_id=1, source_target_pairs={{0,1},{1,0},{2,3},{3,2},{4,5},{5,4},{6,7},{7,6},{8,9},{9,8},{10,11... | collective-permute-start | bytes 1179656 | tf_op jit(solution)/shard_map/ppermute | solution.py:205
  91.4 9.8 %copy-start.3 = (f32[1024]{0:T(1024)S(1)}, f32[1024]{0:T(1024)}, u32[]{:S(2)}) copy-start(f32[1024]{0:T(1024)} %param.7) | copy-start | bytes 12292
  91.5 9.8 %copy-start.4 = (s32[8]{0:T(128)S(1)}, s32[8]{0:T(128)}, u32[]{:S(2)}) copy-start(s32[8]{0:T(128)} %reach_ref.2) | copy-start | bytes 100
  91.5 33.2 %collective-permute-start.11 = (bf16[4,128,640]{2,1,0:T(8,128)(2,1)S(1)}, bf16[4,128,640]{2,1,0:T(8,128)(2,1)}, u32[]{:S(2)}, u32[]{:S(2)}) collective-permute-start(bf16[4,128,640]{2,1,0:T(8,128)(2,1)S(1)} %slice.30.refs_0_), channel_id=1, source_target_pairs={{0,64},{64,128},{128,192},{192,0},{1,65},{65,129},{129,193},{193,1... | collective-permute-start | bytes 1966088 | tf_op jit(solution)/shard_map/ppermute | solution.py:175
  93.5 34.4 %collective-permute-start.10 = (bf16[4,128,640]{2,1,0:T(8,128)(2,1)S(1)}, bf16[4,128,640]{2,1,0:T(8,128)(2,1)}, u32[]{:S(2)}, u32[]{:S(2)}) collective-permute-start(bf16[4,128,640]{2,1,0:T(8,128)(2,1)S(1)} %slice.30.refs_0_), channel_id=1, source_target_pairs={{0,128},{64,192},{128,0},{192,64},{1,129},{65,193},{129,1},{193,65... | collective-permute-start | bytes 1966088 | tf_op jit(solution)/shard_map/ppermute | solution.py:175
  96.8 33.0 %collective-permute-start.5 = (bf16[4,128,640]{2,1,0:T(8,128)(2,1)S(1)}, bf16[4,128,640]{2,1,0:T(8,128)(2,1)}, u32[]{:S(2)}, u32[]{:S(2)}) collective-permute-start(bf16[4,128,640]{2,1,0:T(8,128)(2,1)S(1)} %slice.30.refs_0_), channel_id=1, source_target_pairs={{0,192},{64,0},{128,64},{192,128},{1,193},{65,1},{129,65},{193,129... | collective-permute-start | bytes 1966088 | tf_op jit(solution)/shard_map/ppermute | solution.py:175
  101.3 32.8 %copy-start.5 = (s32[8]{0:T(128)S(1)}, s32[8]{0:T(128)}, u32[]{:S(2)}) copy-start(s32[8]{0:T(128)} %reach_ref.3) | copy-start | bytes 100
  106.0 39.5 %all-to-all-start.2 = ((bf16[64,4,512]{2,1,0:T(4,128)(2,1)}), bf16[64,4,512]{2,1,0:T(4,128)(2,1)S(1)}, u32[]{:S(2)}, u32[]{:S(2)}) async-start(bf16[64,4,512]{2,1,0:T(4,128)(2,1)} %reshape.37), calls=%async_computation.2 | async-start | bytes 524288 | tf_op jit(solution)/shard_map/all_to_all | solution.py:213
  121.8 10.4 %collective-permute-start.12 = (bf16[4,128,640]{2,1,0:T(8,128)(2,1)S(1)}, bf16[4,128,640]{2,1,0:T(8,128)(2,1)S(1)}, u32[]{:S(2)}, u32[]{:S(2)}) collective-permute-start(bf16[4,128,640]{2,1,0:T(8,128)(2,1)S(1)} %slice.30.refs_0_), channel_id=1, source_target_pairs={{0,1},{1,0},{2,3},{3,2},{4,5},{5,4},{6,7},{7,6},{8,9},{9,8},{10,11... | collective-permute-start | bytes 1966088 | tf_op jit(solution)/shard_map/ppermute | solution.py:205
  124.7 7.5 %collective-permute-start.15 = (bf16[4,128,640]{2,1,0:T(8,128)(2,1)}, bf16[4,128,640]{2,1,0:T(8,128)(2,1)S(1)}, u32[]{:S(2)}, u32[]{:S(2)}) collective-permute-start(bf16[4,128,640]{2,1,0:T(8,128)(2,1)} %collective-permute-done.11.refs_3_), channel_id=1, source_target_pairs={{0,1},{1,0},{2,3},{3,2},{4,5},{5,4},{6,7},{7,6},{8,9},{9,8},{10,11... | collective-permute-start | bytes 1966088 | tf_op jit(solution)/shard_map/ppermute | solution.py:205
  127.9 4.4 %collective-permute-start.14 = (bf16[4,128,640]{2,1,0:T(8,128)(2,1)}, bf16[4,128,640]{2,1,0:T(8,128)(2,1)S(1)}, u32[]{:S(2)}, u32[]{:S(2)}) collective-permute-start(bf16[4,128,640]{2,1,0:T(8,128)(2,1)} %collective-permute-done.10.refs_2_), channel_id=1, source_target_pairs={{0,1},{1,0},{2,3},{3,2},{4,5},{5,4},{6,7},{7,6},{8,9},{9,8},{10,11... | collective-permute-start | bytes 1966088 | tf_op jit(solution)/shard_map/ppermute | solution.py:205
  129.8 4.3 %collective-permute-start.13 = (bf16[4,128,640]{2,1,0:T(8,128)(2,1)}, bf16[4,128,640]{2,1,0:T(8,128)(2,1)S(1)}, u32[]{:S(2)}, u32[]{:S(2)}) collective-permute-start(bf16[4,128,640]{2,1,0:T(8,128)(2,1)} %collective-permute-done.5.refs_1_), channel_id=1, source_target_pairs={{0,1},{1,0},{2,3},{3,2},{4,5},{5,4},{6,7},{7,6},{8,9},{9,8},{10,11... | collective-permute-start | bytes 1966088 | tf_op jit(solution)/shard_map/ppermute | solution.py:205
  140.1 5.7 %copy-start.2 = (bf16[512,1024]{1,0:T(8,128)(2,1)S(1)}, bf16[512,1024]{1,0:T(8,128)(2,1)}, u32[]{:S(2)}) copy-start(bf16[512,1024]{1,0:T(8,128)(2,1)} %copy-done.1) | copy-start | bytes 3145732
  (1 other events, 1.0 us)

commit v11 on v10

--- a/solution.py
+++ b/solution.py
@@ -16,7 +16,6 @@
 PART = 384
 SEQ = ("xh", "z", "c")
 FAR = 1 << 20
-COLUMN_PIECES = (1, 3)
 REST_PIECES = (1, 1, 1, 1)
 
 
@@ -85,10 +84,27 @@
     return i, lax.broadcasted_iota(jnp.int32, (STRIDE, STRIDE), 1)
 
 
-def column_kernel(place, reach_ref, gain_ref, x_ref, *refs):
-    *parts, out_ref, w_ref, n_ref, qkv_ref = refs
-    assemble(place, True, parts, COLUMN_PIECES, slice(0, PART), w_ref, 0, PART)
+def column_kernel(place, reach_ref, gain_ref, here_ref, there_ref, other_ref, w0_ref, w1_ref, *refs):
+    out_ref, w_ref, n_ref, qkv_ref, x_ref = refs
+    core, half = place[2], place[3]
+    for a in range(XL):
+        for y in range(Y):
+            for b in range(XH):
+                for ref, c in ((w0_ref, core), (w1_ref, 1 - core)):
+                    rows = pl.ds(pl.multiple_of(32 * (1 - a) + 16 * c, 16), 16)
+                    block = ref[(a * Y + y) * XH + b].reshape(Z // 2, 16, PART)
+                    w_ref[Z // 2 * b : Z // 2 * (b + 1), rows, PART * y : PART * (y + 1)] = block
     i, j = pairs()
+    row = 32 * ((j >> 7) ^ half) + 2 * ((j >> 2) & 15) + (((j >> 6) & 1) ^ core)
+    move = (4 * row + (j & 3) == i).astype(jnp.float32).astype(jnp.bfloat16)
+    n_ref[0:64, :] = here_ref[...]
+    n_ref[64:128, :] = other_ref[0:64, :]
+    n_ref[128:192, :] = there_ref[...]
+    n_ref[192:256, :] = other_ref[64:128, :]
+    for n in range(0, FEATURES, 512):
+        x_ref[:, n : n + 512] = jnp.dot(
+            move, n_ref[:, n : n + 512], preferred_element_type=jnp.float32
+        ).astype(jnp.bfloat16)
     back = (i >> 2) - (j >> 2)
     dist = jnp.where((((i ^ j) & 3) == 0) & (back >= 0), back, FAR)
     attend(reach_ref, gain_ref, x_ref, w_ref, n_ref, qkv_ref, out_ref, dist)
@@ -135,17 +151,17 @@
 )
 
 
-def column_attention(place, reach, gain, x, parts):
+def column_attention(place, reach, gain, *arrays):
     return pl.pallas_call(
         column_kernel,
         out_shape=jax.ShapeDtypeStruct((STRIDE, HALF), jnp.bfloat16),
-        in_specs=[SMEM, SMEM] + [VMEM] * (2 + len(parts)),
+        in_specs=[SMEM, SMEM] + [VMEM] * (1 + len(arrays)),
         out_specs=VMEM,
-        scratch_shapes=WORK,
+        scratch_shapes=WORK + [pltpu.VMEM((STRIDE, FEATURES), jnp.bfloat16)],
         compiler_params=PARAMS,
         cost_estimate=COST,
         name="columns",
-    )(place, reach, gain, x, *parts)
+    )(place, reach, gain, *arrays)
 
 
 def row_attention(place, reach, gain, x, parts):
@@ -181,39 +197,48 @@
     xl, y, xh, c = (lax.axis_index(a) for a in ("xl", "y", "xh", "c"))
     rows = tokens.reshape(STRIDE, FEATURES)
     gain = norm_gain.reshape(1, FEATURES)
-    place = jnp.stack([2 * xh + xl, y, c]).astype(jnp.int32)
+    place = jnp.stack([2 * xh + xl, y, c, xh]).astype(jnp.int32)
 
     block = jnp.concatenate([w_qkv, w_out], axis=1)
     change = [(a * Z + z, (a ^ (z & 1)) * Z + z) for a in range(XL) for z in range(Z)]
     block = lax.ppermute(block, ("xl", "z"), change)
-    column = lax.all_to_all(jnp.broadcast_to(block, (Z, 16, 512)), "z", split_axis=0, concat_axis=0)
-
-    sent, column = lax.optimization_barrier((rows.reshape(64, 4, FEATURES), column))
-    turned = lax.all_to_all(sent, SEQ, split_axis=0, concat_axis=0)
-    turned = turned.reshape(STRIDE, FEATURES)
-
-    halves = column.reshape(Z // 2, 2, 16, 512)
+
+    tokens_out = rows.reshape(XH, Z, C, 4, FEATURES).transpose(1, 0, 2, 3, 4)
+    block = jnp.broadcast_to(block.reshape(XH, C, 4, 512), (Z, XH, C, 4, 512))
+    column = lax.all_to_all(
+        jnp.concatenate([tokens_out, block], axis=4), "z", split_axis=0, concat_axis=0
+    )
+    turned = column[..., :FEATURES]
+    halves = column[..., FEATURES:].reshape(Z // 2, 2, 16, 512)
     row_part = jnp.where(xl == 0, halves[:, 0], halves[:, 1]).reshape(128, 512)
     col_part = jnp.where(xl == 0, halves[:, 1], halves[:, 0]).reshape(128, 512)
-    part = jnp.concatenate([col_part[:, :PART], row_part, col_part[:, PART:]], axis=1)
-    near = jnp.stack([part, *ring(part, ("xl", "xh"), [0, 2, 1, 3])])
-
-    def plane(part):
-        return [part, *ring(part, "y", range(Y))]
-
-    def swap(part):
-        return lax.ppermute(part, "c", [(0, 1), (1, 0)])
-
-    held, *came = plane(near[:, :, :PART])
-    rest, beside = near[:, :, PART:], came[0]
-    came = jnp.concatenate(came)
+    rest_part = jnp.concatenate([row_part, col_part[:, PART:]], axis=1)
+
+    def swap(part, axis="c"):
+        return lax.ppermute(part, axis, [(0, 1), (1, 0)])
+
+    col_own = lax.all_to_all(
+        jnp.broadcast_to(col_part[:, :PART], (X * Y, 128, PART)),
+        ("xl", "y", "xh"),
+        split_axis=0,
+        concat_axis=0,
+    )
+
+    here = jnp.where(xh == 0, turned[:, 0], turned[:, 1])
+    there = swap(jnp.where(xh == 0, turned[:, 1], turned[:, 0]), "xh")
+    others = swap(jnp.stack([jnp.where(c == 0, a[:, 1], a[:, 0]) for a in (here, there)]))
+    here, there = (
+        jnp.where(c == 0, a[:, 0], a[:, 1]).reshape(64, FEATURES) for a in (here, there)
+    )
+    near = jnp.stack([rest_part, *ring(rest_part, ("xl", "xh"), [0, 2, 1, 3])])
+    col_own, others, near = lax.optimization_barrier((col_own, others, near))
+
     col_mid = column_attention(
-        place, col_rows, gain, turned, [held, came, swap(held), swap(came)]
+        place, col_rows, gain, here, there, others.reshape(128, FEATURES), col_own, swap(col_own)
     )
     col_out = lax.all_to_all(col_mid.reshape(64, 4, HALF), SEQ, split_axis=0, concat_axis=0)
 
-    rest, _ = lax.optimization_barrier((rest, beside))
-    rest, *later = plane(rest)
+    rest, *later = [near, *ring(near, "y", range(Y))]
     rest = [rest, *(lax.optimization_barrier((a, col_mid))[0] for a in later)]
     rest = [*rest, *(swap(a) for a in rest)]
     base, low, last = row_attention(place, row_blocks, gain, rows, rest)

time: 148 us -> 163 us (1.10)
  waiting for transfers between devices: 37 us -> 60.6 us
  starting transfers between devices: 92.6 us -> 81.1 us
  other arithmetic: 1.22 us -> 3.25 us
    all_to_all x2, waiting for transfers between devices: 11.8 us -> 34.2 us  [the longest x1 34.2 us: body(): lax.all_to_all(jnp.concatenate([tokens_out, block], axis=4), 'z', split_a...]
    ppermute x6 -> x7, waiting for transfers between devices: 1.89 us -> 21.1 us  [swap(): return lax.ppermute(part, axis, [(0, 1), (1, 0)])]
    ppermute x9 -> x6, waiting for transfers between devices: 18.5 us -> 3.6 us  [ring(): lax.ppermute(part, axes, [(order[i], order[(i - t) % size]) for i in rang...]
    ppermute x9 -> x6, starting transfers between devices: 29.1 us -> 19.3 us  [ring(): lax.ppermute(part, axes, [(order[i], order[(i - t) % size]) for i in rang...]
    all_to_all x2, starting transfers between devices: 32.9 us -> 24.8 us  [the longest x1 17.8 us: body(): lax.all_to_all(jnp.concatenate([tokens_out, block], axis=4), 'z', split_a...]
    ppermute x6 -> x7, starting transfers between devices: 14.1 us -> 21.4 us  [swap(): return lax.ppermute(part, axis, [(0, 1), (1, 0)])]
    all_to_all x1, waiting for transfers between devices: 4.85 us -> 1.71 us  [body(): lax.all_to_all(col_mid.reshape(64, 4, HALF), SEQ, split_axis=0, concat_ax...]
  transfers between devices with their start and end apart: 19 -> 17, of which waited for: 6 -> 7; matrix products, arithmetic and copies ran while one was open for 2% -> 2% of each run, Pallas kernels for 6% -> 6%
where the time goes in v11:
time: 163 us; the launch traced here: 162 us
  starting transfers between devices  81.1 us (50%)
  waiting for transfers between devices  60.6 us (37%)
  Pallas kernels  10.7 us (7%)
  local copies, waits for them, and re-layouts  5.14 us (3%)
  other arithmetic  3.25 us (2%)
    all_to_all x1, waiting for transfers between devices, body(): lax.all_to_all(jnp.concatenate([tokens_out, block], axis=4), 'z', split_a...  34.2 us
    ppermute x7, starting transfers between devices, swap(): return lax.ppermute(part, axis, [(0, 1), (1, 0)])  21.4 us
    ppermute x7, waiting for transfers between devices, swap(): return lax.ppermute(part, axis, [(0, 1), (1, 0)])  21.1 us
    ppermute x6, starting transfers between devices, ring(): lax.ppermute(part, axes, [(order[i], order[(i - t) % size]) for i in rang...  19.3 us
    all_to_all x1, starting transfers between devices, body(): lax.all_to_all(jnp.concatenate([tokens_out, block], axis=4), 'z', split_a...  17.8 us
    all_to_all x1, starting transfers between devices, body(): lax.all_to_all(col_mid.reshape(64, 4, HALF), SEQ, split_axis=0, concat_ax...  14.8 us
    all_to_all x1, starting transfers between devices, body(): lax.all_to_all(jnp.broadcast_to(col_part[:, :PART], (X * Y, 128, PART)),...  7.06 us
    pallas_call x1, Pallas kernels, row_attention(): pl.pallas_call(row_kernel, out_shape=[jax.ShapeDtypeStruct((STRIDE, FEATU...  4.94 us
  transfers between devices with their start and end apart: 17, of which 7 were waited for; matrix products, arithmetic and copies ran while one was open for 2% of the time, Pallas kernels for 6%

profile of v11, /device:TPU:1, one launch (start us, length us, event | category | flops | bytes accessed | tf_op | source)
XLA Modules:
  0.0 161.9 jit_solution(2913153989809838223)
XLA Ops:
  4.4 17.8 %all-to-all-start = ((bf16[16,2,2,4,1536]{4,3,2,1,0:T(4,128)(2,1)}), bf16[16,2,2,4,1536]{4,3,2,1,0:T(4,128)(2,1)S(1)}, u32[]{:S(2)}, u32[]{:S(2)}) async-start(bf16[16,2,2,4,1536]{4,3,2,1,0:T(4,128)(2,1)} %pad_maximum_fusion), calls=%async_computation | async-start | bytes 1572864 | tf_op jit(solution)/shard_map/all_to_all | solution.py:208
  22.1 34.2 %all-to-all-done = bf16[16,2,2,4,1536]{4,3,2,1,0:T(4,128)(2,1)S(1)} async-done(((bf16[16,2,2,4,1536]{4,3,2,1,0:T(4,128)(2,1)}), bf16[16,2,2,4,1536]{4,3,2,1,0:T(4,128)(2,1)S(1)}, u32[]{:S(2)}, u32[]{:S(2)}) %all-to-all-start) | async-done | bytes 786464 | tf_op jit(solution)/shard_map/all_to_all | solution.py:208
  56.6 1.4 broadcast_in_dim.11
  58.0 7.1 %all-to-all-start.1 = ((bf16[16,128,384]{2,1,0:T(8,128)(2,1)}), bf16[16,128,384]{2,1,0:T(8,128)(2,1)S(1)}, u32[]{:S(2)}, u32[]{:S(2)}) async-start(bf16[16,128,384]{2,1,0:T(8,128)(2,1)} %broadcast_in_dim.11), calls=%async_computation.1 | async-start | bytes 3145728 | tf_op jit(solution)/shard_map/all_to_all | solution.py:220
  65.1 4.8 %collective-permute-start.4 = (bf16[128,640]{1,0:T(8,128)(2,1)S(1)}, bf16[128,640]{1,0:T(8,128)(2,1)S(1)}, u32[]{:S(2)}, u32[]{:S(2)}) collective-permute-start(bf16[128,640]{1,0:T(8,128)(2,1)S(1)} %get-tuple-element.33), channel_id=1, source_target_pairs={{0,32},{256,288},{32,0},{288,256},{1,33},{257,289},{33,1},{289,257... | collective-permute-start | bytes 491528 | tf_op jit(solution)/shard_map/ppermute | solution.py:191
  69.9 2.8 %collective-permute-start.3 = (bf16[128,640]{1,0:T(8,128)(2,1)S(1)}, bf16[128,640]{1,0:T(8,128)(2,1)S(1)}, u32[]{:S(2)}, u32[]{:S(2)}) collective-permute-start(bf16[128,640]{1,0:T(8,128)(2,1)S(1)} %get-tuple-element.33), channel_id=1, source_target_pairs={{0,288},{256,0},{32,256},{288,32},{1,289},{257,1},{33,257},{289,33... | collective-permute-start | bytes 491528 | tf_op jit(solution)/shard_map/ppermute | solution.py:191
  72.7 2.5 %collective-permute-start.5 = (bf16[128,640]{1,0:T(8,128)(2,1)S(1)}, bf16[128,640]{1,0:T(8,128)(2,1)S(1)}, u32[]{:S(2)}, u32[]{:S(2)}) collective-permute-start(bf16[128,640]{1,0:T(8,128)(2,1)S(1)} %get-tuple-element.33), channel_id=1, source_target_pairs={{0,256},{256,32},{32,288},{288,0},{1,257},{257,33},{33,289},{289,1... | collective-permute-start | bytes 491528 | tf_op jit(solution)/shard_map/ppermute | solution.py:191
  75.5 2.5 %collective-permute-start.1 = (bf16[16,2,4,1024]{3,2,1,0:T(4,128)(2,1)S(1)}, bf16[16,2,4,1024]{3,2,1,0:T(4,128)(2,1)S(1)}, u32[]{:S(2)}, u32[]{:S(2)}) collective-permute-start(bf16[16,2,4,1024]{3,2,1,0:T(4,128)(2,1)S(1)} %get-tuple-element.24), channel_id=1, source_target_pairs={{0,32},{32,0},{1,33},{33,1},{2,34},{34,2},{3,35},{35,3},{4,36},{36... | collective-permute-start | bytes 786440 | tf_op jit(solution)/shard_map/ppermute | solution.py:218
  78.3 18.2 %collective-permute-done.1 = bf16[16,2,4,1024]{3,2,1,0:T(4,128)(2,1)S(1)} collective-permute-done((bf16[16,2,4,1024]{3,2,1,0:T(4,128)(2,1)S(1)}, bf16[16,2,4,1024]{3,2,1,0:T(4,128)(2,1)S(1)}, u32[]{:S(2)}, u32[]{:S(2)}) %collective-permute-start.1) | collective-permute-done | bytes 262176 | tf_op jit(solution)/shard_map/ppermute | solution.py:218
  96.8 6.8 %collective-permute-start.2 = (bf16[2,16,4,1024]{3,2,1,0:T(4,128)(2,1)S(1)}, bf16[2,16,4,1024]{3,2,1,0:T(4,128)(2,1)S(1)}, u32[]{:S(2)}, u32[]{:S(2)}) collective-permute-start(bf16[2,16,4,1024]{3,2,1,0:T(4,128)(2,1)S(1)} %pad_maximum_fusion.2), channel_id=1, source_target_pairs={{0,1},{1,0},{2,3},{3,2},{4,5},{5,4},{6,7},{7,6},{8,9},{9,8},{10,11... | collective-permute-start | bytes 786440 | tf_op jit(solution)/shard_map/ppermute | solution.py:218
  104.7 2.3 %collective-permute-start.7 = (bf16[16,128,384]{2,1,0:T(8,128)(2,1)S(1)}, bf16[16,128,384]{2,1,0:T(8,128)(2,1)}, u32[]{:S(2)}, u32[]{:S(2)}) collective-permute-start(bf16[16,128,384]{2,1,0:T(8,128)(2,1)S(1)} %all-to-all-done.1.w0_ref), channel_id=1, source_target_pairs={{0,1},{1,0},{2,3},{3,2},{4,5},{5,4},{6,7},{7,6},{8,9},{9,8},{10,11... | collective-permute-start | bytes 4718600 | tf_op jit(solution)/shard_map/ppermute | solution.py:218
  107.0 2.0 %collective-permute-start.9 = (bf16[4,128,640]{2,1,0:T(8,128)(2,1)S(1)}, bf16[4,128,640]{2,1,0:T(8,128)(2,1)}, u32[]{:S(2)}, u32[]{:S(2)}) collective-permute-start(bf16[4,128,640]{2,1,0:T(8,128)(2,1)S(1)} %pad_maximum_fusion.1.refs_0_), channel_id=1, source_target_pairs={{0,64},{64,128},{128,192},{192,0},{1,65},{65,129},{129,193},{193,1... | collective-permute-start | bytes 1966088 | tf_op jit(solution)/shard_map/ppermute | solution.py:191
  109.0 4.2 %collective-permute-start.8 = (bf16[4,128,640]{2,1,0:T(8,128)(2,1)S(1)}, bf16[4,128,640]{2,1,0:T(8,128)(2,1)}, u32[]{:S(2)}, u32[]{:S(2)}) collective-permute-start(bf16[4,128,640]{2,1,0:T(8,128)(2,1)S(1)} %pad_maximum_fusion.1.refs_0_), channel_id=1, source_target_pairs={{0,128},{64,192},{128,0},{192,64},{1,129},{65,193},{129,1},{193,65... | collective-permute-start | bytes 1966088 | tf_op jit(solution)/shard_map/ppermute | solution.py:191
  113.2 3.1 %collective-permute-start.6 = (bf16[4,128,640]{2,1,0:T(8,128)(2,1)S(1)}, bf16[4,128,640]{2,1,0:T(8,128)(2,1)}, u32[]{:S(2)}, u32[]{:S(2)}) collective-permute-start(bf16[4,128,640]{2,1,0:T(8,128)(2,1)S(1)} %pad_maximum_fusion.1.refs_0_), channel_id=1, source_target_pairs={{0,192},{64,0},{128,64},{192,128},{1,193},{65,1},{129,65},{193,129... | collective-permute-start | bytes 1966088 | tf_op jit(solution)/shard_map/ppermute | solution.py:191
  116.6 4.5 %columns.1 = bf16[256,512]{1,0:T(8,128)(2,1)S(1)} custom-call(s32[4]{0:T(128)S(1)} %pad_add_fusion.place, s32[8]{0:T(128)S(1)} %copy-done.4, f32[1,1024]{1,0:T(1,128)S(1)} %bitcast.36, bf16[64,1024]{1,0:T(8,128)(2,1)S(1)} %select_n.110.here_ref, bf16[64,1024]{1,0:T(8,128)(2,1)S(1)} %select_n.112.there_ref, bf16[128,1024]{1,0:T(8,128)(2,1)S(1)} %reshape.92.other_ref, ...), custom_call_target="tpu_custom_call" | custom-call | flops 939524096 | bytes 6291456 | tf_op jit(solution)/shard_map/columns/pallas_call | solution.py:155
  121.8 14.8 %all-to-all-start.2 = ((bf16[64,4,512]{2,1,0:T(4,128)(2,1)}), bf16[64,4,512]{2,1,0:T(4,128)(2,1)S(1)}, u32[]{:S(2)}, u32[]{:S(2)}) async-start(bf16[64,4,512]{2,1,0:T(4,128)(2,1)} %reshape.93), calls=%async_computation.2 | async-start | bytes 524288 | tf_op jit(solution)/shard_map/all_to_all | solution.py:239
  136.7 2.4 %collective-permute-start.10 = (bf16[4,128,640]{2,1,0:T(8,128)(2,1)S(1)}, bf16[4,128,640]{2,1,0:T(8,128)(2,1)S(1)}, u32[]{:S(2)}, u32[]{:S(2)}) collective-permute-start(bf16[4,128,640]{2,1,0:T(8,128)(2,1)S(1)} %pad_maximum_fusion.1.refs_0_), channel_id=1, source_target_pairs={{0,1},{1,0},{2,3},{3,2},{4,5},{5,4},{6,7},{7,6},{8,9},{9,8},{10,11... | collective-permute-start | bytes 1966088 | tf_op jit(solution)/shard_map/ppermute | solution.py:218
  140.2 2.5 %collective-permute-done.6.refs_1_ = bf16[4,128,640]{2,1,0:T(8,128)(2,1)} collective-permute-done((bf16[4,128,640]{2,1,0:T(8,128)(2,1)S(1)}, bf16[4,128,640]{2,1,0:T(8,128)(2,1)}, u32[]{:S(2)}, u32[]{:S(2)}) %collective-permute-start.6) | collective-permute-done | bytes 655392 | tf_op jit(solution)/shard_map/ppermute | solution.py:191
  142.7 3.2 %collective-permute-start.11 = (bf16[4,128,640]{2,1,0:T(8,128)(2,1)}, bf16[4,128,640]{2,1,0:T(8,128)(2,1)S(1)}, u32[]{:S(2)}, u32[]{:S(2)}) collective-permute-start(bf16[4,128,640]{2,1,0:T(8,128)(2,1)} %collective-permute-done.6.refs_1_), channel_id=1, source_target_pairs={{0,1},{1,0},{2,3},{3,2},{4,5},{5,4},{6,7},{7,6},{8,9},{9,8},{10,11... | collective-permute-start | bytes 1966088 | tf_op jit(solution)/shard_map/ppermute | solution.py:218
  145.8 1.9 %collective-permute-start.12 = (bf16[4,128,640]{2,1,0:T(8,128)(2,1)}, bf16[4,128,640]{2,1,0:T(8,128)(2,1)S(1)}, u32[]{:S(2)}, u32[]{:S(2)}) collective-permute-start(bf16[4,128,640]{2,1,0:T(8,128)(2,1)} %collective-permute-done.8.refs_2_), channel_id=1, source_target_pairs={{0,1},{1,0},{2,3},{3,2},{4,5},{5,4},{6,7},{7,6},{8,9},{9,8},{10,11... | collective-permute-start | bytes 1966088 | tf_op jit(solution)/shard_map/ppermute | solution.py:218
  147.8 2.4 %collective-permute-start.13 = (bf16[4,128,640]{2,1,0:T(8,128)(2,1)}, bf16[4,128,640]{2,1,0:T(8,128)(2,1)S(1)}, u32[]{:S(2)}, u32[]{:S(2)}) collective-permute-start(bf16[4,128,640]{2,1,0:T(8,128)(2,1)} %collective-permute-done.9.refs_3_), channel_id=1, source_target_pairs={{0,1},{1,0},{2,3},{3,2},{4,5},{5,4},{6,7},{7,6},{8,9},{9,8},{10,11... | collective-permute-start | bytes 1966088 | tf_op jit(solution)/shard_map/ppermute | solution.py:218
  150.2 1.9 %collective-permute-done.13.refs_7_ = bf16[4,128,640]{2,1,0:T(8,128)(2,1)S(1)} collective-permute-done((bf16[4,128,640]{2,1,0:T(8,128)(2,1)}, bf16[4,128,640]{2,1,0:T(8,128)(2,1)S(1)}, u32[]{:S(2)}, u32[]{:S(2)}) %collective-permute-start.13) | collective-permute-done | bytes 655392 | tf_op jit(solution)/shard_map/ppermute | solution.py:218
  152.1 4.9 %rows.1 = (f32[256,1024]{1,0:T(8,128)S(1)}, bf16[512,1024]{1,0:T(8,128)(2,1)S(1)}, s32[1]{0:T(128)}) custom-call(s32[4]{0:T(128)S(1)} %pad_add_fusion.place, s32[8]{0:T(128)S(1)} %copy-done.5, f32[1,1024]{1,0:T(1,128)S(1)} %bitcast.37, bf16[256,1024]{1,0:T(8,128)(2,1)S(1)} %bitcast.35, bf16[4,128,640]{2,1,0:T(8,128)(2,1)S(1)} %pad_maximum_fusion.1.refs_0_, ...), custom_call_target="tpu_custom_call" | custom-call | flops 1048576 | bytes 1048576 | tf_op jit(solution)/shard_map/rows/pallas_call | solution.py:168
  158.7 1.7 %all-to-all-done.2 = bf16[64,4,512]{2,1,0:T(4,128)(2,1)S(1)} async-done(((bf16[64,4,512]{2,1,0:T(4,128)(2,1)}), bf16[64,4,512]{2,1,0:T(4,128)(2,1)S(1)}, u32[]{:S(2)}, u32[]{:S(2)}) %all-to-all-start.2) | async-done | bytes 262176 | tf_op jit(solution)/shard_map/all_to_all | solution.py:239
  (51 shorter events, 11.0 us)
Async XLA Ops:
  0.7 2.1 %collective-permute-start = (bf16[16,512]{1,0:T(8,128)(2,1)S(1)}, bf16[16,512]{1,0:T(8,128)(2,1)S(1)}, u32[]{:S(2)}, u32[]{:S(2)}) collective-permute-start(bf16[16,512]{1,0:T(8,128)(2,1)S(1)} %pad_maximum_fusion.4), channel_id=1, source_target_pairs={{0,0},{2,258},{4,4},{6,262},{8,8},{10,266},{12,12},{14,270},{16,16... | collective-permute-start | bytes 49160 | tf_op jit(solution)/shard_map/ppermute | solution.py:204
  4.4 52.0 %all-to-all-start = ((bf16[16,2,2,4,1536]{4,3,2,1,0:T(4,128)(2,1)}), bf16[16,2,2,4,1536]{4,3,2,1,0:T(4,128)(2,1)S(1)}, u32[]{:S(2)}, u32[]{:S(2)}) async-start(bf16[16,2,2,4,1536]{4,3,2,1,0:T(4,128)(2,1)} %pad_maximum_fusion), calls=%async_computation | async-start | bytes 1572864 | tf_op jit(solution)/shard_map/all_to_all | solution.py:208
  58.0 46.7 %all-to-all-start.1 = ((bf16[16,128,384]{2,1,0:T(8,128)(2,1)}), bf16[16,128,384]{2,1,0:T(8,128)(2,1)S(1)}, u32[]{:S(2)}, u32[]{:S(2)}) async-start(bf16[16,128,384]{2,1,0:T(8,128)(2,1)} %broadcast_in_dim.11), calls=%async_computation.1 | async-start | bytes 3145728 | tf_op jit(solution)/shard_map/all_to_all | solution.py:220
  65.1 38.5 %collective-permute-start.4 = (bf16[128,640]{1,0:T(8,128)(2,1)S(1)}, bf16[128,640]{1,0:T(8,128)(2,1)S(1)}, u32[]{:S(2)}, u32[]{:S(2)}) collective-permute-start(bf16[128,640]{1,0:T(8,128)(2,1)S(1)} %get-tuple-element.33), channel_id=1, source_target_pairs={{0,32},{256,288},{32,0},{288,256},{1,33},{257,289},{33,1},{289,257... | collective-permute-start | bytes 491528 | tf_op jit(solution)/shard_map/ppermute | solution.py:191
  69.9 33.7 %collective-permute-start.3 = (bf16[128,640]{1,0:T(8,128)(2,1)S(1)}, bf16[128,640]{1,0:T(8,128)(2,1)S(1)}, u32[]{:S(2)}, u32[]{:S(2)}) collective-permute-start(bf16[128,640]{1,0:T(8,128)(2,1)S(1)} %get-tuple-element.33), channel_id=1, source_target_pairs={{0,288},{256,0},{32,256},{288,32},{1,289},{257,1},{33,257},{289,33... | collective-permute-start | bytes 491528 | tf_op jit(solution)/shard_map/ppermute | solution.py:191
  72.7 30.9 %collective-permute-start.5 = (bf16[128,640]{1,0:T(8,128)(2,1)S(1)}, bf16[128,640]{1,0:T(8,128)(2,1)S(1)}, u32[]{:S(2)}, u32[]{:S(2)}) collective-permute-start(bf16[128,640]{1,0:T(8,128)(2,1)S(1)} %get-tuple-element.33), channel_id=1, source_target_pairs={{0,256},{256,32},{32,288},{288,0},{1,257},{257,33},{33,289},{289,1... | collective-permute-start | bytes 491528 | tf_op jit(solution)/shard_map/ppermute | solution.py:191
  75.5 21.0 %collective-permute-start.1 = (bf16[16,2,4,1024]{3,2,1,0:T(4,128)(2,1)S(1)}, bf16[16,2,4,1024]{3,2,1,0:T(4,128)(2,1)S(1)}, u32[]{:S(2)}, u32[]{:S(2)}) collective-permute-start(bf16[16,2,4,1024]{3,2,1,0:T(4,128)(2,1)S(1)} %get-tuple-element.24), channel_id=1, source_target_pairs={{0,32},{32,0},{1,33},{33,1},{2,34},{34,2},{3,35},{35,3},{4,36},{36... | collective-permute-start | bytes 786440 | tf_op jit(solution)/shard_map/ppermute | solution.py:218
  96.6 20.0 %copy-start.3 = (f32[1024]{0:T(1024)S(1)}, f32[1024]{0:T(1024)}, u32[]{:S(2)}) copy-start(f32[1024]{0:T(1024)} %param.7) | copy-start | bytes 12292
  96.6 20.0 %copy-start.4 = (s32[8]{0:T(128)S(1)}, s32[8]{0:T(128)}, u32[]{:S(2)}) copy-start(s32[8]{0:T(128)} %reach_ref.2) | copy-start | bytes 100
  96.8 7.9 %collective-permute-start.2 = (bf16[2,16,4,1024]{3,2,1,0:T(4,128)(2,1)S(1)}, bf16[2,16,4,1024]{3,2,1,0:T(4,128)(2,1)S(1)}, u32[]{:S(2)}, u32[]{:S(2)}) collective-permute-start(bf16[2,16,4,1024]{3,2,1,0:T(4,128)(2,1)S(1)} %pad_maximum_fusion.2), channel_id=1, source_target_pairs={{0,1},{1,0},{2,3},{3,2},{4,5},{5,4},{6,7},{7,6},{8,9},{9,8},{10,11... | collective-permute-start | bytes 786440 | tf_op jit(solution)/shard_map/ppermute | solution.py:218
  104.7 11.8 %collective-permute-start.7 = (bf16[16,128,384]{2,1,0:T(8,128)(2,1)S(1)}, bf16[16,128,384]{2,1,0:T(8,128)(2,1)}, u32[]{:S(2)}, u32[]{:S(2)}) collective-permute-start(bf16[16,128,384]{2,1,0:T(8,128)(2,1)S(1)} %all-to-all-done.1.w0_ref), channel_id=1, source_target_pairs={{0,1},{1,0},{2,3},{3,2},{4,5},{5,4},{6,7},{7,6},{8,9},{9,8},{10,11... | collective-permute-start | bytes 4718600 | tf_op jit(solution)/shard_map/ppermute | solution.py:218
  107.0 32.1 %collective-permute-start.9 = (bf16[4,128,640]{2,1,0:T(8,128)(2,1)S(1)}, bf16[4,128,640]{2,1,0:T(8,128)(2,1)}, u32[]{:S(2)}, u32[]{:S(2)}) collective-permute-start(bf16[4,128,640]{2,1,0:T(8,128)(2,1)S(1)} %pad_maximum_fusion.1.refs_0_), channel_id=1, source_target_pairs={{0,64},{64,128},{128,192},{192,0},{1,65},{65,129},{129,193},{193,1... | collective-permute-start | bytes 1966088 | tf_op jit(solution)/shard_map/ppermute | solution.py:191
  109.0 31.2 %collective-permute-start.8 = (bf16[4,128,640]{2,1,0:T(8,128)(2,1)S(1)}, bf16[4,128,640]{2,1,0:T(8,128)(2,1)}, u32[]{:S(2)}, u32[]{:S(2)}) collective-permute-start(bf16[4,128,640]{2,1,0:T(8,128)(2,1)S(1)} %pad_maximum_fusion.1.refs_0_), channel_id=1, source_target_pairs={{0,128},{64,192},{128,0},{192,64},{1,129},{65,193},{129,1},{193,65... | collective-permute-start | bytes 1966088 | tf_op jit(solution)/shard_map/ppermute | solution.py:191
  113.2 29.5 %collective-permute-start.6 = (bf16[4,128,640]{2,1,0:T(8,128)(2,1)S(1)}, bf16[4,128,640]{2,1,0:T(8,128)(2,1)}, u32[]{:S(2)}, u32[]{:S(2)}) collective-permute-start(bf16[4,128,640]{2,1,0:T(8,128)(2,1)S(1)} %pad_maximum_fusion.1.refs_0_), channel_id=1, source_target_pairs={{0,192},{64,0},{128,64},{192,128},{1,193},{65,1},{129,65},{193,129... | collective-permute-start | bytes 1966088 | tf_op jit(solution)/shard_map/ppermute | solution.py:191
  116.5 35.5 %copy-start = (bf16[1,1,256,1024]{3,2,1,0:T(8,128)(2,1)S(1)}, bf16[1,1,256,1024]{3,2,1,0:T(8,128)(2,1)}, u32[]{:S(2)}) copy-start(bf16[1,1,256,1024]{3,2,1,0:T(8,128)(2,1)} %param.6) | copy-start | bytes 1572868
  116.6 35.5 %copy-start.5 = (s32[8]{0:T(128)S(1)}, s32[8]{0:T(128)}, u32[]{:S(2)}) copy-start(s32[8]{0:T(128)} %reach_ref.3) | copy-start | bytes 100
  121.8 38.6 %all-to-all-start.2 = ((bf16[64,4,512]{2,1,0:T(4,128)(2,1)}), bf16[64,4,512]{2,1,0:T(4,128)(2,1)S(1)}, u32[]{:S(2)}, u32[]{:S(2)}) async-start(bf16[64,4,512]{2,1,0:T(4,128)(2,1)} %reshape.93), calls=%async_computation.2 | async-start | bytes 524288 | tf_op jit(solution)/shard_map/all_to_all | solution.py:239
  136.7 13.5 %collective-permute-start.10 = (bf16[4,128,640]{2,1,0:T(8,128)(2,1)S(1)}, bf16[4,128,640]{2,1,0:T(8,128)(2,1)S(1)}, u32[]{:S(2)}, u32[]{:S(2)}) collective-permute-start(bf16[4,128,640]{2,1,0:T(8,128)(2,1)S(1)} %pad_maximum_fusion.1.refs_0_), channel_id=1, source_target_pairs={{0,1},{1,0},{2,3},{3,2},{4,5},{5,4},{6,7},{7,6},{8,9},{9,8},{10,11... | collective-permute-start | bytes 1966088 | tf_op jit(solution)/shard_map/ppermute | solution.py:218
  142.7 7.5 %collective-permute-start.11 = (bf16[4,128,640]{2,1,0:T(8,128)(2,1)}, bf16[4,128,640]{2,1,0:T(8,128)(2,1)S(1)}, u32[]{:S(2)}, u32[]{:S(2)}) collective-permute-start(bf16[4,128,640]{2,1,0:T(8,128)(2,1)} %collective-permute-done.6.refs_1_), channel_id=1, source_target_pairs={{0,1},{1,0},{2,3},{3,2},{4,5},{5,4},{6,7},{7,6},{8,9},{9,8},{10,11... | collective-permute-start | bytes 1966088 | tf_op jit(solution)/shard_map/ppermute | solution.py:218
  145.8 4.4 %collective-permute-start.12 = (bf16[4,128,640]{2,1,0:T(8,128)(2,1)}, bf16[4,128,640]{2,1,0:T(8,128)(2,1)S(1)}, u32[]{:S(2)}, u32[]{:S(2)}) collective-permute-start(bf16[4,128,640]{2,1,0:T(8,128)(2,1)} %collective-permute-done.8.refs_2_), channel_id=1, source_target_pairs={{0,1},{1,0},{2,3},{3,2},{4,5},{5,4},{6,7},{7,6},{8,9},{9,8},{10,11... | collective-permute-start | bytes 1966088 | tf_op jit(solution)/shard_map/ppermute | solution.py:218
  147.8 4.3 %collective-permute-start.13 = (bf16[4,128,640]{2,1,0:T(8,128)(2,1)}, bf16[4,128,640]{2,1,0:T(8,128)(2,1)S(1)}, u32[]{:S(2)}, u32[]{:S(2)}) collective-permute-start(bf16[4,128,640]{2,1,0:T(8,128)(2,1)} %collective-permute-done.9.refs_3_), channel_id=1, source_target_pairs={{0,1},{1,0},{2,3},{3,2},{4,5},{5,4},{6,7},{7,6},{8,9},{9,8},{10,11... | collective-permute-start | bytes 1966088 | tf_op jit(solution)/shard_map/ppermute | solution.py:218
  157.0 1.0 copy-start.1
  158.0 2.6 %copy-start.2 = (bf16[512,1024]{1,0:T(8,128)(2,1)S(1)}, bf16[512,1024]{1,0:T(8,128)(2,1)}, u32[]{:S(2)}) copy-start(bf16[512,1024]{1,0:T(8,128)(2,1)} %copy-done.1) | copy-start | bytes 3145732

commit v12 on v10

--- a/solution.py
+++ b/solution.py
@@ -20,20 +20,17 @@
 REST_PIECES = (1, 1, 1, 1)
 
 
-def assemble(place, odd, refs, sizes, lanes, w_ref, first, width):
-    x, y, core = place[0], place[1], place[2]
+def assemble(place, refs, sizes, lanes, w_ref, first, width):
+    xh, y, core = place[0], place[1], place[2]
     pieces = [(i, j) for i, size in enumerate(sizes) for j in range(size)]
     for t in range(Y):
         cols = pl.ds(pl.multiple_of(first + width * ((y + t) & 3), 128), width)
         piece, at = pieces[t]
-        for s in range(X):
-            there = (x + s) & 3
-            xh, xl = there >> 1, there & 1
-            turn = 32 * ((1 - xl) if odd else xl)
+        for u in range(XH):
             for ref, c in ((refs[piece], core), (refs[len(sizes) + piece], 1 - core)):
-                rows = pl.ds(pl.multiple_of(turn + 16 * c, 16), 16)
-                block = ref[at * X + s, :, lanes].reshape(Z // 2, 16, width)
-                w_ref[pl.ds(Z // 2 * xh, Z // 2), rows, cols] = block
+                rows = pl.ds(pl.multiple_of(16 * c, 16), 16)
+                block = ref[at * XH + u, :, lanes].reshape(Z, 16, width)
+                w_ref[pl.ds(Z * ((xh + u) & 1), Z), rows, cols] = block
 
 
 def attend(reach_ref, gain_ref, x_ref, w_ref, n_ref, qkv_ref, out_ref, dist):
@@ -87,7 +84,7 @@
 
 def column_kernel(place, reach_ref, gain_ref, x_ref, *refs):
     *parts, out_ref, w_ref, n_ref, qkv_ref = refs
-    assemble(place, True, parts, COLUMN_PIECES, slice(0, PART), w_ref, 0, PART)
+    assemble(place, parts, COLUMN_PIECES, slice(0, PART), w_ref, 0, PART)
     i, j = pairs()
     back = (i >> 2) - (j >> 2)
     dist = jnp.where((((i ^ j) & 3) == 0) & (back >= 0), back, FAR)
@@ -97,19 +94,19 @@
 def row_kernel(place, reach_ref, gain_ref, x_ref, *refs):
     *parts, base_ref, low_ref, done_ref, w_ref, n_ref, qkv_ref, a_ref, o_ref = refs
     done_ref[0] = 0
-    assemble(place, False, parts, REST_PIECES, slice(0, PART), w_ref, 0, PART)
+    assemble(place, parts, REST_PIECES, slice(0, PART), w_ref, 0, PART)
     i, j = pairs()
     dist = jnp.where(j <= i, (i >> 5) - (j >> 5), FAR)
     attend(reach_ref, gain_ref, x_ref, w_ref, n_ref, qkv_ref, a_ref, dist)
-    assemble(place, False, parts, REST_PIECES, slice(PART, PART + 128), o_ref, 0, 128)
-    assemble(place, True, parts, REST_PIECES, slice(PART + 128, PART + 256), o_ref, 512, 128)
+    assemble(place, parts, REST_PIECES, slice(PART, PART + 128), o_ref, 0, 128)
+    assemble(place, parts, REST_PIECES, slice(PART + 128, PART + 256), o_ref, 512, 128)
     for n in range(0, FEATURES, 256):
         base_ref[:, n : n + 256] = x_ref[:, n : n + 256].astype(jnp.float32) + jnp.dot(
             a_ref[...],
-            o_ref[: Z // 2, :, n : n + 256].reshape(HALF, 256),
+            o_ref[:Z, :, n : n + 256].reshape(HALF, 256),
             preferred_element_type=jnp.float32,
         )
-    low_ref[...] = o_ref[Z // 2 :].reshape(HALF, FEATURES)
+    low_ref[...] = o_ref[Z:].reshape(HALF, FEATURES)
 
 
 def last_kernel(base_ref, col_ref, low_ref, out_ref):
@@ -123,7 +120,7 @@
 VMEM = pl.BlockSpec(memory_space=pltpu.VMEM)
 SMEM = pl.BlockSpec(memory_space=pltpu.SMEM)
 WORK = [
-    pltpu.VMEM((Z, 64, WIDTH), jnp.bfloat16),
+    pltpu.VMEM((2 * Z, 32, WIDTH), jnp.bfloat16),
     pltpu.VMEM((STRIDE, FEATURES), jnp.bfloat16),
     pltpu.VMEM((STRIDE, WIDTH), jnp.bfloat16),
 ]
@@ -161,7 +158,7 @@
         scratch_shapes=WORK
         + [
             pltpu.VMEM((STRIDE, HALF), jnp.bfloat16),
-            pltpu.VMEM((Z, 64, FEATURES), jnp.bfloat16),
+            pltpu.VMEM((2 * Z, 32, FEATURES), jnp.bfloat16),
         ],
         compiler_params=PARAMS,
         cost_estimate=pl.CostEstimate(flops=1 << 20, bytes_accessed=1 << 20, transcendentals=0),
@@ -181,22 +178,23 @@
     xl, y, xh, c = (lax.axis_index(a) for a in ("xl", "y", "xh", "c"))
     rows = tokens.reshape(STRIDE, FEATURES)
     gain = norm_gain.reshape(1, FEATURES)
-    place = jnp.stack([2 * xh + xl, y, c]).astype(jnp.int32)
+    place = jnp.stack([xh, y, c]).astype(jnp.int32)
 
     block = jnp.concatenate([w_qkv, w_out], axis=1)
-    change = [(a * Z + z, (a ^ (z & 1)) * Z + z) for a in range(XL) for z in range(Z)]
-    block = lax.ppermute(block, ("xl", "z"), change)
     column = lax.all_to_all(jnp.broadcast_to(block, (Z, 16, 512)), "z", split_axis=0, concat_axis=0)
 
     sent, column = lax.optimization_barrier((rows.reshape(64, 4, FEATURES), column))
     turned = lax.all_to_all(sent, SEQ, split_axis=0, concat_axis=0)
     turned = turned.reshape(STRIDE, FEATURES)
 
-    halves = column.reshape(Z // 2, 2, 16, 512)
-    row_part = jnp.where(xl == 0, halves[:, 0], halves[:, 1]).reshape(128, 512)
-    col_part = jnp.where(xl == 0, halves[:, 1], halves[:, 0]).reshape(128, 512)
-    part = jnp.concatenate([col_part[:, :PART], row_part, col_part[:, PART:]], axis=1)
-    near = jnp.stack([part, *ring(part, ("xl", "xh"), [0, 2, 1, 3])])
+    part = column.reshape(Z * 16, 512)
+    ahead, across, behind = ring(part, ("xl", "xh"), [0, 2, 1, 3])
+    for_rows = [jnp.where(xl == 0, part, behind), jnp.where(xl == 0, across, ahead)]
+    for_columns = [jnp.where(xl == 0, ahead, part), jnp.where(xl == 0, behind, across)]
+    near = jnp.stack([a[:, :PART] for a in for_columns])
+    rest = jnp.stack(
+        [jnp.concatenate([a, b[:, PART:]], axis=1) for a, b in zip(for_rows, for_columns, strict=True)]
+    )
 
     def plane(part):
         return [part, *ring(part, "y", range(Y))]
@@ -204,8 +202,8 @@
     def swap(part):
         return lax.ppermute(part, "c", [(0, 1), (1, 0)])
 
-    held, *came = plane(near[:, :, :PART])
-    rest, beside = near[:, :, PART:], came[0]
+    held, *came = plane(near)
+    beside = came[0]
     came = jnp.concatenate(came)
     col_mid = column_attention(
         place, col_rows, gain, turned, [held, came, swap(held), swap(came)]

time: 148 us -> 144 us (0.973)
  starting transfers between devices: 92.6 us -> 88.1 us
    all_to_all x1, starting transfers between devices: 19.1 us -> 15.7 us  [body(): lax.all_to_all(jnp.broadcast_to(block, (Z, 16, 512)), 'z', split_axis=0,...]
  transfers between devices with their start and end apart: 19 -> 18, of which waited for: 6 -> 6; matrix products, arithmetic and copies ran while one was open for 2% -> 2% of each run, Pallas kernels for 6% -> 6%
where the time goes in v12:
time: 144 us; the launch traced here: 143 us
  starting transfers between devices  88.1 us (61%)
  waiting for transfers between devices  37.4 us (26%)
  Pallas kernels  10.1 us (7%)
  local copies, waits for them, and re-layouts  4.95 us (3%)
    ppermute x9, starting transfers between devices, ring(): lax.ppermute(part, axes, [(order[i], order[(i - t) % size]) for i in rang...  27.8 us
    ppermute x9, waiting for transfers between devices, ring(): lax.ppermute(part, axes, [(order[i], order[(i - t) % size]) for i in rang...  18.5 us
    all_to_all x1, starting transfers between devices, body(): lax.all_to_all(col_mid.reshape(64, 4, HALF), SEQ, split_axis=0, concat_ax...  15.8 us
    all_to_all x1, starting transfers between devices, body(): lax.all_to_all(jnp.broadcast_to(block, (Z, 16, 512)), 'z', split_axis=0,...  15.7 us
    all_to_all x1, starting transfers between devices, body(): turned = lax.all_to_all(sent, SEQ, split_axis=0, concat_axis=0)  14.6 us
    ppermute x6, starting transfers between devices, swap(): return lax.ppermute(part, 'c', [(0, 1), (1, 0)])  14.1 us
    all_to_all x1, waiting for transfers between devices, body(): lax.all_to_all(jnp.broadcast_to(block, (Z, 16, 512)), 'z', split_axis=0,...  12.1 us
    pallas_call x1, Pallas kernels, row_attention(): pl.pallas_call(row_kernel, out_shape=[jax.ShapeDtypeStruct((STRIDE, FEATU...  4.94 us
  transfers between devices with their start and end apart: 18, of which 6 were waited for; matrix products, arithmetic and copies ran while one was open for 2% of the time, Pallas kernels for 6%

profile of v12, /device:TPU:1, one launch (start us, length us, event | category | flops | bytes accessed | tf_op | source)
XLA Modules:
  0.0 142.9 jit_solution(12974187005635987473)
XLA Ops:
  1.5 15.7 %all-to-all-start = ((bf16[16,16,512]{2,1,0:T(8,128)(2,1)}), bf16[16,16,512]{2,1,0:T(8,128)(2,1)S(1)}, u32[]{:S(2)}, u32[]{:S(2)}) async-start(bf16[16,16,512]{2,1,0:T(8,128)(2,1)} %broadcast_in_dim.7), calls=%async_computation | async-start | bytes 524288 | tf_op jit(solution)/shard_map/all_to_all | solution.py:184
  18.3 12.1 %all-to-all-done = bf16[16,16,512]{2,1,0:T(8,128)(2,1)S(1)} async-done(((bf16[16,16,512]{2,1,0:T(8,128)(2,1)}), bf16[16,16,512]{2,1,0:T(8,128)(2,1)S(1)}, u32[]{:S(2)}, u32[]{:S(2)}) %all-to-all-start) | async-done | bytes 262176 | tf_op jit(solution)/shard_map/all_to_all | solution.py:184
  30.4 3.1 %collective-permute-start = (bf16[256,512]{1,0:T(8,128)(2,1)S(1)}, bf16[256,512]{1,0:T(8,128)(2,1)S(1)}, u32[]{:S(2)}, u32[]{:S(2)}) collective-permute-start(bf16[256,512]{1,0:T(8,128)(2,1)S(1)} %bitcast.23), channel_id=1, source_target_pairs={{0,256},{256,32},{32,288},{288,0},{1,257},{257,33},{33,289},{289,1... | collective-permute-start | bytes 786440 | tf_op jit(solution)/shard_map/ppermute | solution.py:172
  33.5 3.4 %collective-permute-start.1 = (bf16[256,512]{1,0:T(8,128)(2,1)S(1)}, bf16[256,512]{1,0:T(8,128)(2,1)S(1)}, u32[]{:S(2)}, u32[]{:S(2)}) collective-permute-start(bf16[256,512]{1,0:T(8,128)(2,1)S(1)} %bitcast.24), channel_id=1, source_target_pairs={{0,288},{256,0},{32,256},{288,32},{1,289},{257,1},{33,257},{289,33... | collective-permute-start | bytes 786440 | tf_op jit(solution)/shard_map/ppermute | solution.py:172
  36.9 3.4 %collective-permute-start.2 = (bf16[256,512]{1,0:T(8,128)(2,1)S(1)}, bf16[256,512]{1,0:T(8,128)(2,1)S(1)}, u32[]{:S(2)}, u32[]{:S(2)}) collective-permute-start(bf16[256,512]{1,0:T(8,128)(2,1)S(1)} %bitcast.25), channel_id=1, source_target_pairs={{0,32},{256,288},{32,0},{288,256},{1,33},{257,289},{33,1},{289,257... | collective-permute-start | bytes 786440 | tf_op jit(solution)/shard_map/ppermute | solution.py:172
  40.4 14.6 %all-to-all-start.1 = ((bf16[64,4,1024]{2,1,0:T(4,128)(2,1)}), bf16[64,4,1024]{2,1,0:T(4,128)(2,1)}, u32[]{:S(2)}, u32[]{:S(2)}) async-start(bf16[64,4,1024]{2,1,0:T(4,128)(2,1)} %reshape_reshape.3), calls=%async_computation.1 | async-start | bytes 1048576 | tf_op jit(solution)/shard_map/all_to_all | solution.py:187
  55.2 4.6 %collective-permute-start.3 = (bf16[2,256,384]{2,1,0:T(8,128)(2,1)S(1)}, bf16[2,256,384]{2,1,0:T(8,128)(2,1)S(1)}, u32[]{:S(2)}, u32[]{:S(2)}) collective-permute-start(bf16[2,256,384]{2,1,0:T(8,128)(2,1)S(1)} %pad_maximum_fusion.1.refs_0_), channel_id=1, source_target_pairs={{0,192},{64,0},{128,64},{192,128},{1,193},{65,1},{129,65},{193,129... | collective-permute-start | bytes 1179656 | tf_op jit(solution)/shard_map/ppermute | solution.py:172
  59.9 2.3 %collective-permute-start.5 = (bf16[2,256,384]{2,1,0:T(8,128)(2,1)S(1)}, bf16[2,256,384]{2,1,0:T(8,128)(2,1)S(1)}, u32[]{:S(2)}, u32[]{:S(2)}) collective-permute-start(bf16[2,256,384]{2,1,0:T(8,128)(2,1)S(1)} %pad_maximum_fusion.1.refs_0_), channel_id=1, source_target_pairs={{0,128},{64,192},{128,0},{192,64},{1,129},{65,193},{129,1},{193,65... | collective-permute-start | bytes 1179656 | tf_op jit(solution)/shard_map/ppermute | solution.py:172
  62.1 2.6 %collective-permute-start.6 = (bf16[2,256,384]{2,1,0:T(8,128)(2,1)S(1)}, bf16[2,256,384]{2,1,0:T(8,128)(2,1)S(1)}, u32[]{:S(2)}, u32[]{:S(2)}) collective-permute-start(bf16[2,256,384]{2,1,0:T(8,128)(2,1)S(1)} %pad_maximum_fusion.1.refs_0_), channel_id=1, source_target_pairs={{0,64},{64,128},{128,192},{192,0},{1,65},{65,129},{129,193},{193,1... | collective-permute-start | bytes 1179656 | tf_op jit(solution)/shard_map/ppermute | solution.py:172
  64.7 11.3 %collective-permute-done.3 = bf16[2,256,384]{2,1,0:T(8,128)(2,1)S(1)} collective-permute-done((bf16[2,256,384]{2,1,0:T(8,128)(2,1)S(1)}, bf16[2,256,384]{2,1,0:T(8,128)(2,1)S(1)}, u32[]{:S(2)}, u32[]{:S(2)}) %collective-permute-start.3) | collective-permute-done | bytes 393248 | tf_op jit(solution)/shard_map/ppermute | solution.py:172
  76.2 6.6 %collective-permute-done.6 = bf16[2,256,384]{2,1,0:T(8,128)(2,1)S(1)} collective-permute-done((bf16[2,256,384]{2,1,0:T(8,128)(2,1)S(1)}, bf16[2,256,384]{2,1,0:T(8,128)(2,1)S(1)}, u32[]{:S(2)}, u32[]{:S(2)}) %collective-permute-start.6) | collective-permute-done | bytes 393248 | tf_op jit(solution)/shard_map/ppermute | solution.py:172
  82.9 2.3 %collective-permute-start.8 = (bf16[6,256,384]{2,1,0:T(8,128)(2,1)S(1)}, bf16[6,256,384]{2,1,0:T(8,128)(2,1)}, u32[]{:S(2)}, u32[]{:S(2)}) collective-permute-start(bf16[6,256,384]{2,1,0:T(8,128)(2,1)S(1)} %constant_dynamic-update-slice_fusion.refs_1_), channel_id=1, source_target_pairs={{0,1},{1,0},{2,3},{3,2},{4,5},{5,4},{6,7},{7,6},{8,9},{9,8},{10,11... | collective-permute-start | bytes 3538952 | tf_op jit(solution)/shard_map/ppermute | solution.py:203
  85.2 2.0 %collective-permute-start.7 = (bf16[2,256,384]{2,1,0:T(8,128)(2,1)S(1)}, bf16[2,256,384]{2,1,0:T(8,128)(2,1)}, u32[]{:S(2)}, u32[]{:S(2)}) collective-permute-start(bf16[2,256,384]{2,1,0:T(8,128)(2,1)S(1)} %pad_maximum_fusion.1.refs_0_), channel_id=1, source_target_pairs={{0,1},{1,0},{2,3},{3,2},{4,5},{5,4},{6,7},{7,6},{8,9},{9,8},{10,11... | collective-permute-start | bytes 1179656 | tf_op jit(solution)/shard_map/ppermute | solution.py:203
  87.5 1.9 %collective-permute-start.10 = (bf16[2,256,640]{2,1,0:T(8,128)(2,1)S(1)}, bf16[2,256,640]{2,1,0:T(8,128)(2,1)}, u32[]{:S(2)}, u32[]{:S(2)}) collective-permute-start(bf16[2,256,640]{2,1,0:T(8,128)(2,1)S(1)} %pad_maximum_fusion.refs_0_), channel_id=1, source_target_pairs={{0,64},{64,128},{128,192},{192,0},{1,65},{65,129},{129,193},{193,1... | collective-permute-start | bytes 1966088 | tf_op jit(solution)/shard_map/ppermute | solution.py:172
  89.4 3.3 %collective-permute-start.9 = (bf16[2,256,640]{2,1,0:T(8,128)(2,1)S(1)}, bf16[2,256,640]{2,1,0:T(8,128)(2,1)}, u32[]{:S(2)}, u32[]{:S(2)}) collective-permute-start(bf16[2,256,640]{2,1,0:T(8,128)(2,1)S(1)} %pad_maximum_fusion.refs_0_), channel_id=1, source_target_pairs={{0,128},{64,192},{128,0},{192,64},{1,129},{65,193},{129,1},{193,65... | collective-permute-start | bytes 1966088 | tf_op jit(solution)/shard_map/ppermute | solution.py:172
  92.7 3.2 %collective-permute-start.4 = (bf16[2,256,640]{2,1,0:T(8,128)(2,1)S(1)}, bf16[2,256,640]{2,1,0:T(8,128)(2,1)}, u32[]{:S(2)}, u32[]{:S(2)}) collective-permute-start(bf16[2,256,640]{2,1,0:T(8,128)(2,1)S(1)} %pad_maximum_fusion.refs_0_), channel_id=1, source_target_pairs={{0,192},{64,0},{128,64},{192,128},{1,193},{65,1},{129,65},{193,129... | collective-permute-start | bytes 1966088 | tf_op jit(solution)/shard_map/ppermute | solution.py:172
  97.2 3.9 %columns.1 = bf16[256,512]{1,0:T(8,128)(2,1)S(1)} custom-call(s32[3]{0:T(128)S(1)} %pad_add_fusion.place, s32[8]{0:T(128)S(1)} %copy-done.4, f32[1,1024]{1,0:T(1,128)S(1)} %bitcast.21, bf16[256,1024]{1,0:T(8,128)(2,1)S(1)} %reshape.26.x_ref, bf16[2,256,384]{2,1,0:T(8,128)(2,1)S(1)} %pad_maximum_fusion.1.refs_0_, ...), custom_call_target="tpu_custom_call" | custom-call | flops 939524096 | bytes 6291456 | tf_op jit(solution)/shard_map/columns/pallas_call | solution.py:136
  101.9 15.8 %all-to-all-start.2 = ((bf16[64,4,512]{2,1,0:T(4,128)(2,1)}), bf16[64,4,512]{2,1,0:T(4,128)(2,1)S(1)}, u32[]{:S(2)}, u32[]{:S(2)}) async-start(bf16[64,4,512]{2,1,0:T(4,128)(2,1)} %reshape.27), calls=%async_computation.2 | async-start | bytes 524288 | tf_op jit(solution)/shard_map/all_to_all | solution.py:211
  117.7 2.4 %collective-permute-start.11 = (bf16[2,256,640]{2,1,0:T(8,128)(2,1)S(1)}, bf16[2,256,640]{2,1,0:T(8,128)(2,1)S(1)}, u32[]{:S(2)}, u32[]{:S(2)}) collective-permute-start(bf16[2,256,640]{2,1,0:T(8,128)(2,1)S(1)} %pad_maximum_fusion.refs_0_), channel_id=1, source_target_pairs={{0,1},{1,0},{2,3},{3,2},{4,5},{5,4},{6,7},{7,6},{8,9},{9,8},{10,11... | collective-permute-start | bytes 1966088 | tf_op jit(solution)/shard_map/ppermute | solution.py:203
  120.6 3.1 %collective-permute-start.14 = (bf16[2,256,640]{2,1,0:T(8,128)(2,1)}, bf16[2,256,640]{2,1,0:T(8,128)(2,1)S(1)}, u32[]{:S(2)}, u32[]{:S(2)}) collective-permute-start(bf16[2,256,640]{2,1,0:T(8,128)(2,1)} %collective-permute-done.10.refs_3_), channel_id=1, source_target_pairs={{0,1},{1,0},{2,3},{3,2},{4,5},{5,4},{6,7},{7,6},{8,9},{9,8},{10,11... | collective-permute-start | bytes 1966088 | tf_op jit(solution)/shard_map/ppermute | solution.py:203
  123.8 1.9 %collective-permute-start.13 = (bf16[2,256,640]{2,1,0:T(8,128)(2,1)}, bf16[2,256,640]{2,1,0:T(8,128)(2,1)S(1)}, u32[]{:S(2)}, u32[]{:S(2)}) collective-permute-start(bf16[2,256,640]{2,1,0:T(8,128)(2,1)} %collective-permute-done.9.refs_2_), channel_id=1, source_target_pairs={{0,1},{1,0},{2,3},{3,2},{4,5},{5,4},{6,7},{7,6},{8,9},{9,8},{10,11... | collective-permute-start | bytes 1966088 | tf_op jit(solution)/shard_map/ppermute | solution.py:203
  125.7 2.4 %collective-permute-start.12 = (bf16[2,256,640]{2,1,0:T(8,128)(2,1)}, bf16[2,256,640]{2,1,0:T(8,128)(2,1)S(1)}, u32[]{:S(2)}, u32[]{:S(2)}) collective-permute-start(bf16[2,256,640]{2,1,0:T(8,128)(2,1)} %collective-permute-done.4.refs_1_), channel_id=1, source_target_pairs={{0,1},{1,0},{2,3},{3,2},{4,5},{5,4},{6,7},{7,6},{8,9},{9,8},{10,11... | collective-permute-start | bytes 1966088 | tf_op jit(solution)/shard_map/ppermute | solution.py:203
  130.0 4.9 %rows.1 = (f32[256,1024]{1,0:T(8,128)S(1)}, bf16[512,1024]{1,0:T(8,128)(2,1)S(1)}, s32[1]{0:T(128)}) custom-call(s32[3]{0:T(128)S(1)} %pad_add_fusion.place, s32[8]{0:T(128)S(1)} %copy-done.5, f32[1,1024]{1,0:T(1,128)S(1)} %bitcast.22, bf16[256,1024]{1,0:T(8,128)(2,1)S(1)} %bitcast.20, bf16[2,256,640]{2,1,0:T(8,128)(2,1)S(1)} %pad_maximum_fusion.refs_0_, ...), custom_call_target="tpu_custom_call" | custom-call | flops 1048576 | bytes 1048576 | tf_op jit(solution)/shard_map/rows/pallas_call | solution.py:149
  136.6 4.8 %all-to-all-done.2 = bf16[64,4,512]{2,1,0:T(4,128)(2,1)S(1)} async-done(((bf16[64,4,512]{2,1,0:T(4,128)(2,1)}), bf16[64,4,512]{2,1,0:T(4,128)(2,1)S(1)}, u32[]{:S(2)}, u32[]{:S(2)}) %all-to-all-start.2) | async-done | bytes 262176 | tf_op jit(solution)/shard_map/all_to_all | solution.py:211
  (45 shorter events, 9.9 us)
Async XLA Ops:
  0.0 17.3 %copy-start = (bf16[1,1,256,1024]{3,2,1,0:T(8,128)(2,1)S(1)}, bf16[1,1,256,1024]{3,2,1,0:T(8,128)(2,1)}, u32[]{:S(2)}) copy-start(bf16[1,1,256,1024]{3,2,1,0:T(8,128)(2,1)} %param.6) | copy-start | bytes 1572868
  1.5 28.9 %all-to-all-start = ((bf16[16,16,512]{2,1,0:T(8,128)(2,1)}), bf16[16,16,512]{2,1,0:T(8,128)(2,1)S(1)}, u32[]{:S(2)}, u32[]{:S(2)}) async-start(bf16[16,16,512]{2,1,0:T(8,128)(2,1)} %broadcast_in_dim.7), calls=%async_computation | async-start | bytes 524288 | tf_op jit(solution)/shard_map/all_to_all | solution.py:184
  30.4 24.6 %collective-permute-start = (bf16[256,512]{1,0:T(8,128)(2,1)S(1)}, bf16[256,512]{1,0:T(8,128)(2,1)S(1)}, u32[]{:S(2)}, u32[]{:S(2)}) collective-permute-start(bf16[256,512]{1,0:T(8,128)(2,1)S(1)} %bitcast.23), channel_id=1, source_target_pairs={{0,256},{256,32},{32,288},{288,0},{1,257},{257,33},{33,289},{289,1... | collective-permute-start | bytes 786440 | tf_op jit(solution)/shard_map/ppermute | solution.py:172
  33.5 21.5 %collective-permute-start.1 = (bf16[256,512]{1,0:T(8,128)(2,1)S(1)}, bf16[256,512]{1,0:T(8,128)(2,1)S(1)}, u32[]{:S(2)}, u32[]{:S(2)}) collective-permute-start(bf16[256,512]{1,0:T(8,128)(2,1)S(1)} %bitcast.24), channel_id=1, source_target_pairs={{0,288},{256,0},{32,256},{288,32},{1,289},{257,1},{33,257},{289,33... | collective-permute-start | bytes 786440 | tf_op jit(solution)/shard_map/ppermute | solution.py:172
  36.9 18.1 %collective-permute-start.2 = (bf16[256,512]{1,0:T(8,128)(2,1)S(1)}, bf16[256,512]{1,0:T(8,128)(2,1)S(1)}, u32[]{:S(2)}, u32[]{:S(2)}) collective-permute-start(bf16[256,512]{1,0:T(8,128)(2,1)S(1)} %bitcast.25), channel_id=1, source_target_pairs={{0,32},{256,288},{32,0},{288,256},{1,33},{257,289},{33,1},{289,257... | collective-permute-start | bytes 786440 | tf_op jit(solution)/shard_map/ppermute | solution.py:172
  40.4 55.6 %all-to-all-start.1 = ((bf16[64,4,1024]{2,1,0:T(4,128)(2,1)}), bf16[64,4,1024]{2,1,0:T(4,128)(2,1)}, u32[]{:S(2)}, u32[]{:S(2)}) async-start(bf16[64,4,1024]{2,1,0:T(4,128)(2,1)} %reshape_reshape.3), calls=%async_computation.1 | async-start | bytes 1048576 | tf_op jit(solution)/shard_map/all_to_all | solution.py:187
  55.2 20.9 %collective-permute-start.3 = (bf16[2,256,384]{2,1,0:T(8,128)(2,1)S(1)}, bf16[2,256,384]{2,1,0:T(8,128)(2,1)S(1)}, u32[]{:S(2)}, u32[]{:S(2)}) collective-permute-start(bf16[2,256,384]{2,1,0:T(8,128)(2,1)S(1)} %pad_maximum_fusion.1.refs_0_), channel_id=1, source_target_pairs={{0,192},{64,0},{128,64},{192,128},{1,193},{65,1},{129,65},{193,129... | collective-permute-start | bytes 1179656 | tf_op jit(solution)/shard_map/ppermute | solution.py:172
  59.9 16.3 %collective-permute-start.5 = (bf16[2,256,384]{2,1,0:T(8,128)(2,1)S(1)}, bf16[2,256,384]{2,1,0:T(8,128)(2,1)S(1)}, u32[]{:S(2)}, u32[]{:S(2)}) collective-permute-start(bf16[2,256,384]{2,1,0:T(8,128)(2,1)S(1)} %pad_maximum_fusion.1.refs_0_), channel_id=1, source_target_pairs={{0,128},{64,192},{128,0},{192,64},{1,129},{65,193},{129,1},{193,65... | collective-permute-start | bytes 1179656 | tf_op jit(solution)/shard_map/ppermute | solution.py:172
  62.1 20.7 %collective-permute-start.6 = (bf16[2,256,384]{2,1,0:T(8,128)(2,1)S(1)}, bf16[2,256,384]{2,1,0:T(8,128)(2,1)S(1)}, u32[]{:S(2)}, u32[]{:S(2)}) collective-permute-start(bf16[2,256,384]{2,1,0:T(8,128)(2,1)S(1)} %pad_maximum_fusion.1.refs_0_), channel_id=1, source_target_pairs={{0,64},{64,128},{128,192},{192,0},{1,65},{65,129},{129,193},{193,1... | collective-permute-start | bytes 1179656 | tf_op jit(solution)/shard_map/ppermute | solution.py:172
  82.9 14.3 %collective-permute-start.8 = (bf16[6,256,384]{2,1,0:T(8,128)(2,1)S(1)}, bf16[6,256,384]{2,1,0:T(8,128)(2,1)}, u32[]{:S(2)}, u32[]{:S(2)}) collective-permute-start(bf16[6,256,384]{2,1,0:T(8,128)(2,1)S(1)} %constant_dynamic-update-slice_fusion.refs_1_), channel_id=1, source_target_pairs={{0,1},{1,0},{2,3},{3,2},{4,5},{5,4},{6,7},{7,6},{8,9},{9,8},{10,11... | collective-permute-start | bytes 3538952 | tf_op jit(solution)/shard_map/ppermute | solution.py:203
  85.2 11.9 %collective-permute-start.7 = (bf16[2,256,384]{2,1,0:T(8,128)(2,1)S(1)}, bf16[2,256,384]{2,1,0:T(8,128)(2,1)}, u32[]{:S(2)}, u32[]{:S(2)}) collective-permute-start(bf16[2,256,384]{2,1,0:T(8,128)(2,1)S(1)} %pad_maximum_fusion.1.refs_0_), channel_id=1, source_target_pairs={{0,1},{1,0},{2,3},{3,2},{4,5},{5,4},{6,7},{7,6},{8,9},{9,8},{10,11... | collective-permute-start | bytes 1179656 | tf_op jit(solution)/shard_map/ppermute | solution.py:203
  87.4 9.8 %copy-start.3 = (f32[1024]{0:T(1024)S(1)}, f32[1024]{0:T(1024)}, u32[]{:S(2)}) copy-start(f32[1024]{0:T(1024)} %param.7) | copy-start | bytes 12292
  87.4 9.8 %copy-start.4 = (s32[8]{0:T(128)S(1)}, s32[8]{0:T(128)}, u32[]{:S(2)}) copy-start(s32[8]{0:T(128)} %reach_ref.2) | copy-start | bytes 100
  87.5 33.2 %collective-permute-start.10 = (bf16[2,256,640]{2,1,0:T(8,128)(2,1)S(1)}, bf16[2,256,640]{2,1,0:T(8,128)(2,1)}, u32[]{:S(2)}, u32[]{:S(2)}) collective-permute-start(bf16[2,256,640]{2,1,0:T(8,128)(2,1)S(1)} %pad_maximum_fusion.refs_0_), channel_id=1, source_target_pairs={{0,64},{64,128},{128,192},{192,0},{1,65},{65,129},{129,193},{193,1... | collective-permute-start | bytes 1966088 | tf_op jit(solution)/shard_map/ppermute | solution.py:172
  89.4 34.4 %collective-permute-start.9 = (bf16[2,256,640]{2,1,0:T(8,128)(2,1)S(1)}, bf16[2,256,640]{2,1,0:T(8,128)(2,1)}, u32[]{:S(2)}, u32[]{:S(2)}) collective-permute-start(bf16[2,256,640]{2,1,0:T(8,128)(2,1)S(1)} %pad_maximum_fusion.refs_0_), channel_id=1, source_target_pairs={{0,128},{64,192},{128,0},{192,64},{1,129},{65,193},{129,1},{193,65... | collective-permute-start | bytes 1966088 | tf_op jit(solution)/shard_map/ppermute | solution.py:172
  92.7 33.0 %collective-permute-start.4 = (bf16[2,256,640]{2,1,0:T(8,128)(2,1)S(1)}, bf16[2,256,640]{2,1,0:T(8,128)(2,1)}, u32[]{:S(2)}, u32[]{:S(2)}) collective-permute-start(bf16[2,256,640]{2,1,0:T(8,128)(2,1)S(1)} %pad_maximum_fusion.refs_0_), channel_id=1, source_target_pairs={{0,192},{64,0},{128,64},{192,128},{1,193},{65,1},{129,65},{193,129... | collective-permute-start | bytes 1966088 | tf_op jit(solution)/shard_map/ppermute | solution.py:172
  97.2 32.9 %copy-start.5 = (s32[8]{0:T(128)S(1)}, s32[8]{0:T(128)}, u32[]{:S(2)}) copy-start(s32[8]{0:T(128)} %reach_ref.3) | copy-start | bytes 100
  101.9 39.5 %all-to-all-start.2 = ((bf16[64,4,512]{2,1,0:T(4,128)(2,1)}), bf16[64,4,512]{2,1,0:T(4,128)(2,1)S(1)}, u32[]{:S(2)}, u32[]{:S(2)}) async-start(bf16[64,4,512]{2,1,0:T(4,128)(2,1)} %reshape.27), calls=%async_computation.2 | async-start | bytes 524288 | tf_op jit(solution)/shard_map/all_to_all | solution.py:211
  117.7 10.4 %collective-permute-start.11 = (bf16[2,256,640]{2,1,0:T(8,128)(2,1)S(1)}, bf16[2,256,640]{2,1,0:T(8,128)(2,1)S(1)}, u32[]{:S(2)}, u32[]{:S(2)}) collective-permute-start(bf16[2,256,640]{2,1,0:T(8,128)(2,1)S(1)} %pad_maximum_fusion.refs_0_), channel_id=1, source_target_pairs={{0,1},{1,0},{2,3},{3,2},{4,5},{5,4},{6,7},{7,6},{8,9},{9,8},{10,11... | collective-permute-start | bytes 1966088 | tf_op jit(solution)/shard_map/ppermute | solution.py:203
  120.6 7.5 %collective-permute-start.14 = (bf16[2,256,640]{2,1,0:T(8,128)(2,1)}, bf16[2,256,640]{2,1,0:T(8,128)(2,1)S(1)}, u32[]{:S(2)}, u32[]{:S(2)}) collective-permute-start(bf16[2,256,640]{2,1,0:T(8,128)(2,1)} %collective-permute-done.10.refs_3_), channel_id=1, source_target_pairs={{0,1},{1,0},{2,3},{3,2},{4,5},{5,4},{6,7},{7,6},{8,9},{9,8},{10,11... | collective-permute-start | bytes 1966088 | tf_op jit(solution)/shard_map/ppermute | solution.py:203
  123.8 4.4 %collective-permute-start.13 = (bf16[2,256,640]{2,1,0:T(8,128)(2,1)}, bf16[2,256,640]{2,1,0:T(8,128)(2,1)S(1)}, u32[]{:S(2)}, u32[]{:S(2)}) collective-permute-start(bf16[2,256,640]{2,1,0:T(8,128)(2,1)} %collective-permute-done.9.refs_2_), channel_id=1, source_target_pairs={{0,1},{1,0},{2,3},{3,2},{4,5},{5,4},{6,7},{7,6},{8,9},{9,8},{10,11... | collective-permute-start | bytes 1966088 | tf_op jit(solution)/shard_map/ppermute | solution.py:203
  125.7 4.3 %collective-permute-start.12 = (bf16[2,256,640]{2,1,0:T(8,128)(2,1)}, bf16[2,256,640]{2,1,0:T(8,128)(2,1)S(1)}, u32[]{:S(2)}, u32[]{:S(2)}) collective-permute-start(bf16[2,256,640]{2,1,0:T(8,128)(2,1)} %collective-permute-done.4.refs_1_), channel_id=1, source_target_pairs={{0,1},{1,0},{2,3},{3,2},{4,5},{5,4},{6,7},{7,6},{8,9},{9,8},{10,11... | collective-permute-start | bytes 1966088 | tf_op jit(solution)/shard_map/ppermute | solution.py:203
  135.0 1.0 copy-start.1
  136.0 5.7 %copy-start.2 = (bf16[512,1024]{1,0:T(8,128)(2,1)S(1)}, bf16[512,1024]{1,0:T(8,128)(2,1)}, u32[]{:S(2)}) copy-start(bf16[512,1024]{1,0:T(8,128)(2,1)} %copy-done.1) | copy-start | bytes 3145732

commit v13 on v12

--- a/solution.py
+++ b/solution.py
@@ -18,14 +18,16 @@
 FAR = 1 << 20
 COLUMN_PIECES = (1, 3)
 REST_PIECES = (1, 1, 1, 1)
-
-
-def assemble(place, refs, sizes, lanes, w_ref, first, width):
+COLUMN_ORDER = (0, 2, 1, 3)
+REST_ORDER = (0, 1, 2, 3)
+
+
+def assemble(place, refs, sizes, order, lanes, w_ref, first, width):
     xh, y, core = place[0], place[1], place[2]
     pieces = [(i, j) for i, size in enumerate(sizes) for j in range(size)]
     for t in range(Y):
         cols = pl.ds(pl.multiple_of(first + width * ((y + t) & 3), 128), width)
-        piece, at = pieces[t]
+        piece, at = pieces[order.index(t)]
         for u in range(XH):
             for ref, c in ((refs[piece], core), (refs[len(sizes) + piece], 1 - core)):
                 rows = pl.ds(pl.multiple_of(16 * c, 16), 16)
@@ -84,7 +86,7 @@
 
 def column_kernel(place, reach_ref, gain_ref, x_ref, *refs):
     *parts, out_ref, w_ref, n_ref, qkv_ref = refs
-    assemble(place, parts, COLUMN_PIECES, slice(0, PART), w_ref, 0, PART)
+    assemble(place, parts, COLUMN_PIECES, COLUMN_ORDER, slice(0, PART), w_ref, 0, PART)
     i, j = pairs()
     back = (i >> 2) - (j >> 2)
     dist = jnp.where((((i ^ j) & 3) == 0) & (back >= 0), back, FAR)
@@ -94,12 +96,12 @@
 def row_kernel(place, reach_ref, gain_ref, x_ref, *refs):
     *parts, base_ref, low_ref, done_ref, w_ref, n_ref, qkv_ref, a_ref, o_ref = refs
     done_ref[0] = 0
-    assemble(place, parts, REST_PIECES, slice(0, PART), w_ref, 0, PART)
+    assemble(place, parts, REST_PIECES, REST_ORDER, slice(0, PART), w_ref, 0, PART)
     i, j = pairs()
     dist = jnp.where(j <= i, (i >> 5) - (j >> 5), FAR)
     attend(reach_ref, gain_ref, x_ref, w_ref, n_ref, qkv_ref, a_ref, dist)
-    assemble(place, parts, REST_PIECES, slice(PART, PART + 128), o_ref, 0, 128)
-    assemble(place, parts, REST_PIECES, slice(PART + 128, PART + 256), o_ref, 512, 128)
+    assemble(place, parts, REST_PIECES, REST_ORDER, slice(PART, PART + 128), o_ref, 0, 128)
+    assemble(place, parts, REST_PIECES, REST_ORDER, slice(PART + 128, PART + 256), o_ref, 512, 128)
     for n in range(0, FEATURES, 256):
         base_ref[:, n : n + 256] = x_ref[:, n : n + 256].astype(jnp.float32) + jnp.dot(
             a_ref[...],
@@ -168,10 +170,11 @@
 
 def ring(part, axes, order):
     size = len(order)
-    return [
-        lax.ppermute(part, axes, [(order[i], order[(i - t) % size]) for i in range(size)])
-        for t in range(1, size)
-    ]
+    got = {
+        t: lax.ppermute(part, axes, [(order[i], order[(i - t) % size]) for i in range(size)])
+        for t in sorted(range(1, size), key=lambda t: -min(t, size - t))
+    }
+    return [got[t] for t in range(1, size)]
 
 
 def body(tokens, norm_gain, w_qkv, w_out, row_blocks, col_rows):
@@ -180,8 +183,8 @@
     gain = norm_gain.reshape(1, FEATURES)
     place = jnp.stack([xh, y, c]).astype(jnp.int32)
 
-    block = jnp.concatenate([w_qkv, w_out], axis=1)
-    column = lax.all_to_all(jnp.broadcast_to(block, (Z, 16, 512)), "z", split_axis=0, concat_axis=0)
+    block = [jnp.broadcast_to(w, (Z, *w.shape)) for w in (w_qkv, w_out)]
+    column = lax.all_to_all(jnp.concatenate(block, axis=2), "z", split_axis=0, concat_axis=0)
 
     sent, column = lax.optimization_barrier((rows.reshape(64, 4, FEATURES), column))
     turned = lax.all_to_all(sent, SEQ, split_axis=0, concat_axis=0)
@@ -204,7 +207,7 @@
 
     held, *came = plane(near)
     beside = came[0]
-    came = jnp.concatenate(came)
+    came = jnp.concatenate([came[t - 1] for t in COLUMN_ORDER[1:]])
     col_mid = column_attention(
         place, col_rows, gain, turned, [held, came, swap(held), swap(came)]
     )

time: 144 us -> 142 us (0.986)
  waiting for transfers between devices: 37.4 us -> 32.9 us
  starting transfers between devices: 88.1 us -> 90.6 us
    ppermute x9, waiting for transfers between devices: 18.5 us -> 12.3 us  [ring(): lax.ppermute(part, axes, [(order[i], order[(i - t) % size]) for i in rang...]
    ppermute x9, starting transfers between devices: 27.8 us -> 30.4 us  [ring(): lax.ppermute(part, axes, [(order[i], order[(i - t) % size]) for i in rang...]
  transfers between devices with their start and end apart: 18 -> 18, of which waited for: 6 -> 5; matrix products, arithmetic and copies ran while one was open for 2% -> 2% of each run, Pallas kernels for 6% -> 6%
where the time goes in v13:
time: 142 us
  starting transfers between devices  90.6 us (64%)
  waiting for transfers between devices  32.9 us (23%)
  Pallas kernels  10.1 us (7%)
  local copies, waits for them, and re-layouts  5.7 us (4%)
    ppermute x9, starting transfers between devices, ring(): lax.ppermute(part, axes, [(order[i], order[(i - t) % size]) for i in rang...  30.4 us
    all_to_all x1, starting transfers between devices, body(): lax.all_to_all(col_mid.reshape(64, 4, HALF), SEQ, split_axis=0, concat_ax...  16 us
    all_to_all x1, starting transfers between devices, body(): lax.all_to_all(jnp.concatenate(block, axis=2), 'z', split_axis=0, concat_...  15.7 us
    all_to_all x1, starting transfers between devices, body(): turned = lax.all_to_all(sent, SEQ, split_axis=0, concat_axis=0)  14.6 us
    ppermute x6, starting transfers between devices, swap(): return lax.ppermute(part, 'c', [(0, 1), (1, 0)])  13.8 us
    ppermute x9, waiting for transfers between devices, ring(): lax.ppermute(part, axes, [(order[i], order[(i - t) % size]) for i in rang...  12.3 us
    all_to_all x1, waiting for transfers between devices, body(): lax.all_to_all(jnp.concatenate(block, axis=2), 'z', split_axis=0, concat_...  12.1 us
    all_to_all x1, waiting for transfers between devices, body(): lax.all_to_all(col_mid.reshape(64, 4, HALF), SEQ, split_axis=0, concat_ax...  6.22 us
  transfers between devices with their start and end apart: 18, of which 5 were waited for; matrix products, arithmetic and copies ran while one was open for 2% of the time, Pallas kernels for 6%

profile of v13, /device:TPU:1, one launch (start us, length us, event | category | flops | bytes accessed | tf_op | source)
XLA Modules:
  0.0 141.5 jit_solution(4512153419797271935)
XLA Ops:
  2.2 15.7 %all-to-all-start = ((bf16[16,16,512]{2,1,0:T(8,128)(2,1)}), bf16[16,16,512]{2,1,0:T(8,128)(2,1)S(1)}, u32[]{:S(2)}, u32[]{:S(2)}) async-start(bf16[16,16,512]{2,1,0:T(8,128)(2,1)} %pad_maximum_fusion.2), calls=%async_computation | async-start | bytes 524288 | tf_op jit(solution)/shard_map/all_to_all | solution.py:187
  19.0 12.1 %all-to-all-done = bf16[16,16,512]{2,1,0:T(8,128)(2,1)S(1)} async-done(((bf16[16,16,512]{2,1,0:T(8,128)(2,1)}), bf16[16,16,512]{2,1,0:T(8,128)(2,1)S(1)}, u32[]{:S(2)}, u32[]{:S(2)}) %all-to-all-start) | async-done | bytes 262176 | tf_op jit(solution)/shard_map/all_to_all | solution.py:187
  31.1 3.1 %collective-permute-start = (bf16[256,512]{1,0:T(8,128)(2,1)S(1)}, bf16[256,512]{1,0:T(8,128)(2,1)S(1)}, u32[]{:S(2)}, u32[]{:S(2)}) collective-permute-start(bf16[256,512]{1,0:T(8,128)(2,1)S(1)} %bitcast.23), channel_id=1, source_target_pairs={{0,256},{256,32},{32,288},{288,0},{1,257},{257,33},{33,289},{289,1... | collective-permute-start | bytes 786440 | tf_op jit(solution)/shard_map/ppermute | solution.py:174
  34.2 3.4 %collective-permute-start.1 = (bf16[256,512]{1,0:T(8,128)(2,1)S(1)}, bf16[256,512]{1,0:T(8,128)(2,1)S(1)}, u32[]{:S(2)}, u32[]{:S(2)}) collective-permute-start(bf16[256,512]{1,0:T(8,128)(2,1)S(1)} %bitcast.24), channel_id=1, source_target_pairs={{0,288},{256,0},{32,256},{288,32},{1,289},{257,1},{33,257},{289,33... | collective-permute-start | bytes 786440 | tf_op jit(solution)/shard_map/ppermute | solution.py:174
  37.6 3.4 %collective-permute-start.2 = (bf16[256,512]{1,0:T(8,128)(2,1)S(1)}, bf16[256,512]{1,0:T(8,128)(2,1)S(1)}, u32[]{:S(2)}, u32[]{:S(2)}) collective-permute-start(bf16[256,512]{1,0:T(8,128)(2,1)S(1)} %bitcast.25), channel_id=1, source_target_pairs={{0,32},{256,288},{32,0},{288,256},{1,33},{257,289},{33,1},{289,257... | collective-permute-start | bytes 786440 | tf_op jit(solution)/shard_map/ppermute | solution.py:174
  41.1 14.6 %all-to-all-start.1 = ((bf16[64,4,1024]{2,1,0:T(4,128)(2,1)}), bf16[64,4,1024]{2,1,0:T(4,128)(2,1)}, u32[]{:S(2)}, u32[]{:S(2)}) async-start(bf16[64,4,1024]{2,1,0:T(4,128)(2,1)} %reshape_reshape.3), calls=%async_computation.1 | async-start | bytes 1048576 | tf_op jit(solution)/shard_map/all_to_all | solution.py:190
  55.9 4.8 %collective-permute-start.5 = (bf16[2,256,384]{2,1,0:T(8,128)(2,1)S(1)}, bf16[2,256,384]{2,1,0:T(8,128)(2,1)S(1)}, u32[]{:S(2)}, u32[]{:S(2)}) collective-permute-start(bf16[2,256,384]{2,1,0:T(8,128)(2,1)S(1)} %pad_maximum_fusion.1.refs_0_), channel_id=1, source_target_pairs={{0,128},{64,192},{128,0},{192,64},{1,129},{65,193},{129,1},{193,65... | collective-permute-start | bytes 1179656 | tf_op jit(solution)/shard_map/ppermute | solution.py:174
  60.8 2.7 %collective-permute-start.3 = (bf16[2,256,384]{2,1,0:T(8,128)(2,1)S(1)}, bf16[2,256,384]{2,1,0:T(8,128)(2,1)S(1)}, u32[]{:S(2)}, u32[]{:S(2)}) collective-permute-start(bf16[2,256,384]{2,1,0:T(8,128)(2,1)S(1)} %pad_maximum_fusion.1.refs_0_), channel_id=1, source_target_pairs={{0,192},{64,0},{128,64},{192,128},{1,193},{65,1},{129,65},{193,129... | collective-permute-start | bytes 1179656 | tf_op jit(solution)/shard_map/ppermute | solution.py:174
  63.4 2.6 %collective-permute-start.6 = (bf16[2,256,384]{2,1,0:T(8,128)(2,1)S(1)}, bf16[2,256,384]{2,1,0:T(8,128)(2,1)S(1)}, u32[]{:S(2)}, u32[]{:S(2)}) collective-permute-start(bf16[2,256,384]{2,1,0:T(8,128)(2,1)S(1)} %pad_maximum_fusion.1.refs_0_), channel_id=1, source_target_pairs={{0,64},{64,128},{128,192},{192,0},{1,65},{65,129},{129,193},{193,1... | collective-permute-start | bytes 1179656 | tf_op jit(solution)/shard_map/ppermute | solution.py:174
  66.1 3.5 %collective-permute-done.5 = bf16[2,256,384]{2,1,0:T(8,128)(2,1)S(1)} collective-permute-done((bf16[2,256,384]{2,1,0:T(8,128)(2,1)S(1)}, bf16[2,256,384]{2,1,0:T(8,128)(2,1)S(1)}, u32[]{:S(2)}, u32[]{:S(2)}) %collective-permute-start.5) | collective-permute-done | bytes 393248 | tf_op jit(solution)/shard_map/ppermute | solution.py:174
  69.6 8.8 %collective-permute-done.3 = bf16[2,256,384]{2,1,0:T(8,128)(2,1)S(1)} collective-permute-done((bf16[2,256,384]{2,1,0:T(8,128)(2,1)S(1)}, bf16[2,256,384]{2,1,0:T(8,128)(2,1)S(1)}, u32[]{:S(2)}, u32[]{:S(2)}) %collective-permute-start.3) | collective-permute-done | bytes 393248 | tf_op jit(solution)/shard_map/ppermute | solution.py:174
  78.5 3.2 %collective-permute-start.8 = (bf16[6,256,384]{2,1,0:T(8,128)(2,1)S(1)}, bf16[6,256,384]{2,1,0:T(8,128)(2,1)}, u32[]{:S(2)}, u32[]{:S(2)}) collective-permute-start(bf16[6,256,384]{2,1,0:T(8,128)(2,1)S(1)} %constant_dynamic-update-slice_fusion.refs_1_), channel_id=1, source_target_pairs={{0,1},{1,0},{2,3},{3,2},{4,5},{5,4},{6,7},{7,6},{8,9},{9,8},{10,11... | collective-permute-start | bytes 3538952 | tf_op jit(solution)/shard_map/ppermute | solution.py:206
  83.9 2.9 %collective-permute-start.10 = (bf16[2,256,640]{2,1,0:T(8,128)(2,1)S(1)}, bf16[2,256,640]{2,1,0:T(8,128)(2,1)}, u32[]{:S(2)}, u32[]{:S(2)}) collective-permute-start(bf16[2,256,640]{2,1,0:T(8,128)(2,1)S(1)} %pad_maximum_fusion.refs_0_), channel_id=1, source_target_pairs={{0,64},{64,128},{128,192},{192,0},{1,65},{65,129},{129,193},{193,1... | collective-permute-start | bytes 1966088 | tf_op jit(solution)/shard_map/ppermute | solution.py:174
  86.8 4.5 %collective-permute-start.9 = (bf16[2,256,640]{2,1,0:T(8,128)(2,1)S(1)}, bf16[2,256,640]{2,1,0:T(8,128)(2,1)}, u32[]{:S(2)}, u32[]{:S(2)}) collective-permute-start(bf16[2,256,640]{2,1,0:T(8,128)(2,1)S(1)} %pad_maximum_fusion.refs_0_), channel_id=1, source_target_pairs={{0,128},{64,192},{128,0},{192,64},{1,129},{65,193},{129,1},{193,65... | collective-permute-start | bytes 1966088 | tf_op jit(solution)/shard_map/ppermute | solution.py:174
  91.3 2.9 %collective-permute-start.4 = (bf16[2,256,640]{2,1,0:T(8,128)(2,1)S(1)}, bf16[2,256,640]{2,1,0:T(8,128)(2,1)}, u32[]{:S(2)}, u32[]{:S(2)}) collective-permute-start(bf16[2,256,640]{2,1,0:T(8,128)(2,1)S(1)} %pad_maximum_fusion.refs_0_), channel_id=1, source_target_pairs={{0,192},{64,0},{128,64},{192,128},{1,193},{65,1},{129,65},{193,129... | collective-permute-start | bytes 1966088 | tf_op jit(solution)/shard_map/ppermute | solution.py:174
  95.6 3.9 %columns.1 = bf16[256,512]{1,0:T(8,128)(2,1)S(1)} custom-call(s32[3]{0:T(128)S(1)} %pad_add_fusion.place, s32[8]{0:T(128)S(1)} %copy-done.4, f32[1,1024]{1,0:T(1,128)S(1)} %bitcast.21, bf16[256,1024]{1,0:T(8,128)(2,1)S(1)} %reshape.26.x_ref, bf16[2,256,384]{2,1,0:T(8,128)(2,1)S(1)} %pad_maximum_fusion.1.refs_0_, ...), custom_call_target="tpu_custom_call" | custom-call | flops 939524096 | bytes 6291456 | tf_op jit(solution)/shard_map/columns/pallas_call | solution.py:138
  100.3 16.0 %all-to-all-start.2 = ((bf16[64,4,512]{2,1,0:T(4,128)(2,1)}), bf16[64,4,512]{2,1,0:T(4,128)(2,1)S(1)}, u32[]{:S(2)}, u32[]{:S(2)}) async-start(bf16[64,4,512]{2,1,0:T(4,128)(2,1)} %reshape.27), calls=%async_computation.2 | async-start | bytes 524288 | tf_op jit(solution)/shard_map/all_to_all | solution.py:214
  116.3 2.4 %collective-permute-start.11 = (bf16[2,256,640]{2,1,0:T(8,128)(2,1)S(1)}, bf16[2,256,640]{2,1,0:T(8,128)(2,1)S(1)}, u32[]{:S(2)}, u32[]{:S(2)}) collective-permute-start(bf16[2,256,640]{2,1,0:T(8,128)(2,1)S(1)} %pad_maximum_fusion.refs_0_), channel_id=1, source_target_pairs={{0,1},{1,0},{2,3},{3,2},{4,5},{5,4},{6,7},{7,6},{8,9},{9,8},{10,11... | collective-permute-start | bytes 1966088 | tf_op jit(solution)/shard_map/ppermute | solution.py:206
  118.7 2.0 %collective-permute-start.14 = (bf16[2,256,640]{2,1,0:T(8,128)(2,1)}, bf16[2,256,640]{2,1,0:T(8,128)(2,1)S(1)}, u32[]{:S(2)}, u32[]{:S(2)}) collective-permute-start(bf16[2,256,640]{2,1,0:T(8,128)(2,1)} %collective-permute-done.10.refs_3_), channel_id=1, source_target_pairs={{0,1},{1,0},{2,3},{3,2},{4,5},{5,4},{6,7},{7,6},{8,9},{9,8},{10,11... | collective-permute-start | bytes 1966088 | tf_op jit(solution)/shard_map/ppermute | solution.py:206
  120.7 2.4 %collective-permute-start.13 = (bf16[2,256,640]{2,1,0:T(8,128)(2,1)}, bf16[2,256,640]{2,1,0:T(8,128)(2,1)S(1)}, u32[]{:S(2)}, u32[]{:S(2)}) collective-permute-start(bf16[2,256,640]{2,1,0:T(8,128)(2,1)} %collective-permute-done.9.refs_2_), channel_id=1, source_target_pairs={{0,1},{1,0},{2,3},{3,2},{4,5},{5,4},{6,7},{7,6},{8,9},{9,8},{10,11... | collective-permute-start | bytes 1966088 | tf_op jit(solution)/shard_map/ppermute | solution.py:206
  123.1 2.0 %collective-permute-start.12 = (bf16[2,256,640]{2,1,0:T(8,128)(2,1)}, bf16[2,256,640]{2,1,0:T(8,128)(2,1)S(1)}, u32[]{:S(2)}, u32[]{:S(2)}) collective-permute-start(bf16[2,256,640]{2,1,0:T(8,128)(2,1)} %collective-permute-done.4.refs_1_), channel_id=1, source_target_pairs={{0,1},{1,0},{2,3},{3,2},{4,5},{5,4},{6,7},{7,6},{8,9},{9,8},{10,11... | collective-permute-start | bytes 1966088 | tf_op jit(solution)/shard_map/ppermute | solution.py:206
  125.1 2.2 %collective-permute-done.12.refs_5_ = bf16[2,256,640]{2,1,0:T(8,128)(2,1)S(1)} collective-permute-done((bf16[2,256,640]{2,1,0:T(8,128)(2,1)}, bf16[2,256,640]{2,1,0:T(8,128)(2,1)S(1)}, u32[]{:S(2)}, u32[]{:S(2)}) %collective-permute-start.12) | collective-permute-done | bytes 655392 | tf_op jit(solution)/shard_map/ppermute | solution.py:206
  127.3 4.9 %rows.1 = (f32[256,1024]{1,0:T(8,128)S(1)}, bf16[512,1024]{1,0:T(8,128)(2,1)S(1)}, s32[1]{0:T(128)}) custom-call(s32[3]{0:T(128)S(1)} %pad_add_fusion.place, s32[8]{0:T(128)S(1)} %copy-done.5, f32[1,1024]{1,0:T(1,128)S(1)} %bitcast.22, bf16[256,1024]{1,0:T(8,128)(2,1)S(1)} %bitcast.20, bf16[2,256,640]{2,1,0:T(8,128)(2,1)S(1)} %pad_maximum_fusion.refs_0_, ...), custom_call_target="tpu_custom_call" | custom-call | flops 1048576 | bytes 1048576 | tf_op jit(solution)/shard_map/rows/pallas_call | solution.py:151
  133.9 6.2 %all-to-all-done.2 = bf16[64,4,512]{2,1,0:T(4,128)(2,1)S(1)} async-done(((bf16[64,4,512]{2,1,0:T(4,128)(2,1)}), bf16[64,4,512]{2,1,0:T(4,128)(2,1)S(1)}, u32[]{:S(2)}, u32[]{:S(2)}) %all-to-all-start.2) | async-done | bytes 262176 | tf_op jit(solution)/shard_map/all_to_all | solution.py:214
  (46 shorter events, 10.1 us)
Async XLA Ops:
  0.0 18.0 %copy-start = (bf16[1,1,256,1024]{3,2,1,0:T(8,128)(2,1)S(1)}, bf16[1,1,256,1024]{3,2,1,0:T(8,128)(2,1)}, u32[]{:S(2)}) copy-start(bf16[1,1,256,1024]{3,2,1,0:T(8,128)(2,1)} %param.6) | copy-start | bytes 1572868
  2.2 28.9 %all-to-all-start = ((bf16[16,16,512]{2,1,0:T(8,128)(2,1)}), bf16[16,16,512]{2,1,0:T(8,128)(2,1)S(1)}, u32[]{:S(2)}, u32[]{:S(2)}) async-start(bf16[16,16,512]{2,1,0:T(8,128)(2,1)} %pad_maximum_fusion.2), calls=%async_computation | async-start | bytes 524288 | tf_op jit(solution)/shard_map/all_to_all | solution.py:187
  31.1 24.6 %collective-permute-start = (bf16[256,512]{1,0:T(8,128)(2,1)S(1)}, bf16[256,512]{1,0:T(8,128)(2,1)S(1)}, u32[]{:S(2)}, u32[]{:S(2)}) collective-permute-start(bf16[256,512]{1,0:T(8,128)(2,1)S(1)} %bitcast.23), channel_id=1, source_target_pairs={{0,256},{256,32},{32,288},{288,0},{1,257},{257,33},{33,289},{289,1... | collective-permute-start | bytes 786440 | tf_op jit(solution)/shard_map/ppermute | solution.py:174
  34.2 21.5 %collective-permute-start.1 = (bf16[256,512]{1,0:T(8,128)(2,1)S(1)}, bf16[256,512]{1,0:T(8,128)(2,1)S(1)}, u32[]{:S(2)}, u32[]{:S(2)}) collective-permute-start(bf16[256,512]{1,0:T(8,128)(2,1)S(1)} %bitcast.24), channel_id=1, source_target_pairs={{0,288},{256,0},{32,256},{288,32},{1,289},{257,1},{33,257},{289,33... | collective-permute-start | bytes 786440 | tf_op jit(solution)/shard_map/ppermute | solution.py:174
  37.6 18.1 %collective-permute-start.2 = (bf16[256,512]{1,0:T(8,128)(2,1)S(1)}, bf16[256,512]{1,0:T(8,128)(2,1)S(1)}, u32[]{:S(2)}, u32[]{:S(2)}) collective-permute-start(bf16[256,512]{1,0:T(8,128)(2,1)S(1)} %bitcast.25), channel_id=1, source_target_pairs={{0,32},{256,288},{32,0},{288,256},{1,33},{257,289},{33,1},{289,257... | collective-permute-start | bytes 786440 | tf_op jit(solution)/shard_map/ppermute | solution.py:174
  41.1 53.3 %all-to-all-start.1 = ((bf16[64,4,1024]{2,1,0:T(4,128)(2,1)}), bf16[64,4,1024]{2,1,0:T(4,128)(2,1)}, u32[]{:S(2)}, u32[]{:S(2)}) async-start(bf16[64,4,1024]{2,1,0:T(4,128)(2,1)} %reshape_reshape.3), calls=%async_computation.1 | async-start | bytes 1048576 | tf_op jit(solution)/shard_map/all_to_all | solution.py:190
  55.9 13.7 %collective-permute-start.5 = (bf16[2,256,384]{2,1,0:T(8,128)(2,1)S(1)}, bf16[2,256,384]{2,1,0:T(8,128)(2,1)S(1)}, u32[]{:S(2)}, u32[]{:S(2)}) collective-permute-start(bf16[2,256,384]{2,1,0:T(8,128)(2,1)S(1)} %pad_maximum_fusion.1.refs_0_), channel_id=1, source_target_pairs={{0,128},{64,192},{128,0},{192,64},{1,129},{65,193},{129,1},{193,65... | collective-permute-start | bytes 1179656 | tf_op jit(solution)/shard_map/ppermute | solution.py:174
  60.8 17.6 %collective-permute-start.3 = (bf16[2,256,384]{2,1,0:T(8,128)(2,1)S(1)}, bf16[2,256,384]{2,1,0:T(8,128)(2,1)S(1)}, u32[]{:S(2)}, u32[]{:S(2)}) collective-permute-start(bf16[2,256,384]{2,1,0:T(8,128)(2,1)S(1)} %pad_maximum_fusion.1.refs_0_), channel_id=1, source_target_pairs={{0,192},{64,0},{128,64},{192,128},{1,193},{65,1},{129,65},{193,129... | collective-permute-start | bytes 1179656 | tf_op jit(solution)/shard_map/ppermute | solution.py:174
  63.4 15.0 %collective-permute-start.6 = (bf16[2,256,384]{2,1,0:T(8,128)(2,1)S(1)}, bf16[2,256,384]{2,1,0:T(8,128)(2,1)S(1)}, u32[]{:S(2)}, u32[]{:S(2)}) collective-permute-start(bf16[2,256,384]{2,1,0:T(8,128)(2,1)S(1)} %pad_maximum_fusion.1.refs_0_), channel_id=1, source_target_pairs={{0,64},{64,128},{128,192},{192,0},{1,65},{65,129},{129,193},{193,1... | collective-permute-start | bytes 1179656 | tf_op jit(solution)/shard_map/ppermute | solution.py:174
  78.5 17.0 %collective-permute-start.8 = (bf16[6,256,384]{2,1,0:T(8,128)(2,1)S(1)}, bf16[6,256,384]{2,1,0:T(8,128)(2,1)}, u32[]{:S(2)}, u32[]{:S(2)}) collective-permute-start(bf16[6,256,384]{2,1,0:T(8,128)(2,1)S(1)} %constant_dynamic-update-slice_fusion.refs_1_), channel_id=1, source_target_pairs={{0,1},{1,0},{2,3},{3,2},{4,5},{5,4},{6,7},{7,6},{8,9},{9,8},{10,11... | collective-permute-start | bytes 3538952 | tf_op jit(solution)/shard_map/ppermute | solution.py:206
  81.7 13.8 %collective-permute-start.7 = (bf16[2,256,384]{2,1,0:T(8,128)(2,1)S(1)}, bf16[2,256,384]{2,1,0:T(8,128)(2,1)}, u32[]{:S(2)}, u32[]{:S(2)}) collective-permute-start(bf16[2,256,384]{2,1,0:T(8,128)(2,1)S(1)} %pad_maximum_fusion.1.refs_0_), channel_id=1, source_target_pairs={{0,1},{1,0},{2,3},{3,2},{4,5},{5,4},{6,7},{7,6},{8,9},{9,8},{10,11... | collective-permute-start | bytes 1179656 | tf_op jit(solution)/shard_map/ppermute | solution.py:206
  83.8 11.8 %copy-start.3 = (f32[1024]{0:T(1024)S(1)}, f32[1024]{0:T(1024)}, u32[]{:S(2)}) copy-start(f32[1024]{0:T(1024)} %param.7) | copy-start | bytes 12292
  83.8 11.8 %copy-start.4 = (s32[8]{0:T(128)S(1)}, s32[8]{0:T(128)}, u32[]{:S(2)}) copy-start(s32[8]{0:T(128)} %reach_ref.2) | copy-start | bytes 100
  83.9 34.8 %collective-permute-start.10 = (bf16[2,256,640]{2,1,0:T(8,128)(2,1)S(1)}, bf16[2,256,640]{2,1,0:T(8,128)(2,1)}, u32[]{:S(2)}, u32[]{:S(2)}) collective-permute-start(bf16[2,256,640]{2,1,0:T(8,128)(2,1)S(1)} %pad_maximum_fusion.refs_0_), channel_id=1, source_target_pairs={{0,64},{64,128},{128,192},{192,0},{1,65},{65,129},{129,193},{193,1... | collective-permute-start | bytes 1966088 | tf_op jit(solution)/shard_map/ppermute | solution.py:174
  86.8 33.9 %collective-permute-start.9 = (bf16[2,256,640]{2,1,0:T(8,128)(2,1)S(1)}, bf16[2,256,640]{2,1,0:T(8,128)(2,1)}, u32[]{:S(2)}, u32[]{:S(2)}) collective-permute-start(bf16[2,256,640]{2,1,0:T(8,128)(2,1)S(1)} %pad_maximum_fusion.refs_0_), channel_id=1, source_target_pairs={{0,128},{64,192},{128,0},{192,64},{1,129},{65,193},{129,1},{193,65... | collective-permute-start | bytes 1966088 | tf_op jit(solution)/shard_map/ppermute | solution.py:174
  91.3 31.7 %collective-permute-start.4 = (bf16[2,256,640]{2,1,0:T(8,128)(2,1)S(1)}, bf16[2,256,640]{2,1,0:T(8,128)(2,1)}, u32[]{:S(2)}, u32[]{:S(2)}) collective-permute-start(bf16[2,256,640]{2,1,0:T(8,128)(2,1)S(1)} %pad_maximum_fusion.refs_0_), channel_id=1, source_target_pairs={{0,192},{64,0},{128,64},{192,128},{1,193},{65,1},{129,65},{193,129... | collective-permute-start | bytes 1966088 | tf_op jit(solution)/shard_map/ppermute | solution.py:174
  95.5 31.7 %copy-start.5 = (s32[8]{0:T(128)S(1)}, s32[8]{0:T(128)}, u32[]{:S(2)}) copy-start(s32[8]{0:T(128)} %reach_ref.3) | copy-start | bytes 100
  100.3 39.8 %all-to-all-start.2 = ((bf16[64,4,512]{2,1,0:T(4,128)(2,1)}), bf16[64,4,512]{2,1,0:T(4,128)(2,1)S(1)}, u32[]{:S(2)}, u32[]{:S(2)}) async-start(bf16[64,4,512]{2,1,0:T(4,128)(2,1)} %reshape.27), calls=%async_computation.2 | async-start | bytes 524288 | tf_op jit(solution)/shard_map/all_to_all | solution.py:214
  116.3 8.7 %collective-permute-start.11 = (bf16[2,256,640]{2,1,0:T(8,128)(2,1)S(1)}, bf16[2,256,640]{2,1,0:T(8,128)(2,1)S(1)}, u32[]{:S(2)}, u32[]{:S(2)}) collective-permute-start(bf16[2,256,640]{2,1,0:T(8,128)(2,1)S(1)} %pad_maximum_fusion.refs_0_), channel_id=1, source_target_pairs={{0,1},{1,0},{2,3},{3,2},{4,5},{5,4},{6,7},{7,6},{8,9},{9,8},{10,11... | collective-permute-start | bytes 1966088 | tf_op jit(solution)/shard_map/ppermute | solution.py:206
  118.7 6.3 %collective-permute-start.14 = (bf16[2,256,640]{2,1,0:T(8,128)(2,1)}, bf16[2,256,640]{2,1,0:T(8,128)(2,1)S(1)}, u32[]{:S(2)}, u32[]{:S(2)}) collective-permute-start(bf16[2,256,640]{2,1,0:T(8,128)(2,1)} %collective-permute-done.10.refs_3_), channel_id=1, source_target_pairs={{0,1},{1,0},{2,3},{3,2},{4,5},{5,4},{6,7},{7,6},{8,9},{9,8},{10,11... | collective-permute-start | bytes 1966088 | tf_op jit(solution)/shard_map/ppermute | solution.py:206
  120.7 4.4 %collective-permute-start.13 = (bf16[2,256,640]{2,1,0:T(8,128)(2,1)}, bf16[2,256,640]{2,1,0:T(8,128)(2,1)S(1)}, u32[]{:S(2)}, u32[]{:S(2)}) collective-permute-start(bf16[2,256,640]{2,1,0:T(8,128)(2,1)} %collective-permute-done.9.refs_2_), channel_id=1, source_target_pairs={{0,1},{1,0},{2,3},{3,2},{4,5},{5,4},{6,7},{7,6},{8,9},{9,8},{10,11... | collective-permute-start | bytes 1966088 | tf_op jit(solution)/shard_map/ppermute | solution.py:206
  123.1 4.2 %collective-permute-start.12 = (bf16[2,256,640]{2,1,0:T(8,128)(2,1)}, bf16[2,256,640]{2,1,0:T(8,128)(2,1)S(1)}, u32[]{:S(2)}, u32[]{:S(2)}) collective-permute-start(bf16[2,256,640]{2,1,0:T(8,128)(2,1)} %collective-permute-done.4.refs_1_), channel_id=1, source_target_pairs={{0,1},{1,0},{2,3},{3,2},{4,5},{5,4},{6,7},{7,6},{8,9},{9,8},{10,11... | collective-permute-start | bytes 1966088 | tf_op jit(solution)/shard_map/ppermute | solution.py:206
  132.2 1.0 copy-start.1
  133.2 7.1 %copy-start.2 = (bf16[512,1024]{1,0:T(8,128)(2,1)S(1)}, bf16[512,1024]{1,0:T(8,128)(2,1)}, u32[]{:S(2)}) copy-start(bf16[512,1024]{1,0:T(8,128)(2,1)} %copy-done.1) | copy-start | bytes 3145732

commit v14 on v13

--- a/solution.py
+++ b/solution.py
@@ -111,6 +111,12 @@
     low_ref[...] = o_ref[Z:].reshape(HALF, FEATURES)
 
 
+def copies_kernel(qkv_ref, out_ref, copies_ref):
+    for z in range(Z):
+        copies_ref[z, :, :PART] = qkv_ref[...]
+        copies_ref[z, :, PART:] = out_ref[...]
+
+
 def last_kernel(base_ref, col_ref, low_ref, out_ref):
     for n in range(0, FEATURES, 256):
         out_ref[:, n : n + 256] = (
@@ -183,8 +189,14 @@
     gain = norm_gain.reshape(1, FEATURES)
     place = jnp.stack([xh, y, c]).astype(jnp.int32)
 
-    block = [jnp.broadcast_to(w, (Z, *w.shape)) for w in (w_qkv, w_out)]
-    column = lax.all_to_all(jnp.concatenate(block, axis=2), "z", split_axis=0, concat_axis=0)
+    block = pl.pallas_call(
+        copies_kernel,
+        out_shape=jax.ShapeDtypeStruct((Z, 16, 512), jnp.bfloat16),
+        in_specs=[VMEM, VMEM],
+        out_specs=VMEM,
+        name="copies",
+    )(w_qkv, w_out)
+    column = lax.all_to_all(block, "z", split_axis=0, concat_axis=0)
 
     sent, column = lax.optimization_barrier((rows.reshape(64, 4, FEATURES), column))
     turned = lax.all_to_all(sent, SEQ, split_axis=0, concat_axis=0)
@@ -207,9 +219,12 @@
 
     held, *came = plane(near)
     beside = came[0]
+    held, came[1] = lax.optimization_barrier((held, came[1]))
+    first = swap(held)
     came = jnp.concatenate([came[t - 1] for t in COLUMN_ORDER[1:]])
+    came, first = lax.optimization_barrier((came, first))
     col_mid = column_attention(
-        place, col_rows, gain, turned, [held, came, swap(held), swap(came)]
+        place, col_rows, gain, turned, [held, came, first, swap(came)]
     )
     col_out = lax.all_to_all(col_mid.reshape(64, 4, HALF), SEQ, split_axis=0, concat_axis=0)
 

time: 142 us -> 139 us (0.979)
  waiting for transfers between devices: 32.9 us -> 26 us
  starting transfers between devices: 90.6 us -> 93.7 us
    ppermute x9, waiting for transfers between devices: 12.3 us -> 8.91 us  [ring(): lax.ppermute(part, axes, [(order[i], order[(i - t) % size]) for i in rang...]
    ppermute x6, starting transfers between devices: 13.8 us -> 16.5 us  [swap(): return lax.ppermute(part, 'c', [(0, 1), (1, 0)])]
    all_to_all x1, waiting for transfers between devices: 6.22 us -> 4.07 us  [body(): lax.all_to_all(col_mid.reshape(64, 4, HALF), SEQ, split_axis=0, concat_ax...]
    broadcast_in_dim x2 -> x0, local copies, waits for them, and re-layouts: 1.48 us -> none  [body(): block = [jnp.broadcast_to(w, (Z, *w.shape)) for w in (w_qkv, w_out)]]
    pallas_call x0 -> x1, Pallas kernels: none -> 1.44 us  [body(): pl.pallas_call(copies_kernel, out_shape=jax.ShapeDtypeStruct((Z, 16, 512)...]
  transfers between devices with their start and end apart: 18 -> 18, of which waited for: 5 -> 7; matrix products, arithmetic and copies ran while one was open for 2% -> 3% of each run, Pallas kernels for 6% -> 6%
where the time goes in v14:
time: 139 us; the launch traced here: 138 us
  starting transfers between devices  93.7 us (67%)
  waiting for transfers between devices  26 us (19%)
  Pallas kernels  11.4 us (8%)
  local copies, waits for them, and re-layouts  5.1 us (4%)
    ppermute x9, starting transfers between devices, ring(): lax.ppermute(part, axes, [(order[i], order[(i - t) % size]) for i in rang...  31 us
    ppermute x6, starting transfers between devices, swap(): return lax.ppermute(part, 'c', [(0, 1), (1, 0)])  16.5 us
    all_to_all x1, starting transfers between devices, body(): column = lax.all_to_all(block, 'z', split_axis=0, concat_axis=0)  15.7 us
    all_to_all x1, starting transfers between devices, body(): lax.all_to_all(col_mid.reshape(64, 4, HALF), SEQ, split_axis=0, concat_ax...  15.7 us
    all_to_all x1, starting transfers between devices, body(): turned = lax.all_to_all(sent, SEQ, split_axis=0, concat_axis=0)  14.8 us
    all_to_all x1, waiting for transfers between devices, body(): column = lax.all_to_all(block, 'z', split_axis=0, concat_axis=0)  11.1 us
    ppermute x9, waiting for transfers between devices, ring(): lax.ppermute(part, axes, [(order[i], order[(i - t) % size]) for i in rang...  8.91 us
    pallas_call x1, Pallas kernels, row_attention(): pl.pallas_call(row_kernel, out_shape=[jax.ShapeDtypeStruct((STRIDE, FEATU...  4.93 us
  transfers between devices with their start and end apart: 18, of which 7 were waited for; matrix products, arithmetic and copies ran while one was open for 3% of the time, Pallas kernels for 6%

profile of v14, /device:TPU:1, one launch (start us, length us, event | category | flops | bytes accessed | tf_op | source)
XLA Modules:
  0.0 137.9 jit_solution(13358003268383406064)
XLA Ops:
  1.4 15.7 %all-to-all-start = ((bf16[16,16,512]{2,1,0:T(8,128)(2,1)}), bf16[16,16,512]{2,1,0:T(8,128)(2,1)S(1)}, u32[]{:S(2)}, u32[]{:S(2)}) async-start(bf16[16,16,512]{2,1,0:T(8,128)(2,1)} %copies.1), calls=%async_computation | async-start | bytes 524288 | tf_op jit(solution)/shard_map/all_to_all | solution.py:199
  17.2 2.0 %reshape_reshape.3 = bf16[64,4,1024]{2,1,0:T(4,128)(2,1)} reshape(bf16[1,1,256,1024]{3,2,1,0:T(8,128)(2,1)} %param.6) | data formatting | bytes 1048576 | tf_op jit(solution)/shard_map/reshape;reshape | solution.py:201
  19.2 11.1 %all-to-all-done = bf16[16,16,512]{2,1,0:T(8,128)(2,1)S(1)} async-done(((bf16[16,16,512]{2,1,0:T(8,128)(2,1)}), bf16[16,16,512]{2,1,0:T(8,128)(2,1)S(1)}, u32[]{:S(2)}, u32[]{:S(2)}) %all-to-all-start) | async-done | bytes 262176 | tf_op jit(solution)/shard_map/all_to_all | solution.py:199
  30.3 4.4 %collective-permute-start.1 = (bf16[256,512]{1,0:T(8,128)(2,1)S(1)}, bf16[256,512]{1,0:T(8,128)(2,1)S(1)}, u32[]{:S(2)}, u32[]{:S(2)}) collective-permute-start(bf16[256,512]{1,0:T(8,128)(2,1)S(1)} %bitcast.23), channel_id=1, source_target_pairs={{0,288},{256,0},{32,256},{288,32},{1,289},{257,1},{33,257},{289,33... | collective-permute-start | bytes 786440 | tf_op jit(solution)/shard_map/ppermute | solution.py:180
  34.7 2.4 %collective-permute-start.2 = (bf16[256,512]{1,0:T(8,128)(2,1)S(1)}, bf16[256,512]{1,0:T(8,128)(2,1)S(1)}, u32[]{:S(2)}, u32[]{:S(2)}) collective-permute-start(bf16[256,512]{1,0:T(8,128)(2,1)S(1)} %bitcast.24), channel_id=1, source_target_pairs={{0,32},{256,288},{32,0},{288,256},{1,33},{257,289},{33,1},{289,257... | collective-permute-start | bytes 786440 | tf_op jit(solution)/shard_map/ppermute | solution.py:180
  37.1 2.5 %collective-permute-start = (bf16[256,512]{1,0:T(8,128)(2,1)S(1)}, bf16[256,512]{1,0:T(8,128)(2,1)S(1)}, u32[]{:S(2)}, u32[]{:S(2)}) collective-permute-start(bf16[256,512]{1,0:T(8,128)(2,1)S(1)} %bitcast.25), channel_id=1, source_target_pairs={{0,256},{256,32},{32,288},{288,0},{1,257},{257,33},{33,289},{289,1... | collective-permute-start | bytes 786440 | tf_op jit(solution)/shard_map/ppermute | solution.py:180
  39.7 14.8 %all-to-all-start.1 = ((bf16[64,4,1024]{2,1,0:T(4,128)(2,1)}), bf16[64,4,1024]{2,1,0:T(4,128)(2,1)}, u32[]{:S(2)}, u32[]{:S(2)}) async-start(bf16[64,4,1024]{2,1,0:T(4,128)(2,1)} %reshape_reshape.3), calls=%async_computation.1 | async-start | bytes 1048576 | tf_op jit(solution)/shard_map/all_to_all | solution.py:202
  54.7 4.8 %collective-permute-start.5 = (bf16[2,256,384]{2,1,0:T(8,128)(2,1)S(1)}, bf16[2,256,384]{2,1,0:T(8,128)(2,1)S(1)}, u32[]{:S(2)}, u32[]{:S(2)}) collective-permute-start(bf16[2,256,384]{2,1,0:T(8,128)(2,1)S(1)} %pad_maximum_fusion.2.refs_0_), channel_id=1, source_target_pairs={{0,128},{64,192},{128,0},{192,64},{1,129},{65,193},{129,1},{193,65... | collective-permute-start | bytes 1179656 | tf_op jit(solution)/shard_map/ppermute | solution.py:180
  59.5 2.3 %collective-permute-start.6 = (bf16[2,256,384]{2,1,0:T(8,128)(2,1)S(1)}, bf16[2,256,384]{2,1,0:T(8,128)(2,1)S(1)}, u32[]{:S(2)}, u32[]{:S(2)}) collective-permute-start(bf16[2,256,384]{2,1,0:T(8,128)(2,1)S(1)} %pad_maximum_fusion.2.refs_0_), channel_id=1, source_target_pairs={{0,64},{64,128},{128,192},{192,0},{1,65},{65,129},{129,193},{193,1... | collective-permute-start | bytes 1179656 | tf_op jit(solution)/shard_map/ppermute | solution.py:180
  61.8 4.2 %collective-permute-start.3 = (bf16[2,256,384]{2,1,0:T(8,128)(2,1)S(1)}, bf16[2,256,384]{2,1,0:T(8,128)(2,1)S(1)}, u32[]{:S(2)}, u32[]{:S(2)}) collective-permute-start(bf16[2,256,384]{2,1,0:T(8,128)(2,1)S(1)} %pad_maximum_fusion.2.refs_0_), channel_id=1, source_target_pairs={{0,192},{64,0},{128,64},{192,128},{1,193},{65,1},{129,65},{193,129... | collective-permute-start | bytes 1179656 | tf_op jit(solution)/shard_map/ppermute | solution.py:180
  66.0 2.4 %collective-permute-done.5 = bf16[2,256,384]{2,1,0:T(8,128)(2,1)S(1)} collective-permute-done((bf16[2,256,384]{2,1,0:T(8,128)(2,1)S(1)}, bf16[2,256,384]{2,1,0:T(8,128)(2,1)S(1)}, u32[]{:S(2)}, u32[]{:S(2)}) %collective-permute-start.5) | collective-permute-done | bytes 393248 | tf_op jit(solution)/shard_map/ppermute | solution.py:180
  68.4 4.2 %collective-permute-start.7 = (bf16[2,256,384]{2,1,0:T(8,128)(2,1)S(1)}, bf16[2,256,384]{2,1,0:T(8,128)(2,1)S(1)}, u32[]{:S(2)}, u32[]{:S(2)}) collective-permute-start(bf16[2,256,384]{2,1,0:T(8,128)(2,1)S(1)} %pad_maximum_fusion.2.refs_0_), channel_id=1, source_target_pairs={{0,1},{1,0},{2,3},{3,2},{4,5},{5,4},{6,7},{7,6},{8,9},{9,8},{10,11... | collective-permute-start | bytes 1179656 | tf_op jit(solution)/shard_map/ppermute | solution.py:218
  72.5 5.1 %collective-permute-done.6 = bf16[2,256,384]{2,1,0:T(8,128)(2,1)S(1)} collective-permute-done((bf16[2,256,384]{2,1,0:T(8,128)(2,1)S(1)}, bf16[2,256,384]{2,1,0:T(8,128)(2,1)S(1)}, u32[]{:S(2)}, u32[]{:S(2)}) %collective-permute-start.6) | collective-permute-done | bytes 393248 | tf_op jit(solution)/shard_map/ppermute | solution.py:180
  77.8 2.6 %collective-permute-start.8 = (bf16[6,256,384]{2,1,0:T(8,128)(2,1)S(1)}, bf16[6,256,384]{2,1,0:T(8,128)(2,1)}, u32[]{:S(2)}, u32[]{:S(2)}) collective-permute-start(bf16[6,256,384]{2,1,0:T(8,128)(2,1)S(1)} %pad_maximum_fusion.refs_1_), channel_id=1, source_target_pairs={{0,1},{1,0},{2,3},{3,2},{4,5},{5,4},{6,7},{7,6},{8,9},{9,8},{10,11... | collective-permute-start | bytes 3538952 | tf_op jit(solution)/shard_map/ppermute | solution.py:218
  80.7 3.0 %collective-permute-start.10 = (bf16[2,256,640]{2,1,0:T(8,128)(2,1)S(1)}, bf16[2,256,640]{2,1,0:T(8,128)(2,1)}, u32[]{:S(2)}, u32[]{:S(2)}) collective-permute-start(bf16[2,256,640]{2,1,0:T(8,128)(2,1)S(1)} %pad_maximum_fusion.1.refs_0_), channel_id=1, source_target_pairs={{0,64},{64,128},{128,192},{192,0},{1,65},{65,129},{129,193},{193,1... | collective-permute-start | bytes 1966088 | tf_op jit(solution)/shard_map/ppermute | solution.py:180
  83.7 4.4 %collective-permute-start.9 = (bf16[2,256,640]{2,1,0:T(8,128)(2,1)S(1)}, bf16[2,256,640]{2,1,0:T(8,128)(2,1)}, u32[]{:S(2)}, u32[]{:S(2)}) collective-permute-start(bf16[2,256,640]{2,1,0:T(8,128)(2,1)S(1)} %pad_maximum_fusion.1.refs_0_), channel_id=1, source_target_pairs={{0,128},{64,192},{128,0},{192,64},{1,129},{65,193},{129,1},{193,65... | collective-permute-start | bytes 1966088 | tf_op jit(solution)/shard_map/ppermute | solution.py:180
  88.1 3.0 %collective-permute-start.4 = (bf16[2,256,640]{2,1,0:T(8,128)(2,1)S(1)}, bf16[2,256,640]{2,1,0:T(8,128)(2,1)}, u32[]{:S(2)}, u32[]{:S(2)}) collective-permute-start(bf16[2,256,640]{2,1,0:T(8,128)(2,1)S(1)} %pad_maximum_fusion.1.refs_0_), channel_id=1, source_target_pairs={{0,192},{64,0},{128,64},{192,128},{1,193},{65,1},{129,65},{193,129... | collective-permute-start | bytes 1966088 | tf_op jit(solution)/shard_map/ppermute | solution.py:180
  92.4 3.8 %columns.1 = bf16[256,512]{1,0:T(8,128)(2,1)S(1)} custom-call(s32[3]{0:T(128)S(1)} %pad_add_fusion.place, s32[8]{0:T(128)S(1)} %copy-done.4, f32[1,1024]{1,0:T(1,128)S(1)} %bitcast.21, bf16[256,1024]{1,0:T(8,128)(2,1)S(1)} %reshape.26.x_ref, bf16[2,256,384]{2,1,0:T(8,128)(2,1)S(1)} %pad_maximum_fusion.2.refs_0_, ...), custom_call_target="tpu_custom_call" | custom-call | flops 939524096 | bytes 6291456 | tf_op jit(solution)/shard_map/columns/pallas_call | solution.py:144
  97.0 15.7 %all-to-all-start.2 = ((bf16[64,4,512]{2,1,0:T(4,128)(2,1)}), bf16[64,4,512]{2,1,0:T(4,128)(2,1)S(1)}, u32[]{:S(2)}, u32[]{:S(2)}) async-start(bf16[64,4,512]{2,1,0:T(4,128)(2,1)} %reshape.27), calls=%async_computation.2 | async-start | bytes 524288 | tf_op jit(solution)/shard_map/all_to_all | solution.py:229
  112.7 2.4 %collective-permute-start.11 = (bf16[2,256,640]{2,1,0:T(8,128)(2,1)S(1)}, bf16[2,256,640]{2,1,0:T(8,128)(2,1)S(1)}, u32[]{:S(2)}, u32[]{:S(2)}) collective-permute-start(bf16[2,256,640]{2,1,0:T(8,128)(2,1)S(1)} %pad_maximum_fusion.1.refs_0_), channel_id=1, source_target_pairs={{0,1},{1,0},{2,3},{3,2},{4,5},{5,4},{6,7},{7,6},{8,9},{9,8},{10,11... | collective-permute-start | bytes 1966088 | tf_op jit(solution)/shard_map/ppermute | solution.py:218
  116.5 3.0 %collective-permute-start.12 = (bf16[2,256,640]{2,1,0:T(8,128)(2,1)}, bf16[2,256,640]{2,1,0:T(8,128)(2,1)S(1)}, u32[]{:S(2)}, u32[]{:S(2)}) collective-permute-start(bf16[2,256,640]{2,1,0:T(8,128)(2,1)} %collective-permute-done.4.refs_1_), channel_id=1, source_target_pairs={{0,1},{1,0},{2,3},{3,2},{4,5},{5,4},{6,7},{7,6},{8,9},{9,8},{10,11... | collective-permute-start | bytes 1966088 | tf_op jit(solution)/shard_map/ppermute | solution.py:218
  121.4 2.4 %collective-permute-start.14 = (bf16[2,256,640]{2,1,0:T(8,128)(2,1)}, bf16[2,256,640]{2,1,0:T(8,128)(2,1)S(1)}, u32[]{:S(2)}, u32[]{:S(2)}) collective-permute-start(bf16[2,256,640]{2,1,0:T(8,128)(2,1)} %collective-permute-done.10.refs_3_), channel_id=1, source_target_pairs={{0,1},{1,0},{2,3},{3,2},{4,5},{5,4},{6,7},{7,6},{8,9},{9,8},{10,11... | collective-permute-start | bytes 1966088 | tf_op jit(solution)/shard_map/ppermute | solution.py:218
  125.8 4.9 %rows.1 = (f32[256,1024]{1,0:T(8,128)S(1)}, bf16[512,1024]{1,0:T(8,128)(2,1)S(1)}, s32[1]{0:T(128)}) custom-call(s32[3]{0:T(128)S(1)} %pad_add_fusion.place, s32[8]{0:T(128)S(1)} %copy-done.5, f32[1,1024]{1,0:T(1,128)S(1)} %bitcast.22, bf16[256,1024]{1,0:T(8,128)(2,1)S(1)} %bitcast.20, bf16[2,256,640]{2,1,0:T(8,128)(2,1)S(1)} %pad_maximum_fusion.1.refs_0_, ...), custom_call_target="tpu_custom_call" | custom-call | flops 1048576 | bytes 1048576 | tf_op jit(solution)/shard_map/rows/pallas_call | solution.py:157
  132.4 4.1 %all-to-all-done.2 = bf16[64,4,512]{2,1,0:T(4,128)(2,1)S(1)} async-done(((bf16[64,4,512]{2,1,0:T(4,128)(2,1)}), bf16[64,4,512]{2,1,0:T(4,128)(2,1)S(1)}, u32[]{:S(2)}, u32[]{:S(2)}) %all-to-all-start.2) | async-done | bytes 262176 | tf_op jit(solution)/shard_map/all_to_all | solution.py:229
  (42 shorter events, 11.6 us)
Async XLA Ops:
  1.4 28.9 %all-to-all-start = ((bf16[16,16,512]{2,1,0:T(8,128)(2,1)}), bf16[16,16,512]{2,1,0:T(8,128)(2,1)S(1)}, u32[]{:S(2)}, u32[]{:S(2)}) async-start(bf16[16,16,512]{2,1,0:T(8,128)(2,1)} %copies.1), calls=%async_computation | async-start | bytes 524288 | tf_op jit(solution)/shard_map/all_to_all | solution.py:199
  30.3 24.1 %collective-permute-start.1 = (bf16[256,512]{1,0:T(8,128)(2,1)S(1)}, bf16[256,512]{1,0:T(8,128)(2,1)S(1)}, u32[]{:S(2)}, u32[]{:S(2)}) collective-permute-start(bf16[256,512]{1,0:T(8,128)(2,1)S(1)} %bitcast.23), channel_id=1, source_target_pairs={{0,288},{256,0},{32,256},{288,32},{1,289},{257,1},{33,257},{289,33... | collective-permute-start | bytes 786440 | tf_op jit(solution)/shard_map/ppermute | solution.py:180
  34.7 19.7 %collective-permute-start.2 = (bf16[256,512]{1,0:T(8,128)(2,1)S(1)}, bf16[256,512]{1,0:T(8,128)(2,1)S(1)}, u32[]{:S(2)}, u32[]{:S(2)}) collective-permute-start(bf16[256,512]{1,0:T(8,128)(2,1)S(1)} %bitcast.24), channel_id=1, source_target_pairs={{0,32},{256,288},{32,0},{288,256},{1,33},{257,289},{33,1},{289,257... | collective-permute-start | bytes 786440 | tf_op jit(solution)/shard_map/ppermute | solution.py:180
  37.1 17.3 %collective-permute-start = (bf16[256,512]{1,0:T(8,128)(2,1)S(1)}, bf16[256,512]{1,0:T(8,128)(2,1)S(1)}, u32[]{:S(2)}, u32[]{:S(2)}) collective-permute-start(bf16[256,512]{1,0:T(8,128)(2,1)S(1)} %bitcast.25), channel_id=1, source_target_pairs={{0,256},{256,32},{32,288},{288,0},{1,257},{257,33},{33,289},{289,1... | collective-permute-start | bytes 786440 | tf_op jit(solution)/shard_map/ppermute | solution.py:180
  39.7 51.5 %all-to-all-start.1 = ((bf16[64,4,1024]{2,1,0:T(4,128)(2,1)}), bf16[64,4,1024]{2,1,0:T(4,128)(2,1)}, u32[]{:S(2)}, u32[]{:S(2)}) async-start(bf16[64,4,1024]{2,1,0:T(4,128)(2,1)} %reshape_reshape.3), calls=%async_computation.1 | async-start | bytes 1048576 | tf_op jit(solution)/shard_map/all_to_all | solution.py:202
  54.7 13.7 %collective-permute-start.5 = (bf16[2,256,384]{2,1,0:T(8,128)(2,1)S(1)}, bf16[2,256,384]{2,1,0:T(8,128)(2,1)S(1)}, u32[]{:S(2)}, u32[]{:S(2)}) collective-permute-start(bf16[2,256,384]{2,1,0:T(8,128)(2,1)S(1)} %pad_maximum_fusion.2.refs_0_), channel_id=1, source_target_pairs={{0,128},{64,192},{128,0},{192,64},{1,129},{65,193},{129,1},{193,65... | collective-permute-start | bytes 1179656 | tf_op jit(solution)/shard_map/ppermute | solution.py:180
  59.5 18.1 %collective-permute-start.6 = (bf16[2,256,384]{2,1,0:T(8,128)(2,1)S(1)}, bf16[2,256,384]{2,1,0:T(8,128)(2,1)S(1)}, u32[]{:S(2)}, u32[]{:S(2)}) collective-permute-start(bf16[2,256,384]{2,1,0:T(8,128)(2,1)S(1)} %pad_maximum_fusion.2.refs_0_), channel_id=1, source_target_pairs={{0,64},{64,128},{128,192},{192,0},{1,65},{65,129},{129,193},{193,1... | collective-permute-start | bytes 1179656 | tf_op jit(solution)/shard_map/ppermute | solution.py:180
  61.8 15.8 %collective-permute-start.3 = (bf16[2,256,384]{2,1,0:T(8,128)(2,1)S(1)}, bf16[2,256,384]{2,1,0:T(8,128)(2,1)S(1)}, u32[]{:S(2)}, u32[]{:S(2)}) collective-permute-start(bf16[2,256,384]{2,1,0:T(8,128)(2,1)S(1)} %pad_maximum_fusion.2.refs_0_), channel_id=1, source_target_pairs={{0,192},{64,0},{128,64},{192,128},{1,193},{65,1},{129,65},{193,129... | collective-permute-start | bytes 1179656 | tf_op jit(solution)/shard_map/ppermute | solution.py:180
  68.4 9.4 %collective-permute-start.7 = (bf16[2,256,384]{2,1,0:T(8,128)(2,1)S(1)}, bf16[2,256,384]{2,1,0:T(8,128)(2,1)S(1)}, u32[]{:S(2)}, u32[]{:S(2)}) collective-permute-start(bf16[2,256,384]{2,1,0:T(8,128)(2,1)S(1)} %pad_maximum_fusion.2.refs_0_), channel_id=1, source_target_pairs={{0,1},{1,0},{2,3},{3,2},{4,5},{5,4},{6,7},{7,6},{8,9},{9,8},{10,11... | collective-permute-start | bytes 1179656 | tf_op jit(solution)/shard_map/ppermute | solution.py:218
  77.8 14.5 %collective-permute-start.8 = (bf16[6,256,384]{2,1,0:T(8,128)(2,1)S(1)}, bf16[6,256,384]{2,1,0:T(8,128)(2,1)}, u32[]{:S(2)}, u32[]{:S(2)}) collective-permute-start(bf16[6,256,384]{2,1,0:T(8,128)(2,1)S(1)} %pad_maximum_fusion.refs_1_), channel_id=1, source_target_pairs={{0,1},{1,0},{2,3},{3,2},{4,5},{5,4},{6,7},{7,6},{8,9},{9,8},{10,11... | collective-permute-start | bytes 3538952 | tf_op jit(solution)/shard_map/ppermute | solution.py:218
  80.6 11.8 %copy-start.3 = (f32[1024]{0:T(1024)S(1)}, f32[1024]{0:T(1024)}, u32[]{:S(2)}) copy-start(f32[1024]{0:T(1024)} %param.7) | copy-start | bytes 12292
  80.6 11.8 %copy-start.4 = (s32[8]{0:T(128)S(1)}, s32[8]{0:T(128)}, u32[]{:S(2)}) copy-start(s32[8]{0:T(128)} %reach_ref.2) | copy-start | bytes 100
  80.7 34.4 %collective-permute-start.10 = (bf16[2,256,640]{2,1,0:T(8,128)(2,1)S(1)}, bf16[2,256,640]{2,1,0:T(8,128)(2,1)}, u32[]{:S(2)}, u32[]{:S(2)}) collective-permute-start(bf16[2,256,640]{2,1,0:T(8,128)(2,1)S(1)} %pad_maximum_fusion.1.refs_0_), channel_id=1, source_target_pairs={{0,64},{64,128},{128,192},{192,0},{1,65},{65,129},{129,193},{193,1... | collective-permute-start | bytes 1966088 | tf_op jit(solution)/shard_map/ppermute | solution.py:180
  83.7 31.5 %collective-permute-start.9 = (bf16[2,256,640]{2,1,0:T(8,128)(2,1)S(1)}, bf16[2,256,640]{2,1,0:T(8,128)(2,1)}, u32[]{:S(2)}, u32[]{:S(2)}) collective-permute-start(bf16[2,256,640]{2,1,0:T(8,128)(2,1)S(1)} %pad_maximum_fusion.1.refs_0_), channel_id=1, source_target_pairs={{0,128},{64,192},{128,0},{192,64},{1,129},{65,193},{129,1},{193,65... | collective-permute-start | bytes 1966088 | tf_op jit(solution)/shard_map/ppermute | solution.py:180
  88.1 28.4 %collective-permute-start.4 = (bf16[2,256,640]{2,1,0:T(8,128)(2,1)S(1)}, bf16[2,256,640]{2,1,0:T(8,128)(2,1)}, u32[]{:S(2)}, u32[]{:S(2)}) collective-permute-start(bf16[2,256,640]{2,1,0:T(8,128)(2,1)S(1)} %pad_maximum_fusion.1.refs_0_), channel_id=1, source_target_pairs={{0,192},{64,0},{128,64},{192,128},{1,193},{65,1},{129,65},{193,129... | collective-permute-start | bytes 1966088 | tf_op jit(solution)/shard_map/ppermute | solution.py:180
  92.4 33.4 %copy-start.5 = (s32[8]{0:T(128)S(1)}, s32[8]{0:T(128)}, u32[]{:S(2)}) copy-start(s32[8]{0:T(128)} %reach_ref.3) | copy-start | bytes 100
  96.2 29.6 %copy-start = (bf16[1,1,256,1024]{3,2,1,0:T(8,128)(2,1)S(1)}, bf16[1,1,256,1024]{3,2,1,0:T(8,128)(2,1)}, u32[]{:S(2)}) copy-start(bf16[1,1,256,1024]{3,2,1,0:T(8,128)(2,1)} %param.6) | copy-start | bytes 1572868
  97.0 39.5 %all-to-all-start.2 = ((bf16[64,4,512]{2,1,0:T(4,128)(2,1)}), bf16[64,4,512]{2,1,0:T(4,128)(2,1)S(1)}, u32[]{:S(2)}, u32[]{:S(2)}) async-start(bf16[64,4,512]{2,1,0:T(4,128)(2,1)} %reshape.27), calls=%async_computation.2 | async-start | bytes 524288 | tf_op jit(solution)/shard_map/all_to_all | solution.py:229
  112.7 11.2 %collective-permute-start.11 = (bf16[2,256,640]{2,1,0:T(8,128)(2,1)S(1)}, bf16[2,256,640]{2,1,0:T(8,128)(2,1)S(1)}, u32[]{:S(2)}, u32[]{:S(2)}) collective-permute-start(bf16[2,256,640]{2,1,0:T(8,128)(2,1)S(1)} %pad_maximum_fusion.1.refs_0_), channel_id=1, source_target_pairs={{0,1},{1,0},{2,3},{3,2},{4,5},{5,4},{6,7},{7,6},{8,9},{9,8},{10,11... | collective-permute-start | bytes 1966088 | tf_op jit(solution)/shard_map/ppermute | solution.py:218
  116.5 7.4 %collective-permute-start.12 = (bf16[2,256,640]{2,1,0:T(8,128)(2,1)}, bf16[2,256,640]{2,1,0:T(8,128)(2,1)S(1)}, u32[]{:S(2)}, u32[]{:S(2)}) collective-permute-start(bf16[2,256,640]{2,1,0:T(8,128)(2,1)} %collective-permute-done.4.refs_1_), channel_id=1, source_target_pairs={{0,1},{1,0},{2,3},{3,2},{4,5},{5,4},{6,7},{7,6},{8,9},{9,8},{10,11... | collective-permute-start | bytes 1966088 | tf_op jit(solution)/shard_map/ppermute | solution.py:218
  119.5 4.4 %collective-permute-start.13 = (bf16[2,256,640]{2,1,0:T(8,128)(2,1)}, bf16[2,256,640]{2,1,0:T(8,128)(2,1)S(1)}, u32[]{:S(2)}, u32[]{:S(2)}) collective-permute-start(bf16[2,256,640]{2,1,0:T(8,128)(2,1)} %collective-permute-done.9.refs_2_), channel_id=1, source_target_pairs={{0,1},{1,0},{2,3},{3,2},{4,5},{5,4},{6,7},{7,6},{8,9},{9,8},{10,11... | collective-permute-start | bytes 1966088 | tf_op jit(solution)/shard_map/ppermute | solution.py:218
  121.4 4.3 %collective-permute-start.14 = (bf16[2,256,640]{2,1,0:T(8,128)(2,1)}, bf16[2,256,640]{2,1,0:T(8,128)(2,1)S(1)}, u32[]{:S(2)}, u32[]{:S(2)}) collective-permute-start(bf16[2,256,640]{2,1,0:T(8,128)(2,1)} %collective-permute-done.10.refs_3_), channel_id=1, source_target_pairs={{0,1},{1,0},{2,3},{3,2},{4,5},{5,4},{6,7},{7,6},{8,9},{9,8},{10,11... | collective-permute-start | bytes 1966088 | tf_op jit(solution)/shard_map/ppermute | solution.py:218
  130.7 1.0 copy-start.1
  131.7 4.9 %copy-start.2 = (bf16[512,1024]{1,0:T(8,128)(2,1)S(1)}, bf16[512,1024]{1,0:T(8,128)(2,1)}, u32[]{:S(2)}) copy-start(bf16[512,1024]{1,0:T(8,128)(2,1)} %copy-done.1) | copy-start | bytes 3145732

commit v15 on v14

--- a/solution.py
+++ b/solution.py
@@ -38,7 +38,11 @@
 def attend(reach_ref, gain_ref, x_ref, w_ref, n_ref, qkv_ref, out_ref, dist):
     def norm(i, _):
         rows = pl.ds(pl.multiple_of(i * 64, 64), 64)
-        x = x_ref[rows, :].astype(jnp.float32)
+        if len(x_ref.shape) == 3:
+            x = x_ref[pl.ds(pl.multiple_of(i * 16, 16), 16)].astype(jnp.float32)
+            x = x.reshape(64, FEATURES)
+        else:
+            x = x_ref[rows, :].astype(jnp.float32)
         scale = lax.rsqrt(jnp.mean(x * x, axis=-1, keepdims=True) + 1e-05)
         n_ref[rows, :] = (x * scale * gain_ref[...]).astype(jnp.bfloat16)
         return 0
@@ -76,7 +80,12 @@
                 ps.append(p.astype(jnp.bfloat16))
             o = jnp.dot(jnp.concatenate(ps), v[:seen], preferred_element_type=jnp.float32)
             both = jnp.where(lane < 64, o[:mid] / sums[0], o[mid:] / sums[1])
-            out_ref[first : first + mid, h * 64 : h * 64 + 128] = both.astype(jnp.bfloat16)
+            lanes = slice(h * 64, h * 64 + 128)
+            if len(out_ref.shape) == 3:
+                both = both.reshape(mid // 4, 4, 128).astype(jnp.bfloat16)
+                out_ref[first // 4 : (first + mid) // 4, :, lanes] = both
+            else:
+                out_ref[first : first + mid, lanes] = both.astype(jnp.bfloat16)
 
 
 def pairs():
@@ -143,7 +152,7 @@
 def column_attention(place, reach, gain, x, parts):
     return pl.pallas_call(
         column_kernel,
-        out_shape=jax.ShapeDtypeStruct((STRIDE, HALF), jnp.bfloat16),
+        out_shape=jax.ShapeDtypeStruct((STRIDE // 4, 4, HALF), jnp.bfloat16),
         in_specs=[SMEM, SMEM] + [VMEM] * (2 + len(parts)),
         out_specs=VMEM,
         scratch_shapes=WORK,
@@ -200,7 +209,6 @@
 
     sent, column = lax.optimization_barrier((rows.reshape(64, 4, FEATURES), column))
     turned = lax.all_to_all(sent, SEQ, split_axis=0, concat_axis=0)
-    turned = turned.reshape(STRIDE, FEATURES)
 
     part = column.reshape(Z * 16, 512)
     ahead, across, behind = ring(part, ("xl", "xh"), [0, 2, 1, 3])
@@ -226,7 +234,7 @@
     col_mid = column_attention(
         place, col_rows, gain, turned, [held, came, first, swap(came)]
     )
-    col_out = lax.all_to_all(col_mid.reshape(64, 4, HALF), SEQ, split_axis=0, concat_axis=0)
+    col_out = lax.all_to_all(col_mid, SEQ, split_axis=0, concat_axis=0)
 
     rest, _ = lax.optimization_barrier((rest, beside))
     rest, *later = plane(rest)

time: 139 us -> 138 us (level)
    reshape x2 -> x0, local copies, waits for them, and re-layouts: 1.93 us -> none  [the longest x1 1.16 us: body(): turned = turned.reshape(STRIDE, FEATURES)]
  transfers between devices with their start and end apart: 18 -> 18, of which waited for: 7 -> 7; matrix products, arithmetic and copies ran while one was open for 3% -> 2% of each run, Pallas kernels for 6% -> 7%
where the time goes in v15:
time: 138 us
  starting transfers between devices  93.5 us (68%)
  waiting for transfers between devices  25.9 us (19%)
  Pallas kernels  12.2 us (9%)
  local copies, waits for them, and re-layouts  4.15 us (3%)
    ppermute x9, starting transfers between devices, ring(): lax.ppermute(part, axes, [(order[i], order[(i - t) % size]) for i in rang...  31 us
    ppermute x6, starting transfers between devices, swap(): return lax.ppermute(part, 'c', [(0, 1), (1, 0)])  16.5 us
    all_to_all x1, starting transfers between devices, body(): column = lax.all_to_all(block, 'z', split_axis=0, concat_axis=0)  15.7 us
    all_to_all x1, starting transfers between devices, body(): col_out = lax.all_to_all(col_mid, SEQ, split_axis=0, concat_axis=0)  15.7 us
    all_to_all x1, starting transfers between devices, body(): turned = lax.all_to_all(sent, SEQ, split_axis=0, concat_axis=0)  14.6 us
    all_to_all x1, waiting for transfers between devices, body(): column = lax.all_to_all(block, 'z', split_axis=0, concat_axis=0)  11.1 us
    ppermute x9, waiting for transfers between devices, ring(): lax.ppermute(part, axes, [(order[i], order[(i - t) % size]) for i in rang...  9.04 us
    pallas_call x1, Pallas kernels, row_attention(): pl.pallas_call(row_kernel, out_shape=[jax.ShapeDtypeStruct((STRIDE, FEATU...  4.94 us
  transfers between devices with their start and end apart: 18, of which 7 were waited for; matrix products, arithmetic and copies ran while one was open for 2% of the time, Pallas kernels for 7%

profile of v15, /device:TPU:1, one launch (start us, length us, event | category | flops | bytes accessed | tf_op | source)
XLA Modules:
  0.0 137.5 jit_solution(8496720727716267352)
XLA Ops:
  1.4 15.7 %all-to-all-start = ((bf16[16,16,512]{2,1,0:T(8,128)(2,1)}), bf16[16,16,512]{2,1,0:T(8,128)(2,1)S(1)}, u32[]{:S(2)}, u32[]{:S(2)}) async-start(bf16[16,16,512]{2,1,0:T(8,128)(2,1)} %copies.1), calls=%async_computation | async-start | bytes 524288 | tf_op jit(solution)/shard_map/all_to_all | solution.py:208
  17.2 2.0 %reshape_reshape.3 = bf16[64,4,1024]{2,1,0:T(4,128)(2,1)} reshape(bf16[1,1,256,1024]{3,2,1,0:T(8,128)(2,1)} %param.6) | data formatting | bytes 1048576 | tf_op jit(solution)/shard_map/reshape;reshape | solution.py:210
  19.2 11.1 %all-to-all-done = bf16[16,16,512]{2,1,0:T(8,128)(2,1)S(1)} async-done(((bf16[16,16,512]{2,1,0:T(8,128)(2,1)}), bf16[16,16,512]{2,1,0:T(8,128)(2,1)S(1)}, u32[]{:S(2)}, u32[]{:S(2)}) %all-to-all-start) | async-done | bytes 262176 | tf_op jit(solution)/shard_map/all_to_all | solution.py:208
  30.3 4.4 %collective-permute-start.1 = (bf16[256,512]{1,0:T(8,128)(2,1)S(1)}, bf16[256,512]{1,0:T(8,128)(2,1)S(1)}, u32[]{:S(2)}, u32[]{:S(2)}) collective-permute-start(bf16[256,512]{1,0:T(8,128)(2,1)S(1)} %bitcast.23), channel_id=1, source_target_pairs={{0,288},{256,0},{32,256},{288,32},{1,289},{257,1},{33,257},{289,33... | collective-permute-start | bytes 786440 | tf_op jit(solution)/shard_map/ppermute | solution.py:189
  34.7 2.4 %collective-permute-start.2 = (bf16[256,512]{1,0:T(8,128)(2,1)S(1)}, bf16[256,512]{1,0:T(8,128)(2,1)S(1)}, u32[]{:S(2)}, u32[]{:S(2)}) collective-permute-start(bf16[256,512]{1,0:T(8,128)(2,1)S(1)} %bitcast.24), channel_id=1, source_target_pairs={{0,32},{256,288},{32,0},{288,256},{1,33},{257,289},{33,1},{289,257... | collective-permute-start | bytes 786440 | tf_op jit(solution)/shard_map/ppermute | solution.py:189
  37.1 2.5 %collective-permute-start = (bf16[256,512]{1,0:T(8,128)(2,1)S(1)}, bf16[256,512]{1,0:T(8,128)(2,1)S(1)}, u32[]{:S(2)}, u32[]{:S(2)}) collective-permute-start(bf16[256,512]{1,0:T(8,128)(2,1)S(1)} %bitcast.25), channel_id=1, source_target_pairs={{0,256},{256,32},{32,288},{288,0},{1,257},{257,33},{33,289},{289,1... | collective-permute-start | bytes 786440 | tf_op jit(solution)/shard_map/ppermute | solution.py:189
  39.7 14.6 %all-to-all-start.1 = ((bf16[64,4,1024]{2,1,0:T(4,128)(2,1)}), bf16[64,4,1024]{2,1,0:T(4,128)(2,1)S(1)}, u32[]{:S(2)}, u32[]{:S(2)}) async-start(bf16[64,4,1024]{2,1,0:T(4,128)(2,1)} %reshape_reshape.3), calls=%async_computation.1 | async-start | bytes 1048576 | tf_op jit(solution)/shard_map/all_to_all | solution.py:211
  54.5 4.8 %collective-permute-start.5 = (bf16[2,256,384]{2,1,0:T(8,128)(2,1)S(1)}, bf16[2,256,384]{2,1,0:T(8,128)(2,1)S(1)}, u32[]{:S(2)}, u32[]{:S(2)}) collective-permute-start(bf16[2,256,384]{2,1,0:T(8,128)(2,1)S(1)} %pad_maximum_fusion.2.refs_0_), channel_id=1, source_target_pairs={{0,128},{64,192},{128,0},{192,64},{1,129},{65,193},{129,1},{193,65... | collective-permute-start | bytes 1179656 | tf_op jit(solution)/shard_map/ppermute | solution.py:189
  59.3 2.3 %collective-permute-start.6 = (bf16[2,256,384]{2,1,0:T(8,128)(2,1)S(1)}, bf16[2,256,384]{2,1,0:T(8,128)(2,1)S(1)}, u32[]{:S(2)}, u32[]{:S(2)}) collective-permute-start(bf16[2,256,384]{2,1,0:T(8,128)(2,1)S(1)} %pad_maximum_fusion.2.refs_0_), channel_id=1, source_target_pairs={{0,64},{64,128},{128,192},{192,0},{1,65},{65,129},{129,193},{193,1... | collective-permute-start | bytes 1179656 | tf_op jit(solution)/shard_map/ppermute | solution.py:189
  61.6 4.2 %collective-permute-start.3 = (bf16[2,256,384]{2,1,0:T(8,128)(2,1)S(1)}, bf16[2,256,384]{2,1,0:T(8,128)(2,1)S(1)}, u32[]{:S(2)}, u32[]{:S(2)}) collective-permute-start(bf16[2,256,384]{2,1,0:T(8,128)(2,1)S(1)} %pad_maximum_fusion.2.refs_0_), channel_id=1, source_target_pairs={{0,192},{64,0},{128,64},{192,128},{1,193},{65,1},{129,65},{193,129... | collective-permute-start | bytes 1179656 | tf_op jit(solution)/shard_map/ppermute | solution.py:189
  65.8 2.3 %collective-permute-done.5 = bf16[2,256,384]{2,1,0:T(8,128)(2,1)S(1)} collective-permute-done((bf16[2,256,384]{2,1,0:T(8,128)(2,1)S(1)}, bf16[2,256,384]{2,1,0:T(8,128)(2,1)S(1)}, u32[]{:S(2)}, u32[]{:S(2)}) %collective-permute-start.5) | collective-permute-done | bytes 393248 | tf_op jit(solution)/shard_map/ppermute | solution.py:189
  68.2 4.1 %collective-permute-start.7 = (bf16[2,256,384]{2,1,0:T(8,128)(2,1)S(1)}, bf16[2,256,384]{2,1,0:T(8,128)(2,1)S(1)}, u32[]{:S(2)}, u32[]{:S(2)}) collective-permute-start(bf16[2,256,384]{2,1,0:T(8,128)(2,1)S(1)} %pad_maximum_fusion.2.refs_0_), channel_id=1, source_target_pairs={{0,1},{1,0},{2,3},{3,2},{4,5},{5,4},{6,7},{7,6},{8,9},{9,8},{10,11... | collective-permute-start | bytes 1179656 | tf_op jit(solution)/shard_map/ppermute | solution.py:226
  72.2 5.1 %collective-permute-done.6 = bf16[2,256,384]{2,1,0:T(8,128)(2,1)S(1)} collective-permute-done((bf16[2,256,384]{2,1,0:T(8,128)(2,1)S(1)}, bf16[2,256,384]{2,1,0:T(8,128)(2,1)S(1)}, u32[]{:S(2)}, u32[]{:S(2)}) %collective-permute-start.6) | collective-permute-done | bytes 393248 | tf_op jit(solution)/shard_map/ppermute | solution.py:189
  77.5 2.7 %collective-permute-start.8 = (bf16[6,256,384]{2,1,0:T(8,128)(2,1)S(1)}, bf16[6,256,384]{2,1,0:T(8,128)(2,1)}, u32[]{:S(2)}, u32[]{:S(2)}) collective-permute-start(bf16[6,256,384]{2,1,0:T(8,128)(2,1)S(1)} %pad_maximum_fusion.refs_1_), channel_id=1, source_target_pairs={{0,1},{1,0},{2,3},{3,2},{4,5},{5,4},{6,7},{7,6},{8,9},{9,8},{10,11... | collective-permute-start | bytes 3538952 | tf_op jit(solution)/shard_map/ppermute | solution.py:226
  80.5 3.0 %collective-permute-start.10 = (bf16[2,256,640]{2,1,0:T(8,128)(2,1)S(1)}, bf16[2,256,640]{2,1,0:T(8,128)(2,1)}, u32[]{:S(2)}, u32[]{:S(2)}) collective-permute-start(bf16[2,256,640]{2,1,0:T(8,128)(2,1)S(1)} %pad_maximum_fusion.1.refs_0_), channel_id=1, source_target_pairs={{0,64},{64,128},{128,192},{192,0},{1,65},{65,129},{129,193},{193,1... | collective-permute-start | bytes 1966088 | tf_op jit(solution)/shard_map/ppermute | solution.py:189
  83.5 4.4 %collective-permute-start.9 = (bf16[2,256,640]{2,1,0:T(8,128)(2,1)S(1)}, bf16[2,256,640]{2,1,0:T(8,128)(2,1)}, u32[]{:S(2)}, u32[]{:S(2)}) collective-permute-start(bf16[2,256,640]{2,1,0:T(8,128)(2,1)S(1)} %pad_maximum_fusion.1.refs_0_), channel_id=1, source_target_pairs={{0,128},{64,192},{128,0},{192,64},{1,129},{65,193},{129,1},{193,65... | collective-permute-start | bytes 1966088 | tf_op jit(solution)/shard_map/ppermute | solution.py:189
  87.9 3.0 %collective-permute-start.4 = (bf16[2,256,640]{2,1,0:T(8,128)(2,1)S(1)}, bf16[2,256,640]{2,1,0:T(8,128)(2,1)}, u32[]{:S(2)}, u32[]{:S(2)}) collective-permute-start(bf16[2,256,640]{2,1,0:T(8,128)(2,1)S(1)} %pad_maximum_fusion.1.refs_0_), channel_id=1, source_target_pairs={{0,192},{64,0},{128,64},{192,128},{1,193},{65,1},{129,65},{193,129... | collective-permute-start | bytes 1966088 | tf_op jit(solution)/shard_map/ppermute | solution.py:189
  92.0 4.6 %columns.1 = bf16[64,4,512]{2,1,0:T(4,128)(2,1)} custom-call(s32[3]{0:T(128)S(1)} %pad_add_fusion.place, s32[8]{0:T(128)S(1)} %copy-done.6, f32[1,1024]{1,0:T(1,128)S(1)} %bitcast.21, bf16[64,4,1024]{2,1,0:T(4,128)(2,1)S(1)} %all-to-all-done.1.x_ref, bf16[2,256,384]{2,1,0:T(8,128)(2,1)S(1)} %pad_maximum_fusion.2.refs_0_, ...), custom_call_target="tpu_custom_call" | custom-call | flops 939524096 | bytes 6291456 | tf_op jit(solution)/shard_map/columns/pallas_call | solution.py:153
  96.6 15.7 %all-to-all-start.2 = ((bf16[64,4,512]{2,1,0:T(4,128)(2,1)}), bf16[64,4,512]{2,1,0:T(4,128)(2,1)S(1)}, u32[]{:S(2)}, u32[]{:S(2)}) async-start(bf16[64,4,512]{2,1,0:T(4,128)(2,1)} %columns.1), calls=%async_computation.2 | async-start | bytes 524288 | tf_op jit(solution)/shard_map/all_to_all | solution.py:237
  112.3 2.4 %collective-permute-start.11 = (bf16[2,256,640]{2,1,0:T(8,128)(2,1)S(1)}, bf16[2,256,640]{2,1,0:T(8,128)(2,1)S(1)}, u32[]{:S(2)}, u32[]{:S(2)}) collective-permute-start(bf16[2,256,640]{2,1,0:T(8,128)(2,1)S(1)} %pad_maximum_fusion.1.refs_0_), channel_id=1, source_target_pairs={{0,1},{1,0},{2,3},{3,2},{4,5},{5,4},{6,7},{7,6},{8,9},{9,8},{10,11... | collective-permute-start | bytes 1966088 | tf_op jit(solution)/shard_map/ppermute | solution.py:226
  116.3 3.0 %collective-permute-start.12 = (bf16[2,256,640]{2,1,0:T(8,128)(2,1)}, bf16[2,256,640]{2,1,0:T(8,128)(2,1)S(1)}, u32[]{:S(2)}, u32[]{:S(2)}) collective-permute-start(bf16[2,256,640]{2,1,0:T(8,128)(2,1)} %collective-permute-done.4.refs_1_), channel_id=1, source_target_pairs={{0,1},{1,0},{2,3},{3,2},{4,5},{5,4},{6,7},{7,6},{8,9},{9,8},{10,11... | collective-permute-start | bytes 1966088 | tf_op jit(solution)/shard_map/ppermute | solution.py:226
  121.3 2.4 %collective-permute-start.14 = (bf16[2,256,640]{2,1,0:T(8,128)(2,1)}, bf16[2,256,640]{2,1,0:T(8,128)(2,1)S(1)}, u32[]{:S(2)}, u32[]{:S(2)}) collective-permute-start(bf16[2,256,640]{2,1,0:T(8,128)(2,1)} %collective-permute-done.10.refs_3_), channel_id=1, source_target_pairs={{0,1},{1,0},{2,3},{3,2},{4,5},{5,4},{6,7},{7,6},{8,9},{9,8},{10,11... | collective-permute-start | bytes 1966088 | tf_op jit(solution)/shard_map/ppermute | solution.py:226
  125.6 4.9 %rows.1 = (f32[256,1024]{1,0:T(8,128)S(1)}, bf16[512,1024]{1,0:T(8,128)(2,1)S(1)}, s32[1]{0:T(128)}) custom-call(s32[3]{0:T(128)S(1)} %pad_add_fusion.place, s32[8]{0:T(128)S(1)} %copy-done.7, f32[1,1024]{1,0:T(1,128)S(1)} %bitcast.22, bf16[256,1024]{1,0:T(8,128)(2,1)S(1)} %bitcast.20, bf16[2,256,640]{2,1,0:T(8,128)(2,1)S(1)} %pad_maximum_fusion.1.refs_0_, ...), custom_call_target="tpu_custom_call" | custom-call | flops 1048576 | bytes 1048576 | tf_op jit(solution)/shard_map/rows/pallas_call | solution.py:166
  132.3 3.8 %all-to-all-done.2 = bf16[64,4,512]{2,1,0:T(4,128)(2,1)S(1)} async-done(((bf16[64,4,512]{2,1,0:T(4,128)(2,1)}), bf16[64,4,512]{2,1,0:T(4,128)(2,1)S(1)}, u32[]{:S(2)}, u32[]{:S(2)}) %all-to-all-start.2) | async-done | bytes 262176 | tf_op jit(solution)/shard_map/all_to_all | solution.py:237
  (44 shorter events, 10.8 us)
Async XLA Ops:
  1.4 28.9 %all-to-all-start = ((bf16[16,16,512]{2,1,0:T(8,128)(2,1)}), bf16[16,16,512]{2,1,0:T(8,128)(2,1)S(1)}, u32[]{:S(2)}, u32[]{:S(2)}) async-start(bf16[16,16,512]{2,1,0:T(8,128)(2,1)} %copies.1), calls=%async_computation | async-start | bytes 524288 | tf_op jit(solution)/shard_map/all_to_all | solution.py:208
  30.3 23.9 %collective-permute-start.1 = (bf16[256,512]{1,0:T(8,128)(2,1)S(1)}, bf16[256,512]{1,0:T(8,128)(2,1)S(1)}, u32[]{:S(2)}, u32[]{:S(2)}) collective-permute-start(bf16[256,512]{1,0:T(8,128)(2,1)S(1)} %bitcast.23), channel_id=1, source_target_pairs={{0,288},{256,0},{32,256},{288,32},{1,289},{257,1},{33,257},{289,33... | collective-permute-start | bytes 786440 | tf_op jit(solution)/shard_map/ppermute | solution.py:189
  34.7 19.6 %collective-permute-start.2 = (bf16[256,512]{1,0:T(8,128)(2,1)S(1)}, bf16[256,512]{1,0:T(8,128)(2,1)S(1)}, u32[]{:S(2)}, u32[]{:S(2)}) collective-permute-start(bf16[256,512]{1,0:T(8,128)(2,1)S(1)} %bitcast.24), channel_id=1, source_target_pairs={{0,32},{256,288},{32,0},{288,256},{1,33},{257,289},{33,1},{289,257... | collective-permute-start | bytes 786440 | tf_op jit(solution)/shard_map/ppermute | solution.py:189
  37.1 17.1 %collective-permute-start = (bf16[256,512]{1,0:T(8,128)(2,1)S(1)}, bf16[256,512]{1,0:T(8,128)(2,1)S(1)}, u32[]{:S(2)}, u32[]{:S(2)}) collective-permute-start(bf16[256,512]{1,0:T(8,128)(2,1)S(1)} %bitcast.25), channel_id=1, source_target_pairs={{0,256},{256,32},{32,288},{288,0},{1,257},{257,33},{33,289},{289,1... | collective-permute-start | bytes 786440 | tf_op jit(solution)/shard_map/ppermute | solution.py:189
  39.7 51.3 %all-to-all-start.1 = ((bf16[64,4,1024]{2,1,0:T(4,128)(2,1)}), bf16[64,4,1024]{2,1,0:T(4,128)(2,1)S(1)}, u32[]{:S(2)}, u32[]{:S(2)}) async-start(bf16[64,4,1024]{2,1,0:T(4,128)(2,1)} %reshape_reshape.3), calls=%async_computation.1 | async-start | bytes 1048576 | tf_op jit(solution)/shard_map/all_to_all | solution.py:211
  54.5 13.7 %collective-permute-start.5 = (bf16[2,256,384]{2,1,0:T(8,128)(2,1)S(1)}, bf16[2,256,384]{2,1,0:T(8,128)(2,1)S(1)}, u32[]{:S(2)}, u32[]{:S(2)}) collective-permute-start(bf16[2,256,384]{2,1,0:T(8,128)(2,1)S(1)} %pad_maximum_fusion.2.refs_0_), channel_id=1, source_target_pairs={{0,128},{64,192},{128,0},{192,64},{1,129},{65,193},{129,1},{193,65... | collective-permute-start | bytes 1179656 | tf_op jit(solution)/shard_map/ppermute | solution.py:189
  59.3 18.0 %collective-permute-start.6 = (bf16[2,256,384]{2,1,0:T(8,128)(2,1)S(1)}, bf16[2,256,384]{2,1,0:T(8,128)(2,1)S(1)}, u32[]{:S(2)}, u32[]{:S(2)}) collective-permute-start(bf16[2,256,384]{2,1,0:T(8,128)(2,1)S(1)} %pad_maximum_fusion.2.refs_0_), channel_id=1, source_target_pairs={{0,64},{64,128},{128,192},{192,0},{1,65},{65,129},{129,193},{193,1... | collective-permute-start | bytes 1179656 | tf_op jit(solution)/shard_map/ppermute | solution.py:189
  61.6 15.7 %collective-permute-start.3 = (bf16[2,256,384]{2,1,0:T(8,128)(2,1)S(1)}, bf16[2,256,384]{2,1,0:T(8,128)(2,1)S(1)}, u32[]{:S(2)}, u32[]{:S(2)}) collective-permute-start(bf16[2,256,384]{2,1,0:T(8,128)(2,1)S(1)} %pad_maximum_fusion.2.refs_0_), channel_id=1, source_target_pairs={{0,192},{64,0},{128,64},{192,128},{1,193},{65,1},{129,65},{193,129... | collective-permute-start | bytes 1179656 | tf_op jit(solution)/shard_map/ppermute | solution.py:189
  68.2 9.4 %collective-permute-start.7 = (bf16[2,256,384]{2,1,0:T(8,128)(2,1)S(1)}, bf16[2,256,384]{2,1,0:T(8,128)(2,1)S(1)}, u32[]{:S(2)}, u32[]{:S(2)}) collective-permute-start(bf16[2,256,384]{2,1,0:T(8,128)(2,1)S(1)} %pad_maximum_fusion.2.refs_0_), channel_id=1, source_target_pairs={{0,1},{1,0},{2,3},{3,2},{4,5},{5,4},{6,7},{7,6},{8,9},{9,8},{10,11... | collective-permute-start | bytes 1179656 | tf_op jit(solution)/shard_map/ppermute | solution.py:226
  77.5 3.0 %copy-start.3 = (bf16[2,256,384]{2,1,0:T(8,128)(2,1)}, bf16[2,256,384]{2,1,0:T(8,128)(2,1)S(1)}, u32[]{:S(2)}) copy-start(bf16[2,256,384]{2,1,0:T(8,128)(2,1)S(1)} %collective-permute-done.7.refs_2_) | copy-start | bytes 1179652
  77.5 13.5 %collective-permute-start.8 = (bf16[6,256,384]{2,1,0:T(8,128)(2,1)S(1)}, bf16[6,256,384]{2,1,0:T(8,128)(2,1)}, u32[]{:S(2)}, u32[]{:S(2)}) collective-permute-start(bf16[6,256,384]{2,1,0:T(8,128)(2,1)S(1)} %pad_maximum_fusion.refs_1_), channel_id=1, source_target_pairs={{0,1},{1,0},{2,3},{3,2},{4,5},{5,4},{6,7},{7,6},{8,9},{9,8},{10,11... | collective-permute-start | bytes 3538952 | tf_op jit(solution)/shard_map/ppermute | solution.py:226
  80.3 10.7 %copy-start.5 = (f32[1024]{0:T(1024)S(1)}, f32[1024]{0:T(1024)}, u32[]{:S(2)}) copy-start(f32[1024]{0:T(1024)} %param.7) | copy-start | bytes 12292
  80.3 10.7 %copy-start.6 = (s32[8]{0:T(128)S(1)}, s32[8]{0:T(128)}, u32[]{:S(2)}) copy-start(s32[8]{0:T(128)} %reach_ref.2) | copy-start | bytes 100
  80.5 34.2 %collective-permute-start.10 = (bf16[2,256,640]{2,1,0:T(8,128)(2,1)S(1)}, bf16[2,256,640]{2,1,0:T(8,128)(2,1)}, u32[]{:S(2)}, u32[]{:S(2)}) collective-permute-start(bf16[2,256,640]{2,1,0:T(8,128)(2,1)S(1)} %pad_maximum_fusion.1.refs_0_), channel_id=1, source_target_pairs={{0,64},{64,128},{128,192},{192,0},{1,65},{65,129},{129,193},{193,1... | collective-permute-start | bytes 1966088 | tf_op jit(solution)/shard_map/ppermute | solution.py:189
  83.5 31.5 %collective-permute-start.9 = (bf16[2,256,640]{2,1,0:T(8,128)(2,1)S(1)}, bf16[2,256,640]{2,1,0:T(8,128)(2,1)}, u32[]{:S(2)}, u32[]{:S(2)}) collective-permute-start(bf16[2,256,640]{2,1,0:T(8,128)(2,1)S(1)} %pad_maximum_fusion.1.refs_0_), channel_id=1, source_target_pairs={{0,128},{64,192},{128,0},{192,64},{1,129},{65,193},{129,1},{193,65... | collective-permute-start | bytes 1966088 | tf_op jit(solution)/shard_map/ppermute | solution.py:189
  87.9 28.4 %collective-permute-start.4 = (bf16[2,256,640]{2,1,0:T(8,128)(2,1)S(1)}, bf16[2,256,640]{2,1,0:T(8,128)(2,1)}, u32[]{:S(2)}, u32[]{:S(2)}) collective-permute-start(bf16[2,256,640]{2,1,0:T(8,128)(2,1)S(1)} %pad_maximum_fusion.1.refs_0_), channel_id=1, source_target_pairs={{0,192},{64,0},{128,64},{192,128},{1,193},{65,1},{129,65},{193,129... | collective-permute-start | bytes 1966088 | tf_op jit(solution)/shard_map/ppermute | solution.py:189
  92.0 33.6 %copy-start = (bf16[1,1,256,1024]{3,2,1,0:T(8,128)(2,1)S(1)}, bf16[1,1,256,1024]{3,2,1,0:T(8,128)(2,1)}, u32[]{:S(2)}) copy-start(bf16[1,1,256,1024]{3,2,1,0:T(8,128)(2,1)} %param.6) | copy-start | bytes 1572868
  92.0 33.6 %copy-start.7 = (s32[8]{0:T(128)S(1)}, s32[8]{0:T(128)}, u32[]{:S(2)}) copy-start(s32[8]{0:T(128)} %reach_ref.3) | copy-start | bytes 100
  96.6 39.5 %all-to-all-start.2 = ((bf16[64,4,512]{2,1,0:T(4,128)(2,1)}), bf16[64,4,512]{2,1,0:T(4,128)(2,1)S(1)}, u32[]{:S(2)}, u32[]{:S(2)}) async-start(bf16[64,4,512]{2,1,0:T(4,128)(2,1)} %columns.1), calls=%async_computation.2 | async-start | bytes 524288 | tf_op jit(solution)/shard_map/all_to_all | solution.py:237
  112.3 11.3 %collective-permute-start.11 = (bf16[2,256,640]{2,1,0:T(8,128)(2,1)S(1)}, bf16[2,256,640]{2,1,0:T(8,128)(2,1)S(1)}, u32[]{:S(2)}, u32[]{:S(2)}) collective-permute-start(bf16[2,256,640]{2,1,0:T(8,128)(2,1)S(1)} %pad_maximum_fusion.1.refs_0_), channel_id=1, source_target_pairs={{0,1},{1,0},{2,3},{3,2},{4,5},{5,4},{6,7},{7,6},{8,9},{9,8},{10,11... | collective-permute-start | bytes 1966088 | tf_op jit(solution)/shard_map/ppermute | solution.py:226
  116.3 7.4 %collective-permute-start.12 = (bf16[2,256,640]{2,1,0:T(8,128)(2,1)}, bf16[2,256,640]{2,1,0:T(8,128)(2,1)S(1)}, u32[]{:S(2)}, u32[]{:S(2)}) collective-permute-start(bf16[2,256,640]{2,1,0:T(8,128)(2,1)} %collective-permute-done.4.refs_1_), channel_id=1, source_target_pairs={{0,1},{1,0},{2,3},{3,2},{4,5},{5,4},{6,7},{7,6},{8,9},{9,8},{10,11... | collective-permute-start | bytes 1966088 | tf_op jit(solution)/shard_map/ppermute | solution.py:226
  119.3 4.4 %collective-permute-start.13 = (bf16[2,256,640]{2,1,0:T(8,128)(2,1)}, bf16[2,256,640]{2,1,0:T(8,128)(2,1)S(1)}, u32[]{:S(2)}, u32[]{:S(2)}) collective-permute-start(bf16[2,256,640]{2,1,0:T(8,128)(2,1)} %collective-permute-done.9.refs_2_), channel_id=1, source_target_pairs={{0,1},{1,0},{2,3},{3,2},{4,5},{5,4},{6,7},{7,6},{8,9},{9,8},{10,11... | collective-permute-start | bytes 1966088 | tf_op jit(solution)/shard_map/ppermute | solution.py:226
  121.3 4.3 %collective-permute-start.14 = (bf16[2,256,640]{2,1,0:T(8,128)(2,1)}, bf16[2,256,640]{2,1,0:T(8,128)(2,1)S(1)}, u32[]{:S(2)}, u32[]{:S(2)}) collective-permute-start(bf16[2,256,640]{2,1,0:T(8,128)(2,1)} %collective-permute-done.10.refs_3_), channel_id=1, source_target_pairs={{0,1},{1,0},{2,3},{3,2},{4,5},{5,4},{6,7},{7,6},{8,9},{9,8},{10,11... | collective-permute-start | bytes 1966088 | tf_op jit(solution)/shard_map/ppermute | solution.py:226
  131.5 4.7 %copy-start.2 = (bf16[512,1024]{1,0:T(8,128)(2,1)S(1)}, bf16[512,1024]{1,0:T(8,128)(2,1)}, u32[]{:S(2)}) copy-start(bf16[512,1024]{1,0:T(8,128)(2,1)} %copy-done.1) | copy-start | bytes 3145732
  (2 other events, 2.0 us)

commit v16 on v14

--- a/solution.py
+++ b/solution.py
@@ -16,7 +16,7 @@
 PART = 384
 SEQ = ("xh", "z", "c")
 FAR = 1 << 20
-COLUMN_PIECES = (1, 3)
+COLUMN_PIECES = (1, 1, 2)
 REST_PIECES = (1, 1, 1, 1)
 COLUMN_ORDER = (0, 2, 1, 3)
 REST_ORDER = (0, 1, 2, 3)
@@ -220,11 +220,12 @@
     held, *came = plane(near)
     beside = came[0]
     held, came[1] = lax.optimization_barrier((held, came[1]))
-    first = swap(held)
-    came = jnp.concatenate([came[t - 1] for t in COLUMN_ORDER[1:]])
+    early = [held, came[1]]
+    first = [swap(a) for a in early]
+    came = jnp.concatenate([came[t - 1] for t in COLUMN_ORDER[2:]])
     came, first = lax.optimization_barrier((came, first))
     col_mid = column_attention(
-        place, col_rows, gain, turned, [held, came, first, swap(came)]
+        place, col_rows, gain, turned, [*early, came, *first, swap(came)]
     )
     col_out = lax.all_to_all(col_mid.reshape(64, 4, HALF), SEQ, split_axis=0, concat_axis=0)
 

time: 139 us -> 141 us (1.014)
  local copies, waits for them, and re-layouts: 5.1 us -> 6.68 us
    ppermute x9, waiting for transfers between devices: 8.91 us -> 5.55 us  [ring(): lax.ppermute(part, axes, [(order[i], order[(i - t) % size]) for i in rang...]
    unnamed x12 -> x20, local copies, waits for them, and re-layouts: 1.01 us -> 3.62 us
    all_to_all x1, waiting for transfers between devices: 4.07 us -> 6.13 us  [body(): lax.all_to_all(col_mid.reshape(64, 4, HALF), SEQ, split_axis=0, concat_ax...]
    ppermute x6 -> x7, starting transfers between devices: 16.5 us -> 17.4 us  [swap(): return lax.ppermute(part, 'c', [(0, 1), (1, 0)])]
  transfers between devices with their start and end apart: 18 -> 19, of which waited for: 7 -> 5; matrix products, arithmetic and copies ran while one was open for 3% -> 2% of each run, Pallas kernels for 6% -> 6%
where the time goes in v16:
time: 141 us; the launch traced here: 140 us
  starting transfers between devices  94.6 us (67%)
  waiting for transfers between devices  26 us (18%)
  Pallas kernels  11.3 us (8%)
  local copies, waits for them, and re-layouts  6.68 us (5%)
    ppermute x9, starting transfers between devices, ring(): lax.ppermute(part, axes, [(order[i], order[(i - t) % size]) for i in rang...  31 us
    ppermute x7, starting transfers between devices, swap(): return lax.ppermute(part, 'c', [(0, 1), (1, 0)])  17.4 us
    all_to_all x1, starting transfers between devices, body(): column = lax.all_to_all(block, 'z', split_axis=0, concat_axis=0)  15.7 us
    all_to_all x1, starting transfers between devices, body(): lax.all_to_all(col_mid.reshape(64, 4, HALF), SEQ, split_axis=0, concat_ax...  15.7 us
    all_to_all x1, starting transfers between devices, body(): turned = lax.all_to_all(sent, SEQ, split_axis=0, concat_axis=0)  14.8 us
    all_to_all x1, waiting for transfers between devices, body(): column = lax.all_to_all(block, 'z', split_axis=0, concat_axis=0)  12.1 us
    all_to_all x1, waiting for transfers between devices, body(): lax.all_to_all(col_mid.reshape(64, 4, HALF), SEQ, split_axis=0, concat_ax...  6.13 us
    ppermute x9, waiting for transfers between devices, ring(): lax.ppermute(part, axes, [(order[i], order[(i - t) % size]) for i in rang...  5.55 us
  transfers between devices with their start and end apart: 19, of which 5 were waited for; matrix products, arithmetic and copies ran while one was open for 2% of the time, Pallas kernels for 6%

profile of v16, /device:TPU:1, one launch (start us, length us, event | category | flops | bytes accessed | tf_op | source)
XLA Modules:
  0.0 140.3 jit_solution(12260659225391722272)
XLA Ops:
  1.5 15.7 %all-to-all-start = ((bf16[16,16,512]{2,1,0:T(8,128)(2,1)}), bf16[16,16,512]{2,1,0:T(8,128)(2,1)S(1)}, u32[]{:S(2)}, u32[]{:S(2)}) async-start(bf16[16,16,512]{2,1,0:T(8,128)(2,1)} %copies.1), calls=%async_computation | async-start | bytes 524288 | tf_op jit(solution)/shard_map/all_to_all | solution.py:199
  18.2 12.1 %all-to-all-done = bf16[16,16,512]{2,1,0:T(8,128)(2,1)S(1)} async-done(((bf16[16,16,512]{2,1,0:T(8,128)(2,1)}), bf16[16,16,512]{2,1,0:T(8,128)(2,1)S(1)}, u32[]{:S(2)}, u32[]{:S(2)}) %all-to-all-start) | async-done | bytes 262176 | tf_op jit(solution)/shard_map/all_to_all | solution.py:199
  30.4 4.4 %collective-permute-start.1 = (bf16[256,512]{1,0:T(8,128)(2,1)S(1)}, bf16[256,512]{1,0:T(8,128)(2,1)S(1)}, u32[]{:S(2)}, u32[]{:S(2)}) collective-permute-start(bf16[256,512]{1,0:T(8,128)(2,1)S(1)} %bitcast.23), channel_id=1, source_target_pairs={{0,288},{256,0},{32,256},{288,32},{1,289},{257,1},{33,257},{289,33... | collective-permute-start | bytes 786440 | tf_op jit(solution)/shard_map/ppermute | solution.py:180
  34.8 2.4 %collective-permute-start.2 = (bf16[256,512]{1,0:T(8,128)(2,1)S(1)}, bf16[256,512]{1,0:T(8,128)(2,1)S(1)}, u32[]{:S(2)}, u32[]{:S(2)}) collective-permute-start(bf16[256,512]{1,0:T(8,128)(2,1)S(1)} %bitcast.24), channel_id=1, source_target_pairs={{0,32},{256,288},{32,0},{288,256},{1,33},{257,289},{33,1},{289,257... | collective-permute-start | bytes 786440 | tf_op jit(solution)/shard_map/ppermute | solution.py:180
  37.2 2.5 %collective-permute-start = (bf16[256,512]{1,0:T(8,128)(2,1)S(1)}, bf16[256,512]{1,0:T(8,128)(2,1)S(1)}, u32[]{:S(2)}, u32[]{:S(2)}) collective-permute-start(bf16[256,512]{1,0:T(8,128)(2,1)S(1)} %bitcast.25), channel_id=1, source_target_pairs={{0,256},{256,32},{32,288},{288,0},{1,257},{257,33},{33,289},{289,1... | collective-permute-start | bytes 786440 | tf_op jit(solution)/shard_map/ppermute | solution.py:180
  39.7 14.8 %all-to-all-start.1 = ((bf16[64,4,1024]{2,1,0:T(4,128)(2,1)}), bf16[64,4,1024]{2,1,0:T(4,128)(2,1)}, u32[]{:S(2)}, u32[]{:S(2)}) async-start(bf16[64,4,1024]{2,1,0:T(4,128)(2,1)} %reshape_reshape.3), calls=%async_computation.1 | async-start | bytes 1048576 | tf_op jit(solution)/shard_map/all_to_all | solution.py:202
  54.7 4.8 %collective-permute-start.5 = (bf16[2,256,384]{2,1,0:T(8,128)(2,1)S(1)}, bf16[2,256,384]{2,1,0:T(8,128)(2,1)S(1)}, u32[]{:S(2)}, u32[]{:S(2)}) collective-permute-start(bf16[2,256,384]{2,1,0:T(8,128)(2,1)S(1)} %pad_maximum_fusion.2.refs_0_), channel_id=1, source_target_pairs={{0,128},{64,192},{128,0},{192,64},{1,129},{65,193},{129,1},{193,65... | collective-permute-start | bytes 1179656 | tf_op jit(solution)/shard_map/ppermute | solution.py:180
  59.5 2.3 %collective-permute-start.6 = (bf16[2,256,384]{2,1,0:T(8,128)(2,1)S(1)}, bf16[2,256,384]{2,1,0:T(8,128)(2,1)S(1)}, u32[]{:S(2)}, u32[]{:S(2)}) collective-permute-start(bf16[2,256,384]{2,1,0:T(8,128)(2,1)S(1)} %pad_maximum_fusion.2.refs_0_), channel_id=1, source_target_pairs={{0,64},{64,128},{128,192},{192,0},{1,65},{65,129},{129,193},{193,1... | collective-permute-start | bytes 1179656 | tf_op jit(solution)/shard_map/ppermute | solution.py:180
  61.9 4.2 %collective-permute-start.3 = (bf16[2,256,384]{2,1,0:T(8,128)(2,1)S(1)}, bf16[2,256,384]{2,1,0:T(8,128)(2,1)S(1)}, u32[]{:S(2)}, u32[]{:S(2)}) collective-permute-start(bf16[2,256,384]{2,1,0:T(8,128)(2,1)S(1)} %pad_maximum_fusion.2.refs_0_), channel_id=1, source_target_pairs={{0,192},{64,0},{128,64},{192,128},{1,193},{65,1},{129,65},{193,129... | collective-permute-start | bytes 1179656 | tf_op jit(solution)/shard_map/ppermute | solution.py:180
  66.1 2.4 %collective-permute-done.5.refs_1_ = bf16[2,256,384]{2,1,0:T(8,128)(2,1)S(1)} collective-permute-done((bf16[2,256,384]{2,1,0:T(8,128)(2,1)S(1)}, bf16[2,256,384]{2,1,0:T(8,128)(2,1)S(1)}, u32[]{:S(2)}, u32[]{:S(2)}) %collective-permute-start.5) | collective-permute-done | bytes 393248 | tf_op jit(solution)/shard_map/ppermute | solution.py:180
  68.4 4.2 %collective-permute-start.7 = (bf16[2,256,384]{2,1,0:T(8,128)(2,1)S(1)}, bf16[2,256,384]{2,1,0:T(8,128)(2,1)S(1)}, u32[]{:S(2)}, u32[]{:S(2)}) collective-permute-start(bf16[2,256,384]{2,1,0:T(8,128)(2,1)S(1)} %pad_maximum_fusion.2.refs_0_), channel_id=1, source_target_pairs={{0,1},{1,0},{2,3},{3,2},{4,5},{5,4},{6,7},{7,6},{8,9},{9,8},{10,11... | collective-permute-start | bytes 1179656 | tf_op jit(solution)/shard_map/ppermute | solution.py:218
  74.5 3.2 %collective-permute-done.6 = bf16[2,256,384]{2,1,0:T(8,128)(2,1)S(1)} collective-permute-done((bf16[2,256,384]{2,1,0:T(8,128)(2,1)S(1)}, bf16[2,256,384]{2,1,0:T(8,128)(2,1)S(1)}, u32[]{:S(2)}, u32[]{:S(2)}) %collective-permute-start.6) | collective-permute-done | bytes 393248 | tf_op jit(solution)/shard_map/ppermute | solution.py:180
  77.8 2.6 %collective-permute-start.9 = (bf16[4,256,384]{2,1,0:T(8,128)(2,1)S(1)}, bf16[4,256,384]{2,1,0:T(8,128)(2,1)}, u32[]{:S(2)}, u32[]{:S(2)}) collective-permute-start(bf16[4,256,384]{2,1,0:T(8,128)(2,1)S(1)} %pad_maximum_fusion.refs_2_), channel_id=1, source_target_pairs={{0,1},{1,0},{2,3},{3,2},{4,5},{5,4},{6,7},{7,6},{8,9},{9,8},{10,11... | collective-permute-start | bytes 2359304 | tf_op jit(solution)/shard_map/ppermute | solution.py:218
  80.7 3.0 %collective-permute-start.11 = (bf16[2,256,640]{2,1,0:T(8,128)(2,1)S(1)}, bf16[2,256,640]{2,1,0:T(8,128)(2,1)}, u32[]{:S(2)}, u32[]{:S(2)}) collective-permute-start(bf16[2,256,640]{2,1,0:T(8,128)(2,1)S(1)} %pad_maximum_fusion.1.refs_0_), channel_id=1, source_target_pairs={{0,64},{64,128},{128,192},{192,0},{1,65},{65,129},{129,193},{193,1... | collective-permute-start | bytes 1966088 | tf_op jit(solution)/shard_map/ppermute | solution.py:180
  83.7 4.4 %collective-permute-start.10 = (bf16[2,256,640]{2,1,0:T(8,128)(2,1)S(1)}, bf16[2,256,640]{2,1,0:T(8,128)(2,1)}, u32[]{:S(2)}, u32[]{:S(2)}) collective-permute-start(bf16[2,256,640]{2,1,0:T(8,128)(2,1)S(1)} %pad_maximum_fusion.1.refs_0_), channel_id=1, source_target_pairs={{0,128},{64,192},{128,0},{192,64},{1,129},{65,193},{129,1},{193,65... | collective-permute-start | bytes 1966088 | tf_op jit(solution)/shard_map/ppermute | solution.py:180
  88.1 3.0 %collective-permute-start.4 = (bf16[2,256,640]{2,1,0:T(8,128)(2,1)S(1)}, bf16[2,256,640]{2,1,0:T(8,128)(2,1)}, u32[]{:S(2)}, u32[]{:S(2)}) collective-permute-start(bf16[2,256,640]{2,1,0:T(8,128)(2,1)S(1)} %pad_maximum_fusion.1.refs_0_), channel_id=1, source_target_pairs={{0,192},{64,0},{128,64},{192,128},{1,193},{65,1},{129,65},{193,129... | collective-permute-start | bytes 1966088 | tf_op jit(solution)/shard_map/ppermute | solution.py:180
  95.0 3.7 %columns.1 = bf16[256,512]{1,0:T(8,128)(2,1)S(1)} custom-call(s32[3]{0:T(128)S(1)} %pad_add_fusion.place, s32[8]{0:T(128)S(1)} %copy-done.8, f32[1,1024]{1,0:T(1,128)S(1)} %bitcast.21, bf16[256,1024]{1,0:T(8,128)(2,1)S(1)} %reshape.26.x_ref, bf16[2,256,384]{2,1,0:T(8,128)(2,1)S(1)} %pad_maximum_fusion.2.refs_0_, ...), custom_call_target="tpu_custom_call" | custom-call | flops 939524096 | bytes 6291456 | tf_op jit(solution)/shard_map/columns/pallas_call | solution.py:144
  99.4 15.7 %all-to-all-start.2 = ((bf16[64,4,512]{2,1,0:T(4,128)(2,1)}), bf16[64,4,512]{2,1,0:T(4,128)(2,1)S(1)}, u32[]{:S(2)}, u32[]{:S(2)}) async-start(bf16[64,4,512]{2,1,0:T(4,128)(2,1)} %reshape.27), calls=%async_computation.2 | async-start | bytes 524288 | tf_op jit(solution)/shard_map/all_to_all | solution.py:230
  115.2 2.4 %collective-permute-start.12 = (bf16[2,256,640]{2,1,0:T(8,128)(2,1)S(1)}, bf16[2,256,640]{2,1,0:T(8,128)(2,1)S(1)}, u32[]{:S(2)}, u32[]{:S(2)}) collective-permute-start(bf16[2,256,640]{2,1,0:T(8,128)(2,1)S(1)} %pad_maximum_fusion.1.refs_0_), channel_id=1, source_target_pairs={{0,1},{1,0},{2,3},{3,2},{4,5},{5,4},{6,7},{7,6},{8,9},{9,8},{10,11... | collective-permute-start | bytes 1966088 | tf_op jit(solution)/shard_map/ppermute | solution.py:218
  117.6 2.0 %collective-permute-start.13 = (bf16[2,256,640]{2,1,0:T(8,128)(2,1)}, bf16[2,256,640]{2,1,0:T(8,128)(2,1)S(1)}, u32[]{:S(2)}, u32[]{:S(2)}) collective-permute-start(bf16[2,256,640]{2,1,0:T(8,128)(2,1)} %collective-permute-done.4.refs_1_), channel_id=1, source_target_pairs={{0,1},{1,0},{2,3},{3,2},{4,5},{5,4},{6,7},{7,6},{8,9},{9,8},{10,11... | collective-permute-start | bytes 1966088 | tf_op jit(solution)/shard_map/ppermute | solution.py:218
  119.5 2.4 %collective-permute-start.14 = (bf16[2,256,640]{2,1,0:T(8,128)(2,1)}, bf16[2,256,640]{2,1,0:T(8,128)(2,1)S(1)}, u32[]{:S(2)}, u32[]{:S(2)}) collective-permute-start(bf16[2,256,640]{2,1,0:T(8,128)(2,1)} %collective-permute-done.10.refs_2_), channel_id=1, source_target_pairs={{0,1},{1,0},{2,3},{3,2},{4,5},{5,4},{6,7},{7,6},{8,9},{9,8},{10,11... | collective-permute-start | bytes 1966088 | tf_op jit(solution)/shard_map/ppermute | solution.py:218
  123.9 2.2 %collective-permute-done.15.refs_7_ = bf16[2,256,640]{2,1,0:T(8,128)(2,1)S(1)} collective-permute-done((bf16[2,256,640]{2,1,0:T(8,128)(2,1)}, bf16[2,256,640]{2,1,0:T(8,128)(2,1)S(1)}, u32[]{:S(2)}, u32[]{:S(2)}) %collective-permute-start.15) | collective-permute-done | bytes 655392 | tf_op jit(solution)/shard_map/ppermute | solution.py:218
  126.1 4.9 %rows.1 = (f32[256,1024]{1,0:T(8,128)S(1)}, bf16[512,1024]{1,0:T(8,128)(2,1)S(1)}, s32[1]{0:T(128)}) custom-call(s32[3]{0:T(128)S(1)} %pad_add_fusion.place, s32[8]{0:T(128)S(1)} %copy-done.9, f32[1,1024]{1,0:T(1,128)S(1)} %bitcast.22, bf16[256,1024]{1,0:T(8,128)(2,1)S(1)} %bitcast.20, bf16[2,256,640]{2,1,0:T(8,128)(2,1)S(1)} %pad_maximum_fusion.1.refs_0_, ...), custom_call_target="tpu_custom_call" | custom-call | flops 1048576 | bytes 1048576 | tf_op jit(solution)/shard_map/rows/pallas_call | solution.py:157
  132.8 6.1 %all-to-all-done.2 = bf16[64,4,512]{2,1,0:T(4,128)(2,1)S(1)} async-done(((bf16[64,4,512]{2,1,0:T(4,128)(2,1)}), bf16[64,4,512]{2,1,0:T(4,128)(2,1)S(1)}, u32[]{:S(2)}, u32[]{:S(2)}) %all-to-all-start.2) | async-done | bytes 262176 | tf_op jit(solution)/shard_map/all_to_all | solution.py:230
  (52 shorter events, 13.9 us)
Async XLA Ops:
  0.0 17.2 %copy-start = (bf16[1,1,256,1024]{3,2,1,0:T(8,128)(2,1)S(1)}, bf16[1,1,256,1024]{3,2,1,0:T(8,128)(2,1)}, u32[]{:S(2)}) copy-start(bf16[1,1,256,1024]{3,2,1,0:T(8,128)(2,1)} %param.6) | copy-start | bytes 1572868
  1.5 28.9 %all-to-all-start = ((bf16[16,16,512]{2,1,0:T(8,128)(2,1)}), bf16[16,16,512]{2,1,0:T(8,128)(2,1)S(1)}, u32[]{:S(2)}, u32[]{:S(2)}) async-start(bf16[16,16,512]{2,1,0:T(8,128)(2,1)} %copies.1), calls=%async_computation | async-start | bytes 524288 | tf_op jit(solution)/shard_map/all_to_all | solution.py:199
  30.4 24.1 %collective-permute-start.1 = (bf16[256,512]{1,0:T(8,128)(2,1)S(1)}, bf16[256,512]{1,0:T(8,128)(2,1)S(1)}, u32[]{:S(2)}, u32[]{:S(2)}) collective-permute-start(bf16[256,512]{1,0:T(8,128)(2,1)S(1)} %bitcast.23), channel_id=1, source_target_pairs={{0,288},{256,0},{32,256},{288,32},{1,289},{257,1},{33,257},{289,33... | collective-permute-start | bytes 786440 | tf_op jit(solution)/shard_map/ppermute | solution.py:180
  34.8 19.7 %collective-permute-start.2 = (bf16[256,512]{1,0:T(8,128)(2,1)S(1)}, bf16[256,512]{1,0:T(8,128)(2,1)S(1)}, u32[]{:S(2)}, u32[]{:S(2)}) collective-permute-start(bf16[256,512]{1,0:T(8,128)(2,1)S(1)} %bitcast.24), channel_id=1, source_target_pairs={{0,32},{256,288},{32,0},{288,256},{1,33},{257,289},{33,1},{289,257... | collective-permute-start | bytes 786440 | tf_op jit(solution)/shard_map/ppermute | solution.py:180
  37.2 17.3 %collective-permute-start = (bf16[256,512]{1,0:T(8,128)(2,1)S(1)}, bf16[256,512]{1,0:T(8,128)(2,1)S(1)}, u32[]{:S(2)}, u32[]{:S(2)}) collective-permute-start(bf16[256,512]{1,0:T(8,128)(2,1)S(1)} %bitcast.25), channel_id=1, source_target_pairs={{0,256},{256,32},{32,288},{288,0},{1,257},{257,33},{33,289},{289,1... | collective-permute-start | bytes 786440 | tf_op jit(solution)/shard_map/ppermute | solution.py:180
  39.7 51.4 %all-to-all-start.1 = ((bf16[64,4,1024]{2,1,0:T(4,128)(2,1)}), bf16[64,4,1024]{2,1,0:T(4,128)(2,1)}, u32[]{:S(2)}, u32[]{:S(2)}) async-start(bf16[64,4,1024]{2,1,0:T(4,128)(2,1)} %reshape_reshape.3), calls=%async_computation.1 | async-start | bytes 1048576 | tf_op jit(solution)/shard_map/all_to_all | solution.py:202
  54.7 13.7 %collective-permute-start.5 = (bf16[2,256,384]{2,1,0:T(8,128)(2,1)S(1)}, bf16[2,256,384]{2,1,0:T(8,128)(2,1)S(1)}, u32[]{:S(2)}, u32[]{:S(2)}) collective-permute-start(bf16[2,256,384]{2,1,0:T(8,128)(2,1)S(1)} %pad_maximum_fusion.2.refs_0_), channel_id=1, source_target_pairs={{0,128},{64,192},{128,0},{192,64},{1,129},{65,193},{129,1},{193,65... | collective-permute-start | bytes 1179656 | tf_op jit(solution)/shard_map/ppermute | solution.py:180
  59.5 18.1 %collective-permute-start.6 = (bf16[2,256,384]{2,1,0:T(8,128)(2,1)S(1)}, bf16[2,256,384]{2,1,0:T(8,128)(2,1)S(1)}, u32[]{:S(2)}, u32[]{:S(2)}) collective-permute-start(bf16[2,256,384]{2,1,0:T(8,128)(2,1)S(1)} %pad_maximum_fusion.2.refs_0_), channel_id=1, source_target_pairs={{0,64},{64,128},{128,192},{192,0},{1,65},{65,129},{129,193},{193,1... | collective-permute-start | bytes 1179656 | tf_op jit(solution)/shard_map/ppermute | solution.py:180
  61.9 15.8 %collective-permute-start.3 = (bf16[2,256,384]{2,1,0:T(8,128)(2,1)S(1)}, bf16[2,256,384]{2,1,0:T(8,128)(2,1)S(1)}, u32[]{:S(2)}, u32[]{:S(2)}) collective-permute-start(bf16[2,256,384]{2,1,0:T(8,128)(2,1)S(1)} %pad_maximum_fusion.2.refs_0_), channel_id=1, source_target_pairs={{0,192},{64,0},{128,64},{192,128},{1,193},{65,1},{129,65},{193,129... | collective-permute-start | bytes 1179656 | tf_op jit(solution)/shard_map/ppermute | solution.py:180
  68.4 9.4 %collective-permute-start.7 = (bf16[2,256,384]{2,1,0:T(8,128)(2,1)S(1)}, bf16[2,256,384]{2,1,0:T(8,128)(2,1)S(1)}, u32[]{:S(2)}, u32[]{:S(2)}) collective-permute-start(bf16[2,256,384]{2,1,0:T(8,128)(2,1)S(1)} %pad_maximum_fusion.2.refs_0_), channel_id=1, source_target_pairs={{0,1},{1,0},{2,3},{3,2},{4,5},{5,4},{6,7},{7,6},{8,9},{9,8},{10,11... | collective-permute-start | bytes 1179656 | tf_op jit(solution)/shard_map/ppermute | solution.py:218
  72.6 5.2 %collective-permute-start.8 = (bf16[2,256,384]{2,1,0:T(8,128)(2,1)S(1)}, bf16[2,256,384]{2,1,0:T(8,128)(2,1)S(1)}, u32[]{:S(2)}, u32[]{:S(2)}) collective-permute-start(bf16[2,256,384]{2,1,0:T(8,128)(2,1)S(1)} %collective-permute-done.5.refs_1_), channel_id=1, source_target_pairs={{0,1},{1,0},{2,3},{3,2},{4,5},{5,4},{6,7},{7,6},{8,9},{9,8},{10,11... | collective-permute-start | bytes 1179656 | tf_op jit(solution)/shard_map/ppermute | solution.py:218
  77.8 2.8 %copy-start.3 = (bf16[2,256,384]{2,1,0:T(8,128)(2,1)}, bf16[2,256,384]{2,1,0:T(8,128)(2,1)S(1)}, u32[]{:S(2)}) copy-start(bf16[2,256,384]{2,1,0:T(8,128)(2,1)S(1)} %collective-permute-done.7.refs_3_) | copy-start | bytes 1179652
  77.8 2.8 %copy-start.5 = (bf16[2,256,384]{2,1,0:T(8,128)(2,1)}, bf16[2,256,384]{2,1,0:T(8,128)(2,1)S(1)}, u32[]{:S(2)}) copy-start(bf16[2,256,384]{2,1,0:T(8,128)(2,1)S(1)} %collective-permute-done.8.refs_4_) | copy-start | bytes 1179652
  77.8 14.5 %collective-permute-start.9 = (bf16[4,256,384]{2,1,0:T(8,128)(2,1)S(1)}, bf16[4,256,384]{2,1,0:T(8,128)(2,1)}, u32[]{:S(2)}, u32[]{:S(2)}) collective-permute-start(bf16[4,256,384]{2,1,0:T(8,128)(2,1)S(1)} %pad_maximum_fusion.refs_2_), channel_id=1, source_target_pairs={{0,1},{1,0},{2,3},{3,2},{4,5},{5,4},{6,7},{7,6},{8,9},{9,8},{10,11... | collective-permute-start | bytes 2359304 | tf_op jit(solution)/shard_map/ppermute | solution.py:218
  80.7 36.9 %collective-permute-start.11 = (bf16[2,256,640]{2,1,0:T(8,128)(2,1)S(1)}, bf16[2,256,640]{2,1,0:T(8,128)(2,1)}, u32[]{:S(2)}, u32[]{:S(2)}) collective-permute-start(bf16[2,256,640]{2,1,0:T(8,128)(2,1)S(1)} %pad_maximum_fusion.1.refs_0_), channel_id=1, source_target_pairs={{0,64},{64,128},{128,192},{192,0},{1,65},{65,129},{129,193},{193,1... | collective-permute-start | bytes 1966088 | tf_op jit(solution)/shard_map/ppermute | solution.py:180
  83.7 33.9 %collective-permute-start.10 = (bf16[2,256,640]{2,1,0:T(8,128)(2,1)S(1)}, bf16[2,256,640]{2,1,0:T(8,128)(2,1)}, u32[]{:S(2)}, u32[]{:S(2)}) collective-permute-start(bf16[2,256,640]{2,1,0:T(8,128)(2,1)S(1)} %pad_maximum_fusion.1.refs_0_), channel_id=1, source_target_pairs={{0,128},{64,192},{128,0},{192,64},{1,129},{65,193},{129,1},{193,65... | collective-permute-start | bytes 1966088 | tf_op jit(solution)/shard_map/ppermute | solution.py:180
  88.1 29.5 %collective-permute-start.4 = (bf16[2,256,640]{2,1,0:T(8,128)(2,1)S(1)}, bf16[2,256,640]{2,1,0:T(8,128)(2,1)}, u32[]{:S(2)}, u32[]{:S(2)}) collective-permute-start(bf16[2,256,640]{2,1,0:T(8,128)(2,1)S(1)} %pad_maximum_fusion.1.refs_0_), channel_id=1, source_target_pairs={{0,192},{64,0},{128,64},{192,128},{1,193},{65,1},{129,65},{193,129... | collective-permute-start | bytes 1966088 | tf_op jit(solution)/shard_map/ppermute | solution.py:180
  99.4 39.5 %all-to-all-start.2 = ((bf16[64,4,512]{2,1,0:T(4,128)(2,1)}), bf16[64,4,512]{2,1,0:T(4,128)(2,1)S(1)}, u32[]{:S(2)}, u32[]{:S(2)}) async-start(bf16[64,4,512]{2,1,0:T(4,128)(2,1)} %reshape.27), calls=%async_computation.2 | async-start | bytes 524288 | tf_op jit(solution)/shard_map/all_to_all | solution.py:230
  115.2 11.0 %copy-start.9 = (s32[8]{0:T(128)S(1)}, s32[8]{0:T(128)}, u32[]{:S(2)}) copy-start(s32[8]{0:T(128)} %reach_ref.3) | copy-start | bytes 100
  115.2 8.7 %collective-permute-start.12 = (bf16[2,256,640]{2,1,0:T(8,128)(2,1)S(1)}, bf16[2,256,640]{2,1,0:T(8,128)(2,1)S(1)}, u32[]{:S(2)}, u32[]{:S(2)}) collective-permute-start(bf16[2,256,640]{2,1,0:T(8,128)(2,1)S(1)} %pad_maximum_fusion.1.refs_0_), channel_id=1, source_target_pairs={{0,1},{1,0},{2,3},{3,2},{4,5},{5,4},{6,7},{7,6},{8,9},{9,8},{10,11... | collective-permute-start | bytes 1966088 | tf_op jit(solution)/shard_map/ppermute | solution.py:218
  117.6 6.3 %collective-permute-start.13 = (bf16[2,256,640]{2,1,0:T(8,128)(2,1)}, bf16[2,256,640]{2,1,0:T(8,128)(2,1)S(1)}, u32[]{:S(2)}, u32[]{:S(2)}) collective-permute-start(bf16[2,256,640]{2,1,0:T(8,128)(2,1)} %collective-permute-done.4.refs_1_), channel_id=1, source_target_pairs={{0,1},{1,0},{2,3},{3,2},{4,5},{5,4},{6,7},{7,6},{8,9},{9,8},{10,11... | collective-permute-start | bytes 1966088 | tf_op jit(solution)/shard_map/ppermute | solution.py:218
  119.5 4.4 %collective-permute-start.14 = (bf16[2,256,640]{2,1,0:T(8,128)(2,1)}, bf16[2,256,640]{2,1,0:T(8,128)(2,1)S(1)}, u32[]{:S(2)}, u32[]{:S(2)}) collective-permute-start(bf16[2,256,640]{2,1,0:T(8,128)(2,1)} %collective-permute-done.10.refs_2_), channel_id=1, source_target_pairs={{0,1},{1,0},{2,3},{3,2},{4,5},{5,4},{6,7},{7,6},{8,9},{9,8},{10,11... | collective-permute-start | bytes 1966088 | tf_op jit(solution)/shard_map/ppermute | solution.py:218
  121.9 4.2 %collective-permute-start.15 = (bf16[2,256,640]{2,1,0:T(8,128)(2,1)}, bf16[2,256,640]{2,1,0:T(8,128)(2,1)S(1)}, u32[]{:S(2)}, u32[]{:S(2)}) collective-permute-start(bf16[2,256,640]{2,1,0:T(8,128)(2,1)} %collective-permute-done.11.refs_3_), channel_id=1, source_target_pairs={{0,1},{1,0},{2,3},{3,2},{4,5},{5,4},{6,7},{7,6},{8,9},{9,8},{10,11... | collective-permute-start | bytes 1966088 | tf_op jit(solution)/shard_map/ppermute | solution.py:218
  132.0 7.0 %copy-start.2 = (bf16[512,1024]{1,0:T(8,128)(2,1)S(1)}, bf16[512,1024]{1,0:T(8,128)(2,1)}, u32[]{:S(2)}) copy-start(bf16[512,1024]{1,0:T(8,128)(2,1)} %copy-done.1) | copy-start | bytes 3145732
  (5 other events, 4.8 us)

commit v17 on v14

--- a/solution.py
+++ b/solution.py
@@ -118,10 +118,10 @@
 
 
 def last_kernel(base_ref, col_ref, low_ref, out_ref):
-    for n in range(0, FEATURES, 256):
-        out_ref[:, n : n + 256] = (
-            base_ref[:, n : n + 256]
-            + jnp.dot(col_ref[...], low_ref[:, n : n + 256], preferred_element_type=jnp.float32)
+    for n in range(0, FEATURES, 512):
+        out_ref[:, n : n + 512] = (
+            base_ref[:, n : n + 512]
+            + jnp.dot(col_ref[...], low_ref[:, n : n + 512], preferred_element_type=jnp.float32)
         ).astype(jnp.bfloat16)
 
 

time: 139 us -> 139 us (level)
  no operation moved by 1% of the time
where the time goes in v17:
time: 139 us; the launch traced here: 138 us
  starting transfers between devices  93.7 us (67%)
  waiting for transfers between devices  26 us (19%)
  Pallas kernels  11.4 us (8%)
  local copies, waits for them, and re-layouts  5.1 us (4%)
    ppermute x9, starting transfers between devices, ring(): lax.ppermute(part, axes, [(order[i], order[(i - t) % size]) for i in rang...  31 us
    ppermute x6, starting transfers between devices, swap(): return lax.ppermute(part, 'c', [(0, 1), (1, 0)])  16.5 us
    all_to_all x1, starting transfers between devices, body(): column = lax.all_to_all(block, 'z', split_axis=0, concat_axis=0)  15.7 us
    all_to_all x1, starting transfers between devices, body(): lax.all_to_all(col_mid.reshape(64, 4, HALF), SEQ, split_axis=0, concat_ax...  15.7 us
    all_to_all x1, starting transfers between devices, body(): turned = lax.all_to_all(sent, SEQ, split_axis=0, concat_axis=0)  14.8 us
    all_to_all x1, waiting for transfers between devices, body(): column = lax.all_to_all(block, 'z', split_axis=0, concat_axis=0)  11.1 us
    ppermute x9, waiting for transfers between devices, ring(): lax.ppermute(part, axes, [(order[i], order[(i - t) % size]) for i in rang...  8.91 us
    pallas_call x1, Pallas kernels, row_attention(): pl.pallas_call(row_kernel, out_shape=[jax.ShapeDtypeStruct((STRIDE, FEATU...  4.93 us
  transfers between devices with their start and end apart: 18, of which 7 were waited for; matrix products, arithmetic and copies ran while one was open for 3% of the time, Pallas kernels for 6%

profile of v17, /device:TPU:1, one launch (start us, length us, event | category | flops | bytes accessed | tf_op | source)
XLA Modules:
  0.0 137.9 jit_solution(13358003268383406064)
XLA Ops:
  1.4 15.7 %all-to-all-start = ((bf16[16,16,512]{2,1,0:T(8,128)(2,1)}), bf16[16,16,512]{2,1,0:T(8,128)(2,1)S(1)}, u32[]{:S(2)}, u32[]{:S(2)}) async-start(bf16[16,16,512]{2,1,0:T(8,128)(2,1)} %copies.1), calls=%async_computation | async-start | bytes 524288 | tf_op jit(solution)/shard_map/all_to_all | solution.py:199
  17.2 2.0 %reshape_reshape.3 = bf16[64,4,1024]{2,1,0:T(4,128)(2,1)} reshape(bf16[1,1,256,1024]{3,2,1,0:T(8,128)(2,1)} %param.6) | data formatting | bytes 1048576 | tf_op jit(solution)/shard_map/reshape;reshape | solution.py:201
  19.2 11.1 %all-to-all-done = bf16[16,16,512]{2,1,0:T(8,128)(2,1)S(1)} async-done(((bf16[16,16,512]{2,1,0:T(8,128)(2,1)}), bf16[16,16,512]{2,1,0:T(8,128)(2,1)S(1)}, u32[]{:S(2)}, u32[]{:S(2)}) %all-to-all-start) | async-done | bytes 262176 | tf_op jit(solution)/shard_map/all_to_all | solution.py:199
  30.3 4.4 %collective-permute-start.1 = (bf16[256,512]{1,0:T(8,128)(2,1)S(1)}, bf16[256,512]{1,0:T(8,128)(2,1)S(1)}, u32[]{:S(2)}, u32[]{:S(2)}) collective-permute-start(bf16[256,512]{1,0:T(8,128)(2,1)S(1)} %bitcast.23), channel_id=1, source_target_pairs={{0,288},{256,0},{32,256},{288,32},{1,289},{257,1},{33,257},{289,33... | collective-permute-start | bytes 786440 | tf_op jit(solution)/shard_map/ppermute | solution.py:180
  34.7 2.4 %collective-permute-start.2 = (bf16[256,512]{1,0:T(8,128)(2,1)S(1)}, bf16[256,512]{1,0:T(8,128)(2,1)S(1)}, u32[]{:S(2)}, u32[]{:S(2)}) collective-permute-start(bf16[256,512]{1,0:T(8,128)(2,1)S(1)} %bitcast.24), channel_id=1, source_target_pairs={{0,32},{256,288},{32,0},{288,256},{1,33},{257,289},{33,1},{289,257... | collective-permute-start | bytes 786440 | tf_op jit(solution)/shard_map/ppermute | solution.py:180
  37.1 2.5 %collective-permute-start = (bf16[256,512]{1,0:T(8,128)(2,1)S(1)}, bf16[256,512]{1,0:T(8,128)(2,1)S(1)}, u32[]{:S(2)}, u32[]{:S(2)}) collective-permute-start(bf16[256,512]{1,0:T(8,128)(2,1)S(1)} %bitcast.25), channel_id=1, source_target_pairs={{0,256},{256,32},{32,288},{288,0},{1,257},{257,33},{33,289},{289,1... | collective-permute-start | bytes 786440 | tf_op jit(solution)/shard_map/ppermute | solution.py:180
  39.7 14.8 %all-to-all-start.1 = ((bf16[64,4,1024]{2,1,0:T(4,128)(2,1)}), bf16[64,4,1024]{2,1,0:T(4,128)(2,1)}, u32[]{:S(2)}, u32[]{:S(2)}) async-start(bf16[64,4,1024]{2,1,0:T(4,128)(2,1)} %reshape_reshape.3), calls=%async_computation.1 | async-start | bytes 1048576 | tf_op jit(solution)/shard_map/all_to_all | solution.py:202
  54.7 4.8 %collective-permute-start.5 = (bf16[2,256,384]{2,1,0:T(8,128)(2,1)S(1)}, bf16[2,256,384]{2,1,0:T(8,128)(2,1)S(1)}, u32[]{:S(2)}, u32[]{:S(2)}) collective-permute-start(bf16[2,256,384]{2,1,0:T(8,128)(2,1)S(1)} %pad_maximum_fusion.2.refs_0_), channel_id=1, source_target_pairs={{0,128},{64,192},{128,0},{192,64},{1,129},{65,193},{129,1},{193,65... | collective-permute-start | bytes 1179656 | tf_op jit(solution)/shard_map/ppermute | solution.py:180
  59.5 2.3 %collective-permute-start.6 = (bf16[2,256,384]{2,1,0:T(8,128)(2,1)S(1)}, bf16[2,256,384]{2,1,0:T(8,128)(2,1)S(1)}, u32[]{:S(2)}, u32[]{:S(2)}) collective-permute-start(bf16[2,256,384]{2,1,0:T(8,128)(2,1)S(1)} %pad_maximum_fusion.2.refs_0_), channel_id=1, source_target_pairs={{0,64},{64,128},{128,192},{192,0},{1,65},{65,129},{129,193},{193,1... | collective-permute-start | bytes 1179656 | tf_op jit(solution)/shard_map/ppermute | solution.py:180
  61.8 4.2 %collective-permute-start.3 = (bf16[2,256,384]{2,1,0:T(8,128)(2,1)S(1)}, bf16[2,256,384]{2,1,0:T(8,128)(2,1)S(1)}, u32[]{:S(2)}, u32[]{:S(2)}) collective-permute-start(bf16[2,256,384]{2,1,0:T(8,128)(2,1)S(1)} %pad_maximum_fusion.2.refs_0_), channel_id=1, source_target_pairs={{0,192},{64,0},{128,64},{192,128},{1,193},{65,1},{129,65},{193,129... | collective-permute-start | bytes 1179656 | tf_op jit(solution)/shard_map/ppermute | solution.py:180
  66.0 2.4 %collective-permute-done.5 = bf16[2,256,384]{2,1,0:T(8,128)(2,1)S(1)} collective-permute-done((bf16[2,256,384]{2,1,0:T(8,128)(2,1)S(1)}, bf16[2,256,384]{2,1,0:T(8,128)(2,1)S(1)}, u32[]{:S(2)}, u32[]{:S(2)}) %collective-permute-start.5) | collective-permute-done | bytes 393248 | tf_op jit(solution)/shard_map/ppermute | solution.py:180
  68.4 4.2 %collective-permute-start.7 = (bf16[2,256,384]{2,1,0:T(8,128)(2,1)S(1)}, bf16[2,256,384]{2,1,0:T(8,128)(2,1)S(1)}, u32[]{:S(2)}, u32[]{:S(2)}) collective-permute-start(bf16[2,256,384]{2,1,0:T(8,128)(2,1)S(1)} %pad_maximum_fusion.2.refs_0_), channel_id=1, source_target_pairs={{0,1},{1,0},{2,3},{3,2},{4,5},{5,4},{6,7},{7,6},{8,9},{9,8},{10,11... | collective-permute-start | bytes 1179656 | tf_op jit(solution)/shard_map/ppermute | solution.py:218
  72.5 5.1 %collective-permute-done.6 = bf16[2,256,384]{2,1,0:T(8,128)(2,1)S(1)} collective-permute-done((bf16[2,256,384]{2,1,0:T(8,128)(2,1)S(1)}, bf16[2,256,384]{2,1,0:T(8,128)(2,1)S(1)}, u32[]{:S(2)}, u32[]{:S(2)}) %collective-permute-start.6) | collective-permute-done | bytes 393248 | tf_op jit(solution)/shard_map/ppermute | solution.py:180
  77.8 2.6 %collective-permute-start.8 = (bf16[6,256,384]{2,1,0:T(8,128)(2,1)S(1)}, bf16[6,256,384]{2,1,0:T(8,128)(2,1)}, u32[]{:S(2)}, u32[]{:S(2)}) collective-permute-start(bf16[6,256,384]{2,1,0:T(8,128)(2,1)S(1)} %pad_maximum_fusion.refs_1_), channel_id=1, source_target_pairs={{0,1},{1,0},{2,3},{3,2},{4,5},{5,4},{6,7},{7,6},{8,9},{9,8},{10,11... | collective-permute-start | bytes 3538952 | tf_op jit(solution)/shard_map/ppermute | solution.py:218
  80.7 3.0 %collective-permute-start.10 = (bf16[2,256,640]{2,1,0:T(8,128)(2,1)S(1)}, bf16[2,256,640]{2,1,0:T(8,128)(2,1)}, u32[]{:S(2)}, u32[]{:S(2)}) collective-permute-start(bf16[2,256,640]{2,1,0:T(8,128)(2,1)S(1)} %pad_maximum_fusion.1.refs_0_), channel_id=1, source_target_pairs={{0,64},{64,128},{128,192},{192,0},{1,65},{65,129},{129,193},{193,1... | collective-permute-start | bytes 1966088 | tf_op jit(solution)/shard_map/ppermute | solution.py:180
  83.7 4.4 %collective-permute-start.9 = (bf16[2,256,640]{2,1,0:T(8,128)(2,1)S(1)}, bf16[2,256,640]{2,1,0:T(8,128)(2,1)}, u32[]{:S(2)}, u32[]{:S(2)}) collective-permute-start(bf16[2,256,640]{2,1,0:T(8,128)(2,1)S(1)} %pad_maximum_fusion.1.refs_0_), channel_id=1, source_target_pairs={{0,128},{64,192},{128,0},{192,64},{1,129},{65,193},{129,1},{193,65... | collective-permute-start | bytes 1966088 | tf_op jit(solution)/shard_map/ppermute | solution.py:180
  88.1 3.0 %collective-permute-start.4 = (bf16[2,256,640]{2,1,0:T(8,128)(2,1)S(1)}, bf16[2,256,640]{2,1,0:T(8,128)(2,1)}, u32[]{:S(2)}, u32[]{:S(2)}) collective-permute-start(bf16[2,256,640]{2,1,0:T(8,128)(2,1)S(1)} %pad_maximum_fusion.1.refs_0_), channel_id=1, source_target_pairs={{0,192},{64,0},{128,64},{192,128},{1,193},{65,1},{129,65},{193,129... | collective-permute-start | bytes 1966088 | tf_op jit(solution)/shard_map/ppermute | solution.py:180
  92.4 3.8 %columns.1 = bf16[256,512]{1,0:T(8,128)(2,1)S(1)} custom-call(s32[3]{0:T(128)S(1)} %pad_add_fusion.place, s32[8]{0:T(128)S(1)} %copy-done.4, f32[1,1024]{1,0:T(1,128)S(1)} %bitcast.21, bf16[256,1024]{1,0:T(8,128)(2,1)S(1)} %reshape.26.x_ref, bf16[2,256,384]{2,1,0:T(8,128)(2,1)S(1)} %pad_maximum_fusion.2.refs_0_, ...), custom_call_target="tpu_custom_call" | custom-call | flops 939524096 | bytes 6291456 | tf_op jit(solution)/shard_map/columns/pallas_call | solution.py:144
  97.0 15.7 %all-to-all-start.2 = ((bf16[64,4,512]{2,1,0:T(4,128)(2,1)}), bf16[64,4,512]{2,1,0:T(4,128)(2,1)S(1)}, u32[]{:S(2)}, u32[]{:S(2)}) async-start(bf16[64,4,512]{2,1,0:T(4,128)(2,1)} %reshape.27), calls=%async_computation.2 | async-start | bytes 524288 | tf_op jit(solution)/shard_map/all_to_all | solution.py:229
  112.7 2.4 %collective-permute-start.11 = (bf16[2,256,640]{2,1,0:T(8,128)(2,1)S(1)}, bf16[2,256,640]{2,1,0:T(8,128)(2,1)S(1)}, u32[]{:S(2)}, u32[]{:S(2)}) collective-permute-start(bf16[2,256,640]{2,1,0:T(8,128)(2,1)S(1)} %pad_maximum_fusion.1.refs_0_), channel_id=1, source_target_pairs={{0,1},{1,0},{2,3},{3,2},{4,5},{5,4},{6,7},{7,6},{8,9},{9,8},{10,11... | collective-permute-start | bytes 1966088 | tf_op jit(solution)/shard_map/ppermute | solution.py:218
  116.5 3.0 %collective-permute-start.12 = (bf16[2,256,640]{2,1,0:T(8,128)(2,1)}, bf16[2,256,640]{2,1,0:T(8,128)(2,1)S(1)}, u32[]{:S(2)}, u32[]{:S(2)}) collective-permute-start(bf16[2,256,640]{2,1,0:T(8,128)(2,1)} %collective-permute-done.4.refs_1_), channel_id=1, source_target_pairs={{0,1},{1,0},{2,3},{3,2},{4,5},{5,4},{6,7},{7,6},{8,9},{9,8},{10,11... | collective-permute-start | bytes 1966088 | tf_op jit(solution)/shard_map/ppermute | solution.py:218
  121.4 2.4 %collective-permute-start.14 = (bf16[2,256,640]{2,1,0:T(8,128)(2,1)}, bf16[2,256,640]{2,1,0:T(8,128)(2,1)S(1)}, u32[]{:S(2)}, u32[]{:S(2)}) collective-permute-start(bf16[2,256,640]{2,1,0:T(8,128)(2,1)} %collective-permute-done.10.refs_3_), channel_id=1, source_target_pairs={{0,1},{1,0},{2,3},{3,2},{4,5},{5,4},{6,7},{7,6},{8,9},{9,8},{10,11... | collective-permute-start | bytes 1966088 | tf_op jit(solution)/shard_map/ppermute | solution.py:218
  125.8 4.9 %rows.1 = (f32[256,1024]{1,0:T(8,128)S(1)}, bf16[512,1024]{1,0:T(8,128)(2,1)S(1)}, s32[1]{0:T(128)}) custom-call(s32[3]{0:T(128)S(1)} %pad_add_fusion.place, s32[8]{0:T(128)S(1)} %copy-done.5, f32[1,1024]{1,0:T(1,128)S(1)} %bitcast.22, bf16[256,1024]{1,0:T(8,128)(2,1)S(1)} %bitcast.20, bf16[2,256,640]{2,1,0:T(8,128)(2,1)S(1)} %pad_maximum_fusion.1.refs_0_, ...), custom_call_target="tpu_custom_call" | custom-call | flops 1048576 | bytes 1048576 | tf_op jit(solution)/shard_map/rows/pallas_call | solution.py:157
  132.4 4.1 %all-to-all-done.2 = bf16[64,4,512]{2,1,0:T(4,128)(2,1)S(1)} async-done(((bf16[64,4,512]{2,1,0:T(4,128)(2,1)}), bf16[64,4,512]{2,1,0:T(4,128)(2,1)S(1)}, u32[]{:S(2)}, u32[]{:S(2)}) %all-to-all-start.2) | async-done | bytes 262176 | tf_op jit(solution)/shard_map/all_to_all | solution.py:229
  (42 shorter events, 11.6 us)
Async XLA Ops:
  1.4 28.9 %all-to-all-start = ((bf16[16,16,512]{2,1,0:T(8,128)(2,1)}), bf16[16,16,512]{2,1,0:T(8,128)(2,1)S(1)}, u32[]{:S(2)}, u32[]{:S(2)}) async-start(bf16[16,16,512]{2,1,0:T(8,128)(2,1)} %copies.1), calls=%async_computation | async-start | bytes 524288 | tf_op jit(solution)/shard_map/all_to_all | solution.py:199
  30.3 24.1 %collective-permute-start.1 = (bf16[256,512]{1,0:T(8,128)(2,1)S(1)}, bf16[256,512]{1,0:T(8,128)(2,1)S(1)}, u32[]{:S(2)}, u32[]{:S(2)}) collective-permute-start(bf16[256,512]{1,0:T(8,128)(2,1)S(1)} %bitcast.23), channel_id=1, source_target_pairs={{0,288},{256,0},{32,256},{288,32},{1,289},{257,1},{33,257},{289,33... | collective-permute-start | bytes 786440 | tf_op jit(solution)/shard_map/ppermute | solution.py:180
  34.7 19.7 %collective-permute-start.2 = (bf16[256,512]{1,0:T(8,128)(2,1)S(1)}, bf16[256,512]{1,0:T(8,128)(2,1)S(1)}, u32[]{:S(2)}, u32[]{:S(2)}) collective-permute-start(bf16[256,512]{1,0:T(8,128)(2,1)S(1)} %bitcast.24), channel_id=1, source_target_pairs={{0,32},{256,288},{32,0},{288,256},{1,33},{257,289},{33,1},{289,257... | collective-permute-start | bytes 786440 | tf_op jit(solution)/shard_map/ppermute | solution.py:180
  37.1 17.3 %collective-permute-start = (bf16[256,512]{1,0:T(8,128)(2,1)S(1)}, bf16[256,512]{1,0:T(8,128)(2,1)S(1)}, u32[]{:S(2)}, u32[]{:S(2)}) collective-permute-start(bf16[256,512]{1,0:T(8,128)(2,1)S(1)} %bitcast.25), channel_id=1, source_target_pairs={{0,256},{256,32},{32,288},{288,0},{1,257},{257,33},{33,289},{289,1... | collective-permute-start | bytes 786440 | tf_op jit(solution)/shard_map/ppermute | solution.py:180
  39.7 51.5 %all-to-all-start.1 = ((bf16[64,4,1024]{2,1,0:T(4,128)(2,1)}), bf16[64,4,1024]{2,1,0:T(4,128)(2,1)}, u32[]{:S(2)}, u32[]{:S(2)}) async-start(bf16[64,4,1024]{2,1,0:T(4,128)(2,1)} %reshape_reshape.3), calls=%async_computation.1 | async-start | bytes 1048576 | tf_op jit(solution)/shard_map/all_to_all | solution.py:202
  54.7 13.7 %collective-permute-start.5 = (bf16[2,256,384]{2,1,0:T(8,128)(2,1)S(1)}, bf16[2,256,384]{2,1,0:T(8,128)(2,1)S(1)}, u32[]{:S(2)}, u32[]{:S(2)}) collective-permute-start(bf16[2,256,384]{2,1,0:T(8,128)(2,1)S(1)} %pad_maximum_fusion.2.refs_0_), channel_id=1, source_target_pairs={{0,128},{64,192},{128,0},{192,64},{1,129},{65,193},{129,1},{193,65... | collective-permute-start | bytes 1179656 | tf_op jit(solution)/shard_map/ppermute | solution.py:180
  59.5 18.1 %collective-permute-start.6 = (bf16[2,256,384]{2,1,0:T(8,128)(2,1)S(1)}, bf16[2,256,384]{2,1,0:T(8,128)(2,1)S(1)}, u32[]{:S(2)}, u32[]{:S(2)}) collective-permute-start(bf16[2,256,384]{2,1,0:T(8,128)(2,1)S(1)} %pad_maximum_fusion.2.refs_0_), channel_id=1, source_target_pairs={{0,64},{64,128},{128,192},{192,0},{1,65},{65,129},{129,193},{193,1... | collective-permute-start | bytes 1179656 | tf_op jit(solution)/shard_map/ppermute | solution.py:180
  61.8 15.8 %collective-permute-start.3 = (bf16[2,256,384]{2,1,0:T(8,128)(2,1)S(1)}, bf16[2,256,384]{2,1,0:T(8,128)(2,1)S(1)}, u32[]{:S(2)}, u32[]{:S(2)}) collective-permute-start(bf16[2,256,384]{2,1,0:T(8,128)(2,1)S(1)} %pad_maximum_fusion.2.refs_0_), channel_id=1, source_target_pairs={{0,192},{64,0},{128,64},{192,128},{1,193},{65,1},{129,65},{193,129... | collective-permute-start | bytes 1179656 | tf_op jit(solution)/shard_map/ppermute | solution.py:180
  68.4 9.4 %collective-permute-start.7 = (bf16[2,256,384]{2,1,0:T(8,128)(2,1)S(1)}, bf16[2,256,384]{2,1,0:T(8,128)(2,1)S(1)}, u32[]{:S(2)}, u32[]{:S(2)}) collective-permute-start(bf16[2,256,384]{2,1,0:T(8,128)(2,1)S(1)} %pad_maximum_fusion.2.refs_0_), channel_id=1, source_target_pairs={{0,1},{1,0},{2,3},{3,2},{4,5},{5,4},{6,7},{7,6},{8,9},{9,8},{10,11... | collective-permute-start | bytes 1179656 | tf_op jit(solution)/shard_map/ppermute | solution.py:218
  77.8 14.5 %collective-permute-start.8 = (bf16[6,256,384]{2,1,0:T(8,128)(2,1)S(1)}, bf16[6,256,384]{2,1,0:T(8,128)(2,1)}, u32[]{:S(2)}, u32[]{:S(2)}) collective-permute-start(bf16[6,256,384]{2,1,0:T(8,128)(2,1)S(1)} %pad_maximum_fusion.refs_1_), channel_id=1, source_target_pairs={{0,1},{1,0},{2,3},{3,2},{4,5},{5,4},{6,7},{7,6},{8,9},{9,8},{10,11... | collective-permute-start | bytes 3538952 | tf_op jit(solution)/shard_map/ppermute | solution.py:218
  80.6 11.8 %copy-start.3 = (f32[1024]{0:T(1024)S(1)}, f32[1024]{0:T(1024)}, u32[]{:S(2)}) copy-start(f32[1024]{0:T(1024)} %param.7) | copy-start | bytes 12292
  80.6 11.8 %copy-start.4 = (s32[8]{0:T(128)S(1)}, s32[8]{0:T(128)}, u32[]{:S(2)}) copy-start(s32[8]{0:T(128)} %reach_ref.2) | copy-start | bytes 100
  80.7 34.4 %collective-permute-start.10 = (bf16[2,256,640]{2,1,0:T(8,128)(2,1)S(1)}, bf16[2,256,640]{2,1,0:T(8,128)(2,1)}, u32[]{:S(2)}, u32[]{:S(2)}) collective-permute-start(bf16[2,256,640]{2,1,0:T(8,128)(2,1)S(1)} %pad_maximum_fusion.1.refs_0_), channel_id=1, source_target_pairs={{0,64},{64,128},{128,192},{192,0},{1,65},{65,129},{129,193},{193,1... | collective-permute-start | bytes 1966088 | tf_op jit(solution)/shard_map/ppermute | solution.py:180
  83.7 31.5 %collective-permute-start.9 = (bf16[2,256,640]{2,1,0:T(8,128)(2,1)S(1)}, bf16[2,256,640]{2,1,0:T(8,128)(2,1)}, u32[]{:S(2)}, u32[]{:S(2)}) collective-permute-start(bf16[2,256,640]{2,1,0:T(8,128)(2,1)S(1)} %pad_maximum_fusion.1.refs_0_), channel_id=1, source_target_pairs={{0,128},{64,192},{128,0},{192,64},{1,129},{65,193},{129,1},{193,65... | collective-permute-start | bytes 1966088 | tf_op jit(solution)/shard_map/ppermute | solution.py:180
  88.1 28.4 %collective-permute-start.4 = (bf16[2,256,640]{2,1,0:T(8,128)(2,1)S(1)}, bf16[2,256,640]{2,1,0:T(8,128)(2,1)}, u32[]{:S(2)}, u32[]{:S(2)}) collective-permute-start(bf16[2,256,640]{2,1,0:T(8,128)(2,1)S(1)} %pad_maximum_fusion.1.refs_0_), channel_id=1, source_target_pairs={{0,192},{64,0},{128,64},{192,128},{1,193},{65,1},{129,65},{193,129... | collective-permute-start | bytes 1966088 | tf_op jit(solution)/shard_map/ppermute | solution.py:180
  92.4 33.4 %copy-start.5 = (s32[8]{0:T(128)S(1)}, s32[8]{0:T(128)}, u32[]{:S(2)}) copy-start(s32[8]{0:T(128)} %reach_ref.3) | copy-start | bytes 100
  96.2 29.6 %copy-start = (bf16[1,1,256,1024]{3,2,1,0:T(8,128)(2,1)S(1)}, bf16[1,1,256,1024]{3,2,1,0:T(8,128)(2,1)}, u32[]{:S(2)}) copy-start(bf16[1,1,256,1024]{3,2,1,0:T(8,128)(2,1)} %param.6) | copy-start | bytes 1572868
  97.0 39.5 %all-to-all-start.2 = ((bf16[64,4,512]{2,1,0:T(4,128)(2,1)}), bf16[64,4,512]{2,1,0:T(4,128)(2,1)S(1)}, u32[]{:S(2)}, u32[]{:S(2)}) async-start(bf16[64,4,512]{2,1,0:T(4,128)(2,1)} %reshape.27), calls=%async_computation.2 | async-start | bytes 524288 | tf_op jit(solution)/shard_map/all_to_all | solution.py:229
  112.7 11.2 %collective-permute-start.11 = (bf16[2,256,640]{2,1,0:T(8,128)(2,1)S(1)}, bf16[2,256,640]{2,1,0:T(8,128)(2,1)S(1)}, u32[]{:S(2)}, u32[]{:S(2)}) collective-permute-start(bf16[2,256,640]{2,1,0:T(8,128)(2,1)S(1)} %pad_maximum_fusion.1.refs_0_), channel_id=1, source_target_pairs={{0,1},{1,0},{2,3},{3,2},{4,5},{5,4},{6,7},{7,6},{8,9},{9,8},{10,11... | collective-permute-start | bytes 1966088 | tf_op jit(solution)/shard_map/ppermute | solution.py:218
  116.5 7.4 %collective-permute-start.12 = (bf16[2,256,640]{2,1,0:T(8,128)(2,1)}, bf16[2,256,640]{2,1,0:T(8,128)(2,1)S(1)}, u32[]{:S(2)}, u32[]{:S(2)}) collective-permute-start(bf16[2,256,640]{2,1,0:T(8,128)(2,1)} %collective-permute-done.4.refs_1_), channel_id=1, source_target_pairs={{0,1},{1,0},{2,3},{3,2},{4,5},{5,4},{6,7},{7,6},{8,9},{9,8},{10,11... | collective-permute-start | bytes 1966088 | tf_op jit(solution)/shard_map/ppermute | solution.py:218
  119.5 4.4 %collective-permute-start.13 = (bf16[2,256,640]{2,1,0:T(8,128)(2,1)}, bf16[2,256,640]{2,1,0:T(8,128)(2,1)S(1)}, u32[]{:S(2)}, u32[]{:S(2)}) collective-permute-start(bf16[2,256,640]{2,1,0:T(8,128)(2,1)} %collective-permute-done.9.refs_2_), channel_id=1, source_target_pairs={{0,1},{1,0},{2,3},{3,2},{4,5},{5,4},{6,7},{7,6},{8,9},{9,8},{10,11... | collective-permute-start | bytes 1966088 | tf_op jit(solution)/shard_map/ppermute | solution.py:218
  121.4 4.3 %collective-permute-start.14 = (bf16[2,256,640]{2,1,0:T(8,128)(2,1)}, bf16[2,256,640]{2,1,0:T(8,128)(2,1)S(1)}, u32[]{:S(2)}, u32[]{:S(2)}) collective-permute-start(bf16[2,256,640]{2,1,0:T(8,128)(2,1)} %collective-permute-done.10.refs_3_), channel_id=1, source_target_pairs={{0,1},{1,0},{2,3},{3,2},{4,5},{5,4},{6,7},{7,6},{8,9},{9,8},{10,11... | collective-permute-start | bytes 1966088 | tf_op jit(solution)/shard_map/ppermute | solution.py:218
  130.7 1.0 copy-start.1
  131.7 4.9 %copy-start.2 = (bf16[512,1024]{1,0:T(8,128)(2,1)S(1)}, bf16[512,1024]{1,0:T(8,128)(2,1)}, u32[]{:S(2)}) copy-start(bf16[512,1024]{1,0:T(8,128)(2,1)} %copy-done.1) | copy-start | bytes 3145732
